TPU v7x, 32 devices: a whole 2x2x4 slice. The times are simulated.
32 devices in a mesh: groups: 2 (over y), expert: 8 (over z, core), replica: 2 (over x).
Axes of the slice: x: 2, y: 2, z: 4, core: 2. Of those that a mesh axis runs over, the one named last changes fastest.
Arguments:
- hidden_in: bfloat16 [2048, 2048], P(('groups', 'expert'), 'replica'), parts along dimension 0, may hold values from -6 to 6
- routes: int32 [2048, 8], P(('groups', 'expert')), parts along dimension 0, may hold values from 0 to 15, all different within a row; in each aligned block of 128 rows (0 to 127, 128 to 255, ...) at most 128 rows name the same one
- route_gain: float32 [2048, 8], P(('groups', 'expert')), parts along dimension 0, may hold values from 0.1 to 1
- w_in: bfloat16 [16, 2048, 768], P('expert', 'replica'), may hold values from -0.125 to 0.125
- w_out: bfloat16 [16, 384, 2048], P('expert', None, 'replica'), may hold values from -0.3125 to 0.3125
- handoff: bfloat16 [2048, 1024], P('replica'), may hold values from -0.125 to 0.125
- speaking: int32 [2048], P(('groups', 'expert')), parts along dimension 0, may hold values 0 or 1
- talker_routes: int32 [2048, 8], P(('groups', 'expert')), parts along dimension 0, may hold values from 0 to 15, all different within a row; in each aligned block of 128 rows (0 to 127, 128 to 255, ...) at most 96 rows name the same one
- talker_gain: float32 [2048, 8], P(('groups', 'expert')), parts along dimension 0, may hold values from 0.1 to 1
- talker_w_in: bfloat16 [16, 1024, 768], P('expert', 'replica'), may hold values from -0.1875 to 0.1875
- talker_w_out: bfloat16 [16, 384, 1024], P('expert', None, 'replica'), may hold values from -0.3125 to 0.3125
Outputs:
- thinker_out: bfloat16 [2048, 2048], P(('groups', 'expert'), 'replica'), parts along dimension 0
- talker_out: bfloat16 [2048, 1024], P(('groups', 'expert'), 'replica'), parts along dimension 0
There are 2 independent parts, one for each index of `groups`. A program takes and returns all parts, laid end to end along the dimension named above; an argument that names none is the same for every part. Nothing has to cross between parts.
Inputs may be any that keep to these rules, and one draw needn't show every extreme that they name: `routes`: each row names 8 different experts; in the 128 rows of one index of expert no expert is named more than 128 times, a bound that some block reaches. `talker_routes`: each row names 8 different experts; in the 128 rows of one index of expert no expert is named more than 96 times, a bound that some block reaches.
All inputs are finite; a program needn't handle non-finite values. No bound on the sum of `speaking` on one device may be relied on, other than what follows from the above.
Results may differ from a plain program's by a relative error of at most 0.04.
Values may be sent and summed in bfloat16 or wider, within the bound.
No kernel may reach another device: no remote copies, remote signals or barrier semaphores. Data moves between devices by JAX's collectives and lax.ppermute only.
A program may use at most 64 MiB of HBM per device.

v0:
```python
import jax
import jax.numpy as jnp
from jax import lax
from jax.sharding import PartitionSpec as P


def place_rows(tok_rows, flat_ids, live_rows, experts, capacity):
    onehot = (flat_ids[:, None] == lax.iota(jnp.int32, experts)[None, :]).astype(
        jnp.int32
    ) * live_rows[:, None]
    before = jnp.cumsum(onehot, axis=0) - onehot
    slot_rank = jnp.sum(before * onehot, axis=1)
    slot_index = jnp.where(live_rows > 0, flat_ids * capacity + slot_rank, experts * capacity)
    buffer = (
        jnp.zeros((experts * capacity, tok_rows.shape[1]), tok_rows.dtype)
        .at[slot_index]
        .set(tok_rows, mode="drop")
    )
    return (buffer, slot_index)


def activate(gate_sum, up_sum):
    return (jax.nn.silu(gate_sum) * up_sum).astype(jnp.bfloat16)


def down_rows(second_weights, piece):
    return jnp.einsum("lrf,lfd->lrd", piece, second_weights, preferred_element_type=jnp.float32)


def on_device(
    hidden_in,
    routes,
    route_gain,
    w_in,
    w_out,
    handoff,
    speaking,
    talker_routes,
    talker_gain,
    talker_w_in,
    talker_w_out,
):
    owners = lax.axis_size("expert")
    token_count, top_count = routes.shape
    local_experts = w_in.shape[0]
    experts = local_experts * owners
    capacity = max(2, token_count * top_count * 2 // experts)
    talker_capacity = max(2, capacity * 3 // 4)
    flat_ids = routes.reshape(-1)
    all_rows = jnp.ones_like(flat_ids)
    spread = jnp.repeat(hidden_in, top_count, axis=0)
    buffer, slot_index = place_rows(spread, flat_ids, all_rows, experts, capacity)
    arrived = lax.all_to_all(
        buffer.reshape(owners, local_experts, capacity, -1),
        "expert",
        split_axis=0,
        concat_axis=2,
        tiled=True,
    )
    partial_value = jnp.einsum("lrd,ldf->lrf", arrived[0], w_in, preferred_element_type=jnp.float32)
    hidden_width = w_in.shape[2] // 2
    share_sum = lax.psum_scatter(
        partial_value.astype(jnp.bfloat16), "replica", scatter_dimension=1, tiled=True
    ).astype(jnp.float32)
    hidden = activate(share_sum[:, :, :hidden_width], share_sum[:, :, hidden_width:])
    expert_out = down_rows(w_out, lax.all_gather(hidden, "replica", axis=1, tiled=True))
    returned = lax.all_to_all(
        expert_out.astype(jnp.bfloat16)[None], "expert", split_axis=2, concat_axis=0, tiled=True
    )
    returned = returned.reshape(experts * capacity, -1)
    picked = returned[slot_index].astype(jnp.float32).reshape(token_count, top_count, -1)
    thinker_out = jnp.sum(picked * route_gain[:, :, None], axis=1).astype(jnp.bfloat16)
    handoff_terms = jnp.dot(thinker_out, handoff, preferred_element_type=jnp.float32)
    talker_in = lax.psum_scatter(
        handoff_terms.astype(jnp.bfloat16), "replica", scatter_dimension=1, tiled=True
    )
    talker_ids = talker_routes.reshape(-1)
    speak_rows = jnp.repeat(speaking, top_count)
    talker_spread = jnp.repeat(talker_in, top_count, axis=0)
    talker_buffer, talker_slots = place_rows(
        talker_spread, talker_ids, speak_rows, experts, talker_capacity
    )
    talker_arrived = lax.all_to_all(
        talker_buffer.reshape(owners, local_experts, talker_capacity, -1),
        "expert",
        split_axis=0,
        concat_axis=2,
        tiled=True,
    )
    talker_partial = jnp.einsum(
        "lrd,ldf->lrf", talker_arrived[0], talker_w_in, preferred_element_type=jnp.float32
    )
    talker_hidden_width = talker_w_in.shape[2] // 2
    talker_share = lax.psum_scatter(
        talker_partial.astype(jnp.bfloat16), "replica", scatter_dimension=1, tiled=True
    ).astype(jnp.float32)
    talker_hidden = activate(
        talker_share[:, :, :talker_hidden_width], talker_share[:, :, talker_hidden_width:]
    )
    talker_expert_out = down_rows(
        talker_w_out, lax.all_gather(talker_hidden, "replica", axis=1, tiled=True)
    )
    talker_returned = lax.all_to_all(
        talker_expert_out.astype(jnp.bfloat16)[None],
        "expert",
        split_axis=2,
        concat_axis=0,
        tiled=True,
    )
    talker_returned = talker_returned.reshape(experts * talker_capacity, -1)
    safe_slots = jnp.minimum(talker_slots, experts * talker_capacity - 1)
    talker_picked = (
        talker_returned[safe_slots].astype(jnp.float32).reshape(token_count, top_count, -1)
    )
    talker_weights = talker_gain * speak_rows.reshape(token_count, top_count).astype(jnp.float32)
    talker_out = jnp.sum(talker_picked * talker_weights[:, :, None], axis=1).astype(jnp.bfloat16)
    return (thinker_out, talker_out)


def solution(mesh):
    return jax.shard_map(
        on_device,
        mesh=mesh,
        in_specs=(
            P(("groups", "expert"), "replica"),
            P(("groups", "expert"), None),
            P(("groups", "expert"), None),
            P("expert", "replica", None),
            P("expert", None, "replica"),
            P("replica", None),
            P(("groups", "expert")),
            P(("groups", "expert"), None),
            P(("groups", "expert"), None),
            P("expert", "replica", None),
            P("expert", None, "replica"),
        ),
        out_specs=(P(("groups", "expert"), "replica"), P(("groups", "expert"), "replica")),
        check_vma=False,
    )
```

profile of v0, /device:TPU:0, one launch (start us, length us, event | category | flops | bytes accessed | tf_op | source)
XLA Modules:
  0.0 516.0 jit_solution(7642129837616495786)
XLA Ops:
  9.1 4.5 reduce-window.14
  14.2 8.2 %scatter_custom_fusion = bf16[2048,1024]{1,0:T(8,128)(2,1)} fusion(s32[1024]{0:T(1024)S(1)} %bitcast.92, bf16[]{:T(256)} %constant.9.clone.1, bf16[128,1024]{1,0:T(8,128)(2,1)} %param.11), kind=kCustom, calls=%fused_computation.10 | custom fusion | bytes 4456450 | tf_op jit(solution)/shard_map/scatter | solution.py:17
  22.5 100.4 %all_to_all.60 = bf16[8,2,128,1024]{3,2,1,0:T(8,128)(2,1)S(1)} all-to-all(bf16[8,2,128,1024]{3,2,1,0:T(8,128)(2,1)} %bitcast.80), channel_id=1, replica_groups=mesh['groups'=2,'expert'=8,'replica'=2] {'expert'}, dimensions={0} | all-to-all | bytes 8388608 | tf_op jit(solution)/shard_map/all_to_all | solution.py:53
  123.4 4.8 convolution_convert_fusion
  128.5 42.2 %reduce-scatter.4.cloned.1.call-done = bf16[2,512,768]{2,1,0:T(8,128)(2,1)} async-done(((bf16[2,1024,768]{2,1,0:T(8,128)(2,1)}), bf16[2,512,768]{2,1,0:T(8,128)(2,1)}) %reduce-scatter.4.cloned.1.call-update) | async-done | bytes 1572880 | tf_op jit(solution)/shard_map/reduce_scatter | solution.py:62
  173.6 27.4 %all-gather.3.cloned.1.call-done = bf16[2,1024,384]{2,1,0:T(8,128)(2,1)} async-done(((bf16[2,512,384]{2,1,0:T(8,128)(2,1)}), bf16[2,1024,384]{2,1,0:T(8,128)(2,1)}) %all-gather.3.cloned.1.call-update) | async-done | bytes 1572880 | tf_op jit(solution)/shard_map/all_gather | solution.py:66
  201.0 6.1 %convert_bitcast_fusion = bf16[1,2,1024,1024]{3,2,1,0:T(8,128)(2,1)} fusion(bf16[2,1024,384]{2,1,0:T(8,128)(2,1)} %all-gather.3.cloned.1.call-done, bf16[2,384,1024]{2,1,0:T(8,128)(2,1)} %param.15), kind=kOutput, calls=%fused_computation.6 | convolution fusion | flops 1612709888 | bytes 7340032 | tf_op jit(solution)/shard_map/lrf,lfd->lrd/dot_general | solution.py:27
  207.1 8.5 %copy.43 = bf16[1,2,1024,1024]{3,1,0,2:T(2,128)(2,1)} copy(bf16[1,2,1024,1024]{3,2,1,0:T(8,128)(2,1)} %convert_bitcast_fusion) | data formatting | bytes 8388608 | tf_op jit(solution)/shard_map/broadcast_in_dim | solution.py:68
  215.6 4.7 all-to-all-start.1
  221.3 4.5 reduce-window.16
  226.7 87.7 %all-to-all-done.1 = bf16[1,2,1024,1024]{3,1,0,2:T(2,128)(2,1)} async-done(((bf16[1,2,1024,1024]{3,1,0,2:T(2,128)(2,1)}), bf16[1,2,1024,1024]{3,1,0,2:T(2,128)(2,1)}, u32[]{:S(2)}, u32[]{:S(2)}) %all-to-all-start.1) | async-done | bytes 4194336 | tf_op jit(solution)/shard_map/all_to_all | solution.py:67
  314.4 5.5 %copy.44 = bf16[1,2,8,128,1024]{4,3,1,2,0:T(8,128)(2,1)} copy(bf16[1,2,8,128,1024]{4,1,3,2,0:T(2,128)(2,1)} %bitcast.10) | data formatting | bytes 8388608 | tf_op jit(solution)/shard_map/all_to_all | solution.py:67
  319.9 7.7 %gather_fusion = bf16[1024,1024]{1,0:T(8,128)(2,1)S(1)} fusion(bf16[2048,1024]{1,0:T(8,128)(2,1)} %bitcast.77, s32[1024]{0:T(1024)S(1)} %broadcast_clamp_fusion.1), kind=kCustom, calls=%fused_computation | custom fusion | bytes 4198400 | tf_op jit(solution)/shard_map/gather | solution.py:71
  330.6 9.6 %reduce-scatter.6.cloned.1.call-done = bf16[128,512]{1,0:T(8,128)(2,1)} async-done(((bf16[128,1024]{1,0:T(8,128)(2,1)}), bf16[128,512]{1,0:T(8,128)(2,1)}) %reduce-scatter.6.cloned.1.call-update) | async-done | bytes 131088 | tf_op jit(solution)/shard_map/reduce_scatter | solution.py:74
  340.2 5.9 %scatter_custom_fusion.1 = bf16[1536,512]{1,0:T(8,128)(2,1)S(1)} fusion(s32[1024]{0:T(1024)S(1)} %bitcast.95, bf16[]{:T(256)} %constant.9.clone.1, bf16[128,512]{1,0:T(8,128)(2,1)} %reduce-scatter.6.cloned.1.call-done), kind=kCustom, calls=%fused_computation.21 | custom fusion | bytes 1703938 | tf_op jit(solution)/shard_map/scatter | solution.py:17
  346.1 42.2 %all_to_all.61 = bf16[8,2,96,512]{3,2,1,0:T(8,128)(2,1)S(1)} all-to-all(bf16[8,2,96,512]{3,2,1,0:T(8,128)(2,1)S(1)} %bitcast.82), channel_id=1, replica_groups=mesh['groups'=2,'expert'=8,'replica'=2] {'expert'}, dimensions={0} | all-to-all | bytes 3145728 | tf_op jit(solution)/shard_map/all_to_all | solution.py:83
  389.7 2.8 convolution_convert_fusion.1
  392.8 32.5 %reduce-scatter.8.cloned.1.call-done = bf16[2,384,768]{2,1,0:T(8,128)(2,1)} async-done(((bf16[2,768,768]{2,1,0:T(8,128)(2,1)}), bf16[2,384,768]{2,1,0:T(8,128)(2,1)}) %reduce-scatter.8.cloned.1.call-update) | async-done | bytes 1179664 | tf_op jit(solution)/shard_map/reduce_scatter | solution.py:94
  428.0 22.9 %all-gather.5.cloned.1.call-done = bf16[2,768,384]{2,1,0:T(8,128)(2,1)} async-done(((bf16[2,384,384]{2,1,0:T(8,128)(2,1)}), bf16[2,768,384]{2,1,0:T(8,128)(2,1)}) %all-gather.5.cloned.1.call-update) | async-done | bytes 1179664 | tf_op jit(solution)/shard_map/all_gather | solution.py:101
  453.2 2.8 copy.52
  456.0 4.7 all-to-all-start.3
  460.8 37.7 %all-to-all-done.3 = bf16[1,2,768,512]{3,1,0,2:T(2,128)(2,1)S(1)} async-done(((bf16[1,2,768,512]{3,1,0,2:T(2,128)(2,1)}), bf16[1,2,768,512]{3,1,0,2:T(2,128)(2,1)S(1)}, u32[]{:S(2)}, u32[]{:S(2)}) %all-to-all-start.3) | async-done | bytes 1572896 | tf_op jit(solution)/shard_map/all_to_all | solution.py:103
  500.0 6.9 %gather_fusion.1 = bf16[1024,512]{1,0:T(8,128)(2,1)} fusion(bf16[1536,512]{1,0:T(8,128)(2,1)} %bitcast.78, s32[1024]{0:T(1024)S(1)} %broadcast_clamp_fusion), kind=kCustom, calls=%fused_computation.1 | custom fusion | bytes 2101248 | tf_op jit(solution)/shard_map/gather | solution.py:113
  506.9 2.6 fusion.1
  (84 shorter events, 19.2 us)
Async XLA Ops:
  7.2 116.3 %copy-start = (bf16[2,1024,768]{2,1,0:T(8,128)(2,1)S(1)}, bf16[2,1024,768]{2,1,0:T(8,128)(2,1)}, u32[]{:S(2)}) copy-start(bf16[2,1024,768]{2,1,0:T(8,128)(2,1)} %param.14) | copy-start | bytes 9437188
  7.2 163.5 %reduce-scatter.4.cloned.1.call-start = ((), (), s32[]{:S(2)}) async-start(), calls=%async_computation.7 | async-start | bytes 4718592 | tf_op jit(solution)/shard_map/reduce_scatter | solution.py:62
  128.3 72.7 %all-gather.3.cloned.1.call-start = ((), (), s32[]{:S(2)}) async-start(), calls=%async_computation.8 | async-start | bytes 2359296 | tf_op jit(solution)/shard_map/all_gather | solution.py:66
  215.6 5.0 copy-start.5
  215.6 5.3 %copy-start.6 = (f32[128,8]{0,1:T(8,128)S(1)}, f32[128,8]{0,1:T(8,128)}, u32[]{:S(2)}) copy-start(f32[128,8]{0,1:T(8,128)} %param.13) | copy-start | bytes 12292
  215.6 5.4 %copy-start.8 = (s32[128]{0:T(128)S(1)}, s32[128]{0:T(128)}, u32[]{:S(2)}) copy-start(s32[128]{0:T(128)} %param.17) | copy-start | bytes 1540
  215.6 98.8 %all-to-all-start.1 = ((bf16[1,2,1024,1024]{3,1,0,2:T(2,128)(2,1)}), bf16[1,2,1024,1024]{3,1,0,2:T(2,128)(2,1)}, u32[]{:S(2)}, u32[]{:S(2)}) async-start(bf16[1,2,1024,1024]{3,1,0,2:T(2,128)(2,1)} %copy.43), calls=%async_computation.2 | async-start | bytes 8388608 | tf_op jit(solution)/shard_map/all_to_all | solution.py:67
  220.3 119.9 %reduce-scatter.6.cloned.1.call-start = ((), (), s32[]{:S(2)}) async-start(), calls=%async_computation.9 | async-start | bytes 393216 | tf_op jit(solution)/shard_map/reduce_scatter | solution.py:74
  327.7 1.6 copy-start.2
  329.3 16.8 %copy-start.3 = (bf16[128,1024]{1,0:T(8,128)(2,1)}, bf16[128,1024]{1,0:T(8,128)(2,1)S(1)}, u32[]{:S(2)}) copy-start(bf16[128,1024]{1,0:T(8,128)(2,1)S(1)} %fusion) | copy-start | bytes 786436
  330.4 94.9 %reduce-scatter.8.cloned.1.call-start = ((), (), s32[]{:S(2)}) async-start(), calls=%async_computation.10 | async-start | bytes 3538944 | tf_op jit(solution)/shard_map/reduce_scatter | solution.py:94
  388.3 1.4 copy-start.9
  392.5 58.4 %all-gather.5.cloned.1.call-start = ((), (), s32[]{:S(2)}) async-start(), calls=%async_computation.11 | async-start | bytes 1769472 | tf_op jit(solution)/shard_map/all_gather | solution.py:101
  426.8 24.2 %copy-start.4 = (bf16[2,384,512]{2,1,0:T(8,128)(2,1)S(1)}, bf16[2,384,512]{2,1,0:T(8,128)(2,1)}, u32[]{:S(2)}) copy-start(bf16[2,384,512]{2,1,0:T(8,128)(2,1)} %param.21) | copy-start | bytes 2359300
  456.0 4.7 copy-start.7
  456.0 42.6 %all-to-all-start.3 = ((bf16[1,2,768,512]{3,1,0,2:T(2,128)(2,1)}), bf16[1,2,768,512]{3,1,0,2:T(2,128)(2,1)S(1)}, u32[]{:S(2)}, u32[]{:S(2)}) async-start(bf16[1,2,768,512]{3,1,0,2:T(2,128)(2,1)} %copy.52), calls=%async_computation.6 | async-start | bytes 3145728 | tf_op jit(solution)/shard_map/all_to_all | solution.py:103
  500.0 9.4 %copy-start.1 = (bf16[2,1024,768]{2,1,0:T(8,128)(2,1)S(1)}, bf16[2,1024,768]{2,1,0:T(8,128)(2,1)}, u32[]{:S(2)}) copy-start(bf16[2,1024,768]{2,1,0:T(8,128)(2,1)} %param.14) | copy-start | bytes 9437188
Sparse Core Ops, SparseCore 0:
  128.4 42.2 reduce-scatter.3
  173.7 27.2 all-gather.2
  330.6 9.5 reduce-scatter.5
  392.6 32.6 reduce-scatter.7
  428.1 22.7 all-gather.4
where the time goes:
time: 517 us; the launch traced here: 516 us
  waiting for transfers between devices  260 us (50%)
  blocking collectives  143 us (28%)
  local copies, waits for them, and re-layouts  52.4 us (10%)
  other arithmetic  19.5 us (4%)
  matrix products  17.1 us (3%)
  between operations  14 us (3%)
  starting transfers between devices  10.3 us (2%)
    all_to_all x1, blocking collectives, on_device(): lax.all_to_all(buffer.reshape(owners, local_experts, capacity, -1), 'expe...  100 us
    all_to_all x1, waiting for transfers between devices, on_device(): lax.all_to_all(expert_out.astype(jnp.bfloat16)[None], 'expert', split_axi...  87.7 us
    all_to_all x1, blocking collectives, on_device(): lax.all_to_all(talker_buffer.reshape(owners, local_experts, talker_capaci...  42.2 us
    reduce_scatter x1, waiting for transfers between devices, on_device(): lax.psum_scatter(partial_value.astype(jnp.bfloat16), 'replica', scatter_d...  42.2 us
    all_to_all x1, waiting for transfers between devices, on_device(): lax.all_to_all(talker_expert_out.astype(jnp.bfloat16)[None], 'expert', sp...  37.7 us
    reduce_scatter x1, waiting for transfers between devices, on_device(): lax.psum_scatter(talker_partial.astype(jnp.bfloat16), 'replica', scatter_...  32.5 us
    all_gather x1, waiting for transfers between devices, on_device(): lax.all_gather(hidden, 'replica', axis=1, tiled=True)  27.4 us
    all_gather x1, waiting for transfers between devices, on_device(): lax.all_gather(talker_hidden, 'replica', axis=1, tiled=True)  22.9 us
  transfers between devices with their start and end apart: 7, of which 7 were waited for; matrix products, arithmetic and copies ran while one was open for 1% of the time, Pallas kernels for 0%

commit v1 on v0

--- a/solution.py
+++ b/solution.py
@@ -1,7 +1,14 @@
+import functools
+
 import jax
 import jax.numpy as jnp
 from jax import lax
+from jax.experimental import pallas as pl
+from jax.experimental.pallas import tpu as pltpu
 from jax.sharding import PartitionSpec as P
+
+LANES = 128
+SWAP = [(0, 1), (1, 0)]
 
 
 def place_rows(tok_rows, flat_ids, live_rows, experts, capacity):
@@ -27,7 +34,7 @@
     return jnp.einsum("lrf,lfd->lrd", piece, second_weights, preferred_element_type=jnp.float32)
 
 
-def on_device(
+def routed_on_device(
     hidden_in,
     routes,
     route_gain,
@@ -117,6 +124,163 @@
     return (thinker_out, talker_out)
 
 
+def split_gain(ids, gain, experts):
+    hits = ids[:, :, None] == lax.iota(jnp.int32, experts)[None, None, :]
+    dense = jnp.sum(jnp.where(hits, gain[:, :, None], 0.0), axis=1)
+    high = lax.reduce_precision(dense, 8, 7)
+    return [high.astype(jnp.bfloat16), (dense - high).astype(jnp.bfloat16)]
+
+
+def expert_kernel(first_lane, experts, owner_ref, x_ref, gain_ref, first_ref, second_ref, out_ref, total):
+    step = pl.program_id(0)
+    halves, part = first_ref.shape[0], first_ref.shape[2]
+    hidden_width = first_ref.shape[3] // 2
+    out_part = second_ref.shape[3]
+    lane = lax.broadcasted_iota(jnp.int32, gain_ref.shape, 1) - (
+        first_lane + owner_ref[0] * pl.num_programs(0) + step
+    )
+    gain = jnp.sum(
+        jnp.where((lane == 0) | (lane == experts), gain_ref[...].astype(jnp.float32), 0.0),
+        axis=1,
+        keepdims=True,
+    )
+    summed = jnp.dot(x_ref[:, :part], first_ref[0, 0], preferred_element_type=jnp.float32)
+    for half in range(1, halves):
+        summed += jnp.dot(
+            x_ref[:, half * part : (half + 1) * part],
+            first_ref[half, 0],
+            preferred_element_type=jnp.float32,
+        )
+    hidden = (jax.nn.silu(summed[:, :hidden_width]) * summed[:, hidden_width:] * gain).astype(
+        jnp.bfloat16
+    )
+    for half in range(halves):
+        columns = slice(half * out_part, (half + 1) * out_part)
+        term = jnp.dot(hidden, second_ref[half, 0], preferred_element_type=jnp.float32)
+
+        @pl.when(step == 0)
+        def _():
+            total[:, columns] = term
+
+        @pl.when(step > 0)
+        def _():
+            total[:, columns] += term
+
+    @pl.when(step == pl.num_programs(0) - 1)
+    def _():
+        out_ref[...] = total[...].astype(jnp.bfloat16)
+
+
+def run_experts(owner, rows, gain_rows, gain_block, first_lane, first, second, experts):
+    count = rows.shape[0]
+    halves, local_experts, part, width = first.shape
+    hidden_width, out_part = second.shape[2:]
+    flops = 2 * count * local_experts * halves * (part * width + hidden_width * out_part)
+    return pl.pallas_call(
+        functools.partial(expert_kernel, first_lane, experts),
+        out_shape=jax.ShapeDtypeStruct((count, halves * out_part), jnp.bfloat16),
+        grid_spec=pltpu.PrefetchScalarGridSpec(
+            num_scalar_prefetch=1,
+            grid=(local_experts,),
+            in_specs=[
+                pl.BlockSpec((count, halves * part), lambda e, o: (0, 0)),
+                pl.BlockSpec((count, LANES), lambda e, o: (0, gain_block)),
+                pl.BlockSpec((halves, 1, part, width), lambda e, o: (0, e, 0, 0)),
+                pl.BlockSpec((halves, 1, hidden_width, out_part), lambda e, o: (0, e, 0, 0)),
+            ],
+            out_specs=pl.BlockSpec((count, halves * out_part), lambda e, o: (0, 0)),
+            scratch_shapes=[pltpu.VMEM((count, halves * out_part), jnp.float32)],
+        ),
+        compiler_params=pltpu.CompilerParams(vmem_limit_bytes=48 * 1024 * 1024),
+        cost_estimate=pl.CostEstimate(
+            flops=flops,
+            bytes_accessed=2 * (rows.size + first.size + second.size + count * halves * out_part),
+            transcendentals=count * local_experts * hidden_width,
+        ),
+    )(owner, rows, gain_rows, first, second)
+
+
+def both_halves(weights):
+    mine = lax.dynamic_index_in_dim(weights, lax.axis_index("groups"), 0, keepdims=False)
+    whole = lax.all_gather(mine, ("replica", "groups"))
+    return whole.reshape((lax.axis_size("replica"), lax.axis_size("groups")) + mine.shape)
+
+
+def in_order(replica, own, other, axis):
+    return jnp.concatenate(
+        [jnp.where(replica == 0, own, other), jnp.where(replica == 0, other, own)], axis=axis
+    )
+
+
+def trade(replica, array, axis):
+    size = array.shape[axis] // 2
+    own = lax.dynamic_slice_in_dim(array, replica * size, size, axis)
+    give = lax.dynamic_slice_in_dim(array, (1 - replica) * size, size, axis)
+    return own, lax.ppermute(give, "replica", SWAP)
+
+
+def dense_on_device(
+    hidden_in,
+    routes,
+    route_gain,
+    w_in,
+    w_out,
+    handoff,
+    speaking,
+    talker_routes,
+    talker_gain,
+    talker_w_in,
+    talker_w_out,
+):
+    owners = lax.axis_size("expert")
+    replica = lax.axis_index("replica")
+    owner = lax.axis_index("expert").astype(jnp.int32).reshape(1)
+    experts = w_in.shape[0] * owners
+    rows = routes.shape[0] // 2
+    first, second = both_halves(w_in), both_halves(w_out)
+    talker_first, talker_second = both_halves(talker_w_in), both_halves(talker_w_out)
+
+    def my_rows(array):
+        return lax.dynamic_slice_in_dim(array, replica * rows, rows, 0)
+
+    live = my_rows(speaking).astype(jnp.float32)[:, None]
+    gains = split_gain(my_rows(routes), my_rows(route_gain), experts) + split_gain(
+        my_rows(talker_routes), my_rows(talker_gain) * live, experts
+    )
+    gains.append(jnp.zeros((rows, LANES - 4 * experts), jnp.bfloat16))
+    own, other = trade(replica, hidden_in, 0)
+    row = jnp.concatenate([in_order(replica, own, other, 1)] + gains, axis=1)
+    gathered = lax.all_gather(row, "expert", tiled=True)
+    gain_block = row.shape[1] // LANES - 1
+    part = run_experts(owner, gathered, gathered, gain_block, 0, first, second, experts)
+    summed = lax.psum_scatter(part, "expert", scatter_dimension=0, tiled=True)
+    own, other = trade(replica, summed, 1)
+    thinker_out = in_order(replica, own, other, 0)
+    terms = jnp.dot(thinker_out, handoff, preferred_element_type=jnp.float32)
+    own, other = trade(replica, terms.astype(jnp.bfloat16), 0)
+    talker_row = (own.astype(jnp.float32) + other.astype(jnp.float32)).astype(jnp.bfloat16)
+    talker_gathered = lax.all_gather(talker_row, "expert", tiled=True)
+    talker_part = run_experts(
+        owner, talker_gathered, gathered, gain_block, 2 * experts, talker_first, talker_second, experts
+    )
+    talker_sum = lax.psum_scatter(talker_part, "expert", scatter_dimension=0, tiled=True)
+    own, other = trade(replica, talker_sum, 1)
+    return (thinker_out, in_order(replica, own, other, 0))
+
+
+def on_device(*arrays):
+    token_count, top_count = arrays[1].shape
+    local_experts = arrays[3].shape[0]
+    experts = local_experts * lax.axis_size("expert")
+    dense = (
+        token_count * top_count * 2 // experts >= token_count
+        and 4 * experts <= LANES
+        and lax.axis_size("replica") == 2
+        and lax.axis_size("groups") == local_experts
+    )
+    return (dense_on_device if dense else routed_on_device)(*arrays)
+
+
 def solution(mesh):
     return jax.shard_map(
         on_device,

time: 517 us -> 378 us (0.73)
  blocking collectives: 143 us -> 0 us
  waiting for transfers between devices: 260 us -> 307 us
  local copies, waits for them, and re-layouts: 52.4 us -> 21 us
  Pallas kernels: 0 us -> 17.7 us
  matrix products: 17.1 us -> 2.22 us
  other arithmetic: 19.5 us -> 6.93 us
    all_gather x2 -> x6, waiting for transfers between devices: 50.3 us -> 232 us  [the longest x4 180 us: both_halves(): whole = lax.all_gather(mine, ('replica', 'groups'))]
    all_to_all x2 -> x0, blocking collectives: 143 us -> none  [the longest x1 100 us: on_device(): lax.all_to_all(buffer.reshape(owners, local_experts, capacity, -1), 'expe...]
    all_to_all x2 -> x0, waiting for transfers between devices: 125 us -> none  [the longest x1 87.7 us: on_device(): lax.all_to_all(expert_out.astype(jnp.bfloat16)[None], 'expert', split_axi...]
    reduce_scatter x3 -> x2, waiting for transfers between devices: 84.2 us -> 64 us  [the longest x1 32.2 us: dense_on_device(): lax.psum_scatter(talker_part, 'expert', scatter_dimension=0, tiled=True)]
    pallas_call x0 -> x2, Pallas kernels: none -> 17.7 us  [run_experts(): pl.pallas_call(functools.partial(expert_kernel, first_lane, experts), out...]
    dot_general x5 -> x1, matrix products: 17.1 us -> 2.22 us  [dense_on_device(): terms = jnp.dot(thinker_out, handoff, preferred_element_type=jnp.float32)]
    gather x2 -> x0, local copies, waits for them, and re-layouts: 14.6 us -> none  [the longest x1 7.7 us: on_device(): returned[slot_index].astype(jnp.float32).reshape(token_count, top_count, -1)]
    scatter x2 -> x0, local copies, waits for them, and re-layouts: 14.1 us -> none  [place_rows(): buffer = jnp.zeros((experts * capacity, tok_rows.shape[1]), tok_rows.dtyp...]
  transfers between devices with their start and end apart: 7 -> 12, of which waited for: 7 -> 11; matrix products, arithmetic and copies ran while one was open for 1% -> 4% of each run, Pallas kernels for 0% -> 0%
where the time goes in v1:
time: 378 us
  waiting for transfers between devices  307 us (81%)
  local copies, waits for them, and re-layouts  21 us (6%)
  Pallas kernels  17.7 us (5%)
  between operations  14.3 us (4%)
  starting transfers between devices  8.03 us (2%)
  other arithmetic  6.93 us (2%)
    all_gather x4, waiting for transfers between devices, both_halves(): whole = lax.all_gather(mine, ('replica', 'groups'))  180 us
    reduce_scatter x1, waiting for transfers between devices, dense_on_device(): lax.psum_scatter(talker_part, 'expert', scatter_dimension=0, tiled=True)  32.2 us
    reduce_scatter x1, waiting for transfers between devices, dense_on_device(): summed = lax.psum_scatter(part, 'expert', scatter_dimension=0, tiled=True)  31.9 us
    all_gather x1, waiting for transfers between devices, dense_on_device(): gathered = lax.all_gather(row, 'expert', tiled=True)  27.8 us
    all_gather x1, waiting for transfers between devices, dense_on_device(): talker_gathered = lax.all_gather(talker_row, 'expert', tiled=True)  24.3 us
    pallas_call x2, Pallas kernels, run_experts(): pl.pallas_call(functools.partial(expert_kernel, first_lane, experts), out...  17.7 us
    ppermute x4, waiting for transfers between devices, trade(): return (own, lax.ppermute(give, 'replica', SWAP))  11.6 us
    unnamed x16, local copies, waits for them, and re-layouts  8.21 us
  transfers between devices with their start and end apart: 12, of which 11 were waited for; matrix products, arithmetic and copies ran while one was open for 4% of the time, Pallas kernels for 0%

profile of v1, /device:TPU:0, one launch (start us, length us, event | category | flops | bytes accessed | tf_op | source)
XLA Modules:
  0.0 377.7 jit_solution(15641292075810655792)
XLA Ops:
  8.3 3.0 collective-permute-start
  16.2 1.5 concatenate.9
  17.8 2.1 constant_dynamic-slice_fusion.5
  21.4 27.8 %all-gather.7.cloned.1.call-done.x_ref.gain_ref = bf16[512,2176]{1,0:T(8,128)(2,1)} async-done(((bf16[64,2176]{1,0:T(8,128)(2,1)}), bf16[512,2176]{1,0:T(8,128)(2,1)}) %all-gather.7.cloned.1.call-update) | async-done | bytes 2228240 | tf_op jit(solution)/shard_map/all_gather | solution.py:253
  49.2 45.3 %all-gather.11.cloned.1.call-done = bf16[4,384,1024]{2,1,0:T(8,128)(2,1)} async-done(((bf16[1,384,1024]{2,1,0:T(8,128)(2,1)}), bf16[4,384,1024]{2,1,0:T(8,128)(2,1)}) %all-gather.11.cloned.1.call-update) | async-done | bytes 3145744 | tf_op jit(solution)/shard_map/all_gather | solution.py:205
  94.5 72.0 %all-gather.9.cloned.1.call-done = bf16[4,1024,768]{2,1,0:T(8,128)(2,1)} async-done(((bf16[1,1024,768]{2,1,0:T(8,128)(2,1)}), bf16[4,1024,768]{2,1,0:T(8,128)(2,1)}) %all-gather.9.cloned.1.call-update) | async-done | bytes 6291472 | tf_op jit(solution)/shard_map/all_gather | solution.py:205
  166.6 1.6 copy-done.2
  168.2 11.5 %shard_map.122 = bf16[512,2048]{1,0:T(8,128)(2,1)S(1)} custom-call(s32[1]{0:T(128)} %bitcast.owner_ref, bf16[512,2176]{1,0:T(8,128)(2,1)S(1)} %copy-done.2, bf16[512,2176]{1,0:T(8,128)(2,1)S(1)} %copy-done.2, bf16[2,2,1024,768]{3,2,1,0:T(8,128)(2,1)} %bitcast.9, bf16[2,2,384,1024]{3,2,1,0:T(8,128)(2,1)} %bitcast.10), custom_call_target="tpu_custom_call" | custom-call | flops 4831838208 | bytes 13762560 | tf_op jit(solution)/shard_map/pallas_call | solution.py:179
  181.1 1.8 constant_dynamic-slice_fusion.1
  183.0 2.1 constant_dynamic-slice_fusion.2
  185.1 31.9 %reduce-scatter.3.cloned.1.call-done = bf16[64,2048]{1,0:T(8,128)(2,1)} async-done(((bf16[512,2048]{1,0:T(8,128)(2,1)}), bf16[64,2048]{1,0:T(8,128)(2,1)}) %reduce-scatter.3.cloned.1.call-update) | async-done | bytes 262160 | tf_op jit(solution)/shard_map/reduce_scatter | solution.py:256
  217.9 1.5 collective-permute-start.1
  219.4 3.5 collective-permute-done.1
  223.9 2.2 convolution_convert_fusion
  226.2 1.6 collective-permute-start.2
  227.8 5.4 %collective-permute-done.2 = bf16[64,1024]{1,0:T(8,128)(2,1)S(1)} collective-permute-done((bf16[64,1024]{1,0:T(8,128)(2,1)S(1)}, bf16[64,1024]{1,0:T(8,128)(2,1)S(1)}, u32[]{:S(2)}, u32[]{:S(2)}) %collective-permute-start.2) | collective-permute-done | bytes 131104 | tf_op jit(solution)/shard_map/ppermute | solution.py:219
  233.9 16.6 %all-gather.17.cloned.1.call-done = bf16[4,384,512]{2,1,0:T(8,128)(2,1)} async-done(((bf16[1,384,512]{2,1,0:T(8,128)(2,1)}), bf16[4,384,512]{2,1,0:T(8,128)(2,1)}) %all-gather.17.cloned.1.call-update) | async-done | bytes 1572880 | tf_op jit(solution)/shard_map/all_gather | solution.py:205
  250.5 45.7 %all-gather.15.cloned.1.call-done = bf16[4,512,768]{2,1,0:T(8,128)(2,1)} async-done(((bf16[1,512,768]{2,1,0:T(8,128)(2,1)}), bf16[4,512,768]{2,1,0:T(8,128)(2,1)}) %all-gather.15.cloned.1.call-update) | async-done | bytes 3145744 | tf_op jit(solution)/shard_map/all_gather | solution.py:205
  296.2 24.3 %all-gather.13.cloned.1.call-done.x_ref = bf16[512,1024]{1,0:T(8,128)(2,1)} async-done(((bf16[64,1024]{1,0:T(8,128)(2,1)}), bf16[512,1024]{1,0:T(8,128)(2,1)}) %all-gather.13.cloned.1.call-update) | async-done | bytes 1048592 | tf_op jit(solution)/shard_map/all_gather | solution.py:262
  320.5 1.6 copy-done.3
  324.7 6.3 %shard_map.123 = bf16[512,1024]{1,0:T(8,128)(2,1)S(1)} custom-call(s32[1]{0:T(128)} %bitcast.owner_ref, bf16[512,1024]{1,0:T(8,128)(2,1)S(1)} %copy-done.6, bf16[512,2176]{1,0:T(8,128)(2,1)S(1)} %copy-done.3, bf16[2,2,512,768]{3,2,1,0:T(8,128)(2,1)} %bitcast.8, bf16[2,2,384,512]{3,2,1,0:T(8,128)(2,1)S(1)} %bitcast.7), custom_call_target="tpu_custom_call" | custom-call | flops 2415919104 | bytes 6815744 | tf_op jit(solution)/shard_map/pallas_call | solution.py:179
  332.0 32.2 %reduce-scatter.5.cloned.1.call-done = bf16[64,1024]{1,0:T(8,128)(2,1)} async-done(((bf16[512,1024]{1,0:T(8,128)(2,1)}), bf16[64,1024]{1,0:T(8,128)(2,1)}) %reduce-scatter.5.cloned.1.call-update) | async-done | bytes 131088 | tf_op jit(solution)/shard_map/reduce_scatter | solution.py:266
  365.0 1.6 collective-permute-start.3
  366.6 2.7 collective-permute-done.3
  (56 shorter events, 17.6 us)
Async XLA Ops:
  7.2 12.8 %copy-start = (bf16[2,1024,768]{2,1,0:T(8,128)(2,1)S(1)}, bf16[2,1024,768]{2,1,0:T(8,128)(2,1)}, u32[]{:S(2)}) copy-start(bf16[2,1024,768]{2,1,0:T(8,128)(2,1)} %param.14) | copy-start | bytes 9437188
  7.2 42.0 %all-gather.7.cloned.1.call-start = ((), (), s32[]{:S(2)}) async-start(), calls=%async_computation.2 | async-start | bytes 2506752 | tf_op jit(solution)/shard_map/all_gather | solution.py:253
  8.3 6.9 %collective-permute-start = (bf16[64,1024]{1,0:T(8,128)(2,1)S(1)}, bf16[64,1024]{1,0:T(8,128)(2,1)S(1)}, u32[]{:S(2)}, u32[]{:S(2)}) collective-permute-start(bf16[64,1024]{1,0:T(8,128)(2,1)S(1)} %constant_dynamic-slice_fusion.10), channel_id=1, source_target_pairs={{0,1},{1,0},{2,3},{3,2},{4,5},{5,4},{6,7},{7,6},{8,9},{9,8},{10,11... | collective-permute-start | bytes 393224 | tf_op jit(solution)/shard_map/ppermute | solution.py:219
  17.8 76.8 %all-gather.11.cloned.1.call-start = ((), (), s32[]{:S(2)}) async-start(), calls=%async_computation.4 | async-start | bytes 3932160 | tf_op jit(solution)/shard_map/all_gather | solution.py:205
  19.9 146.6 %all-gather.9.cloned.1.call-start = ((), (), s32[]{:S(2)}) async-start(), calls=%async_computation.3 | async-start | bytes 7864320 | tf_op jit(solution)/shard_map/all_gather | solution.py:205
  21.3 195.7 %reduce-scatter.3.cloned.1.call-start = ((), (), s32[]{:S(2)}) async-start(), calls=%async_computation.5 | async-start | bytes 2359296 | tf_op jit(solution)/shard_map/reduce_scatter | solution.py:256
  166.6 1.6 copy-start.2
  179.7 1.3 copy-start.4
  181.0 69.4 %all-gather.17.cloned.1.call-start = ((), (), s32[]{:S(2)}) async-start(), calls=%async_computation.8 | async-start | bytes 1966080 | tf_op jit(solution)/shard_map/all_gather | solution.py:205
  182.9 113.3 %all-gather.15.cloned.1.call-start = ((), (), s32[]{:S(2)}) async-start(), calls=%async_computation.7 | async-start | bytes 3932160 | tf_op jit(solution)/shard_map/all_gather | solution.py:205
  185.1 135.4 %all-gather.13.cloned.1.call-start = ((), (), s32[]{:S(2)}) async-start(), calls=%async_computation.6 | async-start | bytes 1179648 | tf_op jit(solution)/shard_map/all_gather | solution.py:262
  217.9 5.0 %collective-permute-start.1 = (bf16[64,1024]{1,0:T(8,128)(2,1)S(1)}, bf16[64,1024]{1,0:T(8,128)(2,1)S(1)}, u32[]{:S(2)}, u32[]{:S(2)}) collective-permute-start(bf16[64,1024]{1,0:T(8,128)(2,1)S(1)} %constant_dynamic-slice_fusion.4), channel_id=1, source_target_pairs={{0,1},{1,0},{2,3},{3,2},{4,5},{5,4},{6,7},{7,6},{8,9},{9,8},{10,11... | collective-permute-start | bytes 393224 | tf_op jit(solution)/shard_map/ppermute | solution.py:219
  223.9 107.1 %copy-start.7 = (bf16[128,1024]{1,0:T(8,128)(2,1)}, bf16[128,1024]{1,0:T(8,128)(2,1)S(1)}, u32[]{:S(2)}) copy-start(bf16[128,1024]{1,0:T(8,128)(2,1)S(1)} %pad_maximum_fusion) | copy-start | bytes 786436
  226.2 7.0 %collective-permute-start.2 = (bf16[64,1024]{1,0:T(8,128)(2,1)S(1)}, bf16[64,1024]{1,0:T(8,128)(2,1)S(1)}, u32[]{:S(2)}, u32[]{:S(2)}) collective-permute-start(bf16[64,1024]{1,0:T(8,128)(2,1)S(1)} %constant_dynamic-slice_fusion.3), channel_id=1, source_target_pairs={{0,1},{1,0},{2,3},{3,2},{4,5},{5,4},{6,7},{7,6},{8,9},{9,8},{10,11... | collective-permute-start | bytes 393224 | tf_op jit(solution)/shard_map/ppermute | solution.py:219
  233.9 130.3 %reduce-scatter.5.cloned.1.call-start = ((), (), s32[]{:S(2)}) async-start(), calls=%async_computation.9 | async-start | bytes 1179648 | tf_op jit(solution)/shard_map/reduce_scatter | solution.py:266
  320.5 1.6 copy-start.3
  322.1 1.4 copy-start.5
  323.5 1.2 copy-start.6
  331.0 1.0 copy-start.1
  365.0 4.3 %collective-permute-start.3 = (bf16[64,512]{1,0:T(8,128)(2,1)S(1)}, bf16[64,512]{1,0:T(8,128)(2,1)S(1)}, u32[]{:S(2)}, u32[]{:S(2)}) collective-permute-start(bf16[64,512]{1,0:T(8,128)(2,1)S(1)} %constant_dynamic-slice_fusion), channel_id=1, source_target_pairs={{0,1},{1,0},{2,3},{3,2},{4,5},{5,4},{6,7},{7,6},{8,9},{9,8},{10,11... | collective-permute-start | bytes 196616 | tf_op jit(solution)/shard_map/ppermute | solution.py:219
Sparse Core Ops, SparseCore 0:
  17.9 31.2 all-gather.6
  51.0 43.4 all-gather.10
  96.4 70.1 all-gather.8
  181.2 35.7 reduce-scatter.2
  218.7 31.7 all-gather.16
  252.2 43.9 all-gather.14
  298.3 22.0 all-gather.12
  332.1 31.9 reduce-scatter.4

commit v2 on v0

--- a/solution.py
+++ b/solution.py
@@ -1,7 +1,14 @@
+import functools
+
 import jax
 import jax.numpy as jnp
 from jax import lax
+from jax.experimental import pallas as pl
+from jax.experimental.pallas import tpu as pltpu
 from jax.sharding import PartitionSpec as P
+
+LANES = 128
+SWAP = [(0, 1), (1, 0)]
 
 
 def place_rows(tok_rows, flat_ids, live_rows, experts, capacity):
@@ -27,7 +34,7 @@
     return jnp.einsum("lrf,lfd->lrd", piece, second_weights, preferred_element_type=jnp.float32)
 
 
-def on_device(
+def routed_on_device(
     hidden_in,
     routes,
     route_gain,
@@ -117,6 +124,275 @@
     return (thinker_out, talker_out)
 
 
+def split_gain(ids, gain, experts):
+    hits = ids[:, :, None] == lax.iota(jnp.int32, experts)[None, None, :]
+    dense = jnp.sum(jnp.where(hits, gain[:, :, None], 0.0), axis=1)
+    high = lax.reduce_precision(dense, 8, 7)
+    return [high.astype(jnp.bfloat16), (dense - high).astype(jnp.bfloat16)]
+
+
+def load(pairs, sems):
+    copies = [
+        pltpu.make_async_copy(source, destination, sems.at[index])
+        for index, (source, destination) in enumerate(pairs)
+    ]
+    for copy in copies:
+        copy.start()
+    return copies
+
+
+def chunk_pairs(chunks, place, first_row=0):
+    pairs, row = [], first_row
+    for chunk in chunks:
+        pairs.append((chunk, place.at[pl.ds(row, chunk.shape[0])]))
+        row += chunk.shape[0]
+    return pairs
+
+
+def hidden_kernel(blocks, gain_blocks, near, far, first_lane, experts, where_ref, *refs):
+    refs = list(refs)
+    take = lambda count: [refs.pop(0) for _ in range(count)]
+    row_refs, gain_refs = take(blocks), take(gain_blocks)
+    (own_ref,) = take(1)
+    near_refs, far_refs = take(near), take(far)
+    (out_ref, rows, gains, weights, sems) = refs
+    width = own_ref.shape[1]
+    half_hidden = own_ref.shape[2] // 2
+    group = where_ref[1]
+    lane_refs = [ref.at[:, pl.ds(ref.shape[1] - LANES, LANES)] for ref in gain_refs or row_refs]
+    row_refs = [ref.at[:, pl.ds(0, 2 * width)] for ref in row_refs]
+    row_copies = load(
+        chunk_pairs(row_refs, rows) + chunk_pairs(lane_refs, gains), sems.at[0]
+    )
+    weight_copies = [
+        load(
+            [(own_ref.at[(group + order) % 2], weights.at[order, pl.ds(0, width)])]
+            + chunk_pairs(parts, weights.at[order], width),
+            sems.at[1 + order],
+        )
+        for order, parts in enumerate((near_refs, far_refs))
+    ]
+    for copy in row_copies:
+        copy.wait()
+    lanes = gains[...].astype(jnp.float32)
+    place = lax.broadcasted_iota(jnp.int32, lanes.shape, 1) - first_lane
+    for order in range(2):
+        for copy in weight_copies[order]:
+            copy.wait()
+        offset = place - (where_ref[0] * 2 + (group + order) % 2)
+        gain = jnp.sum(
+            jnp.where((offset == 0) | (offset == experts), lanes, 0.0), axis=1, keepdims=True
+        )
+        summed = jnp.dot(
+            rows[...], weights[order], preferred_element_type=jnp.float32
+        )
+        hidden = jax.nn.silu(summed[:, :half_hidden]) * summed[:, half_hidden:] * gain
+        out_ref[:, order * half_hidden : (order + 1) * half_hidden] = hidden.astype(jnp.bfloat16)
+
+
+def run_hidden(where, row_blocks, gain_blocks, own, near, far, first_lane, experts):
+    blocks = len(row_blocks)
+    count = blocks * row_blocks[0].shape[0]
+    _, width, columns = own.shape
+    inputs = [*row_blocks, *gain_blocks, own, *near, *far]
+    kernel = functools.partial(
+        hidden_kernel, blocks, len(gain_blocks), len(near), len(far), first_lane, experts
+    )
+    return pl.pallas_call(
+        kernel,
+        out_shape=jax.ShapeDtypeStruct((count, columns), jnp.bfloat16),
+        in_specs=[pl.BlockSpec(memory_space=pltpu.SMEM)]
+        + [pl.BlockSpec(memory_space=pl.ANY)] * len(inputs),
+        out_specs=pl.BlockSpec(memory_space=pltpu.VMEM),
+        scratch_shapes=[
+            pltpu.VMEM((count, 2 * width), jnp.bfloat16),
+            pltpu.VMEM((count, LANES), jnp.bfloat16),
+            pltpu.VMEM((2, 2 * width, columns), jnp.bfloat16),
+            pltpu.SemaphoreType.DMA((3, 2 * blocks + 1 + len(near))),
+        ],
+        compiler_params=pltpu.CompilerParams(vmem_limit_bytes=48 * 1024 * 1024),
+        cost_estimate=pl.CostEstimate(
+            flops=8 * count * width * columns,
+            bytes_accessed=2 * (2 * count * width + 4 * width * columns + count * columns),
+            transcendentals=count * columns,
+        ),
+    )(where, *inputs)
+
+
+def down_kernel(near, far, where_ref, hidden_ref, *refs):
+    refs = list(refs)
+    first_refs = [refs.pop(0) for _ in range(near)]
+    second_refs = [refs.pop(0) for _ in range(far)]
+    mine_ref, away_ref, weights, sems = refs
+    depth = weights.shape[0] // 2
+    if near == 1 and far == 0:
+        (local_ref,) = first_refs
+        first_refs = [local_ref.at[where_ref[1]]]
+        second_refs = [local_ref.at[1 - where_ref[1]]]
+    copies = load(
+        chunk_pairs(first_refs, weights) + chunk_pairs(second_refs, weights, depth), sems
+    )
+    for copy in copies:
+        copy.wait()
+    rows = mine_ref.shape[0]
+    for half, out_ref in enumerate((mine_ref, away_ref)):
+        out_ref[...] = jnp.dot(
+            hidden_ref[half * rows : (half + 1) * rows, :],
+            weights[...],
+            preferred_element_type=jnp.float32,
+        ).astype(jnp.bfloat16)
+
+
+def run_down(where, hidden, near, far):
+    count, depth = hidden.shape
+    columns = near[0].shape[-1]
+    inputs = [*near, *far]
+    shape = jax.ShapeDtypeStruct((count // 2, columns), jnp.bfloat16)
+    return pl.pallas_call(
+        functools.partial(down_kernel, len(near), len(far)),
+        out_shape=(shape, shape),
+        in_specs=[
+            pl.BlockSpec(memory_space=pltpu.SMEM),
+            pl.BlockSpec(memory_space=pltpu.VMEM),
+        ]
+        + [pl.BlockSpec(memory_space=pl.ANY)] * len(inputs),
+        out_specs=(pl.BlockSpec(memory_space=pltpu.VMEM),) * 2,
+        scratch_shapes=[
+            pltpu.VMEM((depth, columns), jnp.bfloat16),
+            pltpu.SemaphoreType.DMA((max(2, len(inputs)),)),
+        ],
+        compiler_params=pltpu.CompilerParams(vmem_limit_bytes=48 * 1024 * 1024),
+        cost_estimate=pl.CostEstimate(
+            flops=2 * count * depth * columns,
+            bytes_accessed=2 * (count * depth + depth * columns + count * columns),
+            transcendentals=0,
+        ),
+    )(where, hidden, *inputs)
+
+
+def over_replica(array):
+    return lax.ppermute(array, "replica", SWAP)
+
+
+def over_groups(array):
+    return lax.ppermute(array, "groups", SWAP)
+
+
+def over_expert(array, distance):
+    return lax.ppermute(
+        array, "expert", [(at, at ^ distance) for at in range(lax.axis_size("expert"))]
+    )
+
+
+def fetch_halves(named, chunk_rows):
+    group = lax.axis_index("groups")
+    arrived, result = [], []
+    for weights in named:
+        near, far = [], []
+        for row in range(0, weights.shape[1], chunk_rows(weights)):
+            piece = lax.dynamic_slice(
+                weights, (group, row, 0), (1, chunk_rows(weights), weights.shape[2])
+            )[0]
+            if len(arrived) > 1:
+                piece, _ = lax.optimization_barrier((piece, arrived[-2]))
+            near.append(over_replica(piece))
+            arrived.append(near[-1])
+            far.append(over_groups(near[-1]))
+        result.append((near, far))
+    return result
+
+
+def gather_rows(row):
+    owners = lax.axis_size("expert")
+    same = [row] + [over_expert(row, distance) for distance in range(2, owners, 2)]
+    return same + [over_expert(block, 1) for block in same]
+
+
+def scatter_sums(mine, away):
+    owners = lax.axis_size("expert")
+    rows = mine.shape[0] // (owners // 2)
+    other = over_expert(away, 1)
+    total = None
+    for index in range(owners // 2 - 1, -1, -1):
+        part = slice(index * rows, (index + 1) * rows)
+        chip = mine[part].astype(jnp.float32) + other[part].astype(jnp.float32)
+        if index:
+            chip = over_expert(chip.astype(jnp.bfloat16), 2 * index).astype(jnp.float32)
+        total = chip if total is None else total + chip
+    return total.astype(jnp.bfloat16)
+
+
+def in_order(replica, own, other, axis):
+    return jnp.concatenate(
+        [jnp.where(replica == 0, own, other), jnp.where(replica == 0, other, own)], axis=axis
+    )
+
+
+def dense_on_device(
+    hidden_in,
+    routes,
+    route_gain,
+    w_in,
+    w_out,
+    handoff,
+    speaking,
+    talker_routes,
+    talker_gain,
+    talker_w_in,
+    talker_w_out,
+):
+    replica = lax.axis_index("replica")
+    where = jnp.stack([lax.axis_index("expert"), lax.axis_index("groups")]).astype(jnp.int32)
+    experts = w_in.shape[0] * lax.axis_size("expert")
+    rows = routes.shape[0] // 2
+
+    def my_rows(array):
+        return lax.dynamic_slice_in_dim(array, replica * rows, rows, 0)
+
+    other = over_replica(lax.dynamic_slice_in_dim(hidden_in, (1 - replica) * rows, rows, 0))
+    chunk_rows = lambda weights: min(weights.shape[1], 384 * 512 // weights.shape[2])
+    fetched = fetch_halves((w_in, w_out, talker_w_in, talker_w_out), chunk_rows)
+    live = my_rows(speaking).astype(jnp.float32)[:, None]
+    gains = split_gain(my_rows(routes), my_rows(route_gain), experts) + split_gain(
+        my_rows(talker_routes), my_rows(talker_gain) * live, experts
+    )
+    gains.append(jnp.zeros((rows, LANES - 4 * experts), jnp.bfloat16))
+    blocks = gather_rows(jnp.concatenate([my_rows(hidden_in), other] + gains, axis=1))
+    hidden = run_hidden(where, blocks, [], w_in, *fetched[0], 0, experts)
+    own = scatter_sums(*run_down(where, hidden, [w_out], []))
+    give = scatter_sums(*run_down(where, hidden, *fetched[1]))
+    got = over_replica(give)
+    thinker_out = in_order(replica, own, got, 0)
+
+    def handed(array):
+        return jnp.dot(array, handoff, preferred_element_type=jnp.float32)
+
+    term = over_replica(handed(got).astype(jnp.bfloat16))
+    talker_row = (handed(own) + term.astype(jnp.float32)).astype(jnp.bfloat16)
+    parts = jnp.split(talker_row, 2, axis=1)
+    talker_row = in_order(replica, parts[0], parts[1], 1)
+    talker_blocks = gather_rows(talker_row)
+    hidden = run_hidden(
+        where, talker_blocks, blocks, talker_w_in, *fetched[2], 2 * experts, experts
+    )
+    own = scatter_sums(*run_down(where, hidden, [talker_w_out], []))
+    give = scatter_sums(*run_down(where, hidden, *fetched[3]))
+    return (thinker_out, in_order(replica, own, over_replica(give), 0))
+
+
+def on_device(*arrays):
+    token_count, top_count = arrays[1].shape
+    local_experts = arrays[3].shape[0]
+    experts = local_experts * lax.axis_size("expert")
+    dense = (
+        token_count * top_count * 2 // experts >= token_count
+        and 4 * experts <= LANES
+        and lax.axis_size("replica") == lax.axis_size("groups") == local_experts == 2
+        and lax.axis_size("expert") in (2, 4, 8, 16)
+    )
+    return (dense_on_device if dense else routed_on_device)(*arrays)
+
+
 def solution(mesh):
     return jax.shard_map(
         on_device,

time: 517 us -> 196 us (0.38)
  waiting for transfers between devices: 260 us -> 78.9 us
  blocking collectives: 143 us -> 0 us
  starting transfers between devices: 10.3 us -> 58.1 us
  local copies, waits for them, and re-layouts: 52.4 us -> 21.9 us
  Pallas kernels: 0 us -> 22.3 us
  matrix products: 17.1 us -> 0.98 us
  between operations: 14 us -> 1.14 us
  other arithmetic: 19.5 us -> 11.2 us
    all_to_all x2 -> x0, blocking collectives: 143 us -> none  [the longest x1 100 us: on_device(): lax.all_to_all(buffer.reshape(owners, local_experts, capacity, -1), 'expe...]
    all_to_all x2 -> x0, waiting for transfers between devices: 125 us -> none  [the longest x1 87.7 us: on_device(): lax.all_to_all(expert_out.astype(jnp.bfloat16)[None], 'expert', split_axi...]
    reduce_scatter x3 -> x0, waiting for transfers between devices: 84.2 us -> none  [the longest x1 42.2 us: on_device(): lax.psum_scatter(partial_value.astype(jnp.bfloat16), 'replica', scatter_d...]
    ppermute x0 -> x52, waiting for transfers between devices: none -> 78.9 us  [the longest x30 32.5 us: over_expert(): lax.ppermute(array, 'expert', [(at, at ^ distance) for at in range(lax.ax...]
    ppermute x0 -> x52, starting transfers between devices: none -> 58.1 us  [the longest x30 34 us: over_expert(): lax.ppermute(array, 'expert', [(at, at ^ distance) for at in range(lax.ax...]
    all_gather x2 -> x0, waiting for transfers between devices: 50.3 us -> none  [the longest x1 27.4 us: on_device(): lax.all_gather(hidden, 'replica', axis=1, tiled=True)]
    pallas_call x0 -> x6, Pallas kernels: none -> 22.3 us  [the longest x2 14.1 us: run_hidden(): pl.pallas_call(kernel, out_shape=jax.ShapeDtypeStruct((count, columns), j...]
    dot_general x5 -> x2, matrix products: 17.1 us -> 0.98 us  [handed(): return jnp.dot(array, handoff, preferred_element_type=jnp.float32)]
  transfers between devices with their start and end apart: 7 -> 52, of which waited for: 7 -> 23; matrix products, arithmetic and copies ran while one was open for 1% -> 11% of each run, Pallas kernels for 0% -> 9%
where the time goes in v2:
time: 196 us; the launch traced here: 195 us
  waiting for transfers between devices  78.9 us (40%)
  starting transfers between devices  58.1 us (30%)
  Pallas kernels  22.3 us (11%)
  local copies, waits for them, and re-layouts  21.9 us (11%)
  other arithmetic  11.2 us (6%)
    ppermute x30, starting transfers between devices, over_expert(): lax.ppermute(array, 'expert', [(at, at ^ distance) for at in range(lax.ax...  34 us
    ppermute x30, waiting for transfers between devices, over_expert(): lax.ppermute(array, 'expert', [(at, at ^ distance) for at in range(lax.ax...  32.5 us
    ppermute x13, waiting for transfers between devices, over_replica(): return lax.ppermute(array, 'replica', SWAP)  27.3 us
    ppermute x9, waiting for transfers between devices, over_groups(): return lax.ppermute(array, 'groups', SWAP)  19.1 us
    pallas_call x2, Pallas kernels, run_hidden(): pl.pallas_call(kernel, out_shape=jax.ShapeDtypeStruct((count, columns), j...  14.1 us
    ppermute x13, starting transfers between devices, over_replica(): return lax.ppermute(array, 'replica', SWAP)  13.2 us
    ppermute x9, starting transfers between devices, over_groups(): return lax.ppermute(array, 'groups', SWAP)  10.9 us
    unnamed x74, local copies, waits for them, and re-layouts  9.57 us
  transfers between devices with their start and end apart: 52, of which 23 were waited for; matrix products, arithmetic and copies ran while one was open for 11% of the time, Pallas kernels for 9%

profile of v2, /device:TPU:0, one launch (start us, length us, event | category | flops | bytes accessed | tf_op | source)
XLA Modules:
  0.0 194.6 jit_solution(11756340935813732015)
XLA Ops:
  2.5 2.9 %collective-permute-start = (bf16[64,1024]{1,0:T(8,128)(2,1)}, bf16[64,1024]{1,0:T(8,128)(2,1)S(1)}, u32[]{:S(2)}, u32[]{:S(2)}) collective-permute-start(bf16[64,1024]{1,0:T(8,128)(2,1)} %get-tuple-element.56), channel_id=1, source_target_pairs={{0,1},{1,0},{2,3},{3,2},{4,5},{5,4},{6,7},{7,6},{8,9},{9,8},{10,11... | collective-permute-start | bytes 393224 | tf_op jit(solution)/shard_map/ppermute | solution.py:274
  5.4 2.4 %dynamic-slice_bitcast_fusion.5 = (bf16[256,768]{1,0:T(8,128)(2,1)}, bf16[256,768]{1,0:T(8,128)(2,1)}, bf16[256,768]{1,0:T(8,128)(2,1)S(1)}, bf16[256,768]{1,0:T(8,128)(2,1)}) fusion(bf16[2,1024,768]{2,1,0:T(8,128)(2,1)} %refs_8_.1, s32[]{:T(128)S(6)} %select_n.66), kind=kLoop, calls=%fused_computation.8 | loop fusion | bytes 3145732 | tf_op jit(solution)/shard_map/squeeze | solution.py:293
  20.1 8.4 %collective-permute-done.9.refs_10_ = bf16[256,768]{1,0:T(8,128)(2,1)S(1)} collective-permute-done((bf16[256,768]{1,0:T(8,128)(2,1)S(1)}, bf16[256,768]{1,0:T(8,128)(2,1)S(1)}, u32[]{:S(2)}, u32[]{:S(2)}) %collective-permute-start.9) | collective-permute-done | bytes 393248 | tf_op jit(solution)/shard_map/ppermute | solution.py:274
  31.8 2.6 %collective-permute-start.2 = (bf16[64,2176]{1,0:T(8,128)(2,1)S(1)}, bf16[64,2176]{1,0:T(8,128)(2,1)S(1)}, u32[]{:S(2)}, u32[]{:S(2)}) collective-permute-start(bf16[64,2176]{1,0:T(8,128)(2,1)S(1)} %concatenate.12.refs_0_.refs_8_), channel_id=1, source_target_pairs={{0,8},{2,10},{4,12},{6,14},{8,0},{10,2},{12,4},{14,6},{1,9},{3,11}... | collective-permute-start | bytes 835592 | tf_op jit(solution)/shard_map/ppermute | solution.py:282
  34.6 6.0 %collective-permute-done.1.refs_1_.refs_9_ = bf16[64,2176]{1,0:T(8,128)(2,1)S(1)} collective-permute-done((bf16[64,2176]{1,0:T(8,128)(2,1)S(1)}, bf16[64,2176]{1,0:T(8,128)(2,1)S(1)}, u32[]{:S(2)}, u32[]{:S(2)}) %collective-permute-start.1) | collective-permute-done | bytes 278560 | tf_op jit(solution)/shard_map/ppermute | solution.py:282
  41.3 11.8 %collective-permute-done.2.refs_2_.refs_10_ = bf16[64,2176]{1,0:T(8,128)(2,1)S(1)} collective-permute-done((bf16[64,2176]{1,0:T(8,128)(2,1)S(1)}, bf16[64,2176]{1,0:T(8,128)(2,1)S(1)}, u32[]{:S(2)}, u32[]{:S(2)}) %collective-permute-start.2) | collective-permute-done | bytes 278560 | tf_op jit(solution)/shard_map/ppermute | solution.py:282
  64.7 3.8 %collective-permute-done.20.refs_0_ = bf16[192,1024]{1,0:T(8,128)(2,1)} collective-permute-done((bf16[192,1024]{1,0:T(8,128)(2,1)}, bf16[192,1024]{1,0:T(8,128)(2,1)}, u32[]{:S(2)}, u32[]{:S(2)}) %collective-permute-start.20) | collective-permute-done | bytes 393248 | tf_op jit(solution)/shard_map/ppermute | solution.py:274
  70.0 6.0 %collective-permute-done.21.refs_1_ = bf16[192,1024]{1,0:T(8,128)(2,1)} collective-permute-done((bf16[192,1024]{1,0:T(8,128)(2,1)}, bf16[192,1024]{1,0:T(8,128)(2,1)}, u32[]{:S(2)}, u32[]{:S(2)}) %collective-permute-start.21) | collective-permute-done | bytes 393248 | tf_op jit(solution)/shard_map/ppermute | solution.py:274
  77.7 2.8 %collective-permute-done.14.refs_15_ = bf16[256,768]{1,0:T(8,128)(2,1)} collective-permute-done((bf16[256,768]{1,0:T(8,128)(2,1)}, bf16[256,768]{1,0:T(8,128)(2,1)}, u32[]{:S(2)}, u32[]{:S(2)}) %collective-permute-start.14) | collective-permute-done | bytes 393248 | tf_op jit(solution)/shard_map/ppermute | solution.py:278
  80.4 8.4 %collective-permute-done.15.refs_16_ = bf16[256,768]{1,0:T(8,128)(2,1)} collective-permute-done((bf16[256,768]{1,0:T(8,128)(2,1)}, bf16[256,768]{1,0:T(8,128)(2,1)}, u32[]{:S(2)}, u32[]{:S(2)}) %collective-permute-start.15) | collective-permute-done | bytes 393248 | tf_op jit(solution)/shard_map/ppermute | solution.py:278
  94.7 7.8 %shard_map.122.hidden_ref = bf16[512,768]{1,0:T(8,128)(2,1)S(1)} custom-call(s32[2]{0:T(128)S(1)} %pad_add_fusion.where_ref, bf16[64,2176]{1,0:T(8,128)(2,1)S(1)} %concatenate.12.refs_0_.refs_8_, bf16[64,2176]{1,0:T(8,128)(2,1)S(1)} %collective-permute-done.1.refs_1_.refs_9_, bf16[64,2176]{1,0:T(8,128)(2,1)S(1)} %collective-permute-done.2.refs_2_.refs_10_, ...), custom_call_target="tpu_custom_call" | custom-call | flops 3221225472 | bytes 9175040 | tf_op jit(solution)/shard_map/pallas_call | solution.py:201
  104.1 2.7 %shard_map.124 = (bf16[256,1024]{1,0:T(8,128)(2,1)S(1)}, bf16[256,1024]{1,0:T(8,128)(2,1)S(1)}) custom-call(s32[2]{0:T(128)S(1)} %pad_add_fusion.where_ref, bf16[512,768]{1,0:T(8,128)(2,1)S(1)} %shard_map.122.hidden_ref, bf16[192,1024]{1,0:T(8,128)(2,1)} %collective-permute-done.20.refs_0_, bf16[192,1024]{1,0:T(8,128)(2,1)} %collective-permute-done.21.refs_1_, ...), custom_call_target="tpu_custom_call" | custom-call | flops 805306368 | bytes 3407872 | tf_op jit(solution)/shard_map/pallas_call | solution.py:251
  108.9 2.5 %shard_map.123 = (bf16[256,1024]{1,0:T(8,128)(2,1)S(1)}, bf16[256,1024]{1,0:T(8,128)(2,1)}) custom-call(s32[2]{0:T(128)S(1)} %pad_add_fusion.where_ref, bf16[512,768]{1,0:T(8,128)(2,1)S(1)} %shard_map.122.hidden_ref, bf16[2,384,1024]{2,1,0:T(8,128)(2,1)S(1)} %copy-done.4), custom_call_target="tpu_custom_call" | custom-call | flops 805306368 | bytes 3407872 | tf_op jit(solution)/shard_map/pallas_call | solution.py:251
  112.6 3.5 %collective-permute-start.27 = (bf16[64,1024]{1,0:T(8,128)(2,1)}, bf16[64,1024]{1,0:T(8,128)(2,1)}, u32[]{:S(2)}, u32[]{:S(2)}) collective-permute-start(bf16[64,1024]{1,0:T(8,128)(2,1)} %get-tuple-element.48), channel_id=1, source_target_pairs={{0,4},{2,6},{4,0},{6,2},{8,12},{10,14},{12,8},{14,10},{1,5},{3,7},... | collective-permute-start | bytes 393224 | tf_op jit(solution)/shard_map/ppermute | solution.py:282
  123.5 5.8 %collective-permute-done.26 = bf16[64,1024]{1,0:T(8,128)(2,1)} collective-permute-done((bf16[64,1024]{1,0:T(8,128)(2,1)}, bf16[64,1024]{1,0:T(8,128)(2,1)}, u32[]{:S(2)}, u32[]{:S(2)}) %collective-permute-start.26) | collective-permute-done | bytes 131104 | tf_op jit(solution)/shard_map/ppermute | solution.py:282
  132.9 2.5 %collective-permute-start.19 = (bf16[64,1024]{1,0:T(8,128)(2,1)S(1)}, bf16[64,1024]{1,0:T(8,128)(2,1)S(1)}, u32[]{:S(2)}, u32[]{:S(2)}) collective-permute-start(bf16[64,1024]{1,0:T(8,128)(2,1)S(1)} %get-tuple-element.45), channel_id=1, source_target_pairs={{0,4},{2,6},{4,0},{6,2},{8,12},{10,14},{12,8},{14,10},{1,5},{3,7},... | collective-permute-start | bytes 393224 | tf_op jit(solution)/shard_map/ppermute | solution.py:282
  136.6 5.2 %collective-permute-done.28 = bf16[64,1024]{1,0:T(8,128)(2,1)S(1)} collective-permute-done((bf16[64,1024]{1,0:T(8,128)(2,1)S(1)}, bf16[64,1024]{1,0:T(8,128)(2,1)S(1)}, u32[]{:S(2)}, u32[]{:S(2)}) %collective-permute-start.28) | collective-permute-done | bytes 131104 | tf_op jit(solution)/shard_map/ppermute | solution.py:274
  151.9 3.2 %collective-permute-start.30 = (bf16[64,1024]{1,0:T(8,128)(2,1)S(1)}, bf16[64,1024]{1,0:T(8,128)(2,1)S(1)}, u32[]{:S(2)}, u32[]{:S(2)}) collective-permute-start(bf16[64,1024]{1,0:T(8,128)(2,1)S(1)} %pad_maximum_fusion.1.refs_0_), channel_id=1, source_target_pairs={{0,4},{2,6},{4,0},{6,2},{8,12},{10,14},{12,8},{14,10},{1,5},{3,7},... | collective-permute-start | bytes 393224 | tf_op jit(solution)/shard_map/ppermute | solution.py:282
  159.8 5.0 %collective-permute-done.40.refs_20_ = bf16[256,768]{1,0:T(8,128)(2,1)S(1)} collective-permute-done((bf16[256,768]{1,0:T(8,128)(2,1)S(1)}, bf16[256,768]{1,0:T(8,128)(2,1)S(1)}, u32[]{:S(2)}, u32[]{:S(2)}) %collective-permute-start.40) | collective-permute-done | bytes 393248 | tf_op jit(solution)/shard_map/ppermute | solution.py:278
  167.0 6.3 %shard_map.125.hidden_ref = bf16[512,768]{1,0:T(8,128)(2,1)S(1)} custom-call(s32[2]{0:T(128)S(1)} %copy-done.23, bf16[64,1024]{1,0:T(8,128)(2,1)S(1)} %pad_maximum_fusion.1.refs_0_, bf16[64,1024]{1,0:T(8,128)(2,1)S(1)} %collective-permute-done.30.refs_1_, bf16[64,1024]{1,0:T(8,128)(2,1)S(1)} %collective-permute-done.31.refs_2_, ...), custom_call_target="tpu_custom_call" | custom-call | flops 1610612736 | bytes 4980736 | tf_op jit(solution)/shard_map/pallas_call | solution.py:201
  177.1 3.2 %collective-permute-start.50 = (bf16[64,512]{1,0:T(8,128)(2,1)S(1)}, bf16[64,512]{1,0:T(8,128)(2,1)S(1)}, u32[]{:S(2)}, u32[]{:S(2)}) collective-permute-start(bf16[64,512]{1,0:T(8,128)(2,1)S(1)} %get-tuple-element.54), channel_id=1, source_target_pairs={{0,4},{2,6},{4,0},{6,2},{8,12},{10,14},{12,8},{14,10},{1,5},{3,7},... | collective-permute-start | bytes 196616 | tf_op jit(solution)/shard_map/ppermute | solution.py:282
  180.2 2.4 %collective-permute-start.48 = (bf16[64,512]{1,0:T(8,128)(2,1)S(1)}, bf16[64,512]{1,0:T(8,128)(2,1)S(1)}, u32[]{:S(2)}, u32[]{:S(2)}) collective-permute-start(bf16[64,512]{1,0:T(8,128)(2,1)S(1)} %get-tuple-element.53), channel_id=1, source_target_pairs={{0,12},{2,14},{4,8},{6,10},{8,4},{10,6},{12,0},{14,2},{1,13},{3,15... | collective-permute-start | bytes 196616 | tf_op jit(solution)/shard_map/ppermute | solution.py:282
  184.7 2.4 %collective-permute-start.42 = (bf16[64,512]{1,0:T(8,128)(2,1)S(1)}, bf16[64,512]{1,0:T(8,128)(2,1)S(1)}, u32[]{:S(2)}, u32[]{:S(2)}) collective-permute-start(bf16[64,512]{1,0:T(8,128)(2,1)S(1)} %get-tuple-element.50), channel_id=1, source_target_pairs={{0,12},{2,14},{4,8},{6,10},{8,4},{10,6},{12,0},{14,2},{1,13},{3,15... | collective-permute-start | bytes 196616 | tf_op jit(solution)/shard_map/ppermute | solution.py:282
  190.5 3.4 %collective-permute-done.43 = bf16[64,512]{1,0:T(8,128)(2,1)S(1)} collective-permute-done((bf16[64,512]{1,0:T(8,128)(2,1)S(1)}, bf16[64,512]{1,0:T(8,128)(2,1)S(1)}, u32[]{:S(2)}, u32[]{:S(2)}) %collective-permute-start.43) | collective-permute-done | bytes 65568 | tf_op jit(solution)/shard_map/ppermute | solution.py:282
  (197 shorter events, 82.3 us)
Async XLA Ops:
  2.5 26.0 %collective-permute-start = (bf16[64,1024]{1,0:T(8,128)(2,1)}, bf16[64,1024]{1,0:T(8,128)(2,1)S(1)}, u32[]{:S(2)}, u32[]{:S(2)}) collective-permute-start(bf16[64,1024]{1,0:T(8,128)(2,1)} %get-tuple-element.56), channel_id=1, source_target_pairs={{0,1},{1,0},{2,3},{3,2},{4,5},{5,4},{6,7},{7,6},{8,9},{9,8},{10,11... | collective-permute-start | bytes 393224 | tf_op jit(solution)/shard_map/ppermute | solution.py:274
  7.8 12.2 %collective-permute-start.8 = (bf16[256,768]{1,0:T(8,128)(2,1)}, bf16[256,768]{1,0:T(8,128)(2,1)S(1)}, u32[]{:S(2)}, u32[]{:S(2)}) collective-permute-start(bf16[256,768]{1,0:T(8,128)(2,1)} %get-tuple-element.39), channel_id=1, source_target_pairs={{0,1},{1,0},{2,3},{3,2},{4,5},{5,4},{6,7},{7,6},{8,9},{9,8},{10,11... | collective-permute-start | bytes 1179656 | tf_op jit(solution)/shard_map/ppermute | solution.py:274
  7.8 20.7 %collective-permute-start.9 = (bf16[256,768]{1,0:T(8,128)(2,1)S(1)}, bf16[256,768]{1,0:T(8,128)(2,1)S(1)}, u32[]{:S(2)}, u32[]{:S(2)}) collective-permute-start(bf16[256,768]{1,0:T(8,128)(2,1)S(1)} %get-tuple-element.38), channel_id=1, source_target_pairs={{0,1},{1,0},{2,3},{3,2},{4,5},{5,4},{6,7},{7,6},{8,9},{9,8},{10,11... | collective-permute-start | bytes 1179656 | tf_op jit(solution)/shard_map/ppermute | solution.py:274
  20.1 33.5 %collective-permute-start.10 = (bf16[256,768]{1,0:T(8,128)(2,1)}, bf16[256,768]{1,0:T(8,128)(2,1)}, u32[]{:S(2)}, u32[]{:S(2)}) collective-permute-start(bf16[256,768]{1,0:T(8,128)(2,1)} %get-tuple-element.17), channel_id=1, source_target_pairs={{0,1},{1,0},{2,3},{3,2},{4,5},{5,4},{6,7},{7,6},{8,9},{9,8},{10,11... | collective-permute-start | bytes 1179656 | tf_op jit(solution)/shard_map/ppermute | solution.py:274
  28.5 25.2 %collective-permute-start.11 = (bf16[256,768]{1,0:T(8,128)(2,1)}, bf16[256,768]{1,0:T(8,128)(2,1)}, u32[]{:S(2)}, u32[]{:S(2)}) collective-permute-start(bf16[256,768]{1,0:T(8,128)(2,1)} %get-tuple-element.18), channel_id=1, source_target_pairs={{0,1},{1,0},{2,3},{3,2},{4,5},{5,4},{6,7},{7,6},{8,9},{9,8},{10,11... | collective-permute-start | bytes 1179656 | tf_op jit(solution)/shard_map/ppermute | solution.py:274
  31.8 21.3 %collective-permute-start.2 = (bf16[64,2176]{1,0:T(8,128)(2,1)S(1)}, bf16[64,2176]{1,0:T(8,128)(2,1)S(1)}, u32[]{:S(2)}, u32[]{:S(2)}) collective-permute-start(bf16[64,2176]{1,0:T(8,128)(2,1)S(1)} %concatenate.12.refs_0_.refs_8_), channel_id=1, source_target_pairs={{0,8},{2,10},{4,12},{6,14},{8,0},{10,2},{12,4},{14,6},{1,9},{3,11}... | collective-permute-start | bytes 835592 | tf_op jit(solution)/shard_map/ppermute | solution.py:282
  34.4 18.7 %collective-permute-start.3 = (bf16[64,2176]{1,0:T(8,128)(2,1)S(1)}, bf16[64,2176]{1,0:T(8,128)(2,1)S(1)}, u32[]{:S(2)}, u32[]{:S(2)}) collective-permute-start(bf16[64,2176]{1,0:T(8,128)(2,1)S(1)} %concatenate.12.refs_0_.refs_8_), channel_id=1, source_target_pairs={{0,12},{2,14},{4,8},{6,10},{8,4},{10,6},{12,0},{14,2},{1,13},{3,15... | collective-permute-start | bytes 835592 | tf_op jit(solution)/shard_map/ppermute | solution.py:282
  40.6 21.8 %collective-permute-start.12 = (bf16[256,768]{1,0:T(8,128)(2,1)}, bf16[256,768]{1,0:T(8,128)(2,1)S(1)}, u32[]{:S(2)}, u32[]{:S(2)}) collective-permute-start(bf16[256,768]{1,0:T(8,128)(2,1)} %copy-done.24), channel_id=1, source_target_pairs={{0,16},{16,0},{1,17},{17,1},{2,18},{18,2},{3,19},{19,3},{4,20},{20... | collective-permute-start | bytes 1179656 | tf_op jit(solution)/shard_map/ppermute | solution.py:278
  56.2 12.3 %collective-permute-start.20 = (bf16[192,1024]{1,0:T(8,128)(2,1)}, bf16[192,1024]{1,0:T(8,128)(2,1)}, u32[]{:S(2)}, u32[]{:S(2)}) collective-permute-start(bf16[192,1024]{1,0:T(8,128)(2,1)} %get-tuple-element.21), channel_id=1, source_target_pairs={{0,1},{1,0},{2,3},{3,2},{4,5},{5,4},{6,7},{7,6},{8,9},{9,8},{10,11... | collective-permute-start | bytes 1179656 | tf_op jit(solution)/shard_map/ppermute | solution.py:274
  57.9 18.1 %collective-permute-start.21 = (bf16[192,1024]{1,0:T(8,128)(2,1)}, bf16[192,1024]{1,0:T(8,128)(2,1)}, u32[]{:S(2)}, u32[]{:S(2)}) collective-permute-start(bf16[192,1024]{1,0:T(8,128)(2,1)} %get-tuple-element.22), channel_id=1, source_target_pairs={{0,1},{1,0},{2,3},{3,2},{4,5},{5,4},{6,7},{7,6},{8,9},{9,8},{10,11... | collective-permute-start | bytes 1179656 | tf_op jit(solution)/shard_map/ppermute | solution.py:274
  59.7 18.0 %collective-permute-start.13 = (bf16[256,768]{1,0:T(8,128)(2,1)}, bf16[256,768]{1,0:T(8,128)(2,1)}, u32[]{:S(2)}, u32[]{:S(2)}) collective-permute-start(bf16[256,768]{1,0:T(8,128)(2,1)} %copy-done.26), channel_id=1, source_target_pairs={{0,16},{16,0},{1,17},{17,1},{2,18},{18,2},{3,19},{19,3},{4,20},{20... | collective-permute-start | bytes 1179656 | tf_op jit(solution)/shard_map/ppermute | solution.py:278
  61.9 18.5 %collective-permute-start.14 = (bf16[256,768]{1,0:T(8,128)(2,1)}, bf16[256,768]{1,0:T(8,128)(2,1)}, u32[]{:S(2)}, u32[]{:S(2)}) collective-permute-start(bf16[256,768]{1,0:T(8,128)(2,1)} %collective-permute-done.10.refs_11_), channel_id=1, source_target_pairs={{0,16},{16,0},{1,17},{17,1},{2,18},{18,2},{3,19},{19,3},{4,20},{20... | collective-permute-start | bytes 1179656 | tf_op jit(solution)/shard_map/ppermute | solution.py:278
  63.2 25.7 %collective-permute-start.15 = (bf16[256,768]{1,0:T(8,128)(2,1)}, bf16[256,768]{1,0:T(8,128)(2,1)}, u32[]{:S(2)}, u32[]{:S(2)}) collective-permute-start(bf16[256,768]{1,0:T(8,128)(2,1)} %collective-permute-done.11.refs_12_), channel_id=1, source_target_pairs={{0,16},{16,0},{1,17},{17,1},{2,18},{18,2},{3,19},{19,3},{4,20},{20... | collective-permute-start | bytes 1179656 | tf_op jit(solution)/shard_map/ppermute | solution.py:278
  68.5 34.1 %collective-permute-start.22 = (bf16[192,1024]{1,0:T(8,128)(2,1)}, bf16[192,1024]{1,0:T(8,128)(2,1)S(1)}, u32[]{:S(2)}, u32[]{:S(2)}) collective-permute-start(bf16[192,1024]{1,0:T(8,128)(2,1)} %collective-permute-done.20.refs_0_), channel_id=1, source_target_pairs={{0,16},{16,0},{1,17},{17,1},{2,18},{18,2},{3,19},{19,3},{4,20},{20... | collective-permute-start | bytes 1179656 | tf_op jit(solution)/shard_map/ppermute | solution.py:278
  76.1 28.0 %collective-permute-start.23 = (bf16[192,1024]{1,0:T(8,128)(2,1)}, bf16[192,1024]{1,0:T(8,128)(2,1)S(1)}, u32[]{:S(2)}, u32[]{:S(2)}) collective-permute-start(bf16[192,1024]{1,0:T(8,128)(2,1)} %collective-permute-done.21.refs_1_), channel_id=1, source_target_pairs={{0,16},{16,0},{1,17},{17,1},{2,18},{18,2},{3,19},{19,3},{4,20},{20... | collective-permute-start | bytes 1179656 | tf_op jit(solution)/shard_map/ppermute | solution.py:278
  111.4 20.2 %collective-permute-start.16 = (bf16[256,1024]{1,0:T(8,128)(2,1)}, bf16[256,1024]{1,0:T(8,128)(2,1)}, u32[]{:S(2)}, u32[]{:S(2)}) collective-permute-start(bf16[256,1024]{1,0:T(8,128)(2,1)} %get-tuple-element.20), channel_id=1, source_target_pairs={{0,2},{2,0},{4,6},{6,4},{8,10},{10,8},{12,14},{14,12},{1,3},{3,1},... | collective-permute-start | bytes 1572872 | tf_op jit(solution)/shard_map/ppermute | solution.py:282
  116.0 13.2 %collective-permute-start.26 = (bf16[64,1024]{1,0:T(8,128)(2,1)}, bf16[64,1024]{1,0:T(8,128)(2,1)}, u32[]{:S(2)}, u32[]{:S(2)}) collective-permute-start(bf16[64,1024]{1,0:T(8,128)(2,1)} %get-tuple-element.49), channel_id=1, source_target_pairs={{0,8},{2,10},{4,12},{6,14},{8,0},{10,2},{12,4},{14,6},{1,9},{3,11}... | collective-permute-start | bytes 393224 | tf_op jit(solution)/shard_map/ppermute | solution.py:282
  117.1 12.2 %collective-permute-start.25 = (bf16[64,1024]{1,0:T(8,128)(2,1)}, bf16[64,1024]{1,0:T(8,128)(2,1)}, u32[]{:S(2)}, u32[]{:S(2)}) collective-permute-start(bf16[64,1024]{1,0:T(8,128)(2,1)} %get-tuple-element.47), channel_id=1, source_target_pairs={{0,12},{2,14},{4,8},{6,10},{8,4},{10,6},{12,0},{14,2},{1,13},{3,15... | collective-permute-start | bytes 393224 | tf_op jit(solution)/shard_map/ppermute | solution.py:282
  119.6 24.8 %collective-permute-start.38 = (bf16[256,768]{1,0:T(8,128)(2,1)}, bf16[256,768]{1,0:T(8,128)(2,1)S(1)}, u32[]{:S(2)}, u32[]{:S(2)}) collective-permute-start(bf16[256,768]{1,0:T(8,128)(2,1)} %get-tuple-element.26), channel_id=1, source_target_pairs={{0,1},{1,0},{2,3},{3,2},{4,5},{5,4},{6,7},{7,6},{8,9},{9,8},{10,11... | collective-permute-start | bytes 1179656 | tf_op jit(solution)/shard_map/ppermute | solution.py:274
  122.5 35.9 %collective-permute-start.45 = (bf16[384,512]{1,0:T(8,128)(2,1)S(1)}, bf16[384,512]{1,0:T(8,128)(2,1)S(1)}, u32[]{:S(2)}, u32[]{:S(2)}) collective-permute-start(bf16[384,512]{1,0:T(8,128)(2,1)S(1)} %dynamic-slice_bitcast_fusion), channel_id=1, source_target_pairs={{0,1},{1,0},{2,3},{3,2},{4,5},{5,4},{6,7},{7,6},{8,9},{9,8},{10,11... | collective-permute-start | bytes 1179656 | tf_op jit(solution)/shard_map/ppermute | solution.py:274
  132.9 13.0 %collective-permute-start.19 = (bf16[64,1024]{1,0:T(8,128)(2,1)S(1)}, bf16[64,1024]{1,0:T(8,128)(2,1)S(1)}, u32[]{:S(2)}, u32[]{:S(2)}) collective-permute-start(bf16[64,1024]{1,0:T(8,128)(2,1)S(1)} %get-tuple-element.45), channel_id=1, source_target_pairs={{0,4},{2,6},{4,0},{6,2},{8,12},{10,14},{12,8},{14,10},{1,5},{3,7},... | collective-permute-start | bytes 393224 | tf_op jit(solution)/shard_map/ppermute | solution.py:282
  145.9 19.0 %collective-permute-start.40 = (bf16[256,768]{1,0:T(8,128)(2,1)S(1)}, bf16[256,768]{1,0:T(8,128)(2,1)S(1)}, u32[]{:S(2)}, u32[]{:S(2)}) collective-permute-start(bf16[256,768]{1,0:T(8,128)(2,1)S(1)} %collective-permute-done.38.refs_18_), channel_id=1, source_target_pairs={{0,16},{16,0},{1,17},{17,1},{2,18},{18,2},{3,19},{19,3},{4,20},{20... | collective-permute-start | bytes 1179656 | tf_op jit(solution)/shard_map/ppermute | solution.py:278
  151.9 12.9 %collective-permute-start.30 = (bf16[64,1024]{1,0:T(8,128)(2,1)S(1)}, bf16[64,1024]{1,0:T(8,128)(2,1)S(1)}, u32[]{:S(2)}, u32[]{:S(2)}) collective-permute-start(bf16[64,1024]{1,0:T(8,128)(2,1)S(1)} %pad_maximum_fusion.1.refs_0_), channel_id=1, source_target_pairs={{0,4},{2,6},{4,0},{6,2},{8,12},{10,14},{12,8},{14,10},{1,5},{3,7},... | collective-permute-start | bytes 393224 | tf_op jit(solution)/shard_map/ppermute | solution.py:282
  158.3 15.0 %collective-permute-start.46 = (bf16[384,512]{1,0:T(8,128)(2,1)S(1)}, bf16[384,512]{1,0:T(8,128)(2,1)S(1)}, u32[]{:S(2)}, u32[]{:S(2)}) collective-permute-start(bf16[384,512]{1,0:T(8,128)(2,1)S(1)} %collective-permute-done.45.refs_0_), channel_id=1, source_target_pairs={{0,16},{16,0},{1,17},{17,1},{2,18},{18,2},{3,19},{19,3},{4,20},{20... | collective-permute-start | bytes 1179656 | tf_op jit(solution)/shard_map/ppermute | solution.py:278
  (65 other events, 852.5 us)

commit v3 on v2

--- a/solution.py
+++ b/solution.py
@@ -124,11 +124,46 @@
     return (thinker_out, talker_out)
 
 
-def split_gain(ids, gain, experts):
-    hits = ids[:, :, None] == lax.iota(jnp.int32, experts)[None, None, :]
-    dense = jnp.sum(jnp.where(hits, gain[:, :, None], 0.0), axis=1)
-    high = lax.reduce_precision(dense, 8, 7)
-    return [high.astype(jnp.bfloat16), (dense - high).astype(jnp.bfloat16)]
+def row_kernel(experts, where_ref, hidden_ref, other_ref, *refs):
+    routes_ref, gain_ref, live_ref, talker_routes_ref, talker_gain_ref = refs[:5]
+    out_ref, lanes = refs[-2:]
+    rows, width = other_ref.shape
+    first = pl.multiple_of(where_ref[2] * rows, rows)
+    out_ref[:, :width] = hidden_ref[pl.ds(first, rows), :]
+    out_ref[:, width : 2 * width] = other_ref[...]
+    stack = []
+    live = live_ref[...].astype(jnp.float32)
+    for ids, gains in ((routes_ref, gain_ref[...]), (talker_routes_ref, talker_gain_ref[...] * live)):
+        expert = lax.broadcasted_iota(jnp.int32, (experts, ids.shape[1]), 0)
+        dense = jnp.zeros(expert.shape, jnp.float32)
+        for choice in range(ids.shape[0]):
+            dense += jnp.where(
+                ids[choice : choice + 1, :] == expert, gains[choice : choice + 1, :], 0.0
+            )
+        high = dense.astype(jnp.bfloat16).astype(jnp.float32)
+        stack += [high, dense - high]
+    stack.append(jnp.zeros((LANES - 4 * experts, live.shape[1]), jnp.float32))
+    lanes[...] = jnp.concatenate(stack, axis=0).T
+    out_ref[:, 2 * width :] = lanes[pl.ds(first, rows), :].astype(jnp.bfloat16)
+
+
+def build_row(before, where, hidden_in, other, experts, routes, gain, live, talker_routes, talker_gain):
+    count = hidden_in.shape[0]
+    rows, width = other.shape
+    inputs = [hidden_in, other, routes.T, gain.T, live[None], talker_routes.T, talker_gain.T]
+    return pl.pallas_call(
+        functools.partial(row_kernel, experts),
+        out_shape=jax.ShapeDtypeStruct((rows, 2 * width + LANES), jnp.bfloat16),
+        in_specs=[pl.BlockSpec(memory_space=pltpu.SMEM)]
+        + [pl.BlockSpec(memory_space=pltpu.VMEM)] * len(inputs)
+        + [pl.BlockSpec(memory_space=pl.ANY)] * len(before),
+        out_specs=pl.BlockSpec(memory_space=pltpu.VMEM),
+        scratch_shapes=[pltpu.VMEM((count, LANES), jnp.float32)],
+        compiler_params=pltpu.CompilerParams(vmem_limit_bytes=4 * 1024 * 1024),
+        cost_estimate=pl.CostEstimate(
+            flops=64 * count * experts, bytes_accessed=8 * rows * width, transcendentals=0
+        ),
+    )(where, *inputs, *before)
 
 
 def load(pairs, sems):
@@ -149,83 +184,85 @@
     return pairs
 
 
-def hidden_kernel(blocks, gain_blocks, near, far, first_lane, experts, where_ref, *refs):
+def hidden_kernel(owners, chunks, orders, first_lane, experts, where_ref, *refs):
     refs = list(refs)
     take = lambda count: [refs.pop(0) for _ in range(count)]
-    row_refs, gain_refs = take(blocks), take(gain_blocks)
-    (own_ref,) = take(1)
-    near_refs, far_refs = take(near), take(far)
-    (out_ref, rows, gains, weights, sems) = refs
+    rows_ref, gains_ref, own_ref = take(3)
+    chunk_refs = [take(count) for count in chunks]
+    (out_ref, rows, gains, weights, sems) = refs[-5:]
     width = own_ref.shape[1]
     half_hidden = own_ref.shape[2] // 2
-    group = where_ref[1]
-    lane_refs = [ref.at[:, pl.ds(ref.shape[1] - LANES, LANES)] for ref in gain_refs or row_refs]
-    row_refs = [ref.at[:, pl.ds(0, 2 * width)] for ref in row_refs]
+    size = rows.shape[0] // owners
+    distances = [*range(0, owners, 2), *range(1, owners, 2)]
+
+    def blocks(ref, first_column, columns):
+        for distance in distances:
+            start = pl.multiple_of((where_ref[0] ^ distance) * size, size)
+            yield ref.at[pl.ds(start, size), pl.ds(first_column, columns)]
+
     row_copies = load(
-        chunk_pairs(row_refs, rows) + chunk_pairs(lane_refs, gains), sems.at[0]
-    )
-    weight_copies = [
-        load(
-            [(own_ref.at[(group + order) % 2], weights.at[order, pl.ds(0, width)])]
-            + chunk_pairs(parts, weights.at[order], width),
-            sems.at[1 + order],
-        )
-        for order, parts in enumerate((near_refs, far_refs))
-    ]
+        chunk_pairs(blocks(rows_ref, 0, 2 * width), rows)
+        + chunk_pairs(blocks(gains_ref, gains_ref.shape[1] - LANES, LANES), gains),
+        sems.at[0],
+    )
+    weight_copies = []
+    for place, order in enumerate(orders):
+        own = (own_ref.at[(where_ref[1] + order) % 2], weights.at[place, pl.ds(0, width)])
+        others = chunk_pairs(chunk_refs[place], weights.at[place], width)
+        weight_copies.append(load([own] + others, sems.at[1 + place]))
     for copy in row_copies:
         copy.wait()
     lanes = gains[...].astype(jnp.float32)
-    place = lax.broadcasted_iota(jnp.int32, lanes.shape, 1) - first_lane
-    for order in range(2):
-        for copy in weight_copies[order]:
+    lane = lax.broadcasted_iota(jnp.int32, lanes.shape, 1) - first_lane
+    for place, order in enumerate(orders):
+        for copy in weight_copies[place]:
             copy.wait()
-        offset = place - (where_ref[0] * 2 + (group + order) % 2)
+        offset = lane - (where_ref[0] * 2 + (where_ref[1] + order) % 2)
         gain = jnp.sum(
             jnp.where((offset == 0) | (offset == experts), lanes, 0.0), axis=1, keepdims=True
         )
-        summed = jnp.dot(
-            rows[...], weights[order], preferred_element_type=jnp.float32
-        )
+        summed = jnp.dot(rows[...], weights[place], preferred_element_type=jnp.float32)
         hidden = jax.nn.silu(summed[:, :half_hidden]) * summed[:, half_hidden:] * gain
-        out_ref[:, order * half_hidden : (order + 1) * half_hidden] = hidden.astype(jnp.bfloat16)
-
-
-def run_hidden(where, row_blocks, gain_blocks, own, near, far, first_lane, experts):
-    blocks = len(row_blocks)
-    count = blocks * row_blocks[0].shape[0]
+        out_ref[:, place * half_hidden : (place + 1) * half_hidden] = hidden.astype(jnp.bfloat16)
+
+
+def run_hidden(before, where, rows, gains, own, chunks, orders, first_lane, experts):
+    count = rows.shape[0]
     _, width, columns = own.shape
-    inputs = [*row_blocks, *gain_blocks, own, *near, *far]
+    places = len(orders)
+    owners = experts // own.shape[0]
+    inputs = [rows, gains, own] + [part for parts in chunks for part in parts] + before
     kernel = functools.partial(
-        hidden_kernel, blocks, len(gain_blocks), len(near), len(far), first_lane, experts
+        hidden_kernel, owners, [len(parts) for parts in chunks], orders, first_lane, experts
     )
     return pl.pallas_call(
         kernel,
-        out_shape=jax.ShapeDtypeStruct((count, columns), jnp.bfloat16),
+        out_shape=jax.ShapeDtypeStruct((count, places * columns // 2), jnp.bfloat16),
         in_specs=[pl.BlockSpec(memory_space=pltpu.SMEM)]
         + [pl.BlockSpec(memory_space=pl.ANY)] * len(inputs),
         out_specs=pl.BlockSpec(memory_space=pltpu.VMEM),
         scratch_shapes=[
             pltpu.VMEM((count, 2 * width), jnp.bfloat16),
             pltpu.VMEM((count, LANES), jnp.bfloat16),
-            pltpu.VMEM((2, 2 * width, columns), jnp.bfloat16),
-            pltpu.SemaphoreType.DMA((3, 2 * blocks + 1 + len(near))),
+            pltpu.VMEM((places, 2 * width, columns), jnp.bfloat16),
+            pltpu.SemaphoreType.DMA((1 + places, max([2 * owners] + [1 + len(c) for c in chunks]))),
         ],
-        compiler_params=pltpu.CompilerParams(vmem_limit_bytes=48 * 1024 * 1024),
+        compiler_params=pltpu.CompilerParams(vmem_limit_bytes=16 * 1024 * 1024),
         cost_estimate=pl.CostEstimate(
-            flops=8 * count * width * columns,
-            bytes_accessed=2 * (2 * count * width + 4 * width * columns + count * columns),
-            transcendentals=count * columns,
+            flops=4 * places * count * width * columns,
+            bytes_accessed=4 * width * (count + places * columns),
+            transcendentals=places * count * columns // 2,
         ),
     )(where, *inputs)
 
 
-def down_kernel(near, far, where_ref, hidden_ref, *refs):
+def down_kernel(pieces, near, far, where_ref, *refs):
     refs = list(refs)
-    first_refs = [refs.pop(0) for _ in range(near)]
-    second_refs = [refs.pop(0) for _ in range(far)]
+    take = lambda count: [refs.pop(0) for _ in range(count)]
+    hidden_refs, first_refs, second_refs = take(pieces), take(near), take(far)
     mine_ref, away_ref, weights, sems = refs
     depth = weights.shape[0] // 2
-    if near == 1 and far == 0:
+    if far == 0:
         (local_ref,) = first_refs
         first_refs = [local_ref.at[where_ref[1]]]
         second_refs = [local_ref.at[1 - where_ref[1]]]
@@ -236,38 +273,41 @@
         copy.wait()
     rows = mine_ref.shape[0]
     for half, out_ref in enumerate((mine_ref, away_ref)):
-        out_ref[...] = jnp.dot(
-            hidden_ref[half * rows : (half + 1) * rows, :],
-            weights[...],
-            preferred_element_type=jnp.float32,
-        ).astype(jnp.bfloat16)
+        total, row = None, 0
+        for ref in hidden_refs:
+            term = jnp.dot(
+                ref[half * rows : (half + 1) * rows, :],
+                weights[row : row + ref.shape[1], :],
+                preferred_element_type=jnp.float32,
+            )
+            total = term if total is None else total + term
+            row += ref.shape[1]
+        out_ref[...] = total.astype(jnp.bfloat16)
 
 
 def run_down(where, hidden, near, far):
-    count, depth = hidden.shape
+    count, depth = hidden[0].shape[0], sum(part.shape[1] for part in hidden)
     columns = near[0].shape[-1]
     inputs = [*near, *far]
     shape = jax.ShapeDtypeStruct((count // 2, columns), jnp.bfloat16)
     return pl.pallas_call(
-        functools.partial(down_kernel, len(near), len(far)),
+        functools.partial(down_kernel, len(hidden), len(near), len(far)),
         out_shape=(shape, shape),
-        in_specs=[
-            pl.BlockSpec(memory_space=pltpu.SMEM),
-            pl.BlockSpec(memory_space=pltpu.VMEM),
-        ]
+        in_specs=[pl.BlockSpec(memory_space=pltpu.SMEM)]
+        + [pl.BlockSpec(memory_space=pltpu.VMEM)] * len(hidden)
         + [pl.BlockSpec(memory_space=pl.ANY)] * len(inputs),
         out_specs=(pl.BlockSpec(memory_space=pltpu.VMEM),) * 2,
         scratch_shapes=[
             pltpu.VMEM((depth, columns), jnp.bfloat16),
             pltpu.SemaphoreType.DMA((max(2, len(inputs)),)),
         ],
-        compiler_params=pltpu.CompilerParams(vmem_limit_bytes=48 * 1024 * 1024),
+        compiler_params=pltpu.CompilerParams(vmem_limit_bytes=16 * 1024 * 1024),
         cost_estimate=pl.CostEstimate(
             flops=2 * count * depth * columns,
             bytes_accessed=2 * (count * depth + depth * columns + count * columns),
             transcendentals=0,
         ),
-    )(where, hidden, *inputs)
+    )(where, *hidden, *inputs)
 
 
 def over_replica(array):
@@ -284,31 +324,16 @@
     )
 
 
-def fetch_halves(named, chunk_rows):
-    group = lax.axis_index("groups")
-    arrived, result = [], []
-    for weights in named:
-        near, far = [], []
-        for row in range(0, weights.shape[1], chunk_rows(weights)):
-            piece = lax.dynamic_slice(
-                weights, (group, row, 0), (1, chunk_rows(weights), weights.shape[2])
-            )[0]
-            if len(arrived) > 1:
-                piece, _ = lax.optimization_barrier((piece, arrived[-2]))
-            near.append(over_replica(piece))
-            arrived.append(near[-1])
-            far.append(over_groups(near[-1]))
-        result.append((near, far))
-    return result
-
-
-def gather_rows(row):
-    owners = lax.axis_size("expert")
-    same = [row] + [over_expert(row, distance) for distance in range(2, owners, 2)]
-    return same + [over_expert(block, 1) for block in same]
-
-
-def scatter_sums(mine, away):
+def after(array, *others):
+    return lax.optimization_barrier((array, *others))[0] if others else array
+
+
+def send(weights, group, first_row, rows, *before):
+    piece = lax.dynamic_slice(weights, (group, first_row, 0), (1, rows, weights.shape[2]))[0]
+    return over_replica(after(piece, *before))
+
+
+def scatter_sums(mine, away, *before):
     owners = lax.axis_size("expert")
     rows = mine.shape[0] // (owners // 2)
     other = over_expert(away, 1)
@@ -317,7 +342,8 @@
         part = slice(index * rows, (index + 1) * rows)
         chip = mine[part].astype(jnp.float32) + other[part].astype(jnp.float32)
         if index:
-            chip = over_expert(chip.astype(jnp.bfloat16), 2 * index).astype(jnp.float32)
+            chip = after(chip.astype(jnp.bfloat16), *before)
+            chip = over_expert(chip, 2 * index).astype(jnp.float32)
         total = chip if total is None else total + chip
     return total.astype(jnp.bfloat16)
 
@@ -341,26 +367,51 @@
     talker_w_in,
     talker_w_out,
 ):
-    replica = lax.axis_index("replica")
-    where = jnp.stack([lax.axis_index("expert"), lax.axis_index("groups")]).astype(jnp.int32)
-    experts = w_in.shape[0] * lax.axis_size("expert")
+    replica, group = lax.axis_index("replica"), lax.axis_index("groups")
+    where = jnp.stack([lax.axis_index("expert"), group, replica]).astype(jnp.int32)
+    owners = lax.axis_size("expert")
+    experts = w_in.shape[0] * owners
     rows = routes.shape[0] // 2
 
-    def my_rows(array):
-        return lax.dynamic_slice_in_dim(array, replica * rows, rows, 0)
-
-    other = over_replica(lax.dynamic_slice_in_dim(hidden_in, (1 - replica) * rows, rows, 0))
-    chunk_rows = lambda weights: min(weights.shape[1], 384 * 512 // weights.shape[2])
-    fetched = fetch_halves((w_in, w_out, talker_w_in, talker_w_out), chunk_rows)
-    live = my_rows(speaking).astype(jnp.float32)[:, None]
-    gains = split_gain(my_rows(routes), my_rows(route_gain), experts) + split_gain(
-        my_rows(talker_routes), my_rows(talker_gain) * live, experts
-    )
-    gains.append(jnp.zeros((rows, LANES - 4 * experts), jnp.bfloat16))
-    blocks = gather_rows(jnp.concatenate([my_rows(hidden_in), other] + gains, axis=1))
-    hidden = run_hidden(where, blocks, [], w_in, *fetched[0], 0, experts)
+    give = lax.dynamic_slice_in_dim(hidden_in, (1 - replica) * rows, rows, 0)
+    other = over_replica(give)
+    chunk, out_chunk = w_in.shape[1] // 4, w_out.shape[1] // 2
+    near_in = [send(w_in, group, 0, chunk, give), send(w_in, group, chunk, chunk, give)]
+    row = build_row(
+        [near_in[0]],
+        where,
+        hidden_in,
+        other,
+        experts,
+        routes,
+        route_gain,
+        speaking,
+        talker_routes,
+        talker_gain,
+    )
+    gathered = lax.all_gather(row, "expert", tiled=True)
+    far_in = [over_groups(near_in[0])]
+    near_in.append(send(w_in, group, 2 * chunk, chunk, near_in[0]))
+    far_in.append(over_groups(near_in[1]))
+    near_in.append(send(w_in, group, 3 * chunk, chunk, near_in[1]))
+    far_in.append(over_groups(near_in[2]))
+    near_out = [send(w_out, group, 0, out_chunk, near_in[2], far_in[0])]
+    far_in.append(over_groups(near_in[3]))
+    near_out.append(send(w_out, group, out_chunk, out_chunk, near_in[3], far_in[1]))
+    far_out = [over_groups(near_out[0])]
+    before = [near_out[0], far_in[2]]
+    near_hidden = run_hidden(before, where, gathered, gathered, w_in, [near_in], [0], 0, experts)
+    near_talker_in = send(talker_w_in, group, 0, talker_w_in.shape[1], near_out[0], far_in[2])
+    before = [near_hidden]
+    far_hidden = run_hidden(before, where, gathered, gathered, w_in, [far_in], [1], 0, experts)
+    far_out.append(over_groups(after(near_out[1], far_hidden)))
+    hidden = [near_hidden, far_hidden]
     own = scatter_sums(*run_down(where, hidden, [w_out], []))
-    give = scatter_sums(*run_down(where, hidden, *fetched[1]))
+    give = run_down(where, hidden, near_out, far_out)
+    far_talker_in = over_groups(near_talker_in)
+    near_talker_out = send(talker_w_out, group, 0, talker_w_out.shape[1], near_talker_in)
+    give = after(scatter_sums(*give, near_talker_in), near_talker_out)
+    far_talker_out = over_groups(near_talker_out)
     got = over_replica(give)
     thinker_out = in_order(replica, own, got, 0)
 
@@ -371,13 +422,21 @@
     talker_row = (handed(own) + term.astype(jnp.float32)).astype(jnp.bfloat16)
     parts = jnp.split(talker_row, 2, axis=1)
     talker_row = in_order(replica, parts[0], parts[1], 1)
-    talker_blocks = gather_rows(talker_row)
     hidden = run_hidden(
-        where, talker_blocks, blocks, talker_w_in, *fetched[2], 2 * experts, experts
-    )
-    own = scatter_sums(*run_down(where, hidden, [talker_w_out], []))
-    give = scatter_sums(*run_down(where, hidden, *fetched[3]))
-    return (thinker_out, in_order(replica, own, over_replica(give), 0))
+        [],
+        where,
+        lax.all_gather(talker_row, "expert", tiled=True),
+        gathered,
+        talker_w_in,
+        [[near_talker_in], [far_talker_in]],
+        [0, 1],
+        2 * experts,
+        experts,
+    )
+    give = run_down(where, [hidden], [near_talker_out], [far_talker_out])
+    got = over_replica(scatter_sums(*give))
+    own = scatter_sums(*run_down(where, [after(hidden, *give)], [talker_w_out], []))
+    return (thinker_out, in_order(replica, own, got, 0))
 
 
 def on_device(*arrays):

time: 196 us -> 204 us (1.041)
  between operations: 1.14 us -> 14.4 us
  starting transfers between devices: 58.1 us -> 46.9 us
  waiting for transfers between devices: 78.9 us -> 85.7 us
  other arithmetic: 11.2 us -> 7.46 us
  Pallas kernels: 22.3 us -> 24.9 us
    ppermute x30 -> x16, starting transfers between devices: 34 us -> 19.2 us  [over_expert(): lax.ppermute(array, 'expert', [(at, at ^ distance) for at in range(lax.ax...]
    ppermute x30 -> x16, waiting for transfers between devices: 32.5 us -> 22.3 us  [over_expert(): lax.ppermute(array, 'expert', [(at, at ^ distance) for at in range(lax.ax...]
    ppermute x13 -> x12, waiting for transfers between devices: 27.3 us -> 37.2 us  [over_replica(): return lax.ppermute(array, 'replica', SWAP)]
    unnamed x74 -> x58, local copies, waits for them, and re-layouts: 9.57 us -> 16.1 us
    ppermute x9 -> x8, waiting for transfers between devices: 19.1 us -> 24.2 us  [over_groups(): return lax.ppermute(array, 'groups', SWAP)]
    convert_element_type x7 -> x4, other arithmetic: 5.29 us -> 2.25 us  [scatter_sums(): chip = after(chip.astype(jnp.bfloat16), *before)]
    ppermute x13 -> x12, starting transfers between devices: 13.2 us -> 16.2 us  [over_replica(): return lax.ppermute(array, 'replica', SWAP)]
    pallas_call x6 -> x8, Pallas kernels: 22.3 us -> 24.9 us  [the longest x3 14.1 us: run_hidden(): pl.pallas_call(kernel, out_shape=jax.ShapeDtypeStruct((count, places * co...]
  transfers between devices with their start and end apart: 52 -> 38, of which waited for: 23 -> 14; matrix products, arithmetic and copies ran while one was open for 11% -> 5% of each run, Pallas kernels for 9% -> 11%
where the time goes in v3:
time: 204 us; the launch traced here: 203 us
  waiting for transfers between devices  85.7 us (42%)
  starting transfers between devices  46.9 us (23%)
  Pallas kernels  24.9 us (12%)
  local copies, waits for them, and re-layouts  22.4 us (11%)
  between operations  14.4 us (7%)
  other arithmetic  7.46 us (4%)
    ppermute x12, waiting for transfers between devices, over_replica(): return lax.ppermute(array, 'replica', SWAP)  37.2 us
    ppermute x8, waiting for transfers between devices, over_groups(): return lax.ppermute(array, 'groups', SWAP)  24.2 us
    ppermute x16, waiting for transfers between devices, over_expert(): lax.ppermute(array, 'expert', [(at, at ^ distance) for at in range(lax.ax...  22.3 us
    ppermute x16, starting transfers between devices, over_expert(): lax.ppermute(array, 'expert', [(at, at ^ distance) for at in range(lax.ax...  19.2 us
    ppermute x12, starting transfers between devices, over_replica(): return lax.ppermute(array, 'replica', SWAP)  16.2 us
    unnamed x58, local copies, waits for them, and re-layouts  16.1 us
    pallas_call x3, Pallas kernels, run_hidden(): pl.pallas_call(kernel, out_shape=jax.ShapeDtypeStruct((count, places * co...  14.1 us
    ppermute x8, starting transfers between devices, over_groups(): return lax.ppermute(array, 'groups', SWAP)  11.3 us
  transfers between devices with their start and end apart: 38, of which 14 were waited for; matrix products, arithmetic and copies ran while one was open for 5% of the time, Pallas kernels for 11%

profile of v3, /device:TPU:0, one launch (start us, length us, event | category | flops | bytes accessed | tf_op | source)
XLA Modules:
  0.0 202.7 jit_solution(17424016918102938305)
XLA Ops:
  8.4 2.4 %dynamic-slice_bitcast_fusion.4 = (bf16[256,768]{1,0:T(8,128)(2,1)}, bf16[256,768]{1,0:T(8,128)(2,1)S(1)}, bf16[256,768]{1,0:T(8,128)(2,1)}, bf16[256,768]{1,0:T(8,128)(2,1)}) fusion(bf16[2,1024,768]{2,1,0:T(8,128)(2,1)} %refs_2_.5, s32[]{:T(128)S(6)} %select_n.47), kind=kLoop, calls=%fused_computation.7 | loop fusion | bytes 3145732 | tf_op jit(solution)/shard_map/squeeze | solution.py:332
  10.8 2.9 %collective-permute-start.1 = (bf16[256,768]{1,0:T(8,128)(2,1)}, bf16[256,768]{1,0:T(8,128)(2,1)S(1)}, u32[]{:S(2)}, u32[]{:S(2)}) collective-permute-start(bf16[256,768]{1,0:T(8,128)(2,1)} %get-tuple-element.24), channel_id=1, source_target_pairs={{0,1},{1,0},{2,3},{3,2},{4,5},{5,4},{6,7},{7,6},{8,9},{9,8},{10,11... | collective-permute-start | bytes 1179656 | tf_op jit(solution)/shard_map/ppermute | solution.py:314
  13.8 12.0 %collective-permute-done.other_ref = bf16[64,1024]{1,0:T(8,128)(2,1)S(1)} collective-permute-done((bf16[64,1024]{1,0:T(8,128)(2,1)S(1)}, bf16[64,1024]{1,0:T(8,128)(2,1)S(1)}, u32[]{:S(2)}, u32[]{:S(2)}) %collective-permute-start) | collective-permute-done | bytes 131104 | tf_op jit(solution)/shard_map/ppermute | solution.py:314
  31.2 8.5 %collective-permute-done.2.refs_4_ = bf16[256,768]{1,0:T(8,128)(2,1)S(1)} collective-permute-done((bf16[256,768]{1,0:T(8,128)(2,1)}, bf16[256,768]{1,0:T(8,128)(2,1)S(1)}, u32[]{:S(2)}, u32[]{:S(2)}) %collective-permute-start.2) | collective-permute-done | bytes 393248 | tf_op jit(solution)/shard_map/ppermute | solution.py:314
  44.9 3.2 %collective-permute-done.3.refs_5_ = bf16[256,768]{1,0:T(8,128)(2,1)S(1)} collective-permute-done((bf16[256,768]{1,0:T(8,128)(2,1)S(1)}, bf16[256,768]{1,0:T(8,128)(2,1)S(1)}, u32[]{:S(2)}, u32[]{:S(2)}) %collective-permute-start.3) | collective-permute-done | bytes 393248 | tf_op jit(solution)/shard_map/ppermute | solution.py:314
  52.1 4.5 %collective-permute-done.4.refs_6_ = bf16[256,768]{1,0:T(8,128)(2,1)} collective-permute-done((bf16[256,768]{1,0:T(8,128)(2,1)}, bf16[256,768]{1,0:T(8,128)(2,1)}, u32[]{:S(2)}, u32[]{:S(2)}) %collective-permute-start.4) | collective-permute-done | bytes 393248 | tf_op jit(solution)/shard_map/ppermute | solution.py:314
  60.7 4.4 %collective-permute-done.6.refs_7_.refs_2_ = bf16[192,1024]{1,0:T(8,128)(2,1)} collective-permute-done((bf16[192,1024]{1,0:T(8,128)(2,1)S(1)}, bf16[192,1024]{1,0:T(8,128)(2,1)}, u32[]{:S(2)}, u32[]{:S(2)}) %collective-permute-start.6) | collective-permute-done | bytes 393248 | tf_op jit(solution)/shard_map/ppermute | solution.py:314
  72.4 4.5 %shard_map.123.refs_7_.refs_0_ = bf16[512,384]{1,0:T(8,128)(2,1)S(1)} custom-call(s32[3]{0:T(128)S(1)} %pad_add_fusion.where_ref, bf16[512,2176]{1,0:T(8,128)(2,1)S(1)} %copy-done.1, bf16[512,2176]{1,0:T(8,128)(2,1)S(1)} %copy-done.1, bf16[2,1024,768]{2,1,0:T(8,128)(2,1)S(1)} %copy-done.4, bf16[256,768]{1,0:T(8,128)(2,1)S(1)} %collective-permute-done.1.refs_5_.refs_3_, ...), custom_call_target="tpu_custom_call" | custom-call | flops 1610612736 | bytes 5242880 | tf_op jit(solution)/shard_map/pallas_call | solution.py:238
  76.9 4.5 %shard_map.124.refs_1_ = bf16[512,384]{1,0:T(8,128)(2,1)S(1)} custom-call(s32[3]{0:T(128)S(1)} %pad_add_fusion.where_ref, bf16[512,2176]{1,0:T(8,128)(2,1)S(1)} %copy-done.2, bf16[512,2176]{1,0:T(8,128)(2,1)S(1)} %copy-done.2, bf16[2,1024,768]{2,1,0:T(8,128)(2,1)S(1)} %copy-done.4, bf16[256,768]{1,0:T(8,128)(2,1)S(1)} %collective-permute-done.5.refs_3_, ...), custom_call_target="tpu_custom_call" | custom-call | flops 1610612736 | bytes 5242880 | tf_op jit(solution)/shard_map/pallas_call | solution.py:238
  83.7 5.8 %collective-permute-done.16.refs_5_ = bf16[192,1024]{1,0:T(8,128)(2,1)S(1)} collective-permute-done((bf16[192,1024]{1,0:T(8,128)(2,1)}, bf16[192,1024]{1,0:T(8,128)(2,1)S(1)}, u32[]{:S(2)}, u32[]{:S(2)}) %collective-permute-start.16) | collective-permute-done | bytes 393248 | tf_op jit(solution)/shard_map/ppermute | solution.py:318
  89.5 3.1 %shard_map.126 = (bf16[256,1024]{1,0:T(8,128)(2,1)S(1)}, bf16[256,1024]{1,0:T(8,128)(2,1)S(1)}) custom-call(s32[3]{0:T(128)S(1)} %pad_add_fusion.where_ref, bf16[512,384]{1,0:T(8,128)(2,1)S(1)} %shard_map.123.refs_7_.refs_0_, bf16[512,384]{1,0:T(8,128)(2,1)S(1)} %shard_map.124.refs_1_, bf16[192,1024]{1,0:T(8,128)(2,1)} %collective-permute-done.6.refs_7_.refs_2_, ...), custom_call_target="tpu_custom_call" | custom-call | flops 805306368 | bytes 3407872 | tf_op jit(solution)/shard_map/pallas_call | solution.py:293
  93.4 4.6 %collective-permute-done.18.refs_3_ = bf16[512,768]{1,0:T(8,128)(2,1)S(1)} collective-permute-done((bf16[512,768]{1,0:T(8,128)(2,1)S(1)}, bf16[512,768]{1,0:T(8,128)(2,1)S(1)}, u32[]{:S(2)}, u32[]{:S(2)}) %collective-permute-start.18) | collective-permute-done | bytes 786464 | tf_op jit(solution)/shard_map/ppermute | solution.py:314
  98.7 2.7 %shard_map.125 = (bf16[256,1024]{1,0:T(8,128)(2,1)S(1)}, bf16[256,1024]{1,0:T(8,128)(2,1)}) custom-call(s32[3]{0:T(128)S(1)} %pad_add_fusion.where_ref, bf16[512,384]{1,0:T(8,128)(2,1)S(1)} %shard_map.123.refs_7_.refs_0_, bf16[512,384]{1,0:T(8,128)(2,1)S(1)} %shard_map.124.refs_1_, bf16[2,384,1024]{2,1,0:T(8,128)(2,1)S(1)} %copy-done.17), custom_call_target="tpu_custom_call" | custom-call | flops 805306368 | bytes 3407872 | tf_op jit(solution)/shard_map/pallas_call | solution.py:293
  105.5 2.6 %collective-permute-start.20 = (bf16[64,1024]{1,0:T(8,128)(2,1)}, bf16[64,1024]{1,0:T(8,128)(2,1)}, u32[]{:S(2)}, u32[]{:S(2)}) collective-permute-start(bf16[64,1024]{1,0:T(8,128)(2,1)} %get-tuple-element.37), channel_id=1, source_target_pairs={{0,8},{2,10},{4,12},{6,14},{8,0},{10,2},{12,4},{14,6},{1,9},{3,11}... | collective-permute-start | bytes 393224 | tf_op jit(solution)/shard_map/ppermute | solution.py:322
  108.3 4.2 %collective-permute-done.21 = bf16[64,1024]{1,0:T(8,128)(2,1)} collective-permute-done((bf16[64,1024]{1,0:T(8,128)(2,1)}, bf16[64,1024]{1,0:T(8,128)(2,1)}, u32[]{:S(2)}, u32[]{:S(2)}) %collective-permute-start.21) | collective-permute-done | bytes 131104 | tf_op jit(solution)/shard_map/ppermute | solution.py:322
  112.5 6.2 %collective-permute-done.20 = bf16[64,1024]{1,0:T(8,128)(2,1)} collective-permute-done((bf16[64,1024]{1,0:T(8,128)(2,1)}, bf16[64,1024]{1,0:T(8,128)(2,1)}, u32[]{:S(2)}, u32[]{:S(2)}) %collective-permute-start.20) | collective-permute-done | bytes 131104 | tf_op jit(solution)/shard_map/ppermute | solution.py:322
  121.8 2.7 %collective-permute-start.13 = (bf16[64,1024]{1,0:T(8,128)(2,1)S(1)}, bf16[64,1024]{1,0:T(8,128)(2,1)S(1)}, u32[]{:S(2)}, u32[]{:S(2)}) collective-permute-start(bf16[64,1024]{1,0:T(8,128)(2,1)S(1)} %get-tuple-element.57), channel_id=1, source_target_pairs={{0,4},{2,6},{4,0},{6,2},{8,12},{10,14},{12,8},{14,10},{1,5},{3,7},... | collective-permute-start | bytes 393224 | tf_op jit(solution)/shard_map/ppermute | solution.py:322
  129.1 7.7 %collective-permute-done.12 = bf16[64,1024]{1,0:T(8,128)(2,1)S(1)} collective-permute-done((bf16[64,1024]{1,0:T(8,128)(2,1)S(1)}, bf16[64,1024]{1,0:T(8,128)(2,1)S(1)}, u32[]{:S(2)}, u32[]{:S(2)}) %collective-permute-start.12) | collective-permute-done | bytes 131104 | tf_op jit(solution)/shard_map/ppermute | solution.py:322
  139.7 2.6 %collective-permute-start.25 = (bf16[512,768]{1,0:T(8,128)(2,1)}, bf16[512,768]{1,0:T(8,128)(2,1)S(1)}, u32[]{:S(2)}, u32[]{:S(2)}) collective-permute-start(bf16[512,768]{1,0:T(8,128)(2,1)} %copy-done.9), channel_id=1, source_target_pairs={{0,16},{16,0},{1,17},{17,1},{2,18},{18,2},{3,19},{19,3},{4,20},{20... | collective-permute-start | bytes 2359304 | tf_op jit(solution)/shard_map/ppermute | solution.py:318
  142.4 18.3 %collective-permute-done.25.refs_4_ = bf16[512,768]{1,0:T(8,128)(2,1)S(1)} collective-permute-done((bf16[512,768]{1,0:T(8,128)(2,1)}, bf16[512,768]{1,0:T(8,128)(2,1)S(1)}, u32[]{:S(2)}, u32[]{:S(2)}) %collective-permute-start.25) | collective-permute-done | bytes 786464 | tf_op jit(solution)/shard_map/ppermute | solution.py:318
  161.7 1.9 all-gather.5.cloned.1.call-done.refs_0_
  170.1 5.2 %shard_map.127.refs_0_ = bf16[512,768]{1,0:T(8,128)(2,1)S(1)} custom-call(s32[3]{0:T(128)S(1)} %pad_add_fusion.where_ref, bf16[512,1024]{1,0:T(8,128)(2,1)S(1)} %copy-done.8, bf16[512,2176]{1,0:T(8,128)(2,1)S(1)} %copy-done.3, bf16[2,512,768]{2,1,0:T(8,128)(2,1)S(1)} %copy-done.6, bf16[512,768]{1,0:T(8,128)(2,1)S(1)} %copy-done.10, ...), custom_call_target="tpu_custom_call" | custom-call | flops 1610612736 | bytes 4194304 | tf_op jit(solution)/shard_map/pallas_call | solution.py:238
  175.3 2.1 %shard_map.128 = (bf16[256,512]{1,0:T(8,128)(2,1)S(1)}, bf16[256,512]{1,0:T(8,128)(2,1)S(1)}) custom-call(s32[3]{0:T(128)S(1)} %pad_add_fusion.where_ref, bf16[512,768]{1,0:T(8,128)(2,1)S(1)} %shard_map.127.refs_0_, bf16[384,512]{1,0:T(8,128)(2,1)} %collective-permute-done.22.refs_1_, bf16[384,512]{1,0:T(8,128)(2,1)S(1)} %collective-permute-done.26.refs_2_), custom_call_target="tpu_custom_call" | custom-call | flops 402653184 | bytes 2097152 | tf_op jit(solution)/shard_map/pallas_call | solution.py:293
  192.4 2.7 %collective-permute-done.29 = bf16[64,512]{1,0:T(8,128)(2,1)S(1)} collective-permute-done((bf16[64,512]{1,0:T(8,128)(2,1)S(1)}, bf16[64,512]{1,0:T(8,128)(2,1)S(1)}, u32[]{:S(2)}, u32[]{:S(2)}) %collective-permute-start.29) | collective-permute-done | bytes 65568 | tf_op jit(solution)/shard_map/ppermute | solution.py:322
  (142 shorter events, 68.9 us)
Async XLA Ops:
  7.2 59.6 %all-gather.3.cloned.1.call-start = ((), (), s32[]{:S(2)}) async-start(), calls=%async_computation | async-start | bytes 2506752 | tf_op jit(solution)/shard_map/all_gather | solution.py:392
  10.8 15.1 %collective-permute-start.1 = (bf16[256,768]{1,0:T(8,128)(2,1)}, bf16[256,768]{1,0:T(8,128)(2,1)S(1)}, u32[]{:S(2)}, u32[]{:S(2)}) collective-permute-start(bf16[256,768]{1,0:T(8,128)(2,1)} %get-tuple-element.24), channel_id=1, source_target_pairs={{0,1},{1,0},{2,3},{3,2},{4,5},{5,4},{6,7},{7,6},{8,9},{9,8},{10,11... | collective-permute-start | bytes 1179656 | tf_op jit(solution)/shard_map/ppermute | solution.py:314
  13.7 12.1 %collective-permute-start = (bf16[64,1024]{1,0:T(8,128)(2,1)S(1)}, bf16[64,1024]{1,0:T(8,128)(2,1)S(1)}, u32[]{:S(2)}, u32[]{:S(2)}) collective-permute-start(bf16[64,1024]{1,0:T(8,128)(2,1)S(1)} %constant_dynamic-slice_fusion), channel_id=1, source_target_pairs={{0,1},{1,0},{2,3},{3,2},{4,5},{5,4},{6,7},{7,6},{8,9},{9,8},{10,11... | collective-permute-start | bytes 393224 | tf_op jit(solution)/shard_map/ppermute | solution.py:314
  27.3 136.3 %all-gather.5.cloned.1.call-start = ((), (), s32[]{:S(2)}) async-start(), calls=%async_computation.1 | async-start | bytes 1179648 | tf_op jit(solution)/shard_map/all_gather | solution.py:428
  27.4 12.3 %collective-permute-start.2 = (bf16[256,768]{1,0:T(8,128)(2,1)}, bf16[256,768]{1,0:T(8,128)(2,1)S(1)}, u32[]{:S(2)}, u32[]{:S(2)}) collective-permute-start(bf16[256,768]{1,0:T(8,128)(2,1)} %get-tuple-element.25), channel_id=1, source_target_pairs={{0,1},{1,0},{2,3},{3,2},{4,5},{5,4},{6,7},{7,6},{8,9},{9,8},{10,11... | collective-permute-start | bytes 1179656 | tf_op jit(solution)/shard_map/ppermute | solution.py:314
  29.2 18.9 %collective-permute-start.3 = (bf16[256,768]{1,0:T(8,128)(2,1)S(1)}, bf16[256,768]{1,0:T(8,128)(2,1)S(1)}, u32[]{:S(2)}, u32[]{:S(2)}) collective-permute-start(bf16[256,768]{1,0:T(8,128)(2,1)S(1)} %get-tuple-element.26), channel_id=1, source_target_pairs={{0,1},{1,0},{2,3},{3,2},{4,5},{5,4},{6,7},{7,6},{8,9},{9,8},{10,11... | collective-permute-start | bytes 1179656 | tf_op jit(solution)/shard_map/ppermute | solution.py:314
  29.5 18.7 %collective-permute-start.5 = (bf16[256,768]{1,0:T(8,128)(2,1)S(1)}, bf16[256,768]{1,0:T(8,128)(2,1)S(1)}, u32[]{:S(2)}, u32[]{:S(2)}) collective-permute-start(bf16[256,768]{1,0:T(8,128)(2,1)S(1)} %collective-permute-done.1.refs_5_.refs_3_), channel_id=1, source_target_pairs={{0,16},{16,0},{1,17},{17,1},{2,18},{18,2},{3,19},{19,3},{4,20},{20... | collective-permute-start | bytes 1179656 | tf_op jit(solution)/shard_map/ppermute | solution.py:318
  39.7 17.0 %collective-permute-start.4 = (bf16[256,768]{1,0:T(8,128)(2,1)}, bf16[256,768]{1,0:T(8,128)(2,1)}, u32[]{:S(2)}, u32[]{:S(2)}) collective-permute-start(bf16[256,768]{1,0:T(8,128)(2,1)} %get-tuple-element.27), channel_id=1, source_target_pairs={{0,1},{1,0},{2,3},{3,2},{4,5},{5,4},{6,7},{7,6},{8,9},{9,8},{10,11... | collective-permute-start | bytes 1179656 | tf_op jit(solution)/shard_map/ppermute | solution.py:314
  41.4 17.0 %collective-permute-start.8 = (bf16[256,768]{1,0:T(8,128)(2,1)S(1)}, bf16[256,768]{1,0:T(8,128)(2,1)S(1)}, u32[]{:S(2)}, u32[]{:S(2)}) collective-permute-start(bf16[256,768]{1,0:T(8,128)(2,1)S(1)} %collective-permute-done.2.refs_4_), channel_id=1, source_target_pairs={{0,16},{16,0},{1,17},{17,1},{2,18},{18,2},{3,19},{19,3},{4,20},{20... | collective-permute-start | bytes 1179656 | tf_op jit(solution)/shard_map/ppermute | solution.py:318
  48.1 17.0 %collective-permute-start.6 = (bf16[192,1024]{1,0:T(8,128)(2,1)S(1)}, bf16[192,1024]{1,0:T(8,128)(2,1)}, u32[]{:S(2)}, u32[]{:S(2)}) collective-permute-start(bf16[192,1024]{1,0:T(8,128)(2,1)S(1)} %get-tuple-element.28), channel_id=1, source_target_pairs={{0,1},{1,0},{2,3},{3,2},{4,5},{5,4},{6,7},{7,6},{8,9},{9,8},{10,11... | collective-permute-start | bytes 1179656 | tf_op jit(solution)/shard_map/ppermute | solution.py:314
  49.9 17.0 %collective-permute-start.7 = (bf16[256,768]{1,0:T(8,128)(2,1)S(1)}, bf16[256,768]{1,0:T(8,128)(2,1)S(1)}, u32[]{:S(2)}, u32[]{:S(2)}) collective-permute-start(bf16[256,768]{1,0:T(8,128)(2,1)S(1)} %collective-permute-done.3.refs_5_), channel_id=1, source_target_pairs={{0,16},{16,0},{1,17},{17,1},{2,18},{18,2},{3,19},{19,3},{4,20},{20... | collective-permute-start | bytes 1179656 | tf_op jit(solution)/shard_map/ppermute | solution.py:318
  56.6 20.2 %collective-permute-start.9 = (bf16[256,768]{1,0:T(8,128)(2,1)}, bf16[256,768]{1,0:T(8,128)(2,1)}, u32[]{:S(2)}, u32[]{:S(2)}) collective-permute-start(bf16[256,768]{1,0:T(8,128)(2,1)} %collective-permute-done.4.refs_6_), channel_id=1, source_target_pairs={{0,16},{16,0},{1,17},{17,1},{2,18},{18,2},{3,19},{19,3},{4,20},{20... | collective-permute-start | bytes 1179656 | tf_op jit(solution)/shard_map/ppermute | solution.py:318
  59.2 22.3 %collective-permute-start.14 = (bf16[192,1024]{1,0:T(8,128)(2,1)}, bf16[192,1024]{1,0:T(8,128)(2,1)}, u32[]{:S(2)}, u32[]{:S(2)}) collective-permute-start(bf16[192,1024]{1,0:T(8,128)(2,1)} %get-tuple-element.31), channel_id=1, source_target_pairs={{0,1},{1,0},{2,3},{3,2},{4,5},{5,4},{6,7},{7,6},{8,9},{9,8},{10,11... | collective-permute-start | bytes 1179656 | tf_op jit(solution)/shard_map/ppermute | solution.py:314
  65.1 18.6 %collective-permute-start.15 = (bf16[192,1024]{1,0:T(8,128)(2,1)}, bf16[192,1024]{1,0:T(8,128)(2,1)}, u32[]{:S(2)}, u32[]{:S(2)}) collective-permute-start(bf16[192,1024]{1,0:T(8,128)(2,1)} %collective-permute-done.6.refs_7_.refs_2_), channel_id=1, source_target_pairs={{0,16},{16,0},{1,17},{17,1},{2,18},{18,2},{3,19},{19,3},{4,20},{20... | collective-permute-start | bytes 1179656 | tf_op jit(solution)/shard_map/ppermute | solution.py:318
  81.8 16.2 %collective-permute-start.18 = (bf16[512,768]{1,0:T(8,128)(2,1)S(1)}, bf16[512,768]{1,0:T(8,128)(2,1)S(1)}, u32[]{:S(2)}, u32[]{:S(2)}) collective-permute-start(bf16[512,768]{1,0:T(8,128)(2,1)S(1)} %dynamic-slice_bitcast_fusion), channel_id=1, source_target_pairs={{0,1},{1,0},{2,3},{3,2},{4,5},{5,4},{6,7},{7,6},{8,9},{9,8},{10,11... | collective-permute-start | bytes 2359304 | tf_op jit(solution)/shard_map/ppermute | solution.py:314
  98.0 21.9 %collective-permute-start.22 = (bf16[384,512]{1,0:T(8,128)(2,1)}, bf16[384,512]{1,0:T(8,128)(2,1)}, u32[]{:S(2)}, u32[]{:S(2)}) collective-permute-start(bf16[384,512]{1,0:T(8,128)(2,1)} %dynamic-slice_bitcast_fusion.1), channel_id=1, source_target_pairs={{0,1},{1,0},{2,3},{3,2},{4,5},{5,4},{6,7},{7,6},{8,9},{9,8},{10,11... | collective-permute-start | bytes 1179656 | tf_op jit(solution)/shard_map/ppermute | solution.py:314
  102.3 18.2 %collective-permute-start.10 = (bf16[256,1024]{1,0:T(8,128)(2,1)}, bf16[256,1024]{1,0:T(8,128)(2,1)}, u32[]{:S(2)}, u32[]{:S(2)}) collective-permute-start(bf16[256,1024]{1,0:T(8,128)(2,1)} %get-tuple-element.30), channel_id=1, source_target_pairs={{0,2},{2,0},{4,6},{6,4},{8,10},{10,8},{12,14},{14,12},{1,3},{3,1},... | collective-permute-start | bytes 1572872 | tf_op jit(solution)/shard_map/ppermute | solution.py:322
  105.5 13.2 %collective-permute-start.20 = (bf16[64,1024]{1,0:T(8,128)(2,1)}, bf16[64,1024]{1,0:T(8,128)(2,1)}, u32[]{:S(2)}, u32[]{:S(2)}) collective-permute-start(bf16[64,1024]{1,0:T(8,128)(2,1)} %get-tuple-element.37), channel_id=1, source_target_pairs={{0,8},{2,10},{4,12},{6,14},{8,0},{10,2},{12,4},{14,6},{1,9},{3,11}... | collective-permute-start | bytes 393224 | tf_op jit(solution)/shard_map/ppermute | solution.py:322
  108.1 10.6 %collective-permute-start.19 = (bf16[64,1024]{1,0:T(8,128)(2,1)S(1)}, bf16[64,1024]{1,0:T(8,128)(2,1)}, u32[]{:S(2)}, u32[]{:S(2)}) collective-permute-start(bf16[64,1024]{1,0:T(8,128)(2,1)S(1)} %get-tuple-element.36), channel_id=1, source_target_pairs={{0,12},{2,14},{4,8},{6,10},{8,4},{10,6},{12,0},{14,2},{1,13},{3,15... | collective-permute-start | bytes 393224 | tf_op jit(solution)/shard_map/ppermute | solution.py:322
  124.6 12.2 %collective-permute-start.12 = (bf16[64,1024]{1,0:T(8,128)(2,1)S(1)}, bf16[64,1024]{1,0:T(8,128)(2,1)S(1)}, u32[]{:S(2)}, u32[]{:S(2)}) collective-permute-start(bf16[64,1024]{1,0:T(8,128)(2,1)S(1)} %get-tuple-element.58), channel_id=1, source_target_pairs={{0,8},{2,10},{4,12},{6,14},{8,0},{10,2},{12,4},{14,6},{1,9},{3,11}... | collective-permute-start | bytes 393224 | tf_op jit(solution)/shard_map/ppermute | solution.py:322
  125.6 11.1 %collective-permute-start.11 = (bf16[64,1024]{1,0:T(8,128)(2,1)S(1)}, bf16[64,1024]{1,0:T(8,128)(2,1)S(1)}, u32[]{:S(2)}, u32[]{:S(2)}) collective-permute-start(bf16[64,1024]{1,0:T(8,128)(2,1)S(1)} %get-tuple-element.56), channel_id=1, source_target_pairs={{0,12},{2,14},{4,8},{6,10},{8,4},{10,6},{12,0},{14,2},{1,13},{3,15... | collective-permute-start | bytes 393224 | tf_op jit(solution)/shard_map/ppermute | solution.py:322
  127.5 11.0 %collective-permute-start.24 = (bf16[64,1024]{1,0:T(8,128)(2,1)S(1)}, bf16[64,1024]{1,0:T(8,128)(2,1)S(1)}, u32[]{:S(2)}, u32[]{:S(2)}) collective-permute-start(bf16[64,1024]{1,0:T(8,128)(2,1)S(1)} %convolution_convert_fusion), channel_id=1, source_target_pairs={{0,1},{1,0},{2,3},{3,2},{4,5},{5,4},{6,7},{7,6},{8,9},{9,8},{10,11... | collective-permute-start | bytes 393224 | tf_op jit(solution)/shard_map/ppermute | solution.py:314
  139.7 21.0 %collective-permute-start.25 = (bf16[512,768]{1,0:T(8,128)(2,1)}, bf16[512,768]{1,0:T(8,128)(2,1)S(1)}, u32[]{:S(2)}, u32[]{:S(2)}) collective-permute-start(bf16[512,768]{1,0:T(8,128)(2,1)} %copy-done.9), channel_id=1, source_target_pairs={{0,16},{16,0},{1,17},{17,1},{2,18},{18,2},{3,19},{19,3},{4,20},{20... | collective-permute-start | bytes 2359304 | tf_op jit(solution)/shard_map/ppermute | solution.py:318
  142.3 32.9 %collective-permute-start.26 = (bf16[384,512]{1,0:T(8,128)(2,1)}, bf16[384,512]{1,0:T(8,128)(2,1)S(1)}, u32[]{:S(2)}, u32[]{:S(2)}) collective-permute-start(bf16[384,512]{1,0:T(8,128)(2,1)} %collective-permute-done.22.refs_1_), channel_id=1, source_target_pairs={{0,16},{16,0},{1,17},{17,1},{2,18},{18,2},{3,19},{19,3},{4,20},{20... | collective-permute-start | bytes 1179656 | tf_op jit(solution)/shard_map/ppermute | solution.py:318
  (43 other events, 436.3 us)
Sparse Core Ops, SparseCore 0:
  27.4 31.6 all-gather.2
  139.9 23.6 all-gather.4

commit v4 on v2

--- a/solution.py
+++ b/solution.py
@@ -124,11 +124,62 @@
     return (thinker_out, talker_out)
 
 
-def split_gain(ids, gain, experts):
-    hits = ids[:, :, None] == lax.iota(jnp.int32, experts)[None, None, :]
-    dense = jnp.sum(jnp.where(hits, gain[:, :, None], 0.0), axis=1)
-    high = lax.reduce_precision(dense, 8, 7)
-    return [high.astype(jnp.bfloat16), (dense - high).astype(jnp.bfloat16)]
+def lanes_kernel(experts, where_ref, *refs):
+    routes_ref, gain_ref, live_ref, talker_routes_ref, talker_gain_ref, out_ref, lanes = refs
+    rows = out_ref.shape[0]
+    stack = []
+    live = live_ref[...].astype(jnp.float32)
+    for ids, gains in ((routes_ref, gain_ref[...]), (talker_routes_ref, talker_gain_ref[...] * live)):
+        expert = lax.broadcasted_iota(jnp.int32, (experts, ids.shape[1]), 0)
+        dense = jnp.zeros(expert.shape, jnp.float32)
+        for choice in range(ids.shape[0]):
+            dense += jnp.where(
+                ids[choice : choice + 1, :] == expert, gains[choice : choice + 1, :], 0.0
+            )
+        high = dense.astype(jnp.bfloat16).astype(jnp.float32)
+        stack += [high, dense - high]
+    stack.append(jnp.zeros((LANES - 4 * experts, live.shape[1]), jnp.float32))
+    lanes[...] = jnp.concatenate(stack, axis=0).T
+    first = pl.multiple_of(where_ref[2] * rows, rows)
+    out_ref[...] = lanes[pl.ds(first, rows), :].astype(jnp.bfloat16)
+
+
+def gain_lanes(where, experts, routes, gain, live, talker_routes, talker_gain):
+    count = routes.shape[0]
+    inputs = [routes.T, gain.T, live[None], talker_routes.T, talker_gain.T]
+    return pl.pallas_call(
+        functools.partial(lanes_kernel, experts),
+        out_shape=jax.ShapeDtypeStruct((count // 2, LANES), jnp.bfloat16),
+        in_specs=[pl.BlockSpec(memory_space=pltpu.SMEM)]
+        + [pl.BlockSpec(memory_space=pltpu.VMEM)] * len(inputs),
+        out_specs=pl.BlockSpec(memory_space=pltpu.VMEM),
+        scratch_shapes=[pltpu.VMEM((count, LANES), jnp.float32)],
+        compiler_params=pltpu.CompilerParams(vmem_limit_bytes=4 * 1024 * 1024),
+        cost_estimate=pl.CostEstimate(
+            flops=1 << 30, bytes_accessed=64 * count * LANES, transcendentals=0
+        ),
+    )(where, *inputs)
+
+
+def row_kernel(where_ref, hidden_ref, other_ref, lanes_ref, out_ref):
+    rows, width = other_ref.shape
+    first = pl.multiple_of(where_ref[2] * rows, rows)
+    out_ref[:, :width] = hidden_ref[pl.ds(first, rows), :]
+    out_ref[:, width : 2 * width] = other_ref[...]
+    out_ref[:, 2 * width :] = lanes_ref[...]
+
+
+def build_row(where, hidden_in, other, lanes):
+    rows, width = other.shape
+    return pl.pallas_call(
+        row_kernel,
+        out_shape=jax.ShapeDtypeStruct((rows, 2 * width + LANES), jnp.bfloat16),
+        in_specs=[pl.BlockSpec(memory_space=pltpu.SMEM)]
+        + [pl.BlockSpec(memory_space=pltpu.VMEM)] * 3,
+        out_specs=pl.BlockSpec(memory_space=pltpu.VMEM),
+        compiler_params=pltpu.CompilerParams(vmem_limit_bytes=4 * 1024 * 1024),
+        cost_estimate=pl.CostEstimate(flops=0, bytes_accessed=8 * rows * width, transcendentals=0),
+    )(where, hidden_in, other, lanes)
 
 
 def load(pairs, sems):
@@ -149,90 +200,83 @@
     return pairs
 
 
-def hidden_kernel(blocks, gain_blocks, near, far, first_lane, experts, where_ref, *refs):
+def hidden_kernel(blocks, gain_blocks, chunks, first_lane, experts, where_ref, *refs):
     refs = list(refs)
     take = lambda count: [refs.pop(0) for _ in range(count)]
     row_refs, gain_refs = take(blocks), take(gain_blocks)
     (own_ref,) = take(1)
-    near_refs, far_refs = take(near), take(far)
+    chunk_refs = [take(chunks), take(chunks)]
+    direct_ref = refs.pop(0) if len(refs) > 5 else None
     (out_ref, rows, gains, weights, sems) = refs
     width = own_ref.shape[1]
     half_hidden = own_ref.shape[2] // 2
-    group = where_ref[1]
     lane_refs = [ref.at[:, pl.ds(ref.shape[1] - LANES, LANES)] for ref in gain_refs or row_refs]
     row_refs = [ref.at[:, pl.ds(0, 2 * width)] for ref in row_refs]
-    row_copies = load(
-        chunk_pairs(row_refs, rows) + chunk_pairs(lane_refs, gains), sems.at[0]
-    )
-    weight_copies = [
-        load(
-            [(own_ref.at[(group + order) % 2], weights.at[order, pl.ds(0, width)])]
-            + chunk_pairs(parts, weights.at[order], width),
-            sems.at[1 + order],
-        )
-        for order, parts in enumerate((near_refs, far_refs))
-    ]
+    row_copies = load(chunk_pairs(row_refs, rows) + chunk_pairs(lane_refs, gains), sems.at[0])
+    weight_copies = []
+    for order in range(2):
+        expert = (where_ref[1] + order) % 2
+        parts = [own_ref.at[expert], *chunk_refs[order]]
+        if direct_ref is not None:
+            parts.append(direct_ref.at[expert])
+        weight_copies.append(load(chunk_pairs(parts, weights.at[order]), sems.at[1 + order]))
     for copy in row_copies:
         copy.wait()
     lanes = gains[...].astype(jnp.float32)
-    place = lax.broadcasted_iota(jnp.int32, lanes.shape, 1) - first_lane
+    lane = lax.broadcasted_iota(jnp.int32, lanes.shape, 1) - first_lane
     for order in range(2):
         for copy in weight_copies[order]:
             copy.wait()
-        offset = place - (where_ref[0] * 2 + (group + order) % 2)
+        offset = lane - (where_ref[0] * 2 + (where_ref[1] + order) % 2)
         gain = jnp.sum(
             jnp.where((offset == 0) | (offset == experts), lanes, 0.0), axis=1, keepdims=True
         )
-        summed = jnp.dot(
-            rows[...], weights[order], preferred_element_type=jnp.float32
-        )
+        summed = jnp.dot(rows[...], weights[order], preferred_element_type=jnp.float32)
         hidden = jax.nn.silu(summed[:, :half_hidden]) * summed[:, half_hidden:] * gain
         out_ref[:, order * half_hidden : (order + 1) * half_hidden] = hidden.astype(jnp.bfloat16)
 
 
-def run_hidden(where, row_blocks, gain_blocks, own, near, far, first_lane, experts):
+def run_hidden(where, row_blocks, gain_blocks, own, near, far, direct, first_lane, experts):
     blocks = len(row_blocks)
-    count = blocks * row_blocks[0].shape[0]
+    count = sum(block.shape[0] for block in row_blocks)
     _, width, columns = own.shape
-    inputs = [*row_blocks, *gain_blocks, own, *near, *far]
-    kernel = functools.partial(
-        hidden_kernel, blocks, len(gain_blocks), len(near), len(far), first_lane, experts
-    )
+    inputs = [*row_blocks, *gain_blocks, own, *near, *far, *direct]
     return pl.pallas_call(
-        kernel,
+        functools.partial(
+            hidden_kernel, blocks, len(gain_blocks), len(near), first_lane, experts
+        ),
         out_shape=jax.ShapeDtypeStruct((count, columns), jnp.bfloat16),
         in_specs=[pl.BlockSpec(memory_space=pltpu.SMEM)]
-        + [pl.BlockSpec(memory_space=pl.ANY)] * len(inputs),
+        + [pl.BlockSpec(memory_space=pltpu.HBM)] * len(inputs),
         out_specs=pl.BlockSpec(memory_space=pltpu.VMEM),
         scratch_shapes=[
             pltpu.VMEM((count, 2 * width), jnp.bfloat16),
             pltpu.VMEM((count, LANES), jnp.bfloat16),
             pltpu.VMEM((2, 2 * width, columns), jnp.bfloat16),
-            pltpu.SemaphoreType.DMA((3, 2 * blocks + 1 + len(near))),
+            pltpu.SemaphoreType.DMA((3, max(2 * blocks, 2 + len(near)))),
         ],
-        compiler_params=pltpu.CompilerParams(vmem_limit_bytes=48 * 1024 * 1024),
+        compiler_params=pltpu.CompilerParams(vmem_limit_bytes=20 * 1024 * 1024),
         cost_estimate=pl.CostEstimate(
             flops=8 * count * width * columns,
-            bytes_accessed=2 * (2 * count * width + 4 * width * columns + count * columns),
+            bytes_accessed=4 * width * (count + 2 * columns),
             transcendentals=count * columns,
         ),
     )(where, *inputs)
 
 
-def down_kernel(near, far, where_ref, hidden_ref, *refs):
+def down_kernel(chunks, where_ref, hidden_ref, *refs):
     refs = list(refs)
-    first_refs = [refs.pop(0) for _ in range(near)]
-    second_refs = [refs.pop(0) for _ in range(far)]
-    mine_ref, away_ref, weights, sems = refs
+    take = lambda count: [refs.pop(0) for _ in range(count)]
+    chunk_refs = [take(chunks), take(chunks)]
+    whole_refs = refs[:-4]
+    mine_ref, away_ref, weights, sems = refs[-4:]
     depth = weights.shape[0] // 2
-    if near == 1 and far == 0:
-        (local_ref,) = first_refs
-        first_refs = [local_ref.at[where_ref[1]]]
-        second_refs = [local_ref.at[1 - where_ref[1]]]
-    copies = load(
-        chunk_pairs(first_refs, weights) + chunk_pairs(second_refs, weights, depth), sems
-    )
-    for copy in copies:
+    pairs = []
+    for order in range(2):
+        expert = (where_ref[1] + order) % 2
+        parts = chunk_refs[order] + [ref.at[expert] for ref in whole_refs]
+        pairs += chunk_pairs(parts, weights, order * depth)
+    for copy in load(pairs, sems):
         copy.wait()
     rows = mine_ref.shape[0]
     for half, out_ref in enumerate((mine_ref, away_ref)):
@@ -243,25 +287,22 @@
         ).astype(jnp.bfloat16)
 
 
-def run_down(where, hidden, near, far):
+def run_down(where, hidden, near, far, whole):
     count, depth = hidden.shape
-    columns = near[0].shape[-1]
-    inputs = [*near, *far]
+    inputs = [*near, *far, *whole]
+    columns = inputs[0].shape[-1]
     shape = jax.ShapeDtypeStruct((count // 2, columns), jnp.bfloat16)
     return pl.pallas_call(
-        functools.partial(down_kernel, len(near), len(far)),
+        functools.partial(down_kernel, len(near)),
         out_shape=(shape, shape),
-        in_specs=[
-            pl.BlockSpec(memory_space=pltpu.SMEM),
-            pl.BlockSpec(memory_space=pltpu.VMEM),
-        ]
-        + [pl.BlockSpec(memory_space=pl.ANY)] * len(inputs),
+        in_specs=[pl.BlockSpec(memory_space=pltpu.SMEM), pl.BlockSpec(memory_space=pltpu.VMEM)]
+        + [pl.BlockSpec(memory_space=pltpu.HBM)] * len(inputs),
         out_specs=(pl.BlockSpec(memory_space=pltpu.VMEM),) * 2,
         scratch_shapes=[
             pltpu.VMEM((depth, columns), jnp.bfloat16),
-            pltpu.SemaphoreType.DMA((max(2, len(inputs)),)),
+            pltpu.SemaphoreType.DMA((2 * (len(near) + len(whole)),)),
         ],
-        compiler_params=pltpu.CompilerParams(vmem_limit_bytes=48 * 1024 * 1024),
+        compiler_params=pltpu.CompilerParams(vmem_limit_bytes=16 * 1024 * 1024),
         cost_estimate=pl.CostEstimate(
             flops=2 * count * depth * columns,
             bytes_accessed=2 * (count * depth + depth * columns + count * columns),
@@ -284,42 +325,31 @@
     )
 
 
-def fetch_halves(named, chunk_rows):
-    group = lax.axis_index("groups")
-    arrived, result = [], []
-    for weights in named:
-        near, far = [], []
-        for row in range(0, weights.shape[1], chunk_rows(weights)):
-            piece = lax.dynamic_slice(
-                weights, (group, row, 0), (1, chunk_rows(weights), weights.shape[2])
-            )[0]
-            if len(arrived) > 1:
-                piece, _ = lax.optimization_barrier((piece, arrived[-2]))
-            near.append(over_replica(piece))
-            arrived.append(near[-1])
-            far.append(over_groups(near[-1]))
-        result.append((near, far))
-    return result
-
-
-def gather_rows(row):
-    owners = lax.axis_size("expert")
-    same = [row] + [over_expert(row, distance) for distance in range(2, owners, 2)]
-    return same + [over_expert(block, 1) for block in same]
-
-
-def scatter_sums(mine, away):
+def after(array, *others):
+    return lax.optimization_barrier((array, *others))[0] if others else array
+
+
+def send(weights, group, first_row, rows, *before):
+    piece = lax.dynamic_slice(weights, (group, first_row, 0), (1, rows, weights.shape[2]))[0]
+    return over_replica(after(piece, *before))
+
+
+def spread_sums(mine, away, *before):
     owners = lax.axis_size("expert")
     rows = mine.shape[0] // (owners // 2)
     other = over_expert(away, 1)
-    total = None
-    for index in range(owners // 2 - 1, -1, -1):
+    terms = []
+    for index in range(owners // 2):
         part = slice(index * rows, (index + 1) * rows)
         chip = mine[part].astype(jnp.float32) + other[part].astype(jnp.float32)
         if index:
-            chip = over_expert(chip.astype(jnp.bfloat16), 2 * index).astype(jnp.float32)
-        total = chip if total is None else total + chip
-    return total.astype(jnp.bfloat16)
+            chip = over_expert(after(chip.astype(jnp.bfloat16), *before), 2 * index)
+        terms.append(chip)
+    return terms
+
+
+def add_up(terms):
+    return sum(term.astype(jnp.float32) for term in terms).astype(jnp.bfloat16)
 
 
 def in_order(replica, own, other, axis):
@@ -341,26 +371,41 @@
     talker_w_in,
     talker_w_out,
 ):
-    replica = lax.axis_index("replica")
-    where = jnp.stack([lax.axis_index("expert"), lax.axis_index("groups")]).astype(jnp.int32)
-    experts = w_in.shape[0] * lax.axis_size("expert")
+    replica, group = lax.axis_index("replica"), lax.axis_index("groups")
+    where = jnp.stack([lax.axis_index("expert"), group, replica]).astype(jnp.int32)
+    owners = lax.axis_size("expert")
+    experts = w_in.shape[0] * owners
     rows = routes.shape[0] // 2
-
-    def my_rows(array):
-        return lax.dynamic_slice_in_dim(array, replica * rows, rows, 0)
-
-    other = over_replica(lax.dynamic_slice_in_dim(hidden_in, (1 - replica) * rows, rows, 0))
-    chunk_rows = lambda weights: min(weights.shape[1], 384 * 512 // weights.shape[2])
-    fetched = fetch_halves((w_in, w_out, talker_w_in, talker_w_out), chunk_rows)
-    live = my_rows(speaking).astype(jnp.float32)[:, None]
-    gains = split_gain(my_rows(routes), my_rows(route_gain), experts) + split_gain(
-        my_rows(talker_routes), my_rows(talker_gain) * live, experts
-    )
-    gains.append(jnp.zeros((rows, LANES - 4 * experts), jnp.bfloat16))
-    blocks = gather_rows(jnp.concatenate([my_rows(hidden_in), other] + gains, axis=1))
-    hidden = run_hidden(where, blocks, [], w_in, *fetched[0], 0, experts)
-    own = scatter_sums(*run_down(where, hidden, [w_out], []))
-    give = scatter_sums(*run_down(where, hidden, *fetched[1]))
+    distances = range(2, owners, 2)
+
+    chunk, out_chunk = w_in.shape[1] * 21 // 32, w_out.shape[1] * 2 // 3
+
+    lanes = gain_lanes(
+        where, experts, routes, route_gain, speaking, talker_routes, talker_gain
+    )
+    give = lax.dynamic_slice_in_dim(hidden_in, (1 - replica) * rows, rows, 0)
+    other = over_replica(give)
+    near_in = send(w_in, group, 0, chunk, other)
+    row = build_row(where, hidden_in, other, lanes)
+    same = [row] + [over_expert(row, distance) for distance in distances]
+    far_in = over_groups(after(near_in, same[2]))
+    direct_in = over_replica(after(w_in[:, chunk:], near_in, same[2]))
+    across = [over_expert(row, 1), over_expert(jnp.concatenate(same[1:]), 1)]
+    near_out = send(w_out, group, 0, out_chunk, *same)
+    direct_out = over_replica(after(w_out[:, out_chunk:], direct_in))
+    blocks = same + across
+    hidden = run_hidden(where, blocks, [], w_in, [near_in], [far_in], [direct_in], 0, experts)
+    own = run_down(where, hidden, [], [], [w_out])
+    far_out = over_groups(after(near_out, *own))
+    own = spread_sums(*own)
+    near_talker_in = send(talker_w_in, group, 0, talker_w_in.shape[1], direct_out, hidden)
+    late_hidden = after(hidden, *own[1:3])
+    give = run_down(where, late_hidden, [near_out], [far_out], [direct_out])
+    near_talker_out = send(talker_w_out, group, 0, talker_w_out.shape[1], near_talker_in)
+    far_talker_in = over_groups(near_talker_in)
+    give = after(add_up(spread_sums(*give, near_talker_in, own[3])), near_talker_out)
+    own = add_up(own)
+    far_talker_out = over_groups(near_talker_out)
     got = over_replica(give)
     thinker_out = in_order(replica, own, got, 0)
 
@@ -371,13 +416,24 @@
     talker_row = (handed(own) + term.astype(jnp.float32)).astype(jnp.bfloat16)
     parts = jnp.split(talker_row, 2, axis=1)
     talker_row = in_order(replica, parts[0], parts[1], 1)
-    talker_blocks = gather_rows(talker_row)
+    same = [talker_row] + [over_expert(talker_row, distance) for distance in distances]
+    talker_blocks = same + [over_expert(talker_row, 1), over_expert(jnp.concatenate(same[1:]), 1)]
     hidden = run_hidden(
-        where, talker_blocks, blocks, talker_w_in, *fetched[2], 2 * experts, experts
-    )
-    own = scatter_sums(*run_down(where, hidden, [talker_w_out], []))
-    give = scatter_sums(*run_down(where, hidden, *fetched[3]))
-    return (thinker_out, in_order(replica, own, over_replica(give), 0))
+        where,
+        talker_blocks,
+        blocks,
+        talker_w_in,
+        [near_talker_in],
+        [far_talker_in],
+        [],
+        2 * experts,
+        experts,
+    )
+    give = run_down(where, hidden, [near_talker_out], [far_talker_out], [])
+    got = over_replica(add_up(spread_sums(*give)))
+    own = run_down(where, after(hidden, *give), [], [], [talker_w_out])
+    own = add_up(spread_sums(*own))
+    return (thinker_out, in_order(replica, own, got, 0))
 
 
 def on_device(*arrays):

time: 196 us -> 175 us (0.89)
  local copies, waits for them, and re-layouts: 21.9 us -> 5.52 us
  waiting for transfers between devices: 78.9 us -> 93.6 us
  starting transfers between devices: 58.1 us -> 46.4 us
  other arithmetic: 11.2 us -> 4.81 us
    ppermute x13 -> x10, waiting for transfers between devices: 27.3 us -> 44.4 us  [over_replica(): return lax.ppermute(array, 'replica', SWAP)]
    ppermute x9 -> x4, waiting for transfers between devices: 19.1 us -> 4.15 us  [over_groups(): return lax.ppermute(array, 'groups', SWAP)]
    ppermute x30 -> x26, waiting for transfers between devices: 32.5 us -> 45.1 us  [over_expert(): lax.ppermute(array, 'expert', [(at, at ^ distance) for at in range(lax.ax...]
    ppermute x9 -> x4, starting transfers between devices: 10.9 us -> 3.1 us  [over_groups(): return lax.ppermute(array, 'groups', SWAP)]
    unnamed x74 -> x56, local copies, waits for them, and re-layouts: 9.57 us -> 1.98 us
    convert_element_type x9 -> x6, other arithmetic: 6.59 us -> 1.15 us  [the longest x2 0.79 us: add_up(): sum((term.astype(jnp.float32) for term in terms)).astype(jnp.bfloat16)]
    squeeze x4, local copies, waits for them, and re-layouts: 5.51 us -> 2.38 us  [send(): lax.dynamic_slice(weights, (group, first_row, 0), (1, rows, weights.shape...]
    ppermute x30 -> x26, starting transfers between devices: 34 us -> 31.6 us  [over_expert(): lax.ppermute(array, 'expert', [(at, at ^ distance) for at in range(lax.ax...]
  transfers between devices with their start and end apart: 52 -> 40, of which waited for: 23 -> 20; matrix products, arithmetic and copies ran while one was open for 11% -> 5% of each run, Pallas kernels for 9% -> 11%
where the time goes in v4:
time: 175 us; the launch traced here: 174 us
  waiting for transfers between devices  93.6 us (53%)
  starting transfers between devices  46.4 us (27%)
  Pallas kernels  20.9 us (12%)
  local copies, waits for them, and re-layouts  5.52 us (3%)
  other arithmetic  4.81 us (3%)
  matrix products  1.86 us (1%)
    ppermute x26, waiting for transfers between devices, over_expert(): lax.ppermute(array, 'expert', [(at, at ^ distance) for at in range(lax.ax...  45.1 us
    ppermute x10, waiting for transfers between devices, over_replica(): return lax.ppermute(array, 'replica', SWAP)  44.4 us
    ppermute x26, starting transfers between devices, over_expert(): lax.ppermute(array, 'expert', [(at, at ^ distance) for at in range(lax.ax...  31.6 us
    pallas_call x2, Pallas kernels, run_hidden(): pl.pallas_call(functools.partial(hidden_kernel, blocks, len(gain_blocks),...  12.7 us
    ppermute x10, starting transfers between devices, over_replica(): return lax.ppermute(array, 'replica', SWAP)  11.7 us
    pallas_call x4, Pallas kernels, run_down(): pl.pallas_call(functools.partial(down_kernel, len(near)), out_shape=(shap...  7.02 us
    ppermute x4, waiting for transfers between devices, over_groups(): return lax.ppermute(array, 'groups', SWAP)  4.15 us
  transfers between devices with their start and end apart: 40, of which 20 were waited for; matrix products, arithmetic and copies ran while one was open for 5% of the time, Pallas kernels for 11%

profile of v4, /device:TPU:0, one launch (start us, length us, event | category | flops | bytes accessed | tf_op | source)
XLA Modules:
  0.0 174.3 jit_solution(10005213955248082184)
XLA Ops:
  1.8 3.0 %collective-permute-start = (bf16[64,1024]{1,0:T(8,128)(2,1)S(1)}, bf16[64,1024]{1,0:T(8,128)(2,1)S(1)}, u32[]{:S(2)}, u32[]{:S(2)}) collective-permute-start(bf16[64,1024]{1,0:T(8,128)(2,1)S(1)} %constant_dynamic-slice_fusion), channel_id=1, source_target_pairs={{0,1},{1,0},{2,3},{3,2},{4,5},{5,4},{6,7},{7,6},{8,9},{9,8},{10,11... | collective-permute-start | bytes 393224 | tf_op jit(solution)/shard_map/ppermute | solution.py:315
  4.8 2.3 %dynamic-slice_bitcast_fusion = bf16[672,768]{1,0:T(8,128)(2,1)} fusion(bf16[2,1024,768]{2,1,0:T(8,128)(2,1)} %refs_6_.1, s32[]{:T(128)S(6)} %select_n.43), kind=kLoop, calls=%fused_computation.3 | loop fusion | bytes 2064388 | tf_op jit(solution)/shard_map/squeeze | solution.py:333
  11.7 2.7 %collective-permute-start.2 = (bf16[64,2176]{1,0:T(8,128)(2,1)S(1)}, bf16[64,2176]{1,0:T(8,128)(2,1)S(1)}, u32[]{:S(2)}, u32[]{:S(2)}) collective-permute-start(bf16[64,2176]{1,0:T(8,128)(2,1)S(1)} %shard_map.123.refs_0_.refs_6_), channel_id=1, source_target_pairs={{0,8},{2,10},{4,12},{6,14},{8,0},{10,2},{12,4},{14,6},{1,9},{3,11}... | collective-permute-start | bytes 835592 | tf_op jit(solution)/shard_map/ppermute | solution.py:323
  16.2 16.8 %collective-permute-done.2.refs_2_.refs_8_ = bf16[64,2176]{1,0:T(8,128)(2,1)S(1)} collective-permute-done((bf16[64,2176]{1,0:T(8,128)(2,1)S(1)}, bf16[64,2176]{1,0:T(8,128)(2,1)S(1)}, u32[]{:S(2)}, u32[]{:S(2)}) %collective-permute-start.2) | collective-permute-done | bytes 278560 | tf_op jit(solution)/shard_map/ppermute | solution.py:323
  37.4 24.0 %collective-permute-done.8.refs_9_ = bf16[2,352,768]{2,1,0:T(8,128)(2,1)S(1)} collective-permute-done((bf16[2,352,768]{2,1,0:T(8,128)(2,1)S(1)}, bf16[2,352,768]{2,1,0:T(8,128)(2,1)S(1)}, u32[]{:S(2)}, u32[]{:S(2)}) %collective-permute-start.8) | collective-permute-done | bytes 1081376 | tf_op jit(solution)/shard_map/ppermute | solution.py:315
  62.4 7.0 %shard_map.124.hidden_ref = bf16[512,768]{1,0:T(8,128)(2,1)S(1)} custom-call(s32[3]{0:T(128)S(1)} %pad_add_fusion.where_ref, bf16[64,2176]{1,0:T(8,128)(2,1)S(1)} %shard_map.123.refs_0_.refs_6_, bf16[64,2176]{1,0:T(8,128)(2,1)S(1)} %collective-permute-done.1.refs_1_.refs_7_, bf16[64,2176]{1,0:T(8,128)(2,1)S(1)} %collective-permute-done.2.refs_2_.refs_8_, ...), custom_call_target="tpu_custom_call" | custom-call | flops 3221225472 | bytes 8388608 | tf_op jit(solution)/shard_map/pallas_call | solution.py:244
  73.1 7.6 %collective-permute-done.15.refs_2_ = bf16[2,128,1024]{2,1,0:T(8,128)(2,1)S(1)} collective-permute-done((bf16[2,128,1024]{2,1,0:T(8,128)(2,1)S(1)}, bf16[2,128,1024]{2,1,0:T(8,128)(2,1)S(1)}, u32[]{:S(2)}, u32[]{:S(2)}) %collective-permute-start.15) | collective-permute-done | bytes 524320 | tf_op jit(solution)/shard_map/ppermute | solution.py:315
  83.8 2.6 %collective-permute-start.11 = (bf16[64,1024]{1,0:T(8,128)(2,1)S(1)}, bf16[64,1024]{1,0:T(8,128)(2,1)S(1)}, u32[]{:S(2)}, u32[]{:S(2)}) collective-permute-start(bf16[64,1024]{1,0:T(8,128)(2,1)S(1)} %get-tuple-element.54), channel_id=1, source_target_pairs={{0,8},{2,10},{4,12},{6,14},{8,0},{10,2},{12,4},{14,6},{1,9},{3,11}... | collective-permute-start | bytes 393224 | tf_op jit(solution)/shard_map/ppermute | solution.py:323
  87.3 3.8 %collective-permute-done.11 = bf16[64,1024]{1,0:T(8,128)(2,1)S(1)} collective-permute-done((bf16[64,1024]{1,0:T(8,128)(2,1)S(1)}, bf16[64,1024]{1,0:T(8,128)(2,1)S(1)}, u32[]{:S(2)}, u32[]{:S(2)}) %collective-permute-start.11) | collective-permute-done | bytes 131104 | tf_op jit(solution)/shard_map/ppermute | solution.py:323
  93.0 2.5 %collective-permute-start.12 = (bf16[64,1024]{1,0:T(8,128)(2,1)S(1)}, bf16[64,1024]{1,0:T(8,128)(2,1)S(1)}, u32[]{:S(2)}, u32[]{:S(2)}) collective-permute-start(bf16[64,1024]{1,0:T(8,128)(2,1)S(1)} %get-tuple-element.53), channel_id=1, source_target_pairs={{0,12},{2,14},{4,8},{6,10},{8,4},{10,6},{12,0},{14,2},{1,13},{3,15... | collective-permute-start | bytes 393224 | tf_op jit(solution)/shard_map/ppermute | solution.py:323
  101.5 2.7 %collective-permute-start.20 = (bf16[64,1024]{1,0:T(8,128)(2,1)S(1)}, bf16[64,1024]{1,0:T(8,128)(2,1)S(1)}, u32[]{:S(2)}, u32[]{:S(2)}) collective-permute-start(bf16[64,1024]{1,0:T(8,128)(2,1)S(1)} %get-tuple-element.38), channel_id=1, source_target_pairs={{0,12},{2,14},{4,8},{6,10},{8,4},{10,6},{12,0},{14,2},{1,13},{3,15... | collective-permute-start | bytes 393224 | tf_op jit(solution)/shard_map/ppermute | solution.py:323
  105.9 3.9 %collective-permute-done.20 = bf16[64,1024]{1,0:T(8,128)(2,1)S(1)} collective-permute-done((bf16[64,1024]{1,0:T(8,128)(2,1)S(1)}, bf16[64,1024]{1,0:T(8,128)(2,1)S(1)}, u32[]{:S(2)}, u32[]{:S(2)}) %collective-permute-start.20) | collective-permute-done | bytes 131104 | tf_op jit(solution)/shard_map/ppermute | solution.py:323
  109.7 5.8 %collective-permute-done.19 = bf16[64,1024]{1,0:T(8,128)(2,1)S(1)} collective-permute-done((bf16[64,1024]{1,0:T(8,128)(2,1)S(1)}, bf16[64,1024]{1,0:T(8,128)(2,1)S(1)}, u32[]{:S(2)}, u32[]{:S(2)}) %collective-permute-start.19) | collective-permute-done | bytes 131104 | tf_op jit(solution)/shard_map/ppermute | solution.py:323
  117.3 4.2 %collective-permute-done.22 = bf16[64,1024]{1,0:T(8,128)(2,1)} collective-permute-done((bf16[64,1024]{1,0:T(8,128)(2,1)}, bf16[64,1024]{1,0:T(8,128)(2,1)}, u32[]{:S(2)}, u32[]{:S(2)}) %collective-permute-start.22) | collective-permute-done | bytes 131104 | tf_op jit(solution)/shard_map/ppermute | solution.py:315
  124.7 3.3 %collective-permute-done.23 = bf16[64,1024]{1,0:T(8,128)(2,1)S(1)} collective-permute-done((bf16[64,1024]{1,0:T(8,128)(2,1)S(1)}, bf16[64,1024]{1,0:T(8,128)(2,1)S(1)}, u32[]{:S(2)}, u32[]{:S(2)}) %collective-permute-start.23) | collective-permute-done | bytes 131104 | tf_op jit(solution)/shard_map/ppermute | solution.py:315
  128.6 3.1 %collective-permute-start.25 = (bf16[64,1024]{1,0:T(8,128)(2,1)S(1)}, bf16[64,1024]{1,0:T(8,128)(2,1)S(1)}, u32[]{:S(2)}, u32[]{:S(2)}) collective-permute-start(bf16[64,1024]{1,0:T(8,128)(2,1)S(1)} %pad_maximum_fusion.3.refs_0_), channel_id=1, source_target_pairs={{0,8},{2,10},{4,12},{6,14},{8,0},{10,2},{12,4},{14,6},{1,9},{3,11}... | collective-permute-start | bytes 393224 | tf_op jit(solution)/shard_map/ppermute | solution.py:323
  133.0 2.5 %collective-permute-done.24.refs_1_ = bf16[64,1024]{1,0:T(8,128)(2,1)S(1)} collective-permute-done((bf16[64,1024]{1,0:T(8,128)(2,1)S(1)}, bf16[64,1024]{1,0:T(8,128)(2,1)S(1)}, u32[]{:S(2)}, u32[]{:S(2)}) %collective-permute-start.24) | collective-permute-done | bytes 131104 | tf_op jit(solution)/shard_map/ppermute | solution.py:323
  135.5 3.5 %collective-permute-done.25.refs_2_ = bf16[64,1024]{1,0:T(8,128)(2,1)S(1)} collective-permute-done((bf16[64,1024]{1,0:T(8,128)(2,1)S(1)}, bf16[64,1024]{1,0:T(8,128)(2,1)S(1)}, u32[]{:S(2)}, u32[]{:S(2)}) %collective-permute-start.25) | collective-permute-done | bytes 131104 | tf_op jit(solution)/shard_map/ppermute | solution.py:323
  141.1 5.6 %shard_map.127.hidden_ref = bf16[512,768]{1,0:T(8,128)(2,1)S(1)} custom-call(s32[3]{0:T(128)S(1)} %pad_add_fusion.where_ref, bf16[64,1024]{1,0:T(8,128)(2,1)S(1)} %pad_maximum_fusion.3.refs_0_, bf16[64,1024]{1,0:T(8,128)(2,1)S(1)} %collective-permute-done.24.refs_1_, bf16[64,1024]{1,0:T(8,128)(2,1)S(1)} %collective-permute-done.25.refs_2_, ...), custom_call_target="tpu_custom_call" | custom-call | flops 1610612736 | bytes 4194304 | tf_op jit(solution)/shard_map/pallas_call | solution.py:244
  146.7 4.1 %collective-permute-done.30.refs_1_ = bf16[384,512]{1,0:T(8,128)(2,1)S(1)} collective-permute-done((bf16[384,512]{1,0:T(8,128)(2,1)}, bf16[384,512]{1,0:T(8,128)(2,1)S(1)}, u32[]{:S(2)}, u32[]{:S(2)}) %collective-permute-start.30) | collective-permute-done | bytes 393248 | tf_op jit(solution)/shard_map/ppermute | solution.py:319
  156.2 2.5 %collective-permute-start.38 = (bf16[64,512]{1,0:T(8,128)(2,1)S(1)}, bf16[64,512]{1,0:T(8,128)(2,1)S(1)}, u32[]{:S(2)}, u32[]{:S(2)}) collective-permute-start(bf16[64,512]{1,0:T(8,128)(2,1)S(1)} %get-tuple-element.60), channel_id=1, source_target_pairs={{0,12},{2,14},{4,8},{6,10},{8,4},{10,6},{12,0},{14,2},{1,13},{3,15... | collective-permute-start | bytes 196616 | tf_op jit(solution)/shard_map/ppermute | solution.py:323
  160.7 2.5 %collective-permute-start.34 = (bf16[64,512]{1,0:T(8,128)(2,1)S(1)}, bf16[64,512]{1,0:T(8,128)(2,1)S(1)}, u32[]{:S(2)}, u32[]{:S(2)}) collective-permute-start(bf16[64,512]{1,0:T(8,128)(2,1)S(1)} %get-tuple-element.57), channel_id=1, source_target_pairs={{0,12},{2,14},{4,8},{6,10},{8,4},{10,6},{12,0},{14,2},{1,13},{3,15... | collective-permute-start | bytes 196616 | tf_op jit(solution)/shard_map/ppermute | solution.py:323
  163.3 2.9 %collective-permute-start.32 = (bf16[64,512]{1,0:T(8,128)(2,1)S(1)}, bf16[64,512]{1,0:T(8,128)(2,1)S(1)}, u32[]{:S(2)}, u32[]{:S(2)}) collective-permute-start(bf16[64,512]{1,0:T(8,128)(2,1)S(1)} %get-tuple-element.56), channel_id=1, source_target_pairs={{0,4},{2,6},{4,0},{6,2},{8,12},{10,14},{12,8},{14,10},{1,5},{3,7},... | collective-permute-start | bytes 196616 | tf_op jit(solution)/shard_map/ppermute | solution.py:323
  166.2 3.0 %collective-permute-done.37 = bf16[64,512]{1,0:T(8,128)(2,1)S(1)} collective-permute-done((bf16[64,512]{1,0:T(8,128)(2,1)S(1)}, bf16[64,512]{1,0:T(8,128)(2,1)S(1)}, u32[]{:S(2)}, u32[]{:S(2)}) %collective-permute-start.37) | collective-permute-done | bytes 65568 | tf_op jit(solution)/shard_map/ppermute | solution.py:323
  (146 shorter events, 51.2 us)
Async XLA Ops:
  8.3 24.8 %collective-permute-start.6 = (bf16[672,768]{1,0:T(8,128)(2,1)}, bf16[672,768]{1,0:T(8,128)(2,1)}, u32[]{:S(2)}, u32[]{:S(2)}) collective-permute-start(bf16[672,768]{1,0:T(8,128)(2,1)} %dynamic-slice_bitcast_fusion), channel_id=1, source_target_pairs={{0,1},{1,0},{2,3},{3,2},{4,5},{5,4},{6,7},{7,6},{8,9},{9,8},{10,11... | collective-permute-start | bytes 3096584 | tf_op jit(solution)/shard_map/ppermute | solution.py:315
  11.7 21.4 %collective-permute-start.2 = (bf16[64,2176]{1,0:T(8,128)(2,1)S(1)}, bf16[64,2176]{1,0:T(8,128)(2,1)S(1)}, u32[]{:S(2)}, u32[]{:S(2)}) collective-permute-start(bf16[64,2176]{1,0:T(8,128)(2,1)S(1)} %shard_map.123.refs_0_.refs_6_), channel_id=1, source_target_pairs={{0,8},{2,10},{4,12},{6,14},{8,0},{10,2},{12,4},{14,6},{1,9},{3,11}... | collective-permute-start | bytes 835592 | tf_op jit(solution)/shard_map/ppermute | solution.py:323
  14.3 21.2 %collective-permute-start.1 = (bf16[64,2176]{1,0:T(8,128)(2,1)S(1)}, bf16[64,2176]{1,0:T(8,128)(2,1)S(1)}, u32[]{:S(2)}, u32[]{:S(2)}) collective-permute-start(bf16[64,2176]{1,0:T(8,128)(2,1)S(1)} %shard_map.123.refs_0_.refs_6_), channel_id=1, source_target_pairs={{0,4},{2,6},{4,0},{6,2},{8,12},{10,14},{12,8},{14,10},{1,5},{3,7},... | collective-permute-start | bytes 835592 | tf_op jit(solution)/shard_map/ppermute | solution.py:323
  15.9 19.6 %collective-permute-start.3 = (bf16[64,2176]{1,0:T(8,128)(2,1)S(1)}, bf16[64,2176]{1,0:T(8,128)(2,1)S(1)}, u32[]{:S(2)}, u32[]{:S(2)}) collective-permute-start(bf16[64,2176]{1,0:T(8,128)(2,1)S(1)} %shard_map.123.refs_0_.refs_6_), channel_id=1, source_target_pairs={{0,12},{2,14},{4,8},{6,10},{8,4},{10,6},{12,0},{14,2},{1,13},{3,15... | collective-permute-start | bytes 835592 | tf_op jit(solution)/shard_map/ppermute | solution.py:323
  33.0 29.3 %collective-permute-start.7 = (bf16[672,768]{1,0:T(8,128)(2,1)}, bf16[672,768]{1,0:T(8,128)(2,1)S(1)}, u32[]{:S(2)}, u32[]{:S(2)}) collective-permute-start(bf16[672,768]{1,0:T(8,128)(2,1)} %collective-permute-done.6.refs_7_), channel_id=1, source_target_pairs={{0,16},{16,0},{1,17},{17,1},{2,18},{18,2},{3,19},{19,3},{4,20},{20... | collective-permute-start | bytes 3096584 | tf_op jit(solution)/shard_map/ppermute | solution.py:319
  34.5 26.8 %collective-permute-start.8 = (bf16[2,352,768]{2,1,0:T(8,128)(2,1)S(1)}, bf16[2,352,768]{2,1,0:T(8,128)(2,1)S(1)}, u32[]{:S(2)}, u32[]{:S(2)}) collective-permute-start(bf16[2,352,768]{2,1,0:T(8,128)(2,1)S(1)} %slice.102), channel_id=1, source_target_pairs={{0,1},{1,0},{2,3},{3,2},{4,5},{5,4},{6,7},{7,6},{8,9},{9,8},{10,11... | collective-permute-start | bytes 3244040 | tf_op jit(solution)/shard_map/ppermute | solution.py:315
  35.6 26.7 %collective-permute-start.5 = (bf16[192,2176]{1,0:T(8,128)(2,1)S(1)}, bf16[192,2176]{1,0:T(8,128)(2,1)S(1)}, u32[]{:S(2)}, u32[]{:S(2)}) collective-permute-start(bf16[192,2176]{1,0:T(8,128)(2,1)S(1)} %pad_maximum_fusion), channel_id=1, source_target_pairs={{0,2},{2,0},{4,6},{6,4},{8,10},{10,8},{12,14},{14,12},{1,3},{3,1},... | collective-permute-start | bytes 2506760 | tf_op jit(solution)/shard_map/ppermute | solution.py:323
  35.7 26.6 %collective-permute-start.4 = (bf16[64,2176]{1,0:T(8,128)(2,1)S(1)}, bf16[64,2176]{1,0:T(8,128)(2,1)S(1)}, u32[]{:S(2)}, u32[]{:S(2)}) collective-permute-start(bf16[64,2176]{1,0:T(8,128)(2,1)S(1)} %shard_map.123.refs_0_.refs_6_), channel_id=1, source_target_pairs={{0,2},{2,0},{4,6},{6,4},{8,10},{10,8},{12,14},{14,12},{1,3},{3,1},... | collective-permute-start | bytes 835592 | tf_op jit(solution)/shard_map/ppermute | solution.py:323
  36.3 36.3 %collective-permute-start.13 = (bf16[256,1024]{1,0:T(8,128)(2,1)S(1)}, bf16[256,1024]{1,0:T(8,128)(2,1)S(1)}, u32[]{:S(2)}, u32[]{:S(2)}) collective-permute-start(bf16[256,1024]{1,0:T(8,128)(2,1)S(1)} %dynamic-slice_bitcast_fusion.2), channel_id=1, source_target_pairs={{0,1},{1,0},{2,3},{3,2},{4,5},{5,4},{6,7},{7,6},{8,9},{9,8},{10,11... | collective-permute-start | bytes 1572872 | tf_op jit(solution)/shard_map/ppermute | solution.py:315
  61.3 19.4 %collective-permute-start.15 = (bf16[2,128,1024]{2,1,0:T(8,128)(2,1)S(1)}, bf16[2,128,1024]{2,1,0:T(8,128)(2,1)S(1)}, u32[]{:S(2)}, u32[]{:S(2)}) collective-permute-start(bf16[2,128,1024]{2,1,0:T(8,128)(2,1)S(1)} %slice.111), channel_id=1, source_target_pairs={{0,1},{1,0},{2,3},{3,2},{4,5},{5,4},{6,7},{7,6},{8,9},{9,8},{10,11... | collective-permute-start | bytes 1572872 | tf_op jit(solution)/shard_map/ppermute | solution.py:315
  72.1 10.0 %collective-permute-start.9 = (bf16[256,1024]{1,0:T(8,128)(2,1)S(1)}, bf16[256,1024]{1,0:T(8,128)(2,1)S(1)}, u32[]{:S(2)}, u32[]{:S(2)}) collective-permute-start(bf16[256,1024]{1,0:T(8,128)(2,1)S(1)} %get-tuple-element.28), channel_id=1, source_target_pairs={{0,2},{2,0},{4,6},{6,4},{8,10},{10,8},{12,14},{14,12},{1,3},{3,1},... | collective-permute-start | bytes 1572872 | tf_op jit(solution)/shard_map/ppermute | solution.py:323
  72.6 18.5 %collective-permute-start.14 = (bf16[256,1024]{1,0:T(8,128)(2,1)S(1)}, bf16[256,1024]{1,0:T(8,128)(2,1)S(1)}, u32[]{:S(2)}, u32[]{:S(2)}) collective-permute-start(bf16[256,1024]{1,0:T(8,128)(2,1)S(1)} %collective-permute-done.13.refs_0_), channel_id=1, source_target_pairs={{0,16},{16,0},{1,17},{17,1},{2,18},{18,2},{3,19},{19,3},{4,20},{20... | collective-permute-start | bytes 1572872 | tf_op jit(solution)/shard_map/ppermute | solution.py:319
  80.8 16.2 %collective-permute-start.17 = (bf16[512,768]{1,0:T(8,128)(2,1)S(1)}, bf16[512,768]{1,0:T(8,128)(2,1)}, u32[]{:S(2)}, u32[]{:S(2)}) collective-permute-start(bf16[512,768]{1,0:T(8,128)(2,1)S(1)} %dynamic-slice_bitcast_fusion.1), channel_id=1, source_target_pairs={{0,1},{1,0},{2,3},{3,2},{4,5},{5,4},{6,7},{7,6},{8,9},{9,8},{10,11... | collective-permute-start | bytes 2359304 | tf_op jit(solution)/shard_map/ppermute | solution.py:315
  97.0 19.3 %collective-permute-start.21 = (bf16[384,512]{1,0:T(8,128)(2,1)S(1)}, bf16[384,512]{1,0:T(8,128)(2,1)}, u32[]{:S(2)}, u32[]{:S(2)}) collective-permute-start(bf16[384,512]{1,0:T(8,128)(2,1)S(1)} %dynamic-slice_bitcast_fusion.3), channel_id=1, source_target_pairs={{0,1},{1,0},{2,3},{3,2},{4,5},{5,4},{6,7},{7,6},{8,9},{9,8},{10,11... | collective-permute-start | bytes 1179656 | tf_op jit(solution)/shard_map/ppermute | solution.py:315
  101.5 8.3 %collective-permute-start.20 = (bf16[64,1024]{1,0:T(8,128)(2,1)S(1)}, bf16[64,1024]{1,0:T(8,128)(2,1)S(1)}, u32[]{:S(2)}, u32[]{:S(2)}) collective-permute-start(bf16[64,1024]{1,0:T(8,128)(2,1)S(1)} %get-tuple-element.38), channel_id=1, source_target_pairs={{0,12},{2,14},{4,8},{6,10},{8,4},{10,6},{12,0},{14,2},{1,13},{3,15... | collective-permute-start | bytes 393224 | tf_op jit(solution)/shard_map/ppermute | solution.py:323
  104.1 11.4 %collective-permute-start.19 = (bf16[64,1024]{1,0:T(8,128)(2,1)S(1)}, bf16[64,1024]{1,0:T(8,128)(2,1)S(1)}, u32[]{:S(2)}, u32[]{:S(2)}) collective-permute-start(bf16[64,1024]{1,0:T(8,128)(2,1)S(1)} %get-tuple-element.37), channel_id=1, source_target_pairs={{0,8},{2,10},{4,12},{6,14},{8,0},{10,2},{12,4},{14,6},{1,9},{3,11}... | collective-permute-start | bytes 393224 | tf_op jit(solution)/shard_map/ppermute | solution.py:323
  104.1 11.4 %collective-permute-start.18 = (bf16[64,1024]{1,0:T(8,128)(2,1)S(1)}, bf16[64,1024]{1,0:T(8,128)(2,1)S(1)}, u32[]{:S(2)}, u32[]{:S(2)}) collective-permute-start(bf16[64,1024]{1,0:T(8,128)(2,1)S(1)} %get-tuple-element.36), channel_id=1, source_target_pairs={{0,4},{2,6},{4,0},{6,2},{8,12},{10,14},{12,8},{14,10},{1,5},{3,7},... | collective-permute-start | bytes 393224 | tf_op jit(solution)/shard_map/ppermute | solution.py:323
  116.8 23.0 %collective-permute-start.29 = (bf16[512,768]{1,0:T(8,128)(2,1)}, bf16[512,768]{1,0:T(8,128)(2,1)S(1)}, u32[]{:S(2)}, u32[]{:S(2)}) collective-permute-start(bf16[512,768]{1,0:T(8,128)(2,1)} %collective-permute-done.17.refs_13_), channel_id=1, source_target_pairs={{0,16},{16,0},{1,17},{17,1},{2,18},{18,2},{3,19},{19,3},{4,20},{20... | collective-permute-start | bytes 2359304 | tf_op jit(solution)/shard_map/ppermute | solution.py:319
  128.6 10.4 %collective-permute-start.25 = (bf16[64,1024]{1,0:T(8,128)(2,1)S(1)}, bf16[64,1024]{1,0:T(8,128)(2,1)S(1)}, u32[]{:S(2)}, u32[]{:S(2)}) collective-permute-start(bf16[64,1024]{1,0:T(8,128)(2,1)S(1)} %pad_maximum_fusion.3.refs_0_), channel_id=1, source_target_pairs={{0,8},{2,10},{4,12},{6,14},{8,0},{10,2},{12,4},{14,6},{1,9},{3,11}... | collective-permute-start | bytes 393224 | tf_op jit(solution)/shard_map/ppermute | solution.py:323
  139.1 11.7 %collective-permute-start.30 = (bf16[384,512]{1,0:T(8,128)(2,1)}, bf16[384,512]{1,0:T(8,128)(2,1)S(1)}, u32[]{:S(2)}, u32[]{:S(2)}) collective-permute-start(bf16[384,512]{1,0:T(8,128)(2,1)} %collective-permute-done.21.refs_0_), channel_id=1, source_target_pairs={{0,16},{16,0},{1,17},{17,1},{2,18},{18,2},{3,19},{19,3},{4,20},{20... | collective-permute-start | bytes 1179656 | tf_op jit(solution)/shard_map/ppermute | solution.py:319
  158.7 10.5 %collective-permute-start.37 = (bf16[64,512]{1,0:T(8,128)(2,1)S(1)}, bf16[64,512]{1,0:T(8,128)(2,1)S(1)}, u32[]{:S(2)}, u32[]{:S(2)}) collective-permute-start(bf16[64,512]{1,0:T(8,128)(2,1)S(1)} %get-tuple-element.61), channel_id=1, source_target_pairs={{0,8},{2,10},{4,12},{6,14},{8,0},{10,2},{12,4},{14,6},{1,9},{3,11}... | collective-permute-start | bytes 196616 | tf_op jit(solution)/shard_map/ppermute | solution.py:323
  159.7 9.5 %collective-permute-start.36 = (bf16[64,512]{1,0:T(8,128)(2,1)S(1)}, bf16[64,512]{1,0:T(8,128)(2,1)S(1)}, u32[]{:S(2)}, u32[]{:S(2)}) collective-permute-start(bf16[64,512]{1,0:T(8,128)(2,1)S(1)} %get-tuple-element.59), channel_id=1, source_target_pairs={{0,4},{2,6},{4,0},{6,2},{8,12},{10,14},{12,8},{14,10},{1,5},{3,7},... | collective-permute-start | bytes 196616 | tf_op jit(solution)/shard_map/ppermute | solution.py:323
  160.7 9.3 %collective-permute-start.34 = (bf16[64,512]{1,0:T(8,128)(2,1)S(1)}, bf16[64,512]{1,0:T(8,128)(2,1)S(1)}, u32[]{:S(2)}, u32[]{:S(2)}) collective-permute-start(bf16[64,512]{1,0:T(8,128)(2,1)S(1)} %get-tuple-element.57), channel_id=1, source_target_pairs={{0,12},{2,14},{4,8},{6,10},{8,4},{10,6},{12,0},{14,2},{1,13},{3,15... | collective-permute-start | bytes 196616 | tf_op jit(solution)/shard_map/ppermute | solution.py:323
  163.2 8.3 %collective-permute-start.33 = (bf16[64,512]{1,0:T(8,128)(2,1)S(1)}, bf16[64,512]{1,0:T(8,128)(2,1)S(1)}, u32[]{:S(2)}, u32[]{:S(2)}) collective-permute-start(bf16[64,512]{1,0:T(8,128)(2,1)S(1)} %get-tuple-element.58), channel_id=1, source_target_pairs={{0,8},{2,10},{4,12},{6,14},{8,0},{10,2},{12,4},{14,6},{1,9},{3,11}... | collective-permute-start | bytes 196616 | tf_op jit(solution)/shard_map/ppermute | solution.py:323
  (44 other events, 511.2 us)

commit v5 on v4

--- a/solution.py
+++ b/solution.py
@@ -200,14 +200,14 @@
     return pairs
 
 
-def hidden_kernel(blocks, gain_blocks, chunks, first_lane, experts, where_ref, *refs):
+def hidden_kernel(blocks, gain_blocks, chunks, direct, first_lane, experts, where_ref, *refs):
     refs = list(refs)
     take = lambda count: [refs.pop(0) for _ in range(count)]
     row_refs, gain_refs = take(blocks), take(gain_blocks)
     (own_ref,) = take(1)
     chunk_refs = [take(chunks), take(chunks)]
-    direct_ref = refs.pop(0) if len(refs) > 5 else None
-    (out_ref, rows, gains, weights, sems) = refs
+    direct_refs = take(direct)
+    out_ref, rows, gains, weights, sems = refs[-5:]
     width = own_ref.shape[1]
     half_hidden = own_ref.shape[2] // 2
     lane_refs = [ref.at[:, pl.ds(ref.shape[1] - LANES, LANES)] for ref in gain_refs or row_refs]
@@ -217,8 +217,7 @@
     for order in range(2):
         expert = (where_ref[1] + order) % 2
         parts = [own_ref.at[expert], *chunk_refs[order]]
-        if direct_ref is not None:
-            parts.append(direct_ref.at[expert])
+        parts += [ref.at[expert] for ref in direct_refs]
         weight_copies.append(load(chunk_pairs(parts, weights.at[order]), sems.at[1 + order]))
     for copy in row_copies:
         copy.wait()
@@ -236,14 +235,14 @@
         out_ref[:, order * half_hidden : (order + 1) * half_hidden] = hidden.astype(jnp.bfloat16)
 
 
-def run_hidden(where, row_blocks, gain_blocks, own, near, far, direct, first_lane, experts):
+def run_hidden(where, row_blocks, gain_blocks, own, near, far, direct, before, first_lane, experts):
     blocks = len(row_blocks)
     count = sum(block.shape[0] for block in row_blocks)
     _, width, columns = own.shape
-    inputs = [*row_blocks, *gain_blocks, own, *near, *far, *direct]
+    inputs = [*row_blocks, *gain_blocks, own, *near, *far, *direct, *before]
     return pl.pallas_call(
         functools.partial(
-            hidden_kernel, blocks, len(gain_blocks), len(near), first_lane, experts
+            hidden_kernel, blocks, len(gain_blocks), len(near), len(direct), first_lane, experts
         ),
         out_shape=jax.ShapeDtypeStruct((count, columns), jnp.bfloat16),
         in_specs=[pl.BlockSpec(memory_space=pltpu.SMEM)]
@@ -378,34 +377,33 @@
     rows = routes.shape[0] // 2
     distances = range(2, owners, 2)
 
-    chunk, out_chunk = w_in.shape[1] * 21 // 32, w_out.shape[1] * 2 // 3
+    chunk, out_chunk = w_in.shape[1] * 13 // 32, w_out.shape[1] * 2 // 3
 
     lanes = gain_lanes(
         where, experts, routes, route_gain, speaking, talker_routes, talker_gain
     )
     give = lax.dynamic_slice_in_dim(hidden_in, (1 - replica) * rows, rows, 0)
     other = over_replica(give)
-    near_in = send(w_in, group, 0, chunk, other)
+    near_in = [send(w_in, group, index * chunk, chunk, other) for index in range(2)]
     row = build_row(where, hidden_in, other, lanes)
     same = [row] + [over_expert(row, distance) for distance in distances]
-    far_in = over_groups(after(near_in, same[2]))
-    direct_in = over_replica(after(w_in[:, chunk:], near_in, same[2]))
+    far_in = [over_groups(after(near_in[0], same[1]))]
+    far_in.append(over_groups(after(near_in[1], far_in[0])))
+    direct_in = over_replica(after(w_in[:, 2 * chunk :], near_in[0]))
     across = [over_expert(row, 1), over_expert(jnp.concatenate(same[1:]), 1)]
-    near_out = send(w_out, group, 0, out_chunk, *same)
+    near_out = send(w_out, group, 0, out_chunk, near_in[1])
     direct_out = over_replica(after(w_out[:, out_chunk:], direct_in))
     blocks = same + across
-    hidden = run_hidden(where, blocks, [], w_in, [near_in], [far_in], [direct_in], 0, experts)
+    hidden = run_hidden(where, blocks, [], w_in, near_in, far_in, [direct_in], [], 0, experts)
     own = run_down(where, hidden, [], [], [w_out])
     far_out = over_groups(after(near_out, *own))
     own = spread_sums(*own)
-    near_talker_in = send(talker_w_in, group, 0, talker_w_in.shape[1], direct_out, hidden)
-    late_hidden = after(hidden, *own[1:3])
+    late_hidden = after(hidden, own[1])
     give = run_down(where, late_hidden, [near_out], [far_out], [direct_out])
-    near_talker_out = send(talker_w_out, group, 0, talker_w_out.shape[1], near_talker_in)
-    far_talker_in = over_groups(near_talker_in)
-    give = after(add_up(spread_sums(*give, near_talker_in, own[3])), near_talker_out)
-    own = add_up(own)
-    far_talker_out = over_groups(near_talker_out)
+    near_talker_in = send(talker_w_in, group, 0, talker_w_in.shape[1], near_out, hidden)
+    give = spread_sums(*give, *own[2:])
+    far_talker_in = over_groups(after(near_talker_in, give[1]))
+    give, own = add_up(give), add_up(own)
     got = over_replica(give)
     thinker_out = in_order(replica, own, got, 0)
 
@@ -413,6 +411,7 @@
         return jnp.dot(array, handoff, preferred_element_type=jnp.float32)
 
     term = over_replica(handed(got).astype(jnp.bfloat16))
+    direct_talker_out = over_replica(after(talker_w_out, term))
     talker_row = (handed(own) + term.astype(jnp.float32)).astype(jnp.bfloat16)
     parts = jnp.split(talker_row, 2, axis=1)
     talker_row = in_order(replica, parts[0], parts[1], 1)
@@ -426,10 +425,11 @@
         [near_talker_in],
         [far_talker_in],
         [],
+        [direct_talker_out],
         2 * experts,
         experts,
     )
-    give = run_down(where, hidden, [near_talker_out], [far_talker_out], [])
+    give = run_down(where, hidden, [], [], [direct_talker_out])
     got = over_replica(add_up(spread_sums(*give)))
     own = run_down(where, after(hidden, *give), [], [], [talker_w_out])
     own = add_up(spread_sums(*own))

time: 175 us -> 170 us (0.971)
  waiting for transfers between devices: 93.6 us -> 89.1 us
  starting transfers between devices: 46.4 us -> 48.3 us
    ppermute x10 -> x11, waiting for transfers between devices: 44.4 us -> 34.1 us  [over_replica(): return lax.ppermute(array, 'replica', SWAP)]
    ppermute x26, waiting for transfers between devices: 45.1 us -> 52.1 us  [over_expert(): lax.ppermute(array, 'expert', [(at, at ^ distance) for at in range(lax.ax...]
    ppermute x10 -> x11, starting transfers between devices: 11.7 us -> 14.9 us  [over_replica(): return lax.ppermute(array, 'replica', SWAP)]
    ppermute x26, starting transfers between devices: 31.6 us -> 29.6 us  [over_expert(): lax.ppermute(array, 'expert', [(at, at ^ distance) for at in range(lax.ax...]
    unnamed x56 -> x46, local copies, waits for them, and re-layouts: 1.98 us -> 0.11 us
  transfers between devices with their start and end apart: 40 -> 41, of which waited for: 20 -> 23; matrix products, arithmetic and copies ran while one was open for 5% -> 6% of each run, Pallas kernels for 11% -> 7%
where the time goes in v5:
time: 170 us
  waiting for transfers between devices  89.1 us (52%)
  starting transfers between devices  48.3 us (28%)
  Pallas kernels  20.2 us (12%)
  other arithmetic  4.81 us (3%)
  local copies, waits for them, and re-layouts  4.61 us (3%)
  matrix products  1.86 us (1%)
    ppermute x26, waiting for transfers between devices, over_expert(): lax.ppermute(array, 'expert', [(at, at ^ distance) for at in range(lax.ax...  52.1 us
    ppermute x11, waiting for transfers between devices, over_replica(): return lax.ppermute(array, 'replica', SWAP)  34.1 us
    ppermute x26, starting transfers between devices, over_expert(): lax.ppermute(array, 'expert', [(at, at ^ distance) for at in range(lax.ax...  29.6 us
    ppermute x11, starting transfers between devices, over_replica(): return lax.ppermute(array, 'replica', SWAP)  14.9 us
    pallas_call x2, Pallas kernels, run_hidden(): pl.pallas_call(functools.partial(hidden_kernel, blocks, len(gain_blocks),...  12.6 us
    pallas_call x4, Pallas kernels, run_down(): pl.pallas_call(functools.partial(down_kernel, len(near)), out_shape=(shap...  6.38 us
    ppermute x4, starting transfers between devices, over_groups(): return lax.ppermute(array, 'groups', SWAP)  3.75 us
  transfers between devices with their start and end apart: 41, of which 23 were waited for; matrix products, arithmetic and copies ran while one was open for 6% of the time, Pallas kernels for 7%

profile of v5, /device:TPU:0, one launch (start us, length us, event | category | flops | bytes accessed | tf_op | source)
XLA Modules:
  0.0 170.0 jit_solution(4337746343910939609)
XLA Ops:
  1.8 3.0 %collective-permute-start = (bf16[64,1024]{1,0:T(8,128)(2,1)S(1)}, bf16[64,1024]{1,0:T(8,128)(2,1)S(1)}, u32[]{:S(2)}, u32[]{:S(2)}) collective-permute-start(bf16[64,1024]{1,0:T(8,128)(2,1)S(1)} %constant_dynamic-slice_fusion), channel_id=1, source_target_pairs={{0,1},{1,0},{2,3},{3,2},{4,5},{5,4},{6,7},{7,6},{8,9},{9,8},{10,11... | collective-permute-start | bytes 393224 | tf_op jit(solution)/shard_map/ppermute | solution.py:314
  4.8 2.4 %dynamic-slice_bitcast_fusion.1 = (bf16[416,768]{1,0:T(8,128)(2,1)}, bf16[416,768]{1,0:T(8,128)(2,1)}) fusion(bf16[2,1024,768]{2,1,0:T(8,128)(2,1)} %refs_6_.1, s32[]{:T(128)S(6)} %select_n.43), kind=kLoop, calls=%fused_computation.5 | loop fusion | bytes 2555908 | tf_op jit(solution)/shard_map/squeeze | solution.py:332
  13.0 2.6 %collective-permute-start.2 = (bf16[64,2176]{1,0:T(8,128)(2,1)S(1)}, bf16[64,2176]{1,0:T(8,128)(2,1)S(1)}, u32[]{:S(2)}, u32[]{:S(2)}) collective-permute-start(bf16[64,2176]{1,0:T(8,128)(2,1)S(1)} %shard_map.123.refs_0_.refs_6_), channel_id=1, source_target_pairs={{0,8},{2,10},{4,12},{6,14},{8,0},{10,2},{12,4},{14,6},{1,9},{3,11}... | collective-permute-start | bytes 835592 | tf_op jit(solution)/shard_map/ppermute | solution.py:322
  16.2 7.2 %collective-permute-done.1.refs_1_.refs_7_ = bf16[64,2176]{1,0:T(8,128)(2,1)S(1)} collective-permute-done((bf16[64,2176]{1,0:T(8,128)(2,1)S(1)}, bf16[64,2176]{1,0:T(8,128)(2,1)S(1)}, u32[]{:S(2)}, u32[]{:S(2)}) %collective-permute-start.1) | collective-permute-done | bytes 278560 | tf_op jit(solution)/shard_map/ppermute | solution.py:322
  23.3 2.6 %collective-permute-done.6.refs_7_ = bf16[416,768]{1,0:T(8,128)(2,1)} collective-permute-done((bf16[416,768]{1,0:T(8,128)(2,1)}, bf16[416,768]{1,0:T(8,128)(2,1)}, u32[]{:S(2)}, u32[]{:S(2)}) %collective-permute-start.6) | collective-permute-done | bytes 639008 | tf_op jit(solution)/shard_map/ppermute | solution.py:314
  27.7 7.8 %collective-permute-done.2.refs_2_.refs_8_ = bf16[64,2176]{1,0:T(8,128)(2,1)S(1)} collective-permute-done((bf16[64,2176]{1,0:T(8,128)(2,1)S(1)}, bf16[64,2176]{1,0:T(8,128)(2,1)S(1)}, u32[]{:S(2)}, u32[]{:S(2)}) %collective-permute-start.2) | collective-permute-done | bytes 278560 | tf_op jit(solution)/shard_map/ppermute | solution.py:322
  35.6 2.1 %collective-permute-done.7.refs_8_ = bf16[416,768]{1,0:T(8,128)(2,1)S(1)} collective-permute-done((bf16[416,768]{1,0:T(8,128)(2,1)S(1)}, bf16[416,768]{1,0:T(8,128)(2,1)S(1)}, u32[]{:S(2)}, u32[]{:S(2)}) %collective-permute-start.7) | collective-permute-done | bytes 639008 | tf_op jit(solution)/shard_map/ppermute | solution.py:314
  43.5 13.0 %collective-permute-done.10.refs_11_ = bf16[2,192,768]{2,1,0:T(8,128)(2,1)S(1)} collective-permute-done((bf16[2,192,768]{2,1,0:T(8,128)(2,1)S(1)}, bf16[2,192,768]{2,1,0:T(8,128)(2,1)S(1)}, u32[]{:S(2)}, u32[]{:S(2)}) %collective-permute-start.10) | collective-permute-done | bytes 589856 | tf_op jit(solution)/shard_map/ppermute | solution.py:314
  56.5 6.9 %shard_map.124.hidden_ref = bf16[512,768]{1,0:T(8,128)(2,1)S(1)} custom-call(s32[3]{0:T(128)S(1)} %pad_add_fusion.where_ref, bf16[64,2176]{1,0:T(8,128)(2,1)S(1)} %shard_map.123.refs_0_.refs_6_, bf16[64,2176]{1,0:T(8,128)(2,1)S(1)} %collective-permute-done.1.refs_1_.refs_7_, bf16[64,2176]{1,0:T(8,128)(2,1)S(1)} %collective-permute-done.2.refs_2_.refs_8_, ...), custom_call_target="tpu_custom_call" | custom-call | flops 3221225472 | bytes 8388608 | tf_op jit(solution)/shard_map/pallas_call | solution.py:243
  65.3 1.8 %collective-permute-start.17 = (bf16[2,128,1024]{2,1,0:T(8,128)(2,1)S(1)}, bf16[2,128,1024]{2,1,0:T(8,128)(2,1)S(1)}, u32[]{:S(2)}, u32[]{:S(2)}) collective-permute-start(bf16[2,128,1024]{2,1,0:T(8,128)(2,1)S(1)} %slice.111), channel_id=1, source_target_pairs={{0,1},{1,0},{2,3},{3,2},{4,5},{5,4},{6,7},{7,6},{8,9},{9,8},{10,11... | collective-permute-start | bytes 1572872 | tf_op jit(solution)/shard_map/ppermute | solution.py:314
  69.1 4.0 %collective-permute-done.12 = bf16[64,1024]{1,0:T(8,128)(2,1)S(1)} collective-permute-done((bf16[64,1024]{1,0:T(8,128)(2,1)S(1)}, bf16[64,1024]{1,0:T(8,128)(2,1)S(1)}, u32[]{:S(2)}, u32[]{:S(2)}) %collective-permute-start.12) | collective-permute-done | bytes 131104 | tf_op jit(solution)/shard_map/ppermute | solution.py:322
  73.1 6.5 %collective-permute-done.17.refs_2_ = bf16[2,128,1024]{2,1,0:T(8,128)(2,1)S(1)} collective-permute-done((bf16[2,128,1024]{2,1,0:T(8,128)(2,1)S(1)}, bf16[2,128,1024]{2,1,0:T(8,128)(2,1)S(1)}, u32[]{:S(2)}, u32[]{:S(2)}) %collective-permute-start.17) | collective-permute-done | bytes 524320 | tf_op jit(solution)/shard_map/ppermute | solution.py:314
  84.2 2.5 %collective-permute-start.13 = (bf16[64,1024]{1,0:T(8,128)(2,1)S(1)}, bf16[64,1024]{1,0:T(8,128)(2,1)S(1)}, u32[]{:S(2)}, u32[]{:S(2)}) collective-permute-start(bf16[64,1024]{1,0:T(8,128)(2,1)S(1)} %get-tuple-element.60), channel_id=1, source_target_pairs={{0,8},{2,10},{4,12},{6,14},{8,0},{10,2},{12,4},{14,6},{1,9},{3,11}... | collective-permute-start | bytes 393224 | tf_op jit(solution)/shard_map/ppermute | solution.py:322
  88.2 8.9 %collective-permute-done.13 = bf16[64,1024]{1,0:T(8,128)(2,1)S(1)} collective-permute-done((bf16[64,1024]{1,0:T(8,128)(2,1)S(1)}, bf16[64,1024]{1,0:T(8,128)(2,1)S(1)}, u32[]{:S(2)}, u32[]{:S(2)}) %collective-permute-start.13) | collective-permute-done | bytes 131104 | tf_op jit(solution)/shard_map/ppermute | solution.py:322
  97.1 2.8 %collective-permute-start.21 = (bf16[64,1024]{1,0:T(8,128)(2,1)S(1)}, bf16[64,1024]{1,0:T(8,128)(2,1)S(1)}, u32[]{:S(2)}, u32[]{:S(2)}) collective-permute-start(bf16[64,1024]{1,0:T(8,128)(2,1)S(1)} %get-tuple-element.41), channel_id=1, source_target_pairs={{0,12},{2,14},{4,8},{6,10},{8,4},{10,6},{12,0},{14,2},{1,13},{3,15... | collective-permute-start | bytes 393224 | tf_op jit(solution)/shard_map/ppermute | solution.py:322
  104.0 8.3 %collective-permute-done.20 = bf16[64,1024]{1,0:T(8,128)(2,1)S(1)} collective-permute-done((bf16[64,1024]{1,0:T(8,128)(2,1)S(1)}, bf16[64,1024]{1,0:T(8,128)(2,1)S(1)}, u32[]{:S(2)}, u32[]{:S(2)}) %collective-permute-start.20) | collective-permute-done | bytes 131104 | tf_op jit(solution)/shard_map/ppermute | solution.py:322
  115.3 3.5 %collective-permute-done.22 = bf16[64,1024]{1,0:T(8,128)(2,1)} collective-permute-done((bf16[64,1024]{1,0:T(8,128)(2,1)}, bf16[64,1024]{1,0:T(8,128)(2,1)}, u32[]{:S(2)}, u32[]{:S(2)}) %collective-permute-start.22) | collective-permute-done | bytes 131104 | tf_op jit(solution)/shard_map/ppermute | solution.py:314
  123.0 2.2 %collective-permute-done.23 = bf16[64,1024]{1,0:T(8,128)(2,1)S(1)} collective-permute-done((bf16[64,1024]{1,0:T(8,128)(2,1)S(1)}, bf16[64,1024]{1,0:T(8,128)(2,1)S(1)}, u32[]{:S(2)}, u32[]{:S(2)}) %collective-permute-start.23) | collective-permute-done | bytes 131104 | tf_op jit(solution)/shard_map/ppermute | solution.py:314
  127.7 3.4 %collective-permute-start.25 = (bf16[64,1024]{1,0:T(8,128)(2,1)S(1)}, bf16[64,1024]{1,0:T(8,128)(2,1)S(1)}, u32[]{:S(2)}, u32[]{:S(2)}) collective-permute-start(bf16[64,1024]{1,0:T(8,128)(2,1)S(1)} %pad_maximum_fusion.3.refs_0_), channel_id=1, source_target_pairs={{0,8},{2,10},{4,12},{6,14},{8,0},{10,2},{12,4},{14,6},{1,9},{3,11}... | collective-permute-start | bytes 393224 | tf_op jit(solution)/shard_map/ppermute | solution.py:322
  132.6 6.9 %collective-permute-done.25.refs_2_ = bf16[64,1024]{1,0:T(8,128)(2,1)S(1)} collective-permute-done((bf16[64,1024]{1,0:T(8,128)(2,1)S(1)}, bf16[64,1024]{1,0:T(8,128)(2,1)S(1)}, u32[]{:S(2)}, u32[]{:S(2)}) %collective-permute-start.25) | collective-permute-done | bytes 131104 | tf_op jit(solution)/shard_map/ppermute | solution.py:322
  143.1 5.7 %shard_map.127.hidden_ref = bf16[512,768]{1,0:T(8,128)(2,1)S(1)} custom-call(s32[3]{0:T(128)S(1)} %pad_add_fusion.where_ref, bf16[64,1024]{1,0:T(8,128)(2,1)S(1)} %pad_maximum_fusion.3.refs_0_, bf16[64,1024]{1,0:T(8,128)(2,1)S(1)} %collective-permute-done.24.refs_1_, bf16[64,1024]{1,0:T(8,128)(2,1)S(1)} %collective-permute-done.25.refs_2_, ...), custom_call_target="tpu_custom_call" | custom-call | flops 1610612736 | bytes 4194304 | tf_op jit(solution)/shard_map/pallas_call | solution.py:243
  153.5 3.2 %collective-permute-start.39 = (bf16[64,512]{1,0:T(8,128)(2,1)S(1)}, bf16[64,512]{1,0:T(8,128)(2,1)S(1)}, u32[]{:S(2)}, u32[]{:S(2)}) collective-permute-start(bf16[64,512]{1,0:T(8,128)(2,1)S(1)} %get-tuple-element.66), channel_id=1, source_target_pairs={{0,12},{2,14},{4,8},{6,10},{8,4},{10,6},{12,0},{14,2},{1,13},{3,15... | collective-permute-start | bytes 196616 | tf_op jit(solution)/shard_map/ppermute | solution.py:322
  158.0 3.2 %collective-permute-start.35 = (bf16[64,512]{1,0:T(8,128)(2,1)S(1)}, bf16[64,512]{1,0:T(8,128)(2,1)S(1)}, u32[]{:S(2)}, u32[]{:S(2)}) collective-permute-start(bf16[64,512]{1,0:T(8,128)(2,1)S(1)} %get-tuple-element.63), channel_id=1, source_target_pairs={{0,12},{2,14},{4,8},{6,10},{8,4},{10,6},{12,0},{14,2},{1,13},{3,15... | collective-permute-start | bytes 196616 | tf_op jit(solution)/shard_map/ppermute | solution.py:322
  162.4 2.4 %collective-permute-done.38 = bf16[64,512]{1,0:T(8,128)(2,1)S(1)} collective-permute-done((bf16[64,512]{1,0:T(8,128)(2,1)S(1)}, bf16[64,512]{1,0:T(8,128)(2,1)S(1)}, u32[]{:S(2)}, u32[]{:S(2)}) %collective-permute-start.38) | collective-permute-done | bytes 65568 | tf_op jit(solution)/shard_map/ppermute | solution.py:322
  (137 shorter events, 56.1 us)
Async XLA Ops:
  8.3 17.6 %collective-permute-start.6 = (bf16[416,768]{1,0:T(8,128)(2,1)}, bf16[416,768]{1,0:T(8,128)(2,1)}, u32[]{:S(2)}, u32[]{:S(2)}) collective-permute-start(bf16[416,768]{1,0:T(8,128)(2,1)} %get-tuple-element.26), channel_id=1, source_target_pairs={{0,1},{1,0},{2,3},{3,2},{4,5},{5,4},{6,7},{7,6},{8,9},{9,8},{10,11... | collective-permute-start | bytes 1916936 | tf_op jit(solution)/shard_map/ppermute | solution.py:314
  11.4 11.9 %collective-permute-start.1 = (bf16[64,2176]{1,0:T(8,128)(2,1)S(1)}, bf16[64,2176]{1,0:T(8,128)(2,1)S(1)}, u32[]{:S(2)}, u32[]{:S(2)}) collective-permute-start(bf16[64,2176]{1,0:T(8,128)(2,1)S(1)} %shard_map.123.refs_0_.refs_6_), channel_id=1, source_target_pairs={{0,4},{2,6},{4,0},{6,2},{8,12},{10,14},{12,8},{14,10},{1,5},{3,7},... | collective-permute-start | bytes 835592 | tf_op jit(solution)/shard_map/ppermute | solution.py:322
  13.0 22.4 %collective-permute-start.2 = (bf16[64,2176]{1,0:T(8,128)(2,1)S(1)}, bf16[64,2176]{1,0:T(8,128)(2,1)S(1)}, u32[]{:S(2)}, u32[]{:S(2)}) collective-permute-start(bf16[64,2176]{1,0:T(8,128)(2,1)S(1)} %shard_map.123.refs_0_.refs_6_), channel_id=1, source_target_pairs={{0,8},{2,10},{4,12},{6,14},{8,0},{10,2},{12,4},{14,6},{1,9},{3,11}... | collective-permute-start | bytes 835592 | tf_op jit(solution)/shard_map/ppermute | solution.py:322
  15.6 19.8 %collective-permute-start.3 = (bf16[64,2176]{1,0:T(8,128)(2,1)S(1)}, bf16[64,2176]{1,0:T(8,128)(2,1)S(1)}, u32[]{:S(2)}, u32[]{:S(2)}) collective-permute-start(bf16[64,2176]{1,0:T(8,128)(2,1)S(1)} %shard_map.123.refs_0_.refs_6_), channel_id=1, source_target_pairs={{0,12},{2,14},{4,8},{6,10},{8,4},{10,6},{12,0},{14,2},{1,13},{3,15... | collective-permute-start | bytes 835592 | tf_op jit(solution)/shard_map/ppermute | solution.py:322
  15.8 21.9 %collective-permute-start.7 = (bf16[416,768]{1,0:T(8,128)(2,1)S(1)}, bf16[416,768]{1,0:T(8,128)(2,1)S(1)}, u32[]{:S(2)}, u32[]{:S(2)}) collective-permute-start(bf16[416,768]{1,0:T(8,128)(2,1)S(1)} %copy-done.15), channel_id=1, source_target_pairs={{0,1},{1,0},{2,3},{3,2},{4,5},{5,4},{6,7},{7,6},{8,9},{9,8},{10,11... | collective-permute-start | bytes 1916936 | tf_op jit(solution)/shard_map/ppermute | solution.py:314
  25.9 13.3 %collective-permute-start.8 = (bf16[416,768]{1,0:T(8,128)(2,1)}, bf16[416,768]{1,0:T(8,128)(2,1)S(1)}, u32[]{:S(2)}, u32[]{:S(2)}) collective-permute-start(bf16[416,768]{1,0:T(8,128)(2,1)} %collective-permute-done.6.refs_7_), channel_id=1, source_target_pairs={{0,16},{16,0},{1,17},{17,1},{2,18},{18,2},{3,19},{19,3},{4,20},{20... | collective-permute-start | bytes 1916936 | tf_op jit(solution)/shard_map/ppermute | solution.py:318
  35.5 8.0 %collective-permute-start.5 = (bf16[192,2176]{1,0:T(8,128)(2,1)S(1)}, bf16[192,2176]{1,0:T(8,128)(2,1)S(1)}, u32[]{:S(2)}, u32[]{:S(2)}) collective-permute-start(bf16[192,2176]{1,0:T(8,128)(2,1)S(1)} %pad_maximum_fusion), channel_id=1, source_target_pairs={{0,2},{2,0},{4,6},{6,4},{8,10},{10,8},{12,14},{14,12},{1,3},{3,1},... | collective-permute-start | bytes 2506760 | tf_op jit(solution)/shard_map/ppermute | solution.py:322
  39.2 17.3 %collective-permute-start.9 = (bf16[416,768]{1,0:T(8,128)(2,1)S(1)}, bf16[416,768]{1,0:T(8,128)(2,1)S(1)}, u32[]{:S(2)}, u32[]{:S(2)}) collective-permute-start(bf16[416,768]{1,0:T(8,128)(2,1)S(1)} %collective-permute-done.7.refs_8_), channel_id=1, source_target_pairs={{0,16},{16,0},{1,17},{17,1},{2,18},{18,2},{3,19},{19,3},{4,20},{20... | collective-permute-start | bytes 1916936 | tf_op jit(solution)/shard_map/ppermute | solution.py:318
  40.2 16.3 %collective-permute-start.10 = (bf16[2,192,768]{2,1,0:T(8,128)(2,1)S(1)}, bf16[2,192,768]{2,1,0:T(8,128)(2,1)S(1)}, u32[]{:S(2)}, u32[]{:S(2)}) collective-permute-start(bf16[2,192,768]{2,1,0:T(8,128)(2,1)S(1)} %slice.102), channel_id=1, source_target_pairs={{0,1},{1,0},{2,3},{3,2},{4,5},{5,4},{6,7},{7,6},{8,9},{9,8},{10,11... | collective-permute-start | bytes 1769480 | tf_op jit(solution)/shard_map/ppermute | solution.py:314
  42.0 25.0 %collective-permute-start.15 = (bf16[256,1024]{1,0:T(8,128)(2,1)S(1)}, bf16[256,1024]{1,0:T(8,128)(2,1)S(1)}, u32[]{:S(2)}, u32[]{:S(2)}) collective-permute-start(bf16[256,1024]{1,0:T(8,128)(2,1)S(1)} %dynamic-slice_bitcast_fusion.3), channel_id=1, source_target_pairs={{0,1},{1,0},{2,3},{3,2},{4,5},{5,4},{6,7},{7,6},{8,9},{9,8},{10,11... | collective-permute-start | bytes 1572872 | tf_op jit(solution)/shard_map/ppermute | solution.py:314
  65.3 14.4 %collective-permute-start.17 = (bf16[2,128,1024]{2,1,0:T(8,128)(2,1)S(1)}, bf16[2,128,1024]{2,1,0:T(8,128)(2,1)S(1)}, u32[]{:S(2)}, u32[]{:S(2)}) collective-permute-start(bf16[2,128,1024]{2,1,0:T(8,128)(2,1)S(1)} %slice.111), channel_id=1, source_target_pairs={{0,1},{1,0},{2,3},{3,2},{4,5},{5,4},{6,7},{7,6},{8,9},{9,8},{10,11... | collective-permute-start | bytes 1572872 | tf_op jit(solution)/shard_map/ppermute | solution.py:314
  67.1 14.0 %collective-permute-start.16 = (bf16[256,1024]{1,0:T(8,128)(2,1)S(1)}, bf16[256,1024]{1,0:T(8,128)(2,1)S(1)}, u32[]{:S(2)}, u32[]{:S(2)}) collective-permute-start(bf16[256,1024]{1,0:T(8,128)(2,1)S(1)} %collective-permute-done.15.refs_0_), channel_id=1, source_target_pairs={{0,16},{16,0},{1,17},{17,1},{2,18},{18,2},{3,19},{19,3},{4,20},{20... | collective-permute-start | bytes 1572872 | tf_op jit(solution)/shard_map/ppermute | solution.py:318
  83.8 30.9 %collective-permute-start.29 = (bf16[512,768]{1,0:T(8,128)(2,1)}, bf16[512,768]{1,0:T(8,128)(2,1)}, u32[]{:S(2)}, u32[]{:S(2)}) collective-permute-start(bf16[512,768]{1,0:T(8,128)(2,1)} %dynamic-slice_bitcast_fusion), channel_id=1, source_target_pairs={{0,1},{1,0},{2,3},{3,2},{4,5},{5,4},{6,7},{7,6},{8,9},{9,8},{10,11... | collective-permute-start | bytes 2359304 | tf_op jit(solution)/shard_map/ppermute | solution.py:314
  84.2 12.9 %collective-permute-start.13 = (bf16[64,1024]{1,0:T(8,128)(2,1)S(1)}, bf16[64,1024]{1,0:T(8,128)(2,1)S(1)}, u32[]{:S(2)}, u32[]{:S(2)}) collective-permute-start(bf16[64,1024]{1,0:T(8,128)(2,1)S(1)} %get-tuple-element.60), channel_id=1, source_target_pairs={{0,8},{2,10},{4,12},{6,14},{8,0},{10,2},{12,4},{14,6},{1,9},{3,11}... | collective-permute-start | bytes 393224 | tf_op jit(solution)/shard_map/ppermute | solution.py:322
  86.7 10.3 %collective-permute-start.14 = (bf16[64,1024]{1,0:T(8,128)(2,1)S(1)}, bf16[64,1024]{1,0:T(8,128)(2,1)S(1)}, u32[]{:S(2)}, u32[]{:S(2)}) collective-permute-start(bf16[64,1024]{1,0:T(8,128)(2,1)S(1)} %get-tuple-element.59), channel_id=1, source_target_pairs={{0,12},{2,14},{4,8},{6,10},{8,4},{10,6},{12,0},{14,2},{1,13},{3,15... | collective-permute-start | bytes 393224 | tf_op jit(solution)/shard_map/ppermute | solution.py:322
  99.9 12.5 %collective-permute-start.20 = (bf16[64,1024]{1,0:T(8,128)(2,1)S(1)}, bf16[64,1024]{1,0:T(8,128)(2,1)S(1)}, u32[]{:S(2)}, u32[]{:S(2)}) collective-permute-start(bf16[64,1024]{1,0:T(8,128)(2,1)S(1)} %get-tuple-element.40), channel_id=1, source_target_pairs={{0,8},{2,10},{4,12},{6,14},{8,0},{10,2},{12,4},{14,6},{1,9},{3,11}... | collective-permute-start | bytes 393224 | tf_op jit(solution)/shard_map/ppermute | solution.py:322
  101.6 10.7 %collective-permute-start.19 = (bf16[64,1024]{1,0:T(8,128)(2,1)S(1)}, bf16[64,1024]{1,0:T(8,128)(2,1)S(1)}, u32[]{:S(2)}, u32[]{:S(2)}) collective-permute-start(bf16[64,1024]{1,0:T(8,128)(2,1)S(1)} %get-tuple-element.39), channel_id=1, source_target_pairs={{0,4},{2,6},{4,0},{6,2},{8,12},{10,14},{12,8},{14,10},{1,5},{3,7},... | collective-permute-start | bytes 393224 | tf_op jit(solution)/shard_map/ppermute | solution.py:322
  114.7 26.8 %collective-permute-start.30 = (bf16[512,768]{1,0:T(8,128)(2,1)}, bf16[512,768]{1,0:T(8,128)(2,1)S(1)}, u32[]{:S(2)}, u32[]{:S(2)}) collective-permute-start(bf16[512,768]{1,0:T(8,128)(2,1)} %collective-permute-done.29.refs_13_), channel_id=1, source_target_pairs={{0,16},{16,0},{1,17},{17,1},{2,18},{18,2},{3,19},{19,3},{4,20},{20... | collective-permute-start | bytes 2359304 | tf_op jit(solution)/shard_map/ppermute | solution.py:318
  125.3 17.8 %collective-permute-start.31 = (bf16[2,384,512]{2,1,0:T(8,128)(2,1)S(1)}, bf16[2,384,512]{2,1,0:T(8,128)(2,1)S(1)}, u32[]{:S(2)}, u32[]{:S(2)}) collective-permute-start(bf16[2,384,512]{2,1,0:T(8,128)(2,1)S(1)} %copy-done.6), channel_id=1, source_target_pairs={{0,1},{1,0},{2,3},{3,2},{4,5},{5,4},{6,7},{7,6},{8,9},{9,8},{10,11... | collective-permute-start | bytes 2359304 | tf_op jit(solution)/shard_map/ppermute | solution.py:314
  127.7 11.8 %collective-permute-start.25 = (bf16[64,1024]{1,0:T(8,128)(2,1)S(1)}, bf16[64,1024]{1,0:T(8,128)(2,1)S(1)}, u32[]{:S(2)}, u32[]{:S(2)}) collective-permute-start(bf16[64,1024]{1,0:T(8,128)(2,1)S(1)} %pad_maximum_fusion.3.refs_0_), channel_id=1, source_target_pairs={{0,8},{2,10},{4,12},{6,14},{8,0},{10,2},{12,4},{14,6},{1,9},{3,11}... | collective-permute-start | bytes 393224 | tf_op jit(solution)/shard_map/ppermute | solution.py:322
  131.1 8.5 %collective-permute-start.26 = (bf16[64,1024]{1,0:T(8,128)(2,1)S(1)}, bf16[64,1024]{1,0:T(8,128)(2,1)S(1)}, u32[]{:S(2)}, u32[]{:S(2)}) collective-permute-start(bf16[64,1024]{1,0:T(8,128)(2,1)S(1)} %pad_maximum_fusion.3.refs_0_), channel_id=1, source_target_pairs={{0,12},{2,14},{4,8},{6,10},{8,4},{10,6},{12,0},{14,2},{1,13},{3,15... | collective-permute-start | bytes 393224 | tf_op jit(solution)/shard_map/ppermute | solution.py:322
  156.6 8.2 %collective-permute-start.38 = (bf16[64,512]{1,0:T(8,128)(2,1)S(1)}, bf16[64,512]{1,0:T(8,128)(2,1)S(1)}, u32[]{:S(2)}, u32[]{:S(2)}) collective-permute-start(bf16[64,512]{1,0:T(8,128)(2,1)S(1)} %get-tuple-element.67), channel_id=1, source_target_pairs={{0,8},{2,10},{4,12},{6,14},{8,0},{10,2},{12,4},{14,6},{1,9},{3,11}... | collective-permute-start | bytes 196616 | tf_op jit(solution)/shard_map/ppermute | solution.py:322
  156.6 8.2 %collective-permute-start.37 = (bf16[64,512]{1,0:T(8,128)(2,1)S(1)}, bf16[64,512]{1,0:T(8,128)(2,1)S(1)}, u32[]{:S(2)}, u32[]{:S(2)}) collective-permute-start(bf16[64,512]{1,0:T(8,128)(2,1)S(1)} %get-tuple-element.65), channel_id=1, source_target_pairs={{0,4},{2,6},{4,0},{6,2},{8,12},{10,14},{12,8},{14,10},{1,5},{3,7},... | collective-permute-start | bytes 196616 | tf_op jit(solution)/shard_map/ppermute | solution.py:322
  158.0 8.3 %collective-permute-start.35 = (bf16[64,512]{1,0:T(8,128)(2,1)S(1)}, bf16[64,512]{1,0:T(8,128)(2,1)S(1)}, u32[]{:S(2)}, u32[]{:S(2)}) collective-permute-start(bf16[64,512]{1,0:T(8,128)(2,1)S(1)} %get-tuple-element.63), channel_id=1, source_target_pairs={{0,12},{2,14},{4,8},{6,10},{8,4},{10,6},{12,0},{14,2},{1,13},{3,15... | collective-permute-start | bytes 196616 | tf_op jit(solution)/shard_map/ppermute | solution.py:322
  (40 other events, 489.2 us)

commit v6 on v5

--- a/solution.py
+++ b/solution.py
@@ -333,16 +333,27 @@
     return over_replica(after(piece, *before))
 
 
-def spread_sums(mine, away, *before):
+def over_both(array, distance):
+    owners = lax.axis_size("expert")
+    pairs = [
+        (2 * at + replica, 2 * (at ^ distance) + 1 - replica)
+        for at in range(owners)
+        for replica in range(2)
+    ]
+    return lax.ppermute(array, ("expert", "replica"), pairs)
+
+
+def spread_sums(mine, away, before=(), hold=(), cross=False):
     owners = lax.axis_size("expert")
     rows = mine.shape[0] // (owners // 2)
-    other = over_expert(away, 1)
+    other = over_expert(after(away, *hold), 1)
     terms = []
     for index in range(owners // 2):
         part = slice(index * rows, (index + 1) * rows)
         chip = mine[part].astype(jnp.float32) + other[part].astype(jnp.float32)
-        if index:
-            chip = over_expert(after(chip.astype(jnp.bfloat16), *before), 2 * index)
+        if cross or index:
+            chip = after(chip.astype(jnp.bfloat16), *before)
+            chip = (over_both if cross else over_expert)(chip, 2 * index)
         terms.append(chip)
     return terms
 
@@ -377,34 +388,35 @@
     rows = routes.shape[0] // 2
     distances = range(2, owners, 2)
 
-    chunk, out_chunk = w_in.shape[1] * 13 // 32, w_out.shape[1] * 2 // 3
+    width, chunk, out_chunk = w_in.shape[1], w_in.shape[1] * 11 // 32, w_out.shape[1] * 2 // 3
 
     lanes = gain_lanes(
         where, experts, routes, route_gain, speaking, talker_routes, talker_gain
     )
     give = lax.dynamic_slice_in_dim(hidden_in, (1 - replica) * rows, rows, 0)
     other = over_replica(give)
-    near_in = [send(w_in, group, index * chunk, chunk, other) for index in range(2)]
+    near_in = [
+        send(w_in, group, first, min(chunk, width - first), other)
+        for first in range(0, width, chunk)
+    ]
     row = build_row(where, hidden_in, other, lanes)
     same = [row] + [over_expert(row, distance) for distance in distances]
     far_in = [over_groups(after(near_in[0], same[1]))]
-    far_in.append(over_groups(after(near_in[1], far_in[0])))
-    direct_in = over_replica(after(w_in[:, 2 * chunk :], near_in[0]))
+    for part in near_in[1:]:
+        far_in.append(over_groups(after(part, far_in[-1])))
     across = [over_expert(row, 1), over_expert(jnp.concatenate(same[1:]), 1)]
     near_out = send(w_out, group, 0, out_chunk, near_in[1])
-    direct_out = over_replica(after(w_out[:, out_chunk:], direct_in))
+    direct_out = over_replica(after(w_out[:, out_chunk:], near_out))
+    far_out = over_groups(near_out)
     blocks = same + across
-    hidden = run_hidden(where, blocks, [], w_in, near_in, far_in, [direct_in], [], 0, experts)
+    hidden = run_hidden(where, blocks, [], w_in, near_in, far_in, [], [near_out], 0, experts)
     own = run_down(where, hidden, [], [], [w_out])
-    far_out = over_groups(after(near_out, *own))
-    own = spread_sums(*own)
-    late_hidden = after(hidden, own[1])
-    give = run_down(where, late_hidden, [near_out], [far_out], [direct_out])
+    own = spread_sums(*own, hold=[direct_out, far_out])
     near_talker_in = send(talker_w_in, group, 0, talker_w_in.shape[1], near_out, hidden)
-    give = spread_sums(*give, *own[2:])
-    far_talker_in = over_groups(after(near_talker_in, give[1]))
-    give, own = add_up(give), add_up(own)
-    got = over_replica(give)
+    give = run_down(where, hidden, [near_out], [far_out], [direct_out])
+    got = spread_sums(*give, before=[own[2], near_talker_in], cross=True)
+    far_talker_in = over_groups(near_talker_in)
+    got, own = add_up(got), add_up(own)
     thinker_out = in_order(replica, own, got, 0)
 
     def handed(array):
@@ -416,7 +428,8 @@
     parts = jnp.split(talker_row, 2, axis=1)
     talker_row = in_order(replica, parts[0], parts[1], 1)
     same = [talker_row] + [over_expert(talker_row, distance) for distance in distances]
-    talker_blocks = same + [over_expert(talker_row, 1), over_expert(jnp.concatenate(same[1:]), 1)]
+    rest = after(jnp.concatenate(same[1:]), far_talker_in)
+    talker_blocks = same + [over_expert(talker_row, 1), over_expert(rest, 1)]
     hidden = run_hidden(
         where,
         talker_blocks,
@@ -430,7 +443,7 @@
         experts,
     )
     give = run_down(where, hidden, [], [], [direct_talker_out])
-    got = over_replica(add_up(spread_sums(*give)))
+    got = add_up(spread_sums(*give, cross=True))
     own = run_down(where, after(hidden, *give), [], [], [talker_w_out])
     own = add_up(spread_sums(*own))
     return (thinker_out, in_order(replica, own, got, 0))

time: 170 us -> 166 us (0.976)
  waiting for transfers between devices: 89.1 us -> 74.8 us
  starting transfers between devices: 48.3 us -> 59.8 us
    ppermute x26 -> x20, waiting for transfers between devices: 52.1 us -> 31.7 us  [over_expert(): lax.ppermute(array, 'expert', [(at, at ^ distance) for at in range(lax.ax...]
    ppermute x0 -> x8, starting transfers between devices: none -> 17.8 us  [over_both(): return lax.ppermute(array, ('expert', 'replica'), pairs)]
    ppermute x0 -> x8, waiting for transfers between devices: none -> 11.1 us  [over_both(): return lax.ppermute(array, ('expert', 'replica'), pairs)]
    ppermute x26 -> x20, starting transfers between devices: 29.6 us -> 25 us  [over_expert(): lax.ppermute(array, 'expert', [(at, at ^ distance) for at in range(lax.ax...]
    ppermute x11 -> x9, starting transfers between devices: 14.9 us -> 10.8 us  [over_replica(): return lax.ppermute(array, 'replica', SWAP)]
    ppermute x11 -> x9, waiting for transfers between devices: 34.1 us -> 30 us  [over_replica(): return lax.ppermute(array, 'replica', SWAP)]
    ppermute x4 -> x5, starting transfers between devices: 3.75 us -> 6.28 us  [over_groups(): return lax.ppermute(array, 'groups', SWAP)]
  transfers between devices with their start and end apart: 41 -> 42, of which waited for: 23 -> 19; matrix products, arithmetic and copies ran while one was open for 6% -> 3% of each run, Pallas kernels for 7% -> 8%
where the time goes in v6:
time: 166 us
  waiting for transfers between devices  74.8 us (45%)
  starting transfers between devices  59.8 us (36%)
  Pallas kernels  20.2 us (12%)
  other arithmetic  5.07 us (3%)
  local copies, waits for them, and re-layouts  4.33 us (3%)
    ppermute x20, waiting for transfers between devices, over_expert(): lax.ppermute(array, 'expert', [(at, at ^ distance) for at in range(lax.ax...  31.7 us
    ppermute x9, waiting for transfers between devices, over_replica(): return lax.ppermute(array, 'replica', SWAP)  30 us
    ppermute x20, starting transfers between devices, over_expert(): lax.ppermute(array, 'expert', [(at, at ^ distance) for at in range(lax.ax...  25 us
    ppermute x8, starting transfers between devices, over_both(): return lax.ppermute(array, ('expert', 'replica'), pairs)  17.8 us
    pallas_call x2, Pallas kernels, run_hidden(): pl.pallas_call(functools.partial(hidden_kernel, blocks, len(gain_blocks),...  12.5 us
    ppermute x8, waiting for transfers between devices, over_both(): return lax.ppermute(array, ('expert', 'replica'), pairs)  11.1 us
    ppermute x9, starting transfers between devices, over_replica(): return lax.ppermute(array, 'replica', SWAP)  10.8 us
    pallas_call x4, Pallas kernels, run_down(): pl.pallas_call(functools.partial(down_kernel, len(near)), out_shape=(shap...  6.41 us
  transfers between devices with their start and end apart: 42, of which 19 were waited for; matrix products, arithmetic and copies ran while one was open for 3% of the time, Pallas kernels for 8%

profile of v6, /device:TPU:0, one launch (start us, length us, event | category | flops | bytes accessed | tf_op | source)
XLA Modules:
  0.0 166.1 jit_solution(9196111775315429963)
XLA Ops:
  1.8 3.0 %collective-permute-start = (bf16[64,1024]{1,0:T(8,128)(2,1)S(1)}, bf16[64,1024]{1,0:T(8,128)(2,1)S(1)}, u32[]{:S(2)}, u32[]{:S(2)}) collective-permute-start(bf16[64,1024]{1,0:T(8,128)(2,1)S(1)} %constant_dynamic-slice_fusion), channel_id=1, source_target_pairs={{0,1},{1,0},{2,3},{3,2},{4,5},{5,4},{6,7},{7,6},{8,9},{9,8},{10,11... | collective-permute-start | bytes 393224 | tf_op jit(solution)/shard_map/ppermute | solution.py:314
  4.8 2.1 %dynamic-slice_bitcast_fusion.1 = (bf16[352,768]{1,0:T(8,128)(2,1)}, bf16[352,768]{1,0:T(8,128)(2,1)S(1)}) fusion(bf16[2,1024,768]{2,1,0:T(8,128)(2,1)} %refs_6_.1, s32[]{:T(128)S(6)} %select_n.44), kind=kLoop, calls=%fused_computation.5 | loop fusion | bytes 2162692 | tf_op jit(solution)/shard_map/squeeze | solution.py:332
  13.5 5.1 %collective-permute-done.1.refs_1_.refs_7_ = bf16[64,2176]{1,0:T(8,128)(2,1)S(1)} collective-permute-done((bf16[64,2176]{1,0:T(8,128)(2,1)S(1)}, bf16[64,2176]{1,0:T(8,128)(2,1)S(1)}, u32[]{:S(2)}, u32[]{:S(2)}) %collective-permute-start.1) | collective-permute-done | bytes 278560 | tf_op jit(solution)/shard_map/ppermute | solution.py:322
  18.7 4.9 %collective-permute-done.6.refs_7_ = bf16[352,768]{1,0:T(8,128)(2,1)} collective-permute-done((bf16[352,768]{1,0:T(8,128)(2,1)S(1)}, bf16[352,768]{1,0:T(8,128)(2,1)}, u32[]{:S(2)}, u32[]{:S(2)}) %collective-permute-start.6) | collective-permute-done | bytes 540704 | tf_op jit(solution)/shard_map/ppermute | solution.py:314
  23.6 1.8 %collective-permute-start.9 = (bf16[352,768]{1,0:T(8,128)(2,1)}, bf16[352,768]{1,0:T(8,128)(2,1)S(1)}, u32[]{:S(2)}, u32[]{:S(2)}) collective-permute-start(bf16[352,768]{1,0:T(8,128)(2,1)} %collective-permute-done.6.refs_7_), channel_id=1, source_target_pairs={{0,16},{16,0},{1,17},{17,1},{2,18},{18,2},{3,19},{19,3},{4,20},{20... | collective-permute-start | bytes 1622024 | tf_op jit(solution)/shard_map/ppermute | solution.py:318
  25.3 2.6 %collective-permute-start.2 = (bf16[64,2176]{1,0:T(8,128)(2,1)S(1)}, bf16[64,2176]{1,0:T(8,128)(2,1)S(1)}, u32[]{:S(2)}, u32[]{:S(2)}) collective-permute-start(bf16[64,2176]{1,0:T(8,128)(2,1)S(1)} %shard_map.123.refs_0_.refs_6_), channel_id=1, source_target_pairs={{0,8},{2,10},{4,12},{6,14},{8,0},{10,2},{12,4},{14,6},{1,9},{3,11}... | collective-permute-start | bytes 835592 | tf_op jit(solution)/shard_map/ppermute | solution.py:322
  30.9 4.2 %collective-permute-done.7.refs_8_ = bf16[352,768]{1,0:T(8,128)(2,1)S(1)} collective-permute-done((bf16[352,768]{1,0:T(8,128)(2,1)}, bf16[352,768]{1,0:T(8,128)(2,1)S(1)}, u32[]{:S(2)}, u32[]{:S(2)}) %collective-permute-start.7) | collective-permute-done | bytes 540704 | tf_op jit(solution)/shard_map/ppermute | solution.py:314
  35.1 1.8 %collective-permute-start.10 = (bf16[352,768]{1,0:T(8,128)(2,1)S(1)}, bf16[352,768]{1,0:T(8,128)(2,1)S(1)}, u32[]{:S(2)}, u32[]{:S(2)}) collective-permute-start(bf16[352,768]{1,0:T(8,128)(2,1)S(1)} %collective-permute-done.7.refs_8_), channel_id=1, source_target_pairs={{0,16},{16,0},{1,17},{17,1},{2,18},{18,2},{3,19},{19,3},{4,20},{20... | collective-permute-start | bytes 1622024 | tf_op jit(solution)/shard_map/ppermute | solution.py:318
  36.8 6.8 %collective-permute-done.2.refs_2_.refs_8_ = bf16[64,2176]{1,0:T(8,128)(2,1)S(1)} collective-permute-done((bf16[64,2176]{1,0:T(8,128)(2,1)S(1)}, bf16[64,2176]{1,0:T(8,128)(2,1)S(1)}, u32[]{:S(2)}, u32[]{:S(2)}) %collective-permute-start.2) | collective-permute-done | bytes 278560 | tf_op jit(solution)/shard_map/ppermute | solution.py:322
  47.3 10.9 %collective-permute-done.12.refs_13_.refs_0_ = bf16[256,1024]{1,0:T(8,128)(2,1)S(1)} collective-permute-done((bf16[256,1024]{1,0:T(8,128)(2,1)S(1)}, bf16[256,1024]{1,0:T(8,128)(2,1)S(1)}, u32[]{:S(2)}, u32[]{:S(2)}) %collective-permute-start.12) | collective-permute-done | bytes 524320 | tf_op jit(solution)/shard_map/ppermute | solution.py:314
  60.2 6.9 %shard_map.124.hidden_ref = bf16[512,768]{1,0:T(8,128)(2,1)S(1)} custom-call(s32[3]{0:T(128)S(1)} %pad_add_fusion.where_ref, bf16[64,2176]{1,0:T(8,128)(2,1)S(1)} %shard_map.123.refs_0_.refs_6_, bf16[64,2176]{1,0:T(8,128)(2,1)S(1)} %collective-permute-done.1.refs_1_.refs_7_, bf16[64,2176]{1,0:T(8,128)(2,1)S(1)} %collective-permute-done.2.refs_2_.refs_8_, ...), custom_call_target="tpu_custom_call" | custom-call | flops 3221225472 | bytes 8388608 | tf_op jit(solution)/shard_map/pallas_call | solution.py:243
  69.7 2.0 %collective-permute-done.13.refs_2_ = bf16[2,128,1024]{2,1,0:T(8,128)(2,1)S(1)} collective-permute-done((bf16[2,128,1024]{2,1,0:T(8,128)(2,1)S(1)}, bf16[2,128,1024]{2,1,0:T(8,128)(2,1)S(1)}, u32[]{:S(2)}, u32[]{:S(2)}) %collective-permute-start.13) | collective-permute-done | bytes 524320 | tf_op jit(solution)/shard_map/ppermute | solution.py:314
  76.4 7.4 %collective-permute-start.17 = (bf16[64,1024]{1,0:T(8,128)(2,1)S(1)}, bf16[64,1024]{1,0:T(8,128)(2,1)S(1)}, u32[]{:S(2)}, u32[]{:S(2)}) collective-permute-start(bf16[64,1024]{1,0:T(8,128)(2,1)S(1)} %get-tuple-element.66), channel_id=1, source_target_pairs={{0,8},{2,10},{4,12},{6,14},{8,0},{10,2},{12,4},{14,6},{1,9},{3,11}... | collective-permute-start | bytes 393224 | tf_op jit(solution)/shard_map/ppermute | solution.py:322
  86.2 5.3 %collective-permute-done.17 = bf16[64,1024]{1,0:T(8,128)(2,1)S(1)} collective-permute-done((bf16[64,1024]{1,0:T(8,128)(2,1)S(1)}, bf16[64,1024]{1,0:T(8,128)(2,1)S(1)}, u32[]{:S(2)}, u32[]{:S(2)}) %collective-permute-start.17) | collective-permute-done | bytes 131104 | tf_op jit(solution)/shard_map/ppermute | solution.py:322
  93.7 6.4 %collective-permute-start.22 = (bf16[64,1024]{1,0:T(8,128)(2,1)}, bf16[64,1024]{1,0:T(8,128)(2,1)}, u32[]{:S(2)}, u32[]{:S(2)}) collective-permute-start(bf16[64,1024]{1,0:T(8,128)(2,1)} %get-tuple-element.42), channel_id=1, source_target_pairs={{0,5},{1,4},{2,7},{3,6},{4,1},{5,0},{6,3},{7,2},{8,13},{9,12},{10,... | collective-permute-start | bytes 393224 | tf_op jit(solution)/shard_map/ppermute | solution.py:343
  100.0 1.9 %collective-permute-start.23 = (bf16[64,1024]{1,0:T(8,128)(2,1)}, bf16[64,1024]{1,0:T(8,128)(2,1)}, u32[]{:S(2)}, u32[]{:S(2)}) collective-permute-start(bf16[64,1024]{1,0:T(8,128)(2,1)} %get-tuple-element.43), channel_id=1, source_target_pairs={{0,9},{1,8},{2,11},{3,10},{4,13},{5,12},{6,15},{7,14},{8,1},{9,0},... | collective-permute-start | bytes 393224 | tf_op jit(solution)/shard_map/ppermute | solution.py:343
  103.9 9.7 %collective-permute-done.23 = bf16[64,1024]{1,0:T(8,128)(2,1)} collective-permute-done((bf16[64,1024]{1,0:T(8,128)(2,1)}, bf16[64,1024]{1,0:T(8,128)(2,1)}, u32[]{:S(2)}, u32[]{:S(2)}) %collective-permute-start.23) | collective-permute-done | bytes 131104 | tf_op jit(solution)/shard_map/ppermute | solution.py:343
  117.1 5.0 %collective-permute-done.25 = bf16[64,1024]{1,0:T(8,128)(2,1)S(1)} collective-permute-done((bf16[64,1024]{1,0:T(8,128)(2,1)S(1)}, bf16[64,1024]{1,0:T(8,128)(2,1)S(1)}, u32[]{:S(2)}, u32[]{:S(2)}) %collective-permute-start.25) | collective-permute-done | bytes 131104 | tf_op jit(solution)/shard_map/ppermute | solution.py:314
  128.4 7.1 %collective-permute-done.27.refs_2_ = bf16[64,1024]{1,0:T(8,128)(2,1)S(1)} collective-permute-done((bf16[64,1024]{1,0:T(8,128)(2,1)S(1)}, bf16[64,1024]{1,0:T(8,128)(2,1)S(1)}, u32[]{:S(2)}, u32[]{:S(2)}) %collective-permute-start.27) | collective-permute-done | bytes 131104 | tf_op jit(solution)/shard_map/ppermute | solution.py:322
  137.5 5.7 %shard_map.127.hidden_ref = bf16[512,768]{1,0:T(8,128)(2,1)S(1)} custom-call(s32[3]{0:T(128)S(1)} %pad_add_fusion.where_ref, bf16[64,1024]{1,0:T(8,128)(2,1)S(1)} %pad_maximum_fusion.3.refs_0_, bf16[64,1024]{1,0:T(8,128)(2,1)S(1)} %collective-permute-done.26.refs_1_, bf16[64,1024]{1,0:T(8,128)(2,1)S(1)} %collective-permute-done.27.refs_2_, ...), custom_call_target="tpu_custom_call" | custom-call | flops 1610612736 | bytes 4194304 | tf_op jit(solution)/shard_map/pallas_call | solution.py:243
  148.2 2.8 %collective-permute-start.39 = (bf16[64,512]{1,0:T(8,128)(2,1)S(1)}, bf16[64,512]{1,0:T(8,128)(2,1)S(1)}, u32[]{:S(2)}, u32[]{:S(2)}) collective-permute-start(bf16[64,512]{1,0:T(8,128)(2,1)S(1)} %get-tuple-element.70), channel_id=1, source_target_pairs={{0,5},{1,4},{2,7},{3,6},{4,1},{5,0},{6,3},{7,2},{8,13},{9,12},{10,... | collective-permute-start | bytes 196616 | tf_op jit(solution)/shard_map/ppermute | solution.py:343
  151.1 1.8 %collective-permute-start.40 = (bf16[64,512]{1,0:T(8,128)(2,1)S(1)}, bf16[64,512]{1,0:T(8,128)(2,1)S(1)}, u32[]{:S(2)}, u32[]{:S(2)}) collective-permute-start(bf16[64,512]{1,0:T(8,128)(2,1)S(1)} %get-tuple-element.69), channel_id=1, source_target_pairs={{0,9},{1,8},{2,11},{3,10},{4,13},{5,12},{6,15},{7,14},{8,1},{9,0},... | collective-permute-start | bytes 196616 | tf_op jit(solution)/shard_map/ppermute | solution.py:343
  155.6 2.9 %collective-permute-start.35 = (bf16[64,512]{1,0:T(8,128)(2,1)S(1)}, bf16[64,512]{1,0:T(8,128)(2,1)S(1)}, u32[]{:S(2)}, u32[]{:S(2)}) collective-permute-start(bf16[64,512]{1,0:T(8,128)(2,1)S(1)} %get-tuple-element.73), channel_id=1, source_target_pairs={{0,8},{2,10},{4,12},{6,14},{8,0},{10,2},{12,4},{14,6},{1,9},{3,11}... | collective-permute-start | bytes 196616 | tf_op jit(solution)/shard_map/ppermute | solution.py:322
  160.6 4.8 %collective-permute-done.35 = bf16[64,512]{1,0:T(8,128)(2,1)S(1)} collective-permute-done((bf16[64,512]{1,0:T(8,128)(2,1)S(1)}, bf16[64,512]{1,0:T(8,128)(2,1)S(1)}, u32[]{:S(2)}, u32[]{:S(2)}) %collective-permute-start.35) | collective-permute-done | bytes 65568 | tf_op jit(solution)/shard_map/ppermute | solution.py:322
  (125 shorter events, 52.3 us)
Async XLA Ops:
  8.3 15.3 %collective-permute-start.6 = (bf16[352,768]{1,0:T(8,128)(2,1)S(1)}, bf16[352,768]{1,0:T(8,128)(2,1)}, u32[]{:S(2)}, u32[]{:S(2)}) collective-permute-start(bf16[352,768]{1,0:T(8,128)(2,1)S(1)} %get-tuple-element.27), channel_id=1, source_target_pairs={{0,1},{1,0},{2,3},{3,2},{4,5},{5,4},{6,7},{7,6},{8,9},{9,8},{10,11... | collective-permute-start | bytes 1622024 | tf_op jit(solution)/shard_map/ppermute | solution.py:314
  13.0 22.0 %collective-permute-start.7 = (bf16[352,768]{1,0:T(8,128)(2,1)}, bf16[352,768]{1,0:T(8,128)(2,1)S(1)}, u32[]{:S(2)}, u32[]{:S(2)}) collective-permute-start(bf16[352,768]{1,0:T(8,128)(2,1)} %get-tuple-element.28), channel_id=1, source_target_pairs={{0,1},{1,0},{2,3},{3,2},{4,5},{5,4},{6,7},{7,6},{8,9},{9,8},{10,11... | collective-permute-start | bytes 1622024 | tf_op jit(solution)/shard_map/ppermute | solution.py:314
  23.6 11.5 %collective-permute-start.9 = (bf16[352,768]{1,0:T(8,128)(2,1)}, bf16[352,768]{1,0:T(8,128)(2,1)S(1)}, u32[]{:S(2)}, u32[]{:S(2)}) collective-permute-start(bf16[352,768]{1,0:T(8,128)(2,1)} %collective-permute-done.6.refs_7_), channel_id=1, source_target_pairs={{0,16},{16,0},{1,17},{17,1},{2,18},{18,2},{3,19},{19,3},{4,20},{20... | collective-permute-start | bytes 1622024 | tf_op jit(solution)/shard_map/ppermute | solution.py:318
  25.3 18.3 %collective-permute-start.2 = (bf16[64,2176]{1,0:T(8,128)(2,1)S(1)}, bf16[64,2176]{1,0:T(8,128)(2,1)S(1)}, u32[]{:S(2)}, u32[]{:S(2)}) collective-permute-start(bf16[64,2176]{1,0:T(8,128)(2,1)S(1)} %shard_map.123.refs_0_.refs_6_), channel_id=1, source_target_pairs={{0,8},{2,10},{4,12},{6,14},{8,0},{10,2},{12,4},{14,6},{1,9},{3,11}... | collective-permute-start | bytes 835592 | tf_op jit(solution)/shard_map/ppermute | solution.py:322
  27.9 15.7 %collective-permute-start.3 = (bf16[64,2176]{1,0:T(8,128)(2,1)S(1)}, bf16[64,2176]{1,0:T(8,128)(2,1)S(1)}, u32[]{:S(2)}, u32[]{:S(2)}) collective-permute-start(bf16[64,2176]{1,0:T(8,128)(2,1)S(1)} %shard_map.123.refs_0_.refs_6_), channel_id=1, source_target_pairs={{0,12},{2,14},{4,8},{6,10},{8,4},{10,6},{12,0},{14,2},{1,13},{3,15... | collective-permute-start | bytes 835592 | tf_op jit(solution)/shard_map/ppermute | solution.py:322
  29.3 16.1 %collective-permute-start.8 = (bf16[320,768]{1,0:T(8,128)(2,1)S(1)}, bf16[320,768]{1,0:T(8,128)(2,1)S(1)}, u32[]{:S(2)}, u32[]{:S(2)}) collective-permute-start(bf16[320,768]{1,0:T(8,128)(2,1)S(1)} %dynamic-slice_bitcast_fusion.4), channel_id=1, source_target_pairs={{0,1},{1,0},{2,3},{3,2},{4,5},{5,4},{6,7},{7,6},{8,9},{9,8},{10,11... | collective-permute-start | bytes 1474568 | tf_op jit(solution)/shard_map/ppermute | solution.py:314
  35.1 11.1 %collective-permute-start.10 = (bf16[352,768]{1,0:T(8,128)(2,1)S(1)}, bf16[352,768]{1,0:T(8,128)(2,1)S(1)}, u32[]{:S(2)}, u32[]{:S(2)}) collective-permute-start(bf16[352,768]{1,0:T(8,128)(2,1)S(1)} %collective-permute-done.7.refs_8_), channel_id=1, source_target_pairs={{0,16},{16,0},{1,17},{17,1},{2,18},{18,2},{3,19},{19,3},{4,20},{20... | collective-permute-start | bytes 1622024 | tf_op jit(solution)/shard_map/ppermute | solution.py:318
  43.7 16.5 %collective-permute-start.5 = (bf16[192,2176]{1,0:T(8,128)(2,1)S(1)}, bf16[192,2176]{1,0:T(8,128)(2,1)S(1)}, u32[]{:S(2)}, u32[]{:S(2)}) collective-permute-start(bf16[192,2176]{1,0:T(8,128)(2,1)S(1)} %pad_maximum_fusion), channel_id=1, source_target_pairs={{0,2},{2,0},{4,6},{6,4},{8,10},{10,8},{12,14},{14,12},{1,3},{3,1},... | collective-permute-start | bytes 2506760 | tf_op jit(solution)/shard_map/ppermute | solution.py:322
  43.8 14.4 %collective-permute-start.12 = (bf16[256,1024]{1,0:T(8,128)(2,1)S(1)}, bf16[256,1024]{1,0:T(8,128)(2,1)S(1)}, u32[]{:S(2)}, u32[]{:S(2)}) collective-permute-start(bf16[256,1024]{1,0:T(8,128)(2,1)S(1)} %dynamic-slice_bitcast_fusion.3), channel_id=1, source_target_pairs={{0,1},{1,0},{2,3},{3,2},{4,5},{5,4},{6,7},{7,6},{8,9},{9,8},{10,11... | collective-permute-start | bytes 1572872 | tf_op jit(solution)/shard_map/ppermute | solution.py:314
  46.2 14.0 %collective-permute-start.11 = (bf16[320,768]{1,0:T(8,128)(2,1)S(1)}, bf16[320,768]{1,0:T(8,128)(2,1)S(1)}, u32[]{:S(2)}, u32[]{:S(2)}) collective-permute-start(bf16[320,768]{1,0:T(8,128)(2,1)S(1)} %collective-permute-done.8.refs_9_), channel_id=1, source_target_pairs={{0,16},{16,0},{1,17},{17,1},{2,18},{18,2},{3,19},{19,3},{4,20},{20... | collective-permute-start | bytes 1474568 | tf_op jit(solution)/shard_map/ppermute | solution.py:318
  47.3 12.9 %collective-permute-start.4 = (bf16[64,2176]{1,0:T(8,128)(2,1)S(1)}, bf16[64,2176]{1,0:T(8,128)(2,1)S(1)}, u32[]{:S(2)}, u32[]{:S(2)}) collective-permute-start(bf16[64,2176]{1,0:T(8,128)(2,1)S(1)} %shard_map.123.refs_0_.refs_6_), channel_id=1, source_target_pairs={{0,2},{2,0},{4,6},{6,4},{8,10},{10,8},{12,14},{14,12},{1,3},{3,1},... | collective-permute-start | bytes 835592 | tf_op jit(solution)/shard_map/ppermute | solution.py:322
  58.2 13.5 %collective-permute-start.13 = (bf16[2,128,1024]{2,1,0:T(8,128)(2,1)S(1)}, bf16[2,128,1024]{2,1,0:T(8,128)(2,1)S(1)}, u32[]{:S(2)}, u32[]{:S(2)}) collective-permute-start(bf16[2,128,1024]{2,1,0:T(8,128)(2,1)S(1)} %slice.100), channel_id=1, source_target_pairs={{0,1},{1,0},{2,3},{3,2},{4,5},{5,4},{6,7},{7,6},{8,9},{9,8},{10,11... | collective-permute-start | bytes 1572872 | tf_op jit(solution)/shard_map/ppermute | solution.py:314
  59.7 13.2 %collective-permute-start.14 = (bf16[256,1024]{1,0:T(8,128)(2,1)S(1)}, bf16[256,1024]{1,0:T(8,128)(2,1)S(1)}, u32[]{:S(2)}, u32[]{:S(2)}) collective-permute-start(bf16[256,1024]{1,0:T(8,128)(2,1)S(1)} %collective-permute-done.12.refs_13_.refs_0_), channel_id=1, source_target_pairs={{0,16},{16,0},{1,17},{17,1},{2,18},{18,2},{3,19},{19,3},{4,20},{20... | collective-permute-start | bytes 1572872 | tf_op jit(solution)/shard_map/ppermute | solution.py:318
  73.0 20.1 %collective-permute-start.20 = (bf16[512,768]{1,0:T(8,128)(2,1)S(1)}, bf16[512,768]{1,0:T(8,128)(2,1)}, u32[]{:S(2)}, u32[]{:S(2)}) collective-permute-start(bf16[512,768]{1,0:T(8,128)(2,1)S(1)} %dynamic-slice_bitcast_fusion), channel_id=1, source_target_pairs={{0,1},{1,0},{2,3},{3,2},{4,5},{5,4},{6,7},{7,6},{8,9},{9,8},{10,11... | collective-permute-start | bytes 2359304 | tf_op jit(solution)/shard_map/ppermute | solution.py:314
  76.4 15.1 %collective-permute-start.17 = (bf16[64,1024]{1,0:T(8,128)(2,1)S(1)}, bf16[64,1024]{1,0:T(8,128)(2,1)S(1)}, u32[]{:S(2)}, u32[]{:S(2)}) collective-permute-start(bf16[64,1024]{1,0:T(8,128)(2,1)S(1)} %get-tuple-element.66), channel_id=1, source_target_pairs={{0,8},{2,10},{4,12},{6,14},{8,0},{10,2},{12,4},{14,6},{1,9},{3,11}... | collective-permute-start | bytes 393224 | tf_op jit(solution)/shard_map/ppermute | solution.py:322
  83.8 18.2 %collective-permute-start.16 = (bf16[64,1024]{1,0:T(8,128)(2,1)S(1)}, bf16[64,1024]{1,0:T(8,128)(2,1)}, u32[]{:S(2)}, u32[]{:S(2)}) collective-permute-start(bf16[64,1024]{1,0:T(8,128)(2,1)S(1)} %get-tuple-element.64), channel_id=1, source_target_pairs={{0,4},{2,6},{4,0},{6,2},{8,12},{10,14},{12,8},{14,10},{1,5},{3,7},... | collective-permute-start | bytes 393224 | tf_op jit(solution)/shard_map/ppermute | solution.py:322
  83.8 19.6 %collective-permute-start.18 = (bf16[64,1024]{1,0:T(8,128)(2,1)}, bf16[64,1024]{1,0:T(8,128)(2,1)}, u32[]{:S(2)}, u32[]{:S(2)}) collective-permute-start(bf16[64,1024]{1,0:T(8,128)(2,1)} %get-tuple-element.65), channel_id=1, source_target_pairs={{0,12},{2,14},{4,8},{6,10},{8,4},{10,6},{12,0},{14,2},{1,13},{3,15... | collective-permute-start | bytes 393224 | tf_op jit(solution)/shard_map/ppermute | solution.py:322
  93.1 10.3 %collective-permute-start.21 = (bf16[64,1024]{1,0:T(8,128)(2,1)}, bf16[64,1024]{1,0:T(8,128)(2,1)}, u32[]{:S(2)}, u32[]{:S(2)}) collective-permute-start(bf16[64,1024]{1,0:T(8,128)(2,1)} %get-tuple-element.41), channel_id=1, source_target_pairs={{0,1},{1,0},{2,3},{3,2},{4,5},{5,4},{6,7},{7,6},{8,9},{9,8},{10,11... | collective-permute-start | bytes 393224 | tf_op jit(solution)/shard_map/ppermute | solution.py:343
  93.7 10.3 %collective-permute-start.22 = (bf16[64,1024]{1,0:T(8,128)(2,1)}, bf16[64,1024]{1,0:T(8,128)(2,1)}, u32[]{:S(2)}, u32[]{:S(2)}) collective-permute-start(bf16[64,1024]{1,0:T(8,128)(2,1)} %get-tuple-element.42), channel_id=1, source_target_pairs={{0,5},{1,4},{2,7},{3,6},{4,1},{5,0},{6,3},{7,2},{8,13},{9,12},{10,... | collective-permute-start | bytes 393224 | tf_op jit(solution)/shard_map/ppermute | solution.py:343
  100.0 13.6 %collective-permute-start.23 = (bf16[64,1024]{1,0:T(8,128)(2,1)}, bf16[64,1024]{1,0:T(8,128)(2,1)}, u32[]{:S(2)}, u32[]{:S(2)}) collective-permute-start(bf16[64,1024]{1,0:T(8,128)(2,1)} %get-tuple-element.43), channel_id=1, source_target_pairs={{0,9},{1,8},{2,11},{3,10},{4,13},{5,12},{6,15},{7,14},{8,1},{9,0},... | collective-permute-start | bytes 393224 | tf_op jit(solution)/shard_map/ppermute | solution.py:343
  102.0 11.7 %collective-permute-start.24 = (bf16[64,1024]{1,0:T(8,128)(2,1)}, bf16[64,1024]{1,0:T(8,128)(2,1)}, u32[]{:S(2)}, u32[]{:S(2)}) collective-permute-start(bf16[64,1024]{1,0:T(8,128)(2,1)} %get-tuple-element.44), channel_id=1, source_target_pairs={{0,13},{1,12},{2,15},{3,14},{4,9},{5,8},{6,11},{7,10},{8,5},{9,4},... | collective-permute-start | bytes 393224 | tf_op jit(solution)/shard_map/ppermute | solution.py:343
  116.0 19.5 %collective-permute-start.30 = (bf16[512,768]{1,0:T(8,128)(2,1)}, bf16[512,768]{1,0:T(8,128)(2,1)S(1)}, u32[]{:S(2)}, u32[]{:S(2)}) collective-permute-start(bf16[512,768]{1,0:T(8,128)(2,1)} %collective-permute-done.20.refs_13_), channel_id=1, source_target_pairs={{0,16},{16,0},{1,17},{17,1},{2,18},{18,2},{3,19},{19,3},{4,20},{20... | collective-permute-start | bytes 2359304 | tf_op jit(solution)/shard_map/ppermute | solution.py:318
  122.1 15.3 %collective-permute-start.32 = (bf16[2,384,512]{2,1,0:T(8,128)(2,1)S(1)}, bf16[2,384,512]{2,1,0:T(8,128)(2,1)S(1)}, u32[]{:S(2)}, u32[]{:S(2)}) collective-permute-start(bf16[2,384,512]{2,1,0:T(8,128)(2,1)S(1)} %copy-done.6), channel_id=1, source_target_pairs={{0,1},{1,0},{2,3},{3,2},{4,5},{5,4},{6,7},{7,6},{8,9},{9,8},{10,11... | collective-permute-start | bytes 2359304 | tf_op jit(solution)/shard_map/ppermute | solution.py:314
  124.4 11.1 %collective-permute-start.27 = (bf16[64,1024]{1,0:T(8,128)(2,1)S(1)}, bf16[64,1024]{1,0:T(8,128)(2,1)S(1)}, u32[]{:S(2)}, u32[]{:S(2)}) collective-permute-start(bf16[64,1024]{1,0:T(8,128)(2,1)S(1)} %pad_maximum_fusion.3.refs_0_), channel_id=1, source_target_pairs={{0,8},{2,10},{4,12},{6,14},{8,0},{10,2},{12,4},{14,6},{1,9},{3,11}... | collective-permute-start | bytes 393224 | tf_op jit(solution)/shard_map/ppermute | solution.py:322
  (35 other events, 431.1 us)

commit v7 on v6

--- a/solution.py
+++ b/solution.py
@@ -401,7 +401,7 @@
     ]
     row = build_row(where, hidden_in, other, lanes)
     same = [row] + [over_expert(row, distance) for distance in distances]
-    far_in = [over_groups(after(near_in[0], same[1]))]
+    far_in = [over_groups(after(near_in[0], same[2]))]
     for part in near_in[1:]:
         far_in.append(over_groups(after(part, far_in[-1])))
     across = [over_expert(row, 1), over_expert(jnp.concatenate(same[1:]), 1)]

time: 166 us -> 165 us (level)
  starting transfers between devices: 59.8 us -> 57.8 us
    ppermute x5, waiting for transfers between devices: 2 us -> 16.9 us  [over_groups(): return lax.ppermute(array, 'groups', SWAP)]
    ppermute x9, waiting for transfers between devices: 30 us -> 20.7 us  [over_replica(): return lax.ppermute(array, 'replica', SWAP)]
    ppermute x20, waiting for transfers between devices: 31.7 us -> 27.5 us  [over_expert(): lax.ppermute(array, 'expert', [(at, at ^ distance) for at in range(lax.ax...]
  transfers between devices with their start and end apart: 42 -> 42, of which waited for: 19 -> 18; matrix products, arithmetic and copies ran while one was open for 3% -> 3% of each run, Pallas kernels for 8% -> 8%
where the time goes in v7:
time: 165 us
  waiting for transfers between devices  75.5 us (46%)
  starting transfers between devices  57.8 us (35%)
  Pallas kernels  20.2 us (12%)
  other arithmetic  5.07 us (3%)
  local copies, waits for them, and re-layouts  4.33 us (3%)
    ppermute x20, waiting for transfers between devices, over_expert(): lax.ppermute(array, 'expert', [(at, at ^ distance) for at in range(lax.ax...  27.5 us
    ppermute x20, starting transfers between devices, over_expert(): lax.ppermute(array, 'expert', [(at, at ^ distance) for at in range(lax.ax...  24.7 us
    ppermute x9, waiting for transfers between devices, over_replica(): return lax.ppermute(array, 'replica', SWAP)  20.7 us
    ppermute x8, starting transfers between devices, over_both(): return lax.ppermute(array, ('expert', 'replica'), pairs)  16.9 us
    ppermute x5, waiting for transfers between devices, over_groups(): return lax.ppermute(array, 'groups', SWAP)  16.9 us
    pallas_call x2, Pallas kernels, run_hidden(): pl.pallas_call(functools.partial(hidden_kernel, blocks, len(gain_blocks),...  12.5 us
    ppermute x8, waiting for transfers between devices, over_both(): return lax.ppermute(array, ('expert', 'replica'), pairs)  10.5 us
    ppermute x9, starting transfers between devices, over_replica(): return lax.ppermute(array, 'replica', SWAP)  9.6 us
  transfers between devices with their start and end apart: 42, of which 18 were waited for; matrix products, arithmetic and copies ran while one was open for 3% of the time, Pallas kernels for 8%

profile of v7, /device:TPU:0, one launch (start us, length us, event | category | flops | bytes accessed | tf_op | source)
XLA Modules:
  0.0 164.9 jit_solution(16580606749856637244)
XLA Ops:
  1.8 3.0 %collective-permute-start = (bf16[64,1024]{1,0:T(8,128)(2,1)S(1)}, bf16[64,1024]{1,0:T(8,128)(2,1)S(1)}, u32[]{:S(2)}, u32[]{:S(2)}) collective-permute-start(bf16[64,1024]{1,0:T(8,128)(2,1)S(1)} %constant_dynamic-slice_fusion), channel_id=1, source_target_pairs={{0,1},{1,0},{2,3},{3,2},{4,5},{5,4},{6,7},{7,6},{8,9},{9,8},{10,11... | collective-permute-start | bytes 393224 | tf_op jit(solution)/shard_map/ppermute | solution.py:314
  4.8 2.1 %dynamic-slice_bitcast_fusion.1 = (bf16[352,768]{1,0:T(8,128)(2,1)}, bf16[352,768]{1,0:T(8,128)(2,1)S(1)}) fusion(bf16[2,1024,768]{2,1,0:T(8,128)(2,1)} %refs_6_.1, s32[]{:T(128)S(6)} %select_n.44), kind=kLoop, calls=%fused_computation.5 | loop fusion | bytes 2162692 | tf_op jit(solution)/shard_map/squeeze | solution.py:332
  11.4 2.7 %collective-permute-start.2 = (bf16[64,2176]{1,0:T(8,128)(2,1)S(1)}, bf16[64,2176]{1,0:T(8,128)(2,1)S(1)}, u32[]{:S(2)}, u32[]{:S(2)}) collective-permute-start(bf16[64,2176]{1,0:T(8,128)(2,1)S(1)} %shard_map.123.refs_0_.refs_6_), channel_id=1, source_target_pairs={{0,8},{2,10},{4,12},{6,14},{8,0},{10,2},{12,4},{14,6},{1,9},{3,11}... | collective-permute-start | bytes 835592 | tf_op jit(solution)/shard_map/ppermute | solution.py:322
  14.6 11.0 %collective-permute-done.2.refs_2_.refs_8_ = bf16[64,2176]{1,0:T(8,128)(2,1)S(1)} collective-permute-done((bf16[64,2176]{1,0:T(8,128)(2,1)S(1)}, bf16[64,2176]{1,0:T(8,128)(2,1)S(1)}, u32[]{:S(2)}, u32[]{:S(2)}) %collective-permute-start.2) | collective-permute-done | bytes 278560 | tf_op jit(solution)/shard_map/ppermute | solution.py:322
  27.7 2.8 %collective-permute-start.3 = (bf16[64,2176]{1,0:T(8,128)(2,1)S(1)}, bf16[64,2176]{1,0:T(8,128)(2,1)S(1)}, u32[]{:S(2)}, u32[]{:S(2)}) collective-permute-start(bf16[64,2176]{1,0:T(8,128)(2,1)S(1)} %shard_map.123.refs_0_.refs_6_), channel_id=1, source_target_pairs={{0,12},{2,14},{4,8},{6,10},{8,4},{10,6},{12,0},{14,2},{1,13},{3,15... | collective-permute-start | bytes 835592 | tf_op jit(solution)/shard_map/ppermute | solution.py:322
  31.2 2.6 %collective-permute-done.7.refs_8_ = bf16[352,768]{1,0:T(8,128)(2,1)S(1)} collective-permute-done((bf16[352,768]{1,0:T(8,128)(2,1)}, bf16[352,768]{1,0:T(8,128)(2,1)S(1)}, u32[]{:S(2)}, u32[]{:S(2)}) %collective-permute-start.7) | collective-permute-done | bytes 540704 | tf_op jit(solution)/shard_map/ppermute | solution.py:314
  33.8 5.0 %collective-permute-done.9.refs_10_ = bf16[352,768]{1,0:T(8,128)(2,1)S(1)} collective-permute-done((bf16[352,768]{1,0:T(8,128)(2,1)}, bf16[352,768]{1,0:T(8,128)(2,1)S(1)}, u32[]{:S(2)}, u32[]{:S(2)}) %collective-permute-start.9) | collective-permute-done | bytes 540704 | tf_op jit(solution)/shard_map/ppermute | solution.py:318
  40.4 2.8 %collective-permute-done.3.refs_3_.refs_9_ = bf16[64,2176]{1,0:T(8,128)(2,1)S(1)} collective-permute-done((bf16[64,2176]{1,0:T(8,128)(2,1)S(1)}, bf16[64,2176]{1,0:T(8,128)(2,1)S(1)}, u32[]{:S(2)}, u32[]{:S(2)}) %collective-permute-start.3) | collective-permute-done | bytes 278560 | tf_op jit(solution)/shard_map/ppermute | solution.py:322
  44.0 7.3 %collective-permute-done.10.refs_11_ = bf16[352,768]{1,0:T(8,128)(2,1)S(1)} collective-permute-done((bf16[352,768]{1,0:T(8,128)(2,1)S(1)}, bf16[352,768]{1,0:T(8,128)(2,1)S(1)}, u32[]{:S(2)}, u32[]{:S(2)}) %collective-permute-start.10) | collective-permute-done | bytes 540704 | tf_op jit(solution)/shard_map/ppermute | solution.py:318
  52.9 4.9 %collective-permute-done.12.refs_13_.refs_0_ = bf16[256,1024]{1,0:T(8,128)(2,1)S(1)} collective-permute-done((bf16[256,1024]{1,0:T(8,128)(2,1)S(1)}, bf16[256,1024]{1,0:T(8,128)(2,1)S(1)}, u32[]{:S(2)}, u32[]{:S(2)}) %collective-permute-start.12) | collective-permute-done | bytes 524320 | tf_op jit(solution)/shard_map/ppermute | solution.py:314
  58.8 4.1 %collective-permute-done.11.refs_12_ = bf16[320,768]{1,0:T(8,128)(2,1)S(1)} collective-permute-done((bf16[320,768]{1,0:T(8,128)(2,1)S(1)}, bf16[320,768]{1,0:T(8,128)(2,1)S(1)}, u32[]{:S(2)}, u32[]{:S(2)}) %collective-permute-start.11) | collective-permute-done | bytes 491552 | tf_op jit(solution)/shard_map/ppermute | solution.py:318
  62.9 6.9 %shard_map.124.hidden_ref = bf16[512,768]{1,0:T(8,128)(2,1)S(1)} custom-call(s32[3]{0:T(128)S(1)} %pad_add_fusion.where_ref, bf16[64,2176]{1,0:T(8,128)(2,1)S(1)} %shard_map.123.refs_0_.refs_6_, bf16[64,2176]{1,0:T(8,128)(2,1)S(1)} %collective-permute-done.1.refs_1_.refs_7_, bf16[64,2176]{1,0:T(8,128)(2,1)S(1)} %collective-permute-done.2.refs_2_.refs_8_, ...), custom_call_target="tpu_custom_call" | custom-call | flops 3221225472 | bytes 8388608 | tf_op jit(solution)/shard_map/pallas_call | solution.py:243
  77.9 6.7 %collective-permute-start.16 = (bf16[64,1024]{1,0:T(8,128)(2,1)S(1)}, bf16[64,1024]{1,0:T(8,128)(2,1)}, u32[]{:S(2)}, u32[]{:S(2)}) collective-permute-start(bf16[64,1024]{1,0:T(8,128)(2,1)S(1)} %get-tuple-element.64), channel_id=1, source_target_pairs={{0,4},{2,6},{4,0},{6,2},{8,12},{10,14},{12,8},{14,10},{1,5},{3,7},... | collective-permute-start | bytes 393224 | tf_op jit(solution)/shard_map/ppermute | solution.py:322
  85.6 7.5 %collective-permute-done.20.refs_13_ = bf16[512,768]{1,0:T(8,128)(2,1)} collective-permute-done((bf16[512,768]{1,0:T(8,128)(2,1)S(1)}, bf16[512,768]{1,0:T(8,128)(2,1)}, u32[]{:S(2)}, u32[]{:S(2)}) %collective-permute-start.20) | collective-permute-done | bytes 786464 | tf_op jit(solution)/shard_map/ppermute | solution.py:314
  93.8 5.6 %collective-permute-start.22 = (bf16[64,1024]{1,0:T(8,128)(2,1)}, bf16[64,1024]{1,0:T(8,128)(2,1)}, u32[]{:S(2)}, u32[]{:S(2)}) collective-permute-start(bf16[64,1024]{1,0:T(8,128)(2,1)} %get-tuple-element.42), channel_id=1, source_target_pairs={{0,5},{1,4},{2,7},{3,6},{4,1},{5,0},{6,3},{7,2},{8,13},{9,12},{10,... | collective-permute-start | bytes 393224 | tf_op jit(solution)/shard_map/ppermute | solution.py:343
  99.4 3.4 %collective-permute-start.23 = (bf16[64,1024]{1,0:T(8,128)(2,1)}, bf16[64,1024]{1,0:T(8,128)(2,1)}, u32[]{:S(2)}, u32[]{:S(2)}) collective-permute-start(bf16[64,1024]{1,0:T(8,128)(2,1)} %get-tuple-element.43), channel_id=1, source_target_pairs={{0,9},{1,8},{2,11},{3,10},{4,13},{5,12},{6,15},{7,14},{8,1},{9,0},... | collective-permute-start | bytes 393224 | tf_op jit(solution)/shard_map/ppermute | solution.py:343
  102.8 10.3 %collective-permute-done.23 = bf16[64,1024]{1,0:T(8,128)(2,1)} collective-permute-done((bf16[64,1024]{1,0:T(8,128)(2,1)}, bf16[64,1024]{1,0:T(8,128)(2,1)}, u32[]{:S(2)}, u32[]{:S(2)}) %collective-permute-start.23) | collective-permute-done | bytes 131104 | tf_op jit(solution)/shard_map/ppermute | solution.py:343
  117.6 3.9 %collective-permute-done.25 = bf16[64,1024]{1,0:T(8,128)(2,1)S(1)} collective-permute-done((bf16[64,1024]{1,0:T(8,128)(2,1)S(1)}, bf16[64,1024]{1,0:T(8,128)(2,1)S(1)}, u32[]{:S(2)}, u32[]{:S(2)}) %collective-permute-start.25) | collective-permute-done | bytes 131104 | tf_op jit(solution)/shard_map/ppermute | solution.py:314
  127.4 2.9 %collective-permute-done.26.refs_1_ = bf16[64,1024]{1,0:T(8,128)(2,1)S(1)} collective-permute-done((bf16[64,1024]{1,0:T(8,128)(2,1)S(1)}, bf16[64,1024]{1,0:T(8,128)(2,1)S(1)}, u32[]{:S(2)}, u32[]{:S(2)}) %collective-permute-start.26) | collective-permute-done | bytes 131104 | tf_op jit(solution)/shard_map/ppermute | solution.py:322
  130.3 4.4 %collective-permute-done.27.refs_2_ = bf16[64,1024]{1,0:T(8,128)(2,1)S(1)} collective-permute-done((bf16[64,1024]{1,0:T(8,128)(2,1)S(1)}, bf16[64,1024]{1,0:T(8,128)(2,1)S(1)}, u32[]{:S(2)}, u32[]{:S(2)}) %collective-permute-start.27) | collective-permute-done | bytes 131104 | tf_op jit(solution)/shard_map/ppermute | solution.py:322
  137.0 5.7 %shard_map.127.hidden_ref = bf16[512,768]{1,0:T(8,128)(2,1)S(1)} custom-call(s32[3]{0:T(128)S(1)} %pad_add_fusion.where_ref, bf16[64,1024]{1,0:T(8,128)(2,1)S(1)} %pad_maximum_fusion.3.refs_0_, bf16[64,1024]{1,0:T(8,128)(2,1)S(1)} %collective-permute-done.26.refs_1_, bf16[64,1024]{1,0:T(8,128)(2,1)S(1)} %collective-permute-done.27.refs_2_, ...), custom_call_target="tpu_custom_call" | custom-call | flops 1610612736 | bytes 4194304 | tf_op jit(solution)/shard_map/pallas_call | solution.py:243
  147.0 3.2 %collective-permute-start.39 = (bf16[64,512]{1,0:T(8,128)(2,1)S(1)}, bf16[64,512]{1,0:T(8,128)(2,1)S(1)}, u32[]{:S(2)}, u32[]{:S(2)}) collective-permute-start(bf16[64,512]{1,0:T(8,128)(2,1)S(1)} %get-tuple-element.70), channel_id=1, source_target_pairs={{0,5},{1,4},{2,7},{3,6},{4,1},{5,0},{6,3},{7,2},{8,13},{9,12},{10,... | collective-permute-start | bytes 196616 | tf_op jit(solution)/shard_map/ppermute | solution.py:343
  151.6 2.1 %collective-permute-start.41 = (bf16[64,512]{1,0:T(8,128)(2,1)S(1)}, bf16[64,512]{1,0:T(8,128)(2,1)S(1)}, u32[]{:S(2)}, u32[]{:S(2)}) collective-permute-start(bf16[64,512]{1,0:T(8,128)(2,1)S(1)} %get-tuple-element.68), channel_id=1, source_target_pairs={{0,13},{1,12},{2,15},{3,14},{4,9},{5,8},{6,11},{7,10},{8,5},{9,4},... | collective-permute-start | bytes 196616 | tf_op jit(solution)/shard_map/ppermute | solution.py:343
  159.2 4.9 %collective-permute-done.35 = bf16[64,512]{1,0:T(8,128)(2,1)S(1)} collective-permute-done((bf16[64,512]{1,0:T(8,128)(2,1)S(1)}, bf16[64,512]{1,0:T(8,128)(2,1)S(1)}, u32[]{:S(2)}, u32[]{:S(2)}) %collective-permute-start.35) | collective-permute-done | bytes 65568 | tf_op jit(solution)/shard_map/ppermute | solution.py:322
  (125 shorter events, 48.1 us)
Async XLA Ops:
  8.3 17.3 %collective-permute-start.6 = (bf16[352,768]{1,0:T(8,128)(2,1)S(1)}, bf16[352,768]{1,0:T(8,128)(2,1)}, u32[]{:S(2)}, u32[]{:S(2)}) collective-permute-start(bf16[352,768]{1,0:T(8,128)(2,1)S(1)} %get-tuple-element.27), channel_id=1, source_target_pairs={{0,1},{1,0},{2,3},{3,2},{4,5},{5,4},{6,7},{7,6},{8,9},{9,8},{10,11... | collective-permute-start | bytes 1622024 | tf_op jit(solution)/shard_map/ppermute | solution.py:314
  11.4 14.2 %collective-permute-start.2 = (bf16[64,2176]{1,0:T(8,128)(2,1)S(1)}, bf16[64,2176]{1,0:T(8,128)(2,1)S(1)}, u32[]{:S(2)}, u32[]{:S(2)}) collective-permute-start(bf16[64,2176]{1,0:T(8,128)(2,1)S(1)} %shard_map.123.refs_0_.refs_6_), channel_id=1, source_target_pairs={{0,8},{2,10},{4,12},{6,14},{8,0},{10,2},{12,4},{14,6},{1,9},{3,11}... | collective-permute-start | bytes 835592 | tf_op jit(solution)/shard_map/ppermute | solution.py:322
  14.0 19.8 %collective-permute-start.7 = (bf16[352,768]{1,0:T(8,128)(2,1)}, bf16[352,768]{1,0:T(8,128)(2,1)S(1)}, u32[]{:S(2)}, u32[]{:S(2)}) collective-permute-start(bf16[352,768]{1,0:T(8,128)(2,1)} %get-tuple-element.28), channel_id=1, source_target_pairs={{0,1},{1,0},{2,3},{3,2},{4,5},{5,4},{6,7},{7,6},{8,9},{9,8},{10,11... | collective-permute-start | bytes 1622024 | tf_op jit(solution)/shard_map/ppermute | solution.py:314
  25.6 13.3 %collective-permute-start.9 = (bf16[352,768]{1,0:T(8,128)(2,1)}, bf16[352,768]{1,0:T(8,128)(2,1)S(1)}, u32[]{:S(2)}, u32[]{:S(2)}) collective-permute-start(bf16[352,768]{1,0:T(8,128)(2,1)} %collective-permute-done.6.refs_7_), channel_id=1, source_target_pairs={{0,16},{16,0},{1,17},{17,1},{2,18},{18,2},{3,19},{19,3},{4,20},{20... | collective-permute-start | bytes 1622024 | tf_op jit(solution)/shard_map/ppermute | solution.py:318
  27.1 13.3 %collective-permute-start.1 = (bf16[64,2176]{1,0:T(8,128)(2,1)S(1)}, bf16[64,2176]{1,0:T(8,128)(2,1)S(1)}, u32[]{:S(2)}, u32[]{:S(2)}) collective-permute-start(bf16[64,2176]{1,0:T(8,128)(2,1)S(1)} %shard_map.123.refs_0_.refs_6_), channel_id=1, source_target_pairs={{0,4},{2,6},{4,0},{6,2},{8,12},{10,14},{12,8},{14,10},{1,5},{3,7},... | collective-permute-start | bytes 835592 | tf_op jit(solution)/shard_map/ppermute | solution.py:322
  27.7 15.4 %collective-permute-start.3 = (bf16[64,2176]{1,0:T(8,128)(2,1)S(1)}, bf16[64,2176]{1,0:T(8,128)(2,1)S(1)}, u32[]{:S(2)}, u32[]{:S(2)}) collective-permute-start(bf16[64,2176]{1,0:T(8,128)(2,1)S(1)} %shard_map.123.refs_0_.refs_6_), channel_id=1, source_target_pairs={{0,12},{2,14},{4,8},{6,10},{8,4},{10,6},{12,0},{14,2},{1,13},{3,15... | collective-permute-start | bytes 835592 | tf_op jit(solution)/shard_map/ppermute | solution.py:322
  30.6 13.4 %collective-permute-start.8 = (bf16[320,768]{1,0:T(8,128)(2,1)S(1)}, bf16[320,768]{1,0:T(8,128)(2,1)S(1)}, u32[]{:S(2)}, u32[]{:S(2)}) collective-permute-start(bf16[320,768]{1,0:T(8,128)(2,1)S(1)} %dynamic-slice_bitcast_fusion.4), channel_id=1, source_target_pairs={{0,1},{1,0},{2,3},{3,2},{4,5},{5,4},{6,7},{7,6},{8,9},{9,8},{10,11... | collective-permute-start | bytes 1474568 | tf_op jit(solution)/shard_map/ppermute | solution.py:314
  38.9 12.4 %collective-permute-start.10 = (bf16[352,768]{1,0:T(8,128)(2,1)S(1)}, bf16[352,768]{1,0:T(8,128)(2,1)S(1)}, u32[]{:S(2)}, u32[]{:S(2)}) collective-permute-start(bf16[352,768]{1,0:T(8,128)(2,1)S(1)} %collective-permute-done.7.refs_8_), channel_id=1, source_target_pairs={{0,16},{16,0},{1,17},{17,1},{2,18},{18,2},{3,19},{19,3},{4,20},{20... | collective-permute-start | bytes 1622024 | tf_op jit(solution)/shard_map/ppermute | solution.py:318
  43.3 15.6 %collective-permute-start.5 = (bf16[192,2176]{1,0:T(8,128)(2,1)S(1)}, bf16[192,2176]{1,0:T(8,128)(2,1)S(1)}, u32[]{:S(2)}, u32[]{:S(2)}) collective-permute-start(bf16[192,2176]{1,0:T(8,128)(2,1)S(1)} %pad_maximum_fusion), channel_id=1, source_target_pairs={{0,2},{2,0},{4,6},{6,4},{8,10},{10,8},{12,14},{14,12},{1,3},{3,1},... | collective-permute-start | bytes 2506760 | tf_op jit(solution)/shard_map/ppermute | solution.py:322
  43.4 14.4 %collective-permute-start.12 = (bf16[256,1024]{1,0:T(8,128)(2,1)S(1)}, bf16[256,1024]{1,0:T(8,128)(2,1)S(1)}, u32[]{:S(2)}, u32[]{:S(2)}) collective-permute-start(bf16[256,1024]{1,0:T(8,128)(2,1)S(1)} %dynamic-slice_bitcast_fusion.3), channel_id=1, source_target_pairs={{0,1},{1,0},{2,3},{3,2},{4,5},{5,4},{6,7},{7,6},{8,9},{9,8},{10,11... | collective-permute-start | bytes 1572872 | tf_op jit(solution)/shard_map/ppermute | solution.py:314
  51.3 11.6 %collective-permute-start.11 = (bf16[320,768]{1,0:T(8,128)(2,1)S(1)}, bf16[320,768]{1,0:T(8,128)(2,1)S(1)}, u32[]{:S(2)}, u32[]{:S(2)}) collective-permute-start(bf16[320,768]{1,0:T(8,128)(2,1)S(1)} %collective-permute-done.8.refs_9_), channel_id=1, source_target_pairs={{0,16},{16,0},{1,17},{17,1},{2,18},{18,2},{3,19},{19,3},{4,20},{20... | collective-permute-start | bytes 1474568 | tf_op jit(solution)/shard_map/ppermute | solution.py:318
  57.8 14.6 %collective-permute-start.13 = (bf16[2,128,1024]{2,1,0:T(8,128)(2,1)S(1)}, bf16[2,128,1024]{2,1,0:T(8,128)(2,1)S(1)}, u32[]{:S(2)}, u32[]{:S(2)}) collective-permute-start(bf16[2,128,1024]{2,1,0:T(8,128)(2,1)S(1)} %slice.100), channel_id=1, source_target_pairs={{0,1},{1,0},{2,3},{3,2},{4,5},{5,4},{6,7},{7,6},{8,9},{9,8},{10,11... | collective-permute-start | bytes 1572872 | tf_op jit(solution)/shard_map/ppermute | solution.py:314
  58.3 14.5 %collective-permute-start.14 = (bf16[256,1024]{1,0:T(8,128)(2,1)S(1)}, bf16[256,1024]{1,0:T(8,128)(2,1)S(1)}, u32[]{:S(2)}, u32[]{:S(2)}) collective-permute-start(bf16[256,1024]{1,0:T(8,128)(2,1)S(1)} %collective-permute-done.12.refs_13_.refs_0_), channel_id=1, source_target_pairs={{0,16},{16,0},{1,17},{17,1},{2,18},{18,2},{3,19},{19,3},{4,20},{20... | collective-permute-start | bytes 1572872 | tf_op jit(solution)/shard_map/ppermute | solution.py:318
  72.9 20.1 %collective-permute-start.20 = (bf16[512,768]{1,0:T(8,128)(2,1)S(1)}, bf16[512,768]{1,0:T(8,128)(2,1)}, u32[]{:S(2)}, u32[]{:S(2)}) collective-permute-start(bf16[512,768]{1,0:T(8,128)(2,1)S(1)} %dynamic-slice_bitcast_fusion), channel_id=1, source_target_pairs={{0,1},{1,0},{2,3},{3,2},{4,5},{5,4},{6,7},{7,6},{8,9},{9,8},{10,11... | collective-permute-start | bytes 2359304 | tf_op jit(solution)/shard_map/ppermute | solution.py:314
  77.9 24.9 %collective-permute-start.16 = (bf16[64,1024]{1,0:T(8,128)(2,1)S(1)}, bf16[64,1024]{1,0:T(8,128)(2,1)}, u32[]{:S(2)}, u32[]{:S(2)}) collective-permute-start(bf16[64,1024]{1,0:T(8,128)(2,1)S(1)} %get-tuple-element.64), channel_id=1, source_target_pairs={{0,4},{2,6},{4,0},{6,2},{8,12},{10,14},{12,8},{14,10},{1,5},{3,7},... | collective-permute-start | bytes 393224 | tf_op jit(solution)/shard_map/ppermute | solution.py:322
  84.6 18.1 %collective-permute-start.18 = (bf16[64,1024]{1,0:T(8,128)(2,1)}, bf16[64,1024]{1,0:T(8,128)(2,1)}, u32[]{:S(2)}, u32[]{:S(2)}) collective-permute-start(bf16[64,1024]{1,0:T(8,128)(2,1)} %get-tuple-element.65), channel_id=1, source_target_pairs={{0,12},{2,14},{4,8},{6,10},{8,4},{10,6},{12,0},{14,2},{1,13},{3,15... | collective-permute-start | bytes 393224 | tf_op jit(solution)/shard_map/ppermute | solution.py:322
  93.0 9.8 %collective-permute-start.21 = (bf16[64,1024]{1,0:T(8,128)(2,1)}, bf16[64,1024]{1,0:T(8,128)(2,1)}, u32[]{:S(2)}, u32[]{:S(2)}) collective-permute-start(bf16[64,1024]{1,0:T(8,128)(2,1)} %get-tuple-element.41), channel_id=1, source_target_pairs={{0,1},{1,0},{2,3},{3,2},{4,5},{5,4},{6,7},{7,6},{8,9},{9,8},{10,11... | collective-permute-start | bytes 393224 | tf_op jit(solution)/shard_map/ppermute | solution.py:343
  99.4 13.7 %collective-permute-start.23 = (bf16[64,1024]{1,0:T(8,128)(2,1)}, bf16[64,1024]{1,0:T(8,128)(2,1)}, u32[]{:S(2)}, u32[]{:S(2)}) collective-permute-start(bf16[64,1024]{1,0:T(8,128)(2,1)} %get-tuple-element.43), channel_id=1, source_target_pairs={{0,9},{1,8},{2,11},{3,10},{4,13},{5,12},{6,15},{7,14},{8,1},{9,0},... | collective-permute-start | bytes 393224 | tf_op jit(solution)/shard_map/ppermute | solution.py:343
  102.8 10.3 %collective-permute-start.24 = (bf16[64,1024]{1,0:T(8,128)(2,1)}, bf16[64,1024]{1,0:T(8,128)(2,1)}, u32[]{:S(2)}, u32[]{:S(2)}) collective-permute-start(bf16[64,1024]{1,0:T(8,128)(2,1)} %get-tuple-element.44), channel_id=1, source_target_pairs={{0,13},{1,12},{2,15},{3,14},{4,9},{5,8},{6,11},{7,10},{8,5},{9,4},... | collective-permute-start | bytes 393224 | tf_op jit(solution)/shard_map/ppermute | solution.py:343
  116.1 18.6 %collective-permute-start.30 = (bf16[512,768]{1,0:T(8,128)(2,1)}, bf16[512,768]{1,0:T(8,128)(2,1)S(1)}, u32[]{:S(2)}, u32[]{:S(2)}) collective-permute-start(bf16[512,768]{1,0:T(8,128)(2,1)} %collective-permute-done.20.refs_13_), channel_id=1, source_target_pairs={{0,16},{16,0},{1,17},{17,1},{2,18},{18,2},{3,19},{19,3},{4,20},{20... | collective-permute-start | bytes 2359304 | tf_op jit(solution)/shard_map/ppermute | solution.py:318
  121.6 15.5 %collective-permute-start.32 = (bf16[2,384,512]{2,1,0:T(8,128)(2,1)S(1)}, bf16[2,384,512]{2,1,0:T(8,128)(2,1)S(1)}, u32[]{:S(2)}, u32[]{:S(2)}) collective-permute-start(bf16[2,384,512]{2,1,0:T(8,128)(2,1)S(1)} %copy-done.6), channel_id=1, source_target_pairs={{0,1},{1,0},{2,3},{3,2},{4,5},{5,4},{6,7},{7,6},{8,9},{9,8},{10,11... | collective-permute-start | bytes 2359304 | tf_op jit(solution)/shard_map/ppermute | solution.py:314
  124.1 10.6 %collective-permute-start.27 = (bf16[64,1024]{1,0:T(8,128)(2,1)S(1)}, bf16[64,1024]{1,0:T(8,128)(2,1)S(1)}, u32[]{:S(2)}, u32[]{:S(2)}) collective-permute-start(bf16[64,1024]{1,0:T(8,128)(2,1)S(1)} %pad_maximum_fusion.3.refs_0_), channel_id=1, source_target_pairs={{0,8},{2,10},{4,12},{6,14},{8,0},{10,2},{12,4},{14,6},{1,9},{3,11}... | collective-permute-start | bytes 393224 | tf_op jit(solution)/shard_map/ppermute | solution.py:322
  147.0 9.5 %collective-permute-start.39 = (bf16[64,512]{1,0:T(8,128)(2,1)S(1)}, bf16[64,512]{1,0:T(8,128)(2,1)S(1)}, u32[]{:S(2)}, u32[]{:S(2)}) collective-permute-start(bf16[64,512]{1,0:T(8,128)(2,1)S(1)} %get-tuple-element.70), channel_id=1, source_target_pairs={{0,5},{1,4},{2,7},{3,6},{4,1},{5,0},{6,3},{7,2},{8,13},{9,12},{10,... | collective-permute-start | bytes 196616 | tf_op jit(solution)/shard_map/ppermute | solution.py:343
  154.8 9.4 %collective-permute-start.35 = (bf16[64,512]{1,0:T(8,128)(2,1)S(1)}, bf16[64,512]{1,0:T(8,128)(2,1)S(1)}, u32[]{:S(2)}, u32[]{:S(2)}) collective-permute-start(bf16[64,512]{1,0:T(8,128)(2,1)S(1)} %get-tuple-element.73), channel_id=1, source_target_pairs={{0,8},{2,10},{4,12},{6,14},{8,0},{10,2},{12,4},{14,6},{1,9},{3,11}... | collective-permute-start | bytes 196616 | tf_op jit(solution)/shard_map/ppermute | solution.py:322
  (35 other events, 428.7 us)

commit v8 on v7

--- a/solution.py
+++ b/solution.py
@@ -388,34 +388,31 @@
     rows = routes.shape[0] // 2
     distances = range(2, owners, 2)
 
-    width, chunk, out_chunk = w_in.shape[1], w_in.shape[1] * 11 // 32, w_out.shape[1] * 2 // 3
+    chunk = w_in.shape[1] * 13 // 32
 
     lanes = gain_lanes(
         where, experts, routes, route_gain, speaking, talker_routes, talker_gain
     )
     give = lax.dynamic_slice_in_dim(hidden_in, (1 - replica) * rows, rows, 0)
     other = over_replica(give)
-    near_in = [
-        send(w_in, group, first, min(chunk, width - first), other)
-        for first in range(0, width, chunk)
-    ]
+    near_in = [send(w_in, group, index * chunk, chunk, other) for index in range(2)]
     row = build_row(where, hidden_in, other, lanes)
     same = [row] + [over_expert(row, distance) for distance in distances]
     far_in = [over_groups(after(near_in[0], same[2]))]
-    for part in near_in[1:]:
-        far_in.append(over_groups(after(part, far_in[-1])))
-    across = [over_expert(row, 1), over_expert(jnp.concatenate(same[1:]), 1)]
-    near_out = send(w_out, group, 0, out_chunk, near_in[1])
-    direct_out = over_replica(after(w_out[:, out_chunk:], near_out))
-    far_out = over_groups(near_out)
+    far_in.append(over_groups(near_in[1]))
+    direct_in = over_replica(after(w_in[:, 2 * chunk :], near_in[0]))
+    across = [over_expert(after(row, far_in[0]), 1), over_expert(jnp.concatenate(same[1:]), 1)]
     blocks = same + across
-    hidden = run_hidden(where, blocks, [], w_in, near_in, far_in, [], [near_out], 0, experts)
-    own = run_down(where, hidden, [], [], [w_out])
-    own = spread_sums(*own, hold=[direct_out, far_out])
-    near_talker_in = send(talker_w_in, group, 0, talker_w_in.shape[1], near_out, hidden)
-    give = run_down(where, hidden, [near_out], [far_out], [direct_out])
-    got = spread_sums(*give, before=[own[2], near_talker_in], cross=True)
-    far_talker_in = over_groups(near_talker_in)
+    hidden = run_hidden(where, blocks, [], w_in, near_in, far_in, [direct_in], [], 0, experts)
+    half = talker_w_in.shape[1] // 2
+    near_talker_in = [send(talker_w_in, group, 0, half, direct_in)]
+    far_talker_in = [over_groups(near_talker_in[0])]
+    other_hidden = over_replica(after(hidden, near_talker_in[0]))
+    own = spread_sums(*run_down(where, hidden, [], [], [w_out]))
+    got = run_down(where, after(other_hidden, own[2]), [], [], [w_out])
+    near_talker_in.append(send(talker_w_in, group, half, half, own[3], *got))
+    got = spread_sums(*got, before=[own[1]])
+    far_talker_in.append(over_groups(after(near_talker_in[1], far_talker_in[0])))
     got, own = add_up(got), add_up(own)
     thinker_out = in_order(replica, own, got, 0)
 
@@ -428,15 +425,15 @@
     parts = jnp.split(talker_row, 2, axis=1)
     talker_row = in_order(replica, parts[0], parts[1], 1)
     same = [talker_row] + [over_expert(talker_row, distance) for distance in distances]
-    rest = after(jnp.concatenate(same[1:]), far_talker_in)
+    rest = after(jnp.concatenate(same[1:]), far_talker_in[1])
     talker_blocks = same + [over_expert(talker_row, 1), over_expert(rest, 1)]
     hidden = run_hidden(
         where,
         talker_blocks,
         blocks,
         talker_w_in,
-        [near_talker_in],
-        [far_talker_in],
+        near_talker_in,
+        far_talker_in,
         [],
         [direct_talker_out],
         2 * experts,

time: 165 us -> 165 us (level)
  starting transfers between devices: 57.8 us -> 46.7 us
  waiting for transfers between devices: 75.5 us -> 86.6 us
    ppermute x20 -> x23, waiting for transfers between devices: 27.5 us -> 51 us  [over_expert(): lax.ppermute(array, 'expert', [(at, at ^ distance) for at in range(lax.ax...]
    ppermute x8 -> x4, starting transfers between devices: 16.9 us -> 5.79 us  [over_both(): return lax.ppermute(array, ('expert', 'replica'), pairs)]
    ppermute x8 -> x4, waiting for transfers between devices: 10.5 us -> 3.36 us  [over_both(): return lax.ppermute(array, ('expert', 'replica'), pairs)]
    ppermute x5 -> x4, waiting for transfers between devices: 16.9 us -> 9.98 us  [over_groups(): return lax.ppermute(array, 'groups', SWAP)]
    ppermute x5 -> x4, starting transfers between devices: 6.58 us -> 6.01 us  [over_groups(): return lax.ppermute(array, 'groups', SWAP)]
    ppermute x20 -> x23, starting transfers between devices: 24.7 us -> 24.4 us  [over_expert(): lax.ppermute(array, 'expert', [(at, at ^ distance) for at in range(lax.ax...]
  transfers between devices with their start and end apart: 42 -> 40, of which waited for: 18 -> 21; matrix products, arithmetic and copies ran while one was open for 3% -> 5% of each run, Pallas kernels for 8% -> 6%
where the time goes in v8:
time: 165 us
  waiting for transfers between devices  86.6 us (52%)
  starting transfers between devices  46.7 us (28%)
  Pallas kernels  19.9 us (12%)
  other arithmetic  5.15 us (3%)
  local copies, waits for them, and re-layouts  4.41 us (3%)
    ppermute x23, waiting for transfers between devices, over_expert(): lax.ppermute(array, 'expert', [(at, at ^ distance) for at in range(lax.ax...  51 us
    ppermute x23, starting transfers between devices, over_expert(): lax.ppermute(array, 'expert', [(at, at ^ distance) for at in range(lax.ax...  24.4 us
    ppermute x9, waiting for transfers between devices, over_replica(): return lax.ppermute(array, 'replica', SWAP)  22.2 us
    pallas_call x2, Pallas kernels, run_hidden(): pl.pallas_call(functools.partial(hidden_kernel, blocks, len(gain_blocks),...  12.4 us
    ppermute x9, starting transfers between devices, over_replica(): return lax.ppermute(array, 'replica', SWAP)  10.6 us
    ppermute x4, waiting for transfers between devices, over_groups(): return lax.ppermute(array, 'groups', SWAP)  9.98 us
    pallas_call x4, Pallas kernels, run_down(): pl.pallas_call(functools.partial(down_kernel, len(near)), out_shape=(shap...  6.36 us
    ppermute x4, starting transfers between devices, over_groups(): return lax.ppermute(array, 'groups', SWAP)  6.01 us
  transfers between devices with their start and end apart: 40, of which 21 were waited for; matrix products, arithmetic and copies ran while one was open for 5% of the time, Pallas kernels for 6%

profile of v8, /device:TPU:0, one launch (start us, length us, event | category | flops | bytes accessed | tf_op | source)
XLA Modules:
  0.0 164.8 jit_solution(6675040406435320908)
XLA Ops:
  1.8 3.0 %collective-permute-start = (bf16[64,1024]{1,0:T(8,128)(2,1)S(1)}, bf16[64,1024]{1,0:T(8,128)(2,1)S(1)}, u32[]{:S(2)}, u32[]{:S(2)}) collective-permute-start(bf16[64,1024]{1,0:T(8,128)(2,1)S(1)} %constant_dynamic-slice_fusion), channel_id=1, source_target_pairs={{0,1},{1,0},{2,3},{3,2},{4,5},{5,4},{6,7},{7,6},{8,9},{9,8},{10,11... | collective-permute-start | bytes 393224 | tf_op jit(solution)/shard_map/ppermute | solution.py:314
  4.8 2.4 %dynamic-slice_bitcast_fusion = (bf16[416,768]{1,0:T(8,128)(2,1)}, bf16[416,768]{1,0:T(8,128)(2,1)}) fusion(bf16[2,1024,768]{2,1,0:T(8,128)(2,1)} %refs_6_.1, s32[]{:T(128)S(6)} %select_n.43), kind=kLoop, calls=%fused_computation.4 | loop fusion | bytes 2555908 | tf_op jit(solution)/shard_map/squeeze | solution.py:332
  11.4 2.7 %collective-permute-start.2 = (bf16[64,2176]{1,0:T(8,128)(2,1)S(1)}, bf16[64,2176]{1,0:T(8,128)(2,1)S(1)}, u32[]{:S(2)}, u32[]{:S(2)}) collective-permute-start(bf16[64,2176]{1,0:T(8,128)(2,1)S(1)} %shard_map.123.refs_0_.refs_6_), channel_id=1, source_target_pairs={{0,8},{2,10},{4,12},{6,14},{8,0},{10,2},{12,4},{14,6},{1,9},{3,11}... | collective-permute-start | bytes 835592 | tf_op jit(solution)/shard_map/ppermute | solution.py:322
  16.2 16.6 %collective-permute-done.2.refs_2_.refs_8_ = bf16[64,2176]{1,0:T(8,128)(2,1)S(1)} collective-permute-done((bf16[64,2176]{1,0:T(8,128)(2,1)S(1)}, bf16[64,2176]{1,0:T(8,128)(2,1)S(1)}, u32[]{:S(2)}, u32[]{:S(2)}) %collective-permute-start.2) | collective-permute-done | bytes 278560 | tf_op jit(solution)/shard_map/ppermute | solution.py:322
  34.4 3.3 %collective-permute-done.8.refs_8_ = bf16[416,768]{1,0:T(8,128)(2,1)S(1)} collective-permute-done((bf16[416,768]{1,0:T(8,128)(2,1)S(1)}, bf16[416,768]{1,0:T(8,128)(2,1)S(1)}, u32[]{:S(2)}, u32[]{:S(2)}) %collective-permute-start.8) | collective-permute-done | bytes 639008 | tf_op jit(solution)/shard_map/ppermute | solution.py:314
  40.8 7.2 %collective-permute-done.5.refs_9_ = bf16[416,768]{1,0:T(8,128)(2,1)S(1)} collective-permute-done((bf16[416,768]{1,0:T(8,128)(2,1)}, bf16[416,768]{1,0:T(8,128)(2,1)S(1)}, u32[]{:S(2)}, u32[]{:S(2)}) %collective-permute-start.5) | collective-permute-done | bytes 639008 | tf_op jit(solution)/shard_map/ppermute | solution.py:318
  48.8 3.8 %collective-permute-done.10.refs_11_ = bf16[2,192,768]{2,1,0:T(8,128)(2,1)S(1)} collective-permute-done((bf16[2,192,768]{2,1,0:T(8,128)(2,1)S(1)}, bf16[2,192,768]{2,1,0:T(8,128)(2,1)S(1)}, u32[]{:S(2)}, u32[]{:S(2)}) %collective-permute-start.10) | collective-permute-done | bytes 589856 | tf_op jit(solution)/shard_map/ppermute | solution.py:314
  54.3 2.8 %collective-permute-done.9.refs_10_ = bf16[416,768]{1,0:T(8,128)(2,1)S(1)} collective-permute-done((bf16[416,768]{1,0:T(8,128)(2,1)S(1)}, bf16[416,768]{1,0:T(8,128)(2,1)S(1)}, u32[]{:S(2)}, u32[]{:S(2)}) %collective-permute-start.9) | collective-permute-done | bytes 639008 | tf_op jit(solution)/shard_map/ppermute | solution.py:318
  57.1 6.9 %shard_map.124.hidden_ref = bf16[512,768]{1,0:T(8,128)(2,1)S(1)} custom-call(s32[3]{0:T(128)S(1)} %pad_add_fusion.where_ref, bf16[64,2176]{1,0:T(8,128)(2,1)S(1)} %shard_map.123.refs_0_.refs_6_, bf16[64,2176]{1,0:T(8,128)(2,1)S(1)} %collective-permute-done.1.refs_1_.refs_7_, bf16[64,2176]{1,0:T(8,128)(2,1)S(1)} %collective-permute-done.2.refs_2_.refs_8_, ...), custom_call_target="tpu_custom_call" | custom-call | flops 3221225472 | bytes 8388608 | tf_op jit(solution)/shard_map/pallas_call | solution.py:243
  69.3 8.4 %collective-permute-done.13 = bf16[64,1024]{1,0:T(8,128)(2,1)S(1)} collective-permute-done((bf16[64,1024]{1,0:T(8,128)(2,1)S(1)}, bf16[64,1024]{1,0:T(8,128)(2,1)S(1)}, u32[]{:S(2)}, u32[]{:S(2)}) %collective-permute-start.13) | collective-permute-done | bytes 131104 | tf_op jit(solution)/shard_map/ppermute | solution.py:322
  77.7 8.0 %collective-permute-done.16.hidden_ref = bf16[512,768]{1,0:T(8,128)(2,1)S(1)} collective-permute-done((bf16[512,768]{1,0:T(8,128)(2,1)S(1)}, bf16[512,768]{1,0:T(8,128)(2,1)S(1)}, u32[]{:S(2)}, u32[]{:S(2)}) %collective-permute-start.16) | collective-permute-done | bytes 786464 | tf_op jit(solution)/shard_map/ppermute | solution.py:314
  87.5 4.4 %collective-permute-start.14 = (bf16[64,1024]{1,0:T(8,128)(2,1)}, bf16[64,1024]{1,0:T(8,128)(2,1)}, u32[]{:S(2)}, u32[]{:S(2)}) collective-permute-start(bf16[64,1024]{1,0:T(8,128)(2,1)} %get-tuple-element.64), channel_id=1, source_target_pairs={{0,12},{2,14},{4,8},{6,10},{8,4},{10,6},{12,0},{14,2},{1,13},{3,15... | collective-permute-start | bytes 393224 | tf_op jit(solution)/shard_map/ppermute | solution.py:322
  92.9 6.2 %collective-permute-done.12 = bf16[64,1024]{1,0:T(8,128)(2,1)S(1)} collective-permute-done((bf16[64,1024]{1,0:T(8,128)(2,1)S(1)}, bf16[64,1024]{1,0:T(8,128)(2,1)S(1)}, u32[]{:S(2)}, u32[]{:S(2)}) %collective-permute-start.12) | collective-permute-done | bytes 131104 | tf_op jit(solution)/shard_map/ppermute | solution.py:322
  105.6 2.1 %collective-permute-done.20 = bf16[64,1024]{1,0:T(8,128)(2,1)} collective-permute-done((bf16[64,1024]{1,0:T(8,128)(2,1)}, bf16[64,1024]{1,0:T(8,128)(2,1)}, u32[]{:S(2)}, u32[]{:S(2)}) %collective-permute-start.20) | collective-permute-done | bytes 131104 | tf_op jit(solution)/shard_map/ppermute | solution.py:322
  107.8 6.3 %collective-permute-done.19 = bf16[64,1024]{1,0:T(8,128)(2,1)} collective-permute-done((bf16[64,1024]{1,0:T(8,128)(2,1)}, bf16[64,1024]{1,0:T(8,128)(2,1)}, u32[]{:S(2)}, u32[]{:S(2)}) %collective-permute-start.19) | collective-permute-done | bytes 131104 | tf_op jit(solution)/shard_map/ppermute | solution.py:322
  118.4 2.9 %collective-permute-done.21 = bf16[64,1024]{1,0:T(8,128)(2,1)S(1)} collective-permute-done((bf16[64,1024]{1,0:T(8,128)(2,1)S(1)}, bf16[64,1024]{1,0:T(8,128)(2,1)S(1)}, u32[]{:S(2)}, u32[]{:S(2)}) %collective-permute-start.21) | collective-permute-done | bytes 131104 | tf_op jit(solution)/shard_map/ppermute | solution.py:314
  124.1 2.6 %collective-permute-start.24 = (bf16[64,1024]{1,0:T(8,128)(2,1)S(1)}, bf16[64,1024]{1,0:T(8,128)(2,1)S(1)}, u32[]{:S(2)}, u32[]{:S(2)}) collective-permute-start(bf16[64,1024]{1,0:T(8,128)(2,1)S(1)} %pad_maximum_fusion.3.refs_0_), channel_id=1, source_target_pairs={{0,12},{2,14},{4,8},{6,10},{8,4},{10,6},{12,0},{14,2},{1,13},{3,15... | collective-permute-start | bytes 393224 | tf_op jit(solution)/shard_map/ppermute | solution.py:322
  126.8 2.0 %collective-permute-done.22.refs_1_ = bf16[64,1024]{1,0:T(8,128)(2,1)S(1)} collective-permute-done((bf16[64,1024]{1,0:T(8,128)(2,1)S(1)}, bf16[64,1024]{1,0:T(8,128)(2,1)S(1)}, u32[]{:S(2)}, u32[]{:S(2)}) %collective-permute-start.22) | collective-permute-done | bytes 131104 | tf_op jit(solution)/shard_map/ppermute | solution.py:322
  128.8 4.5 %collective-permute-done.23.refs_2_ = bf16[64,1024]{1,0:T(8,128)(2,1)S(1)} collective-permute-done((bf16[64,1024]{1,0:T(8,128)(2,1)S(1)}, bf16[64,1024]{1,0:T(8,128)(2,1)S(1)}, u32[]{:S(2)}, u32[]{:S(2)}) %collective-permute-start.23) | collective-permute-done | bytes 131104 | tf_op jit(solution)/shard_map/ppermute | solution.py:322
  135.3 3.1 %collective-permute-done.30.refs_17_.refs_0_ = bf16[2,384,512]{2,1,0:T(8,128)(2,1)S(1)} collective-permute-done((bf16[2,384,512]{2,1,0:T(8,128)(2,1)S(1)}, bf16[2,384,512]{2,1,0:T(8,128)(2,1)S(1)}, u32[]{:S(2)}, u32[]{:S(2)}) %collective-permute-start.30) | collective-permute-done | bytes 786464 | tf_op jit(solution)/shard_map/ppermute | solution.py:314
  138.5 5.5 %shard_map.127.hidden_ref = bf16[512,768]{1,0:T(8,128)(2,1)S(1)} custom-call(s32[3]{0:T(128)S(1)} %pad_add_fusion.where_ref, bf16[64,1024]{1,0:T(8,128)(2,1)S(1)} %pad_maximum_fusion.3.refs_0_, bf16[64,1024]{1,0:T(8,128)(2,1)S(1)} %collective-permute-done.22.refs_1_, bf16[64,1024]{1,0:T(8,128)(2,1)S(1)} %collective-permute-done.23.refs_2_, ...), custom_call_target="tpu_custom_call" | custom-call | flops 1610612736 | bytes 4194304 | tf_op jit(solution)/shard_map/pallas_call | solution.py:243
  150.3 2.8 %collective-permute-start.32 = (bf16[64,512]{1,0:T(8,128)(2,1)S(1)}, bf16[64,512]{1,0:T(8,128)(2,1)S(1)}, u32[]{:S(2)}, u32[]{:S(2)}) collective-permute-start(bf16[64,512]{1,0:T(8,128)(2,1)S(1)} %get-tuple-element.70), channel_id=1, source_target_pairs={{0,4},{2,6},{4,0},{6,2},{8,12},{10,14},{12,8},{14,10},{1,5},{3,7},... | collective-permute-start | bytes 196616 | tf_op jit(solution)/shard_map/ppermute | solution.py:322
  155.6 2.9 %collective-permute-start.37 = (bf16[64,512]{1,0:T(8,128)(2,1)S(1)}, bf16[64,512]{1,0:T(8,128)(2,1)S(1)}, u32[]{:S(2)}, u32[]{:S(2)}) collective-permute-start(bf16[64,512]{1,0:T(8,128)(2,1)S(1)} %get-tuple-element.69), channel_id=1, source_target_pairs={{0,5},{1,4},{2,7},{3,6},{4,1},{5,0},{6,3},{7,2},{8,13},{9,12},{10,... | collective-permute-start | bytes 196616 | tf_op jit(solution)/shard_map/ppermute | solution.py:343
  160.7 2.7 %collective-permute-done.38 = bf16[64,512]{1,0:T(8,128)(2,1)S(1)} collective-permute-done((bf16[64,512]{1,0:T(8,128)(2,1)S(1)}, bf16[64,512]{1,0:T(8,128)(2,1)S(1)}, u32[]{:S(2)}, u32[]{:S(2)}) %collective-permute-start.38) | collective-permute-done | bytes 65568 | tf_op jit(solution)/shard_map/ppermute | solution.py:343
  (131 shorter events, 50.5 us)
Async XLA Ops:
  8.3 24.5 %collective-permute-start.4 = (bf16[416,768]{1,0:T(8,128)(2,1)}, bf16[416,768]{1,0:T(8,128)(2,1)}, u32[]{:S(2)}, u32[]{:S(2)}) collective-permute-start(bf16[416,768]{1,0:T(8,128)(2,1)} %get-tuple-element.26), channel_id=1, source_target_pairs={{0,1},{1,0},{2,3},{3,2},{4,5},{5,4},{6,7},{7,6},{8,9},{9,8},{10,11... | collective-permute-start | bytes 1916936 | tf_op jit(solution)/shard_map/ppermute | solution.py:314
  11.4 21.4 %collective-permute-start.2 = (bf16[64,2176]{1,0:T(8,128)(2,1)S(1)}, bf16[64,2176]{1,0:T(8,128)(2,1)S(1)}, u32[]{:S(2)}, u32[]{:S(2)}) collective-permute-start(bf16[64,2176]{1,0:T(8,128)(2,1)S(1)} %shard_map.123.refs_0_.refs_6_), channel_id=1, source_target_pairs={{0,8},{2,10},{4,12},{6,14},{8,0},{10,2},{12,4},{14,6},{1,9},{3,11}... | collective-permute-start | bytes 835592 | tf_op jit(solution)/shard_map/ppermute | solution.py:322
  14.0 20.2 %collective-permute-start.1 = (bf16[64,2176]{1,0:T(8,128)(2,1)S(1)}, bf16[64,2176]{1,0:T(8,128)(2,1)S(1)}, u32[]{:S(2)}, u32[]{:S(2)}) collective-permute-start(bf16[64,2176]{1,0:T(8,128)(2,1)S(1)} %shard_map.123.refs_0_.refs_6_), channel_id=1, source_target_pairs={{0,4},{2,6},{4,0},{6,2},{8,12},{10,14},{12,8},{14,10},{1,5},{3,7},... | collective-permute-start | bytes 835592 | tf_op jit(solution)/shard_map/ppermute | solution.py:322
  15.6 18.7 %collective-permute-start.3 = (bf16[64,2176]{1,0:T(8,128)(2,1)S(1)}, bf16[64,2176]{1,0:T(8,128)(2,1)S(1)}, u32[]{:S(2)}, u32[]{:S(2)}) collective-permute-start(bf16[64,2176]{1,0:T(8,128)(2,1)S(1)} %shard_map.123.refs_0_.refs_6_), channel_id=1, source_target_pairs={{0,12},{2,14},{4,8},{6,10},{8,4},{10,6},{12,0},{14,2},{1,13},{3,15... | collective-permute-start | bytes 835592 | tf_op jit(solution)/shard_map/ppermute | solution.py:322
  15.8 21.9 %collective-permute-start.8 = (bf16[416,768]{1,0:T(8,128)(2,1)S(1)}, bf16[416,768]{1,0:T(8,128)(2,1)S(1)}, u32[]{:S(2)}, u32[]{:S(2)}) collective-permute-start(bf16[416,768]{1,0:T(8,128)(2,1)S(1)} %copy-done.18), channel_id=1, source_target_pairs={{0,1},{1,0},{2,3},{3,2},{4,5},{5,4},{6,7},{7,6},{8,9},{9,8},{10,11... | collective-permute-start | bytes 1916936 | tf_op jit(solution)/shard_map/ppermute | solution.py:314
  32.7 15.2 %collective-permute-start.5 = (bf16[416,768]{1,0:T(8,128)(2,1)}, bf16[416,768]{1,0:T(8,128)(2,1)S(1)}, u32[]{:S(2)}, u32[]{:S(2)}) collective-permute-start(bf16[416,768]{1,0:T(8,128)(2,1)} %collective-permute-done.4.refs_7_), channel_id=1, source_target_pairs={{0,16},{16,0},{1,17},{17,1},{2,18},{18,2},{3,19},{19,3},{4,20},{20... | collective-permute-start | bytes 1916936 | tf_op jit(solution)/shard_map/ppermute | solution.py:318
  34.3 19.9 %collective-permute-start.7 = (bf16[192,2176]{1,0:T(8,128)(2,1)S(1)}, bf16[192,2176]{1,0:T(8,128)(2,1)S(1)}, u32[]{:S(2)}, u32[]{:S(2)}) collective-permute-start(bf16[192,2176]{1,0:T(8,128)(2,1)S(1)} %pad_maximum_fusion), channel_id=1, source_target_pairs={{0,2},{2,0},{4,6},{6,4},{8,10},{10,8},{12,14},{14,12},{1,3},{3,1},... | collective-permute-start | bytes 2506760 | tf_op jit(solution)/shard_map/ppermute | solution.py:322
  37.7 19.3 %collective-permute-start.9 = (bf16[416,768]{1,0:T(8,128)(2,1)S(1)}, bf16[416,768]{1,0:T(8,128)(2,1)S(1)}, u32[]{:S(2)}, u32[]{:S(2)}) collective-permute-start(bf16[416,768]{1,0:T(8,128)(2,1)S(1)} %collective-permute-done.8.refs_8_), channel_id=1, source_target_pairs={{0,16},{16,0},{1,17},{17,1},{2,18},{18,2},{3,19},{19,3},{4,20},{20... | collective-permute-start | bytes 1916936 | tf_op jit(solution)/shard_map/ppermute | solution.py:318
  39.2 13.4 %collective-permute-start.10 = (bf16[2,192,768]{2,1,0:T(8,128)(2,1)S(1)}, bf16[2,192,768]{2,1,0:T(8,128)(2,1)S(1)}, u32[]{:S(2)}, u32[]{:S(2)}) collective-permute-start(bf16[2,192,768]{2,1,0:T(8,128)(2,1)S(1)} %slice.99), channel_id=1, source_target_pairs={{0,1},{1,0},{2,3},{3,2},{4,5},{5,4},{6,7},{7,6},{8,9},{9,8},{10,11... | collective-permute-start | bytes 1769480 | tf_op jit(solution)/shard_map/ppermute | solution.py:314
  48.0 9.1 %collective-permute-start.6 = (bf16[64,2176]{1,0:T(8,128)(2,1)S(1)}, bf16[64,2176]{1,0:T(8,128)(2,1)S(1)}, u32[]{:S(2)}, u32[]{:S(2)}) collective-permute-start(bf16[64,2176]{1,0:T(8,128)(2,1)S(1)} %shard_map.123.refs_0_.refs_6_), channel_id=1, source_target_pairs={{0,2},{2,0},{4,6},{6,4},{8,10},{10,8},{12,14},{14,12},{1,3},{3,1},... | collective-permute-start | bytes 835592 | tf_op jit(solution)/shard_map/ppermute | solution.py:322
  52.6 13.2 %collective-permute-start.15 = (bf16[256,768]{1,0:T(8,128)(2,1)S(1)}, bf16[256,768]{1,0:T(8,128)(2,1)S(1)}, u32[]{:S(2)}, u32[]{:S(2)}) collective-permute-start(bf16[256,768]{1,0:T(8,128)(2,1)S(1)} %get-tuple-element.33), channel_id=1, source_target_pairs={{0,1},{1,0},{2,3},{3,2},{4,5},{5,4},{6,7},{7,6},{8,9},{9,8},{10,11... | collective-permute-start | bytes 1179656 | tf_op jit(solution)/shard_map/ppermute | solution.py:314
  65.8 19.9 %collective-permute-start.16 = (bf16[512,768]{1,0:T(8,128)(2,1)S(1)}, bf16[512,768]{1,0:T(8,128)(2,1)S(1)}, u32[]{:S(2)}, u32[]{:S(2)}) collective-permute-start(bf16[512,768]{1,0:T(8,128)(2,1)S(1)} %shard_map.124.hidden_ref), channel_id=1, source_target_pairs={{0,1},{1,0},{2,3},{3,2},{4,5},{5,4},{6,7},{7,6},{8,9},{9,8},{10,11... | collective-permute-start | bytes 2359304 | tf_op jit(solution)/shard_map/ppermute | solution.py:314
  68.5 9.2 %collective-permute-start.13 = (bf16[64,1024]{1,0:T(8,128)(2,1)S(1)}, bf16[64,1024]{1,0:T(8,128)(2,1)S(1)}, u32[]{:S(2)}, u32[]{:S(2)}) collective-permute-start(bf16[64,1024]{1,0:T(8,128)(2,1)S(1)} %get-tuple-element.65), channel_id=1, source_target_pairs={{0,8},{2,10},{4,12},{6,14},{8,0},{10,2},{12,4},{14,6},{1,9},{3,11}... | collective-permute-start | bytes 393224 | tf_op jit(solution)/shard_map/ppermute | solution.py:322
  87.5 17.6 %collective-permute-start.14 = (bf16[64,1024]{1,0:T(8,128)(2,1)}, bf16[64,1024]{1,0:T(8,128)(2,1)}, u32[]{:S(2)}, u32[]{:S(2)}) collective-permute-start(bf16[64,1024]{1,0:T(8,128)(2,1)} %get-tuple-element.64), channel_id=1, source_target_pairs={{0,12},{2,14},{4,8},{6,10},{8,4},{10,6},{12,0},{14,2},{1,13},{3,15... | collective-permute-start | bytes 393224 | tf_op jit(solution)/shard_map/ppermute | solution.py:322
  100.6 13.5 %collective-permute-start.19 = (bf16[64,1024]{1,0:T(8,128)(2,1)}, bf16[64,1024]{1,0:T(8,128)(2,1)}, u32[]{:S(2)}, u32[]{:S(2)}) collective-permute-start(bf16[64,1024]{1,0:T(8,128)(2,1)} %get-tuple-element.39), channel_id=1, source_target_pairs={{0,8},{2,10},{4,12},{6,14},{8,0},{10,2},{12,4},{14,6},{1,9},{3,11}... | collective-permute-start | bytes 393224 | tf_op jit(solution)/shard_map/ppermute | solution.py:322
  102.3 11.8 %collective-permute-start.18 = (bf16[64,1024]{1,0:T(8,128)(2,1)}, bf16[64,1024]{1,0:T(8,128)(2,1)}, u32[]{:S(2)}, u32[]{:S(2)}) collective-permute-start(bf16[64,1024]{1,0:T(8,128)(2,1)} %get-tuple-element.38), channel_id=1, source_target_pairs={{0,4},{2,6},{4,0},{6,2},{8,12},{10,14},{12,8},{14,10},{1,5},{3,7},... | collective-permute-start | bytes 393224 | tf_op jit(solution)/shard_map/ppermute | solution.py:322
  103.6 13.3 %collective-permute-start.27 = (bf16[256,768]{1,0:T(8,128)(2,1)}, bf16[256,768]{1,0:T(8,128)(2,1)S(1)}, u32[]{:S(2)}, u32[]{:S(2)}) collective-permute-start(bf16[256,768]{1,0:T(8,128)(2,1)} %copy-done.10), channel_id=1, source_target_pairs={{0,16},{16,0},{1,17},{17,1},{2,18},{18,2},{3,19},{19,3},{4,20},{20... | collective-permute-start | bytes 1179656 | tf_op jit(solution)/shard_map/ppermute | solution.py:318
  105.1 11.7 %collective-permute-start.26 = (bf16[256,768]{1,0:T(8,128)(2,1)}, bf16[256,768]{1,0:T(8,128)(2,1)S(1)}, u32[]{:S(2)}, u32[]{:S(2)}) collective-permute-start(bf16[256,768]{1,0:T(8,128)(2,1)} %get-tuple-element.41), channel_id=1, source_target_pairs={{0,1},{1,0},{2,3},{3,2},{4,5},{5,4},{6,7},{7,6},{8,9},{9,8},{10,11... | collective-permute-start | bytes 1179656 | tf_op jit(solution)/shard_map/ppermute | solution.py:314
  116.8 16.5 %collective-permute-start.28 = (bf16[256,768]{1,0:T(8,128)(2,1)S(1)}, bf16[256,768]{1,0:T(8,128)(2,1)S(1)}, u32[]{:S(2)}, u32[]{:S(2)}) collective-permute-start(bf16[256,768]{1,0:T(8,128)(2,1)S(1)} %collective-permute-done.26.refs_14_), channel_id=1, source_target_pairs={{0,16},{16,0},{1,17},{17,1},{2,18},{18,2},{3,19},{19,3},{4,20},{20... | collective-permute-start | bytes 1179656 | tf_op jit(solution)/shard_map/ppermute | solution.py:318
  121.3 17.2 %collective-permute-start.30 = (bf16[2,384,512]{2,1,0:T(8,128)(2,1)S(1)}, bf16[2,384,512]{2,1,0:T(8,128)(2,1)S(1)}, u32[]{:S(2)}, u32[]{:S(2)}) collective-permute-start(bf16[2,384,512]{2,1,0:T(8,128)(2,1)S(1)} %copy-done.6), channel_id=1, source_target_pairs={{0,1},{1,0},{2,3},{3,2},{4,5},{5,4},{6,7},{7,6},{8,9},{9,8},{10,11... | collective-permute-start | bytes 2359304 | tf_op jit(solution)/shard_map/ppermute | solution.py:314
  122.4 10.9 %collective-permute-start.23 = (bf16[64,1024]{1,0:T(8,128)(2,1)S(1)}, bf16[64,1024]{1,0:T(8,128)(2,1)S(1)}, u32[]{:S(2)}, u32[]{:S(2)}) collective-permute-start(bf16[64,1024]{1,0:T(8,128)(2,1)S(1)} %pad_maximum_fusion.3.refs_0_), channel_id=1, source_target_pairs={{0,8},{2,10},{4,12},{6,14},{8,0},{10,2},{12,4},{14,6},{1,9},{3,11}... | collective-permute-start | bytes 393224 | tf_op jit(solution)/shard_map/ppermute | solution.py:322
  124.1 9.2 %collective-permute-start.24 = (bf16[64,1024]{1,0:T(8,128)(2,1)S(1)}, bf16[64,1024]{1,0:T(8,128)(2,1)S(1)}, u32[]{:S(2)}, u32[]{:S(2)}) collective-permute-start(bf16[64,1024]{1,0:T(8,128)(2,1)S(1)} %pad_maximum_fusion.3.refs_0_), channel_id=1, source_target_pairs={{0,12},{2,14},{4,8},{6,10},{8,4},{10,6},{12,0},{14,2},{1,13},{3,15... | collective-permute-start | bytes 393224 | tf_op jit(solution)/shard_map/ppermute | solution.py:322
  150.3 9.2 %collective-permute-start.33 = (bf16[64,512]{1,0:T(8,128)(2,1)S(1)}, bf16[64,512]{1,0:T(8,128)(2,1)S(1)}, u32[]{:S(2)}, u32[]{:S(2)}) collective-permute-start(bf16[64,512]{1,0:T(8,128)(2,1)S(1)} %get-tuple-element.72), channel_id=1, source_target_pairs={{0,8},{2,10},{4,12},{6,14},{8,0},{10,2},{12,4},{14,6},{1,9},{3,11}... | collective-permute-start | bytes 196616 | tf_op jit(solution)/shard_map/ppermute | solution.py:322
  150.3 10.4 %collective-permute-start.32 = (bf16[64,512]{1,0:T(8,128)(2,1)S(1)}, bf16[64,512]{1,0:T(8,128)(2,1)S(1)}, u32[]{:S(2)}, u32[]{:S(2)}) collective-permute-start(bf16[64,512]{1,0:T(8,128)(2,1)S(1)} %get-tuple-element.70), channel_id=1, source_target_pairs={{0,4},{2,6},{4,0},{6,2},{8,12},{10,14},{12,8},{14,10},{1,5},{3,7},... | collective-permute-start | bytes 196616 | tf_op jit(solution)/shard_map/ppermute | solution.py:322
  (39 other events, 519.6 us)

commit v9 on v8

--- a/solution.py
+++ b/solution.py
@@ -263,12 +263,12 @@
     )(where, *inputs)
 
 
-def down_kernel(chunks, where_ref, hidden_ref, *refs):
+def down_kernel(halves, chunks, where_ref, hidden_ref, *refs):
     refs = list(refs)
     take = lambda count: [refs.pop(0) for _ in range(count)]
     chunk_refs = [take(chunks), take(chunks)]
-    whole_refs = refs[:-4]
-    mine_ref, away_ref, weights, sems = refs[-4:]
+    weights, sems = refs[-2:]
+    out_refs, whole_refs = refs[-2 - len(halves) : -2], refs[: -2 - len(halves)]
     depth = weights.shape[0] // 2
     pairs = []
     for order in range(2):
@@ -277,8 +277,8 @@
         pairs += chunk_pairs(parts, weights, order * depth)
     for copy in load(pairs, sems):
         copy.wait()
-    rows = mine_ref.shape[0]
-    for half, out_ref in enumerate((mine_ref, away_ref)):
+    rows = hidden_ref.shape[0] // 2
+    for half, out_ref in zip(halves, out_refs):
         out_ref[...] = jnp.dot(
             hidden_ref[half * rows : (half + 1) * rows, :],
             weights[...],
@@ -286,25 +286,25 @@
         ).astype(jnp.bfloat16)
 
 
-def run_down(where, hidden, near, far, whole):
+def run_down(where, hidden, near, far, whole, halves=(0, 1)):
     count, depth = hidden.shape
     inputs = [*near, *far, *whole]
     columns = inputs[0].shape[-1]
-    shape = jax.ShapeDtypeStruct((count // 2, columns), jnp.bfloat16)
+    outs = len(halves)
     return pl.pallas_call(
-        functools.partial(down_kernel, len(near)),
-        out_shape=(shape, shape),
+        functools.partial(down_kernel, halves, len(near)),
+        out_shape=(jax.ShapeDtypeStruct((count // 2, columns), jnp.bfloat16),) * outs,
         in_specs=[pl.BlockSpec(memory_space=pltpu.SMEM), pl.BlockSpec(memory_space=pltpu.VMEM)]
         + [pl.BlockSpec(memory_space=pltpu.HBM)] * len(inputs),
-        out_specs=(pl.BlockSpec(memory_space=pltpu.VMEM),) * 2,
+        out_specs=(pl.BlockSpec(memory_space=pltpu.VMEM),) * outs,
         scratch_shapes=[
             pltpu.VMEM((depth, columns), jnp.bfloat16),
             pltpu.SemaphoreType.DMA((2 * (len(near) + len(whole)),)),
         ],
         compiler_params=pltpu.CompilerParams(vmem_limit_bytes=16 * 1024 * 1024),
         cost_estimate=pl.CostEstimate(
-            flops=2 * count * depth * columns,
-            bytes_accessed=2 * (count * depth + depth * columns + count * columns),
+            flops=outs * count * depth * columns,
+            bytes_accessed=2 * depth * (count + columns) + outs * count * columns,
             transcendentals=0,
         ),
     )(where, hidden, *inputs)
@@ -343,19 +343,21 @@
     return lax.ppermute(array, ("expert", "replica"), pairs)
 
 
-def spread_sums(mine, away, before=(), hold=(), cross=False):
+def chip_sums(mine, other, cross=False):
     owners = lax.axis_size("expert")
     rows = mine.shape[0] // (owners // 2)
-    other = over_expert(after(away, *hold), 1)
     terms = []
     for index in range(owners // 2):
         part = slice(index * rows, (index + 1) * rows)
         chip = mine[part].astype(jnp.float32) + other[part].astype(jnp.float32)
         if cross or index:
-            chip = after(chip.astype(jnp.bfloat16), *before)
-            chip = (over_both if cross else over_expert)(chip, 2 * index)
+            chip = (over_both if cross else over_expert)(chip.astype(jnp.bfloat16), 2 * index)
         terms.append(chip)
     return terms
+
+
+def spread_sums(mine, away, cross=False):
+    return chip_sums(mine, over_expert(away, 1), cross)
 
 
 def add_up(terms):
@@ -401,17 +403,20 @@
     far_in = [over_groups(after(near_in[0], same[2]))]
     far_in.append(over_groups(near_in[1]))
     direct_in = over_replica(after(w_in[:, 2 * chunk :], near_in[0]))
-    across = [over_expert(after(row, far_in[0]), 1), over_expert(jnp.concatenate(same[1:]), 1)]
+    across = [over_expert(after(row, far_in[0]), 1), over_expert(jnp.concatenate([*same[1:3], after(same[3], near_in[1])]), 1)]
     blocks = same + across
     hidden = run_hidden(where, blocks, [], w_in, near_in, far_in, [direct_in], [], 0, experts)
+    other_hidden = over_replica(hidden)
+    own = spread_sums(*run_down(where, hidden, [], [], [w_out]))
+    other_hidden = after(other_hidden, *own[1:])
+    (got_away,) = run_down(where, other_hidden, [], [], [w_out], (1,))
+    other_hidden = after(other_hidden, got_away)
+    (got_mine,) = run_down(where, other_hidden, [], [], [w_out], (0,))
+    got_away = over_expert(got_away, 1)
     half = talker_w_in.shape[1] // 2
-    near_talker_in = [send(talker_w_in, group, 0, half, direct_in)]
+    near_talker_in = [send(talker_w_in, group, first, half, got_mine) for first in (0, half)]
+    got = chip_sums(got_mine, got_away)
     far_talker_in = [over_groups(near_talker_in[0])]
-    other_hidden = over_replica(after(hidden, near_talker_in[0]))
-    own = spread_sums(*run_down(where, hidden, [], [], [w_out]))
-    got = run_down(where, after(other_hidden, own[2]), [], [], [w_out])
-    near_talker_in.append(send(talker_w_in, group, half, half, own[3], *got))
-    got = spread_sums(*got, before=[own[1]])
     far_talker_in.append(over_groups(after(near_talker_in[1], far_talker_in[0])))
     got, own = add_up(got), add_up(own)
     thinker_out = in_order(replica, own, got, 0)

time: 165 us -> 164 us (level)
  waiting for transfers between devices: 86.6 us -> 82.2 us
  starting transfers between devices: 46.7 us -> 49 us
    ppermute x23, waiting for transfers between devices: 51 us -> 43 us  [over_expert(): lax.ppermute(array, 'expert', [(at, at ^ distance) for at in range(lax.ax...]
    ppermute x4, waiting for transfers between devices: 9.98 us -> 17 us  [over_groups(): return lax.ppermute(array, 'groups', SWAP)]
    ppermute x9, waiting for transfers between devices: 22.2 us -> 18.3 us  [over_replica(): return lax.ppermute(array, 'replica', SWAP)]
    pallas_call x4 -> x5, Pallas kernels: 6.36 us -> 7.23 us  [run_down(): pl.pallas_call(functools.partial(down_kernel, halves, len(near)), out_sha...]
  transfers between devices with their start and end apart: 40 -> 40, of which waited for: 21 -> 23; matrix products, arithmetic and copies ran while one was open for 5% -> 5% of each run, Pallas kernels for 6% -> 2%
where the time goes in v9:
time: 164 us
  waiting for transfers between devices  82.2 us (50%)
  starting transfers between devices  49 us (30%)
  Pallas kernels  21.2 us (13%)
  local copies, waits for them, and re-layouts  5.37 us (3%)
  other arithmetic  4.29 us (3%)
    ppermute x23, waiting for transfers between devices, over_expert(): lax.ppermute(array, 'expert', [(at, at ^ distance) for at in range(lax.ax...  43 us
    ppermute x23, starting transfers between devices, over_expert(): lax.ppermute(array, 'expert', [(at, at ^ distance) for at in range(lax.ax...  25.2 us
    ppermute x9, waiting for transfers between devices, over_replica(): return lax.ppermute(array, 'replica', SWAP)  18.3 us
    ppermute x4, waiting for transfers between devices, over_groups(): return lax.ppermute(array, 'groups', SWAP)  17 us
    pallas_call x2, Pallas kernels, run_hidden(): pl.pallas_call(functools.partial(hidden_kernel, blocks, len(gain_blocks),...  12.7 us
    ppermute x9, starting transfers between devices, over_replica(): return lax.ppermute(array, 'replica', SWAP)  11.2 us
    pallas_call x5, Pallas kernels, run_down(): pl.pallas_call(functools.partial(down_kernel, halves, len(near)), out_sha...  7.23 us
    ppermute x4, starting transfers between devices, over_both(): return lax.ppermute(array, ('expert', 'replica'), pairs)  6.82 us
  transfers between devices with their start and end apart: 40, of which 23 were waited for; matrix products, arithmetic and copies ran while one was open for 5% of the time, Pallas kernels for 2%

profile of v9, /device:TPU:0, one launch (start us, length us, event | category | flops | bytes accessed | tf_op | source)
XLA Modules:
  0.0 164.0 jit_solution(9911500261040665184)
XLA Ops:
  1.8 3.0 %collective-permute-start = (bf16[64,1024]{1,0:T(8,128)(2,1)S(1)}, bf16[64,1024]{1,0:T(8,128)(2,1)S(1)}, u32[]{:S(2)}, u32[]{:S(2)}) collective-permute-start(bf16[64,1024]{1,0:T(8,128)(2,1)S(1)} %constant_dynamic-slice_fusion), channel_id=1, source_target_pairs={{0,1},{1,0},{2,3},{3,2},{4,5},{5,4},{6,7},{7,6},{8,9},{9,8},{10,11... | collective-permute-start | bytes 393224 | tf_op jit(solution)/shard_map/ppermute | solution.py:314
  4.8 2.4 %dynamic-slice_bitcast_fusion = (bf16[416,768]{1,0:T(8,128)(2,1)}, bf16[416,768]{1,0:T(8,128)(2,1)}) fusion(bf16[2,1024,768]{2,1,0:T(8,128)(2,1)} %refs_6_.1, s32[]{:T(128)S(6)} %select_n.43), kind=kLoop, calls=%fused_computation.4 | loop fusion | bytes 2555908 | tf_op jit(solution)/shard_map/squeeze | solution.py:332
  8.3 1.7 %collective-permute-start.4 = (bf16[416,768]{1,0:T(8,128)(2,1)}, bf16[416,768]{1,0:T(8,128)(2,1)}, u32[]{:S(2)}, u32[]{:S(2)}) collective-permute-start(bf16[416,768]{1,0:T(8,128)(2,1)} %get-tuple-element.22), channel_id=1, source_target_pairs={{0,1},{1,0},{2,3},{3,2},{4,5},{5,4},{6,7},{7,6},{8,9},{9,8},{10,11... | collective-permute-start | bytes 1916936 | tf_op jit(solution)/shard_map/ppermute | solution.py:314
  11.7 2.9 %collective-permute-start.2 = (bf16[64,2176]{1,0:T(8,128)(2,1)S(1)}, bf16[64,2176]{1,0:T(8,128)(2,1)S(1)}, u32[]{:S(2)}, u32[]{:S(2)}) collective-permute-start(bf16[64,2176]{1,0:T(8,128)(2,1)S(1)} %shard_map.123.refs_0_.refs_6_), channel_id=1, source_target_pairs={{0,8},{2,10},{4,12},{6,14},{8,0},{10,2},{12,4},{14,6},{1,9},{3,11}... | collective-permute-start | bytes 835592 | tf_op jit(solution)/shard_map/ppermute | solution.py:322
  16.1 16.9 %collective-permute-done.2.refs_2_.refs_8_ = bf16[64,2176]{1,0:T(8,128)(2,1)S(1)} collective-permute-done((bf16[64,2176]{1,0:T(8,128)(2,1)S(1)}, bf16[64,2176]{1,0:T(8,128)(2,1)S(1)}, u32[]{:S(2)}, u32[]{:S(2)}) %collective-permute-start.2) | collective-permute-done | bytes 278560 | tf_op jit(solution)/shard_map/ppermute | solution.py:322
  34.5 3.3 %collective-permute-done.7.refs_8_ = bf16[416,768]{1,0:T(8,128)(2,1)} collective-permute-done((bf16[416,768]{1,0:T(8,128)(2,1)}, bf16[416,768]{1,0:T(8,128)(2,1)}, u32[]{:S(2)}, u32[]{:S(2)}) %collective-permute-start.7) | collective-permute-done | bytes 639008 | tf_op jit(solution)/shard_map/ppermute | solution.py:314
  41.1 9.4 %collective-permute-done.5.refs_9_ = bf16[416,768]{1,0:T(8,128)(2,1)S(1)} collective-permute-done((bf16[416,768]{1,0:T(8,128)(2,1)}, bf16[416,768]{1,0:T(8,128)(2,1)S(1)}, u32[]{:S(2)}, u32[]{:S(2)}) %collective-permute-start.5) | collective-permute-done | bytes 639008 | tf_op jit(solution)/shard_map/ppermute | solution.py:318
  50.5 4.5 %collective-permute-done.10.refs_11_ = bf16[2,192,768]{2,1,0:T(8,128)(2,1)S(1)} collective-permute-done((bf16[2,192,768]{2,1,0:T(8,128)(2,1)S(1)}, bf16[2,192,768]{2,1,0:T(8,128)(2,1)S(1)}, u32[]{:S(2)}, u32[]{:S(2)}) %collective-permute-start.10) | collective-permute-done | bytes 589856 | tf_op jit(solution)/shard_map/ppermute | solution.py:314
  55.0 6.1 %collective-permute-done.9.refs_10_ = bf16[416,768]{1,0:T(8,128)(2,1)S(1)} collective-permute-done((bf16[416,768]{1,0:T(8,128)(2,1)}, bf16[416,768]{1,0:T(8,128)(2,1)S(1)}, u32[]{:S(2)}, u32[]{:S(2)}) %collective-permute-start.9) | collective-permute-done | bytes 639008 | tf_op jit(solution)/shard_map/ppermute | solution.py:318
  61.1 7.1 %shard_map.124.hidden_ref = bf16[512,768]{1,0:T(8,128)(2,1)S(1)} custom-call(s32[3]{0:T(128)S(1)} %pad_add_fusion.where_ref, bf16[64,2176]{1,0:T(8,128)(2,1)S(1)} %shard_map.123.refs_0_.refs_6_, bf16[64,2176]{1,0:T(8,128)(2,1)S(1)} %collective-permute-done.1.refs_1_.refs_7_, bf16[64,2176]{1,0:T(8,128)(2,1)S(1)} %collective-permute-done.2.refs_2_.refs_8_, ...), custom_call_target="tpu_custom_call" | custom-call | flops 3221225472 | bytes 8388608 | tf_op jit(solution)/shard_map/pallas_call | solution.py:243
  68.3 1.7 %shard_map.125 = (bf16[256,1024]{1,0:T(8,128)(2,1)S(1)}, bf16[256,1024]{1,0:T(8,128)(2,1)S(1)}) custom-call(s32[3]{0:T(128)S(1)} %pad_add_fusion.where_ref, bf16[512,768]{1,0:T(8,128)(2,1)S(1)} %shard_map.124.hidden_ref, bf16[2,384,1024]{2,1,0:T(8,128)(2,1)S(1)} %copy-done.1), custom_call_target="tpu_custom_call" | custom-call | flops 805306368 | bytes 3407872 | tf_op jit(solution)/shard_map/pallas_call | solution.py:294
  72.1 4.5 %collective-permute-start.14 = (bf16[64,1024]{1,0:T(8,128)(2,1)S(1)}, bf16[64,1024]{1,0:T(8,128)(2,1)S(1)}, u32[]{:S(2)}, u32[]{:S(2)}) collective-permute-start(bf16[64,1024]{1,0:T(8,128)(2,1)S(1)} %get-tuple-element.56), channel_id=1, source_target_pairs={{0,12},{2,14},{4,8},{6,10},{8,4},{10,6},{12,0},{14,2},{1,13},{3,15... | collective-permute-start | bytes 393224 | tf_op jit(solution)/shard_map/ppermute | solution.py:322
  77.2 3.7 %collective-permute-done.14 = bf16[64,1024]{1,0:T(8,128)(2,1)S(1)} collective-permute-done((bf16[64,1024]{1,0:T(8,128)(2,1)S(1)}, bf16[64,1024]{1,0:T(8,128)(2,1)S(1)}, u32[]{:S(2)}, u32[]{:S(2)}) %collective-permute-start.14) | collective-permute-done | bytes 131104 | tf_op jit(solution)/shard_map/ppermute | solution.py:322
  81.0 6.2 %collective-permute-done.13 = bf16[64,1024]{1,0:T(8,128)(2,1)S(1)} collective-permute-done((bf16[64,1024]{1,0:T(8,128)(2,1)S(1)}, bf16[64,1024]{1,0:T(8,128)(2,1)S(1)}, u32[]{:S(2)}, u32[]{:S(2)}) %collective-permute-start.13) | collective-permute-done | bytes 131104 | tf_op jit(solution)/shard_map/ppermute | solution.py:322
  87.2 2.8 %collective-permute-done.15.hidden_ref = bf16[512,768]{1,0:T(8,128)(2,1)S(1)} collective-permute-done((bf16[512,768]{1,0:T(8,128)(2,1)S(1)}, bf16[512,768]{1,0:T(8,128)(2,1)S(1)}, u32[]{:S(2)}, u32[]{:S(2)}) %collective-permute-start.15) | collective-permute-done | bytes 786464 | tf_op jit(solution)/shard_map/ppermute | solution.py:314
  96.6 4.5 %collective-permute-start.19 = (bf16[64,1024]{1,0:T(8,128)(2,1)}, bf16[64,1024]{1,0:T(8,128)(2,1)}, u32[]{:S(2)}, u32[]{:S(2)}) collective-permute-start(bf16[64,1024]{1,0:T(8,128)(2,1)} %get-tuple-element.53), channel_id=1, source_target_pairs={{0,12},{2,14},{4,8},{6,10},{8,4},{10,6},{12,0},{14,2},{1,13},{3,15... | collective-permute-start | bytes 393224 | tf_op jit(solution)/shard_map/ppermute | solution.py:322
  102.3 3.6 %collective-permute-done.26.refs_13_ = bf16[256,768]{1,0:T(8,128)(2,1)} collective-permute-done((bf16[256,768]{1,0:T(8,128)(2,1)}, bf16[256,768]{1,0:T(8,128)(2,1)}, u32[]{:S(2)}, u32[]{:S(2)}) %collective-permute-start.26) | collective-permute-done | bytes 393248 | tf_op jit(solution)/shard_map/ppermute | solution.py:314
  107.3 4.9 %collective-permute-done.18 = bf16[64,1024]{1,0:T(8,128)(2,1)} collective-permute-done((bf16[64,1024]{1,0:T(8,128)(2,1)}, bf16[64,1024]{1,0:T(8,128)(2,1)}, u32[]{:S(2)}, u32[]{:S(2)}) %collective-permute-start.18) | collective-permute-done | bytes 131104 | tf_op jit(solution)/shard_map/ppermute | solution.py:322
  121.6 3.4 %collective-permute-start.22 = (bf16[64,1024]{1,0:T(8,128)(2,1)S(1)}, bf16[64,1024]{1,0:T(8,128)(2,1)S(1)}, u32[]{:S(2)}, u32[]{:S(2)}) collective-permute-start(bf16[64,1024]{1,0:T(8,128)(2,1)S(1)} %pad_maximum_fusion.3.refs_0_), channel_id=1, source_target_pairs={{0,8},{2,10},{4,12},{6,14},{8,0},{10,2},{12,4},{14,6},{1,9},{3,11}... | collective-permute-start | bytes 393224 | tf_op jit(solution)/shard_map/ppermute | solution.py:322
  126.4 7.1 %collective-permute-done.22.refs_2_ = bf16[64,1024]{1,0:T(8,128)(2,1)S(1)} collective-permute-done((bf16[64,1024]{1,0:T(8,128)(2,1)S(1)}, bf16[64,1024]{1,0:T(8,128)(2,1)S(1)}, u32[]{:S(2)}, u32[]{:S(2)}) %collective-permute-start.22) | collective-permute-done | bytes 131104 | tf_op jit(solution)/shard_map/ppermute | solution.py:322
  137.0 5.6 %shard_map.128.hidden_ref = bf16[512,768]{1,0:T(8,128)(2,1)S(1)} custom-call(s32[3]{0:T(128)S(1)} %pad_add_fusion.where_ref, bf16[64,1024]{1,0:T(8,128)(2,1)S(1)} %pad_maximum_fusion.3.refs_0_, bf16[64,1024]{1,0:T(8,128)(2,1)S(1)} %collective-permute-done.21.refs_1_, bf16[64,1024]{1,0:T(8,128)(2,1)S(1)} %collective-permute-done.22.refs_2_, ...), custom_call_target="tpu_custom_call" | custom-call | flops 1610612736 | bytes 4194304 | tf_op jit(solution)/shard_map/pallas_call | solution.py:243
  147.3 3.0 %collective-permute-start.34 = (bf16[64,512]{1,0:T(8,128)(2,1)S(1)}, bf16[64,512]{1,0:T(8,128)(2,1)S(1)}, u32[]{:S(2)}, u32[]{:S(2)}) collective-permute-start(bf16[64,512]{1,0:T(8,128)(2,1)S(1)} %get-tuple-element.63), channel_id=1, source_target_pairs={{0,12},{2,14},{4,8},{6,10},{8,4},{10,6},{12,0},{14,2},{1,13},{3,15... | collective-permute-start | bytes 196616 | tf_op jit(solution)/shard_map/ppermute | solution.py:322
  151.8 4.2 %collective-permute-start.39 = (bf16[64,512]{1,0:T(8,128)(2,1)S(1)}, bf16[64,512]{1,0:T(8,128)(2,1)S(1)}, u32[]{:S(2)}, u32[]{:S(2)}) collective-permute-start(bf16[64,512]{1,0:T(8,128)(2,1)S(1)} %get-tuple-element.59), channel_id=1, source_target_pairs={{0,13},{1,12},{2,15},{3,14},{4,9},{5,8},{6,11},{7,10},{8,5},{9,4},... | collective-permute-start | bytes 196616 | tf_op jit(solution)/shard_map/ppermute | solution.py:343
  159.6 2.8 %collective-permute-done.38 = bf16[64,512]{1,0:T(8,128)(2,1)S(1)} collective-permute-done((bf16[64,512]{1,0:T(8,128)(2,1)S(1)}, bf16[64,512]{1,0:T(8,128)(2,1)S(1)}, u32[]{:S(2)}, u32[]{:S(2)}) %collective-permute-start.38) | collective-permute-done | bytes 65568 | tf_op jit(solution)/shard_map/ppermute | solution.py:343
  (134 shorter events, 47.6 us)
Async XLA Ops:
  8.3 24.7 %collective-permute-start.4 = (bf16[416,768]{1,0:T(8,128)(2,1)}, bf16[416,768]{1,0:T(8,128)(2,1)}, u32[]{:S(2)}, u32[]{:S(2)}) collective-permute-start(bf16[416,768]{1,0:T(8,128)(2,1)} %get-tuple-element.22), channel_id=1, source_target_pairs={{0,1},{1,0},{2,3},{3,2},{4,5},{5,4},{6,7},{7,6},{8,9},{9,8},{10,11... | collective-permute-start | bytes 1916936 | tf_op jit(solution)/shard_map/ppermute | solution.py:314
  10.0 27.8 %collective-permute-start.7 = (bf16[416,768]{1,0:T(8,128)(2,1)}, bf16[416,768]{1,0:T(8,128)(2,1)}, u32[]{:S(2)}, u32[]{:S(2)}) collective-permute-start(bf16[416,768]{1,0:T(8,128)(2,1)} %get-tuple-element.25), channel_id=1, source_target_pairs={{0,1},{1,0},{2,3},{3,2},{4,5},{5,4},{6,7},{7,6},{8,9},{9,8},{10,11... | collective-permute-start | bytes 1916936 | tf_op jit(solution)/shard_map/ppermute | solution.py:314
  11.7 21.3 %collective-permute-start.2 = (bf16[64,2176]{1,0:T(8,128)(2,1)S(1)}, bf16[64,2176]{1,0:T(8,128)(2,1)S(1)}, u32[]{:S(2)}, u32[]{:S(2)}) collective-permute-start(bf16[64,2176]{1,0:T(8,128)(2,1)S(1)} %shard_map.123.refs_0_.refs_6_), channel_id=1, source_target_pairs={{0,8},{2,10},{4,12},{6,14},{8,0},{10,2},{12,4},{14,6},{1,9},{3,11}... | collective-permute-start | bytes 835592 | tf_op jit(solution)/shard_map/ppermute | solution.py:322
  14.6 20.0 %collective-permute-start.3 = (bf16[64,2176]{1,0:T(8,128)(2,1)S(1)}, bf16[64,2176]{1,0:T(8,128)(2,1)S(1)}, u32[]{:S(2)}, u32[]{:S(2)}) collective-permute-start(bf16[64,2176]{1,0:T(8,128)(2,1)S(1)} %shard_map.123.refs_0_.refs_6_), channel_id=1, source_target_pairs={{0,12},{2,14},{4,8},{6,10},{8,4},{10,6},{12,0},{14,2},{1,13},{3,15... | collective-permute-start | bytes 835592 | tf_op jit(solution)/shard_map/ppermute | solution.py:322
  15.9 21.9 %collective-permute-start.1 = (bf16[64,2176]{1,0:T(8,128)(2,1)S(1)}, bf16[64,2176]{1,0:T(8,128)(2,1)S(1)}, u32[]{:S(2)}, u32[]{:S(2)}) collective-permute-start(bf16[64,2176]{1,0:T(8,128)(2,1)S(1)} %shard_map.123.refs_0_.refs_6_), channel_id=1, source_target_pairs={{0,4},{2,6},{4,0},{6,2},{8,12},{10,14},{12,8},{14,10},{1,5},{3,7},... | collective-permute-start | bytes 835592 | tf_op jit(solution)/shard_map/ppermute | solution.py:322
  33.0 17.5 %collective-permute-start.5 = (bf16[416,768]{1,0:T(8,128)(2,1)}, bf16[416,768]{1,0:T(8,128)(2,1)S(1)}, u32[]{:S(2)}, u32[]{:S(2)}) collective-permute-start(bf16[416,768]{1,0:T(8,128)(2,1)} %collective-permute-done.4.refs_7_), channel_id=1, source_target_pairs={{0,16},{16,0},{1,17},{17,1},{2,18},{18,2},{3,19},{19,3},{4,20},{20... | collective-permute-start | bytes 1916936 | tf_op jit(solution)/shard_map/ppermute | solution.py:318
  37.9 23.2 %collective-permute-start.8 = (bf16[192,2176]{1,0:T(8,128)(2,1)S(1)}, bf16[192,2176]{1,0:T(8,128)(2,1)S(1)}, u32[]{:S(2)}, u32[]{:S(2)}) collective-permute-start(bf16[192,2176]{1,0:T(8,128)(2,1)S(1)} %pad_maximum_fusion), channel_id=1, source_target_pairs={{0,2},{2,0},{4,6},{6,4},{8,10},{10,8},{12,14},{14,12},{1,3},{3,1},... | collective-permute-start | bytes 2506760 | tf_op jit(solution)/shard_map/ppermute | solution.py:322
  38.0 23.1 %collective-permute-start.9 = (bf16[416,768]{1,0:T(8,128)(2,1)}, bf16[416,768]{1,0:T(8,128)(2,1)S(1)}, u32[]{:S(2)}, u32[]{:S(2)}) collective-permute-start(bf16[416,768]{1,0:T(8,128)(2,1)} %collective-permute-done.7.refs_8_), channel_id=1, source_target_pairs={{0,16},{16,0},{1,17},{17,1},{2,18},{18,2},{3,19},{19,3},{4,20},{20... | collective-permute-start | bytes 1916936 | tf_op jit(solution)/shard_map/ppermute | solution.py:318
  39.6 15.5 %collective-permute-start.10 = (bf16[2,192,768]{2,1,0:T(8,128)(2,1)S(1)}, bf16[2,192,768]{2,1,0:T(8,128)(2,1)S(1)}, u32[]{:S(2)}, u32[]{:S(2)}) collective-permute-start(bf16[2,192,768]{2,1,0:T(8,128)(2,1)S(1)} %slice.99), channel_id=1, source_target_pairs={{0,1},{1,0},{2,3},{3,2},{4,5},{5,4},{6,7},{7,6},{8,9},{9,8},{10,11... | collective-permute-start | bytes 1769480 | tf_op jit(solution)/shard_map/ppermute | solution.py:314
  50.5 10.6 %collective-permute-start.6 = (bf16[64,2176]{1,0:T(8,128)(2,1)S(1)}, bf16[64,2176]{1,0:T(8,128)(2,1)S(1)}, u32[]{:S(2)}, u32[]{:S(2)}) collective-permute-start(bf16[64,2176]{1,0:T(8,128)(2,1)S(1)} %shard_map.123.refs_0_.refs_6_), channel_id=1, source_target_pairs={{0,2},{2,0},{4,6},{6,4},{8,10},{10,8},{12,14},{14,12},{1,3},{3,1},... | collective-permute-start | bytes 835592 | tf_op jit(solution)/shard_map/ppermute | solution.py:322
  70.0 20.0 %collective-permute-start.15 = (bf16[512,768]{1,0:T(8,128)(2,1)S(1)}, bf16[512,768]{1,0:T(8,128)(2,1)S(1)}, u32[]{:S(2)}, u32[]{:S(2)}) collective-permute-start(bf16[512,768]{1,0:T(8,128)(2,1)S(1)} %shard_map.124.hidden_ref), channel_id=1, source_target_pairs={{0,1},{1,0},{2,3},{3,2},{4,5},{5,4},{6,7},{7,6},{8,9},{9,8},{10,11... | collective-permute-start | bytes 2359304 | tf_op jit(solution)/shard_map/ppermute | solution.py:314
  72.1 8.9 %collective-permute-start.14 = (bf16[64,1024]{1,0:T(8,128)(2,1)S(1)}, bf16[64,1024]{1,0:T(8,128)(2,1)S(1)}, u32[]{:S(2)}, u32[]{:S(2)}) collective-permute-start(bf16[64,1024]{1,0:T(8,128)(2,1)S(1)} %get-tuple-element.56), channel_id=1, source_target_pairs={{0,12},{2,14},{4,8},{6,10},{8,4},{10,6},{12,0},{14,2},{1,13},{3,15... | collective-permute-start | bytes 393224 | tf_op jit(solution)/shard_map/ppermute | solution.py:322
  76.6 10.6 %collective-permute-start.13 = (bf16[64,1024]{1,0:T(8,128)(2,1)S(1)}, bf16[64,1024]{1,0:T(8,128)(2,1)S(1)}, u32[]{:S(2)}, u32[]{:S(2)}) collective-permute-start(bf16[64,1024]{1,0:T(8,128)(2,1)S(1)} %get-tuple-element.57), channel_id=1, source_target_pairs={{0,8},{2,10},{4,12},{6,14},{8,0},{10,2},{12,4},{14,6},{1,9},{3,11}... | collective-permute-start | bytes 393224 | tf_op jit(solution)/shard_map/ppermute | solution.py:322
  76.6 10.6 %collective-permute-start.12 = (bf16[64,1024]{1,0:T(8,128)(2,1)S(1)}, bf16[64,1024]{1,0:T(8,128)(2,1)S(1)}, u32[]{:S(2)}, u32[]{:S(2)}) collective-permute-start(bf16[64,1024]{1,0:T(8,128)(2,1)S(1)} %get-tuple-element.55), channel_id=1, source_target_pairs={{0,4},{2,6},{4,0},{6,2},{8,12},{10,14},{12,8},{14,10},{1,5},{3,7},... | collective-permute-start | bytes 393224 | tf_op jit(solution)/shard_map/ppermute | solution.py:322
  93.6 12.3 %collective-permute-start.26 = (bf16[256,768]{1,0:T(8,128)(2,1)}, bf16[256,768]{1,0:T(8,128)(2,1)}, u32[]{:S(2)}, u32[]{:S(2)}) collective-permute-start(bf16[256,768]{1,0:T(8,128)(2,1)} %get-tuple-element.33), channel_id=1, source_target_pairs={{0,1},{1,0},{2,3},{3,2},{4,5},{5,4},{6,7},{7,6},{8,9},{9,8},{10,11... | collective-permute-start | bytes 1179656 | tf_op jit(solution)/shard_map/ppermute | solution.py:314
  96.6 10.6 %collective-permute-start.19 = (bf16[64,1024]{1,0:T(8,128)(2,1)}, bf16[64,1024]{1,0:T(8,128)(2,1)}, u32[]{:S(2)}, u32[]{:S(2)}) collective-permute-start(bf16[64,1024]{1,0:T(8,128)(2,1)} %get-tuple-element.53), channel_id=1, source_target_pairs={{0,12},{2,14},{4,8},{6,10},{8,4},{10,6},{12,0},{14,2},{1,13},{3,15... | collective-permute-start | bytes 393224 | tf_op jit(solution)/shard_map/ppermute | solution.py:322
  101.2 11.0 %collective-permute-start.18 = (bf16[64,1024]{1,0:T(8,128)(2,1)}, bf16[64,1024]{1,0:T(8,128)(2,1)}, u32[]{:S(2)}, u32[]{:S(2)}) collective-permute-start(bf16[64,1024]{1,0:T(8,128)(2,1)} %get-tuple-element.54), channel_id=1, source_target_pairs={{0,8},{2,10},{4,12},{6,14},{8,0},{10,2},{12,4},{14,6},{1,9},{3,11}... | collective-permute-start | bytes 393224 | tf_op jit(solution)/shard_map/ppermute | solution.py:322
  101.2 11.0 %collective-permute-start.17 = (bf16[64,1024]{1,0:T(8,128)(2,1)}, bf16[64,1024]{1,0:T(8,128)(2,1)}, u32[]{:S(2)}, u32[]{:S(2)}) collective-permute-start(bf16[64,1024]{1,0:T(8,128)(2,1)} %get-tuple-element.52), channel_id=1, source_target_pairs={{0,4},{2,6},{4,0},{6,2},{8,12},{10,14},{12,8},{14,10},{1,5},{3,7},... | collective-permute-start | bytes 393224 | tf_op jit(solution)/shard_map/ppermute | solution.py:322
  101.7 13.1 %collective-permute-start.25 = (bf16[256,768]{1,0:T(8,128)(2,1)}, bf16[256,768]{1,0:T(8,128)(2,1)S(1)}, u32[]{:S(2)}, u32[]{:S(2)}) collective-permute-start(bf16[256,768]{1,0:T(8,128)(2,1)} %get-tuple-element.32), channel_id=1, source_target_pairs={{0,1},{1,0},{2,3},{3,2},{4,5},{5,4},{6,7},{7,6},{8,9},{9,8},{10,11... | collective-permute-start | bytes 1179656 | tf_op jit(solution)/shard_map/ppermute | solution.py:314
  105.9 10.5 %collective-permute-start.27 = (bf16[256,768]{1,0:T(8,128)(2,1)}, bf16[256,768]{1,0:T(8,128)(2,1)S(1)}, u32[]{:S(2)}, u32[]{:S(2)}) collective-permute-start(bf16[256,768]{1,0:T(8,128)(2,1)} %collective-permute-done.26.refs_13_), channel_id=1, source_target_pairs={{0,16},{16,0},{1,17},{17,1},{2,18},{18,2},{3,19},{19,3},{4,20},{20... | collective-permute-start | bytes 1179656 | tf_op jit(solution)/shard_map/ppermute | solution.py:318
  116.4 17.1 %collective-permute-start.28 = (bf16[256,768]{1,0:T(8,128)(2,1)S(1)}, bf16[256,768]{1,0:T(8,128)(2,1)S(1)}, u32[]{:S(2)}, u32[]{:S(2)}) collective-permute-start(bf16[256,768]{1,0:T(8,128)(2,1)S(1)} %collective-permute-done.25.refs_14_), channel_id=1, source_target_pairs={{0,16},{16,0},{1,17},{17,1},{2,18},{18,2},{3,19},{19,3},{4,20},{20... | collective-permute-start | bytes 1179656 | tf_op jit(solution)/shard_map/ppermute | solution.py:318
  119.3 17.7 %collective-permute-start.30 = (bf16[2,384,512]{2,1,0:T(8,128)(2,1)S(1)}, bf16[2,384,512]{2,1,0:T(8,128)(2,1)S(1)}, u32[]{:S(2)}, u32[]{:S(2)}) collective-permute-start(bf16[2,384,512]{2,1,0:T(8,128)(2,1)S(1)} %copy-done.9), channel_id=1, source_target_pairs={{0,1},{1,0},{2,3},{3,2},{4,5},{5,4},{6,7},{7,6},{8,9},{9,8},{10,11... | collective-permute-start | bytes 2359304 | tf_op jit(solution)/shard_map/ppermute | solution.py:314
  121.6 11.9 %collective-permute-start.22 = (bf16[64,1024]{1,0:T(8,128)(2,1)S(1)}, bf16[64,1024]{1,0:T(8,128)(2,1)S(1)}, u32[]{:S(2)}, u32[]{:S(2)}) collective-permute-start(bf16[64,1024]{1,0:T(8,128)(2,1)S(1)} %pad_maximum_fusion.3.refs_0_), channel_id=1, source_target_pairs={{0,8},{2,10},{4,12},{6,14},{8,0},{10,2},{12,4},{14,6},{1,9},{3,11}... | collective-permute-start | bytes 393224 | tf_op jit(solution)/shard_map/ppermute | solution.py:322
  150.3 9.0 %collective-permute-start.32 = (bf16[64,512]{1,0:T(8,128)(2,1)S(1)}, bf16[64,512]{1,0:T(8,128)(2,1)S(1)}, u32[]{:S(2)}, u32[]{:S(2)}) collective-permute-start(bf16[64,512]{1,0:T(8,128)(2,1)S(1)} %get-tuple-element.62), channel_id=1, source_target_pairs={{0,4},{2,6},{4,0},{6,2},{8,12},{10,14},{12,8},{14,10},{1,5},{3,7},... | collective-permute-start | bytes 196616 | tf_op jit(solution)/shard_map/ppermute | solution.py:322
  (40 other events, 564.2 us)

commit v10 on v9

--- a/solution.py
+++ b/solution.py
@@ -400,7 +400,7 @@
     near_in = [send(w_in, group, index * chunk, chunk, other) for index in range(2)]
     row = build_row(where, hidden_in, other, lanes)
     same = [row] + [over_expert(row, distance) for distance in distances]
-    far_in = [over_groups(after(near_in[0], same[2]))]
+    far_in = [over_groups(after(near_in[0], same[1]))]
     far_in.append(over_groups(near_in[1]))
     direct_in = over_replica(after(w_in[:, 2 * chunk :], near_in[0]))
     across = [over_expert(after(row, far_in[0]), 1), over_expert(jnp.concatenate([*same[1:3], after(same[3], near_in[1])]), 1)]

time: 164 us -> 158 us (0.963)
  waiting for transfers between devices: 82.2 us -> 76.3 us
    ppermute x9, waiting for transfers between devices: 18.3 us -> 39.5 us  [over_replica(): return lax.ppermute(array, 'replica', SWAP)]
    ppermute x4, waiting for transfers between devices: 17 us -> 2.61 us  [over_groups(): return lax.ppermute(array, 'groups', SWAP)]
    ppermute x23, waiting for transfers between devices: 43 us -> 30.6 us  [over_expert(): lax.ppermute(array, 'expert', [(at, at ^ distance) for at in range(lax.ax...]
where the time goes in v10:
time: 158 us
  waiting for transfers between devices  76.3 us (48%)
  starting transfers between devices  48.7 us (31%)
  Pallas kernels  21.1 us (13%)
  local copies, waits for them, and re-layouts  5.37 us (3%)
  other arithmetic  4.29 us (3%)
    ppermute x9, waiting for transfers between devices, over_replica(): return lax.ppermute(array, 'replica', SWAP)  39.5 us
    ppermute x23, waiting for transfers between devices, over_expert(): lax.ppermute(array, 'expert', [(at, at ^ distance) for at in range(lax.ax...  30.6 us
    ppermute x23, starting transfers between devices, over_expert(): lax.ppermute(array, 'expert', [(at, at ^ distance) for at in range(lax.ax...  23.6 us
    pallas_call x2, Pallas kernels, run_hidden(): pl.pallas_call(functools.partial(hidden_kernel, blocks, len(gain_blocks),...  12.7 us
    ppermute x9, starting transfers between devices, over_replica(): return lax.ppermute(array, 'replica', SWAP)  12.1 us
    pallas_call x5, Pallas kernels, run_down(): pl.pallas_call(functools.partial(down_kernel, halves, len(near)), out_sha...  7.23 us
    ppermute x4, starting transfers between devices, over_both(): return lax.ppermute(array, ('expert', 'replica'), pairs)  6.82 us
    ppermute x4, starting transfers between devices, over_groups(): return lax.ppermute(array, 'groups', SWAP)  6.19 us
  transfers between devices with their start and end apart: 40, of which 23 were waited for; matrix products, arithmetic and copies ran while one was open for 5% of the time, Pallas kernels for 2%

profile of v10, /device:TPU:0, one launch (start us, length us, event | category | flops | bytes accessed | tf_op | source)
XLA Modules:
  0.0 157.9 jit_solution(5321111563423589159)
XLA Ops:
  1.8 3.0 %collective-permute-start = (bf16[64,1024]{1,0:T(8,128)(2,1)S(1)}, bf16[64,1024]{1,0:T(8,128)(2,1)S(1)}, u32[]{:S(2)}, u32[]{:S(2)}) collective-permute-start(bf16[64,1024]{1,0:T(8,128)(2,1)S(1)} %constant_dynamic-slice_fusion), channel_id=1, source_target_pairs={{0,1},{1,0},{2,3},{3,2},{4,5},{5,4},{6,7},{7,6},{8,9},{9,8},{10,11... | collective-permute-start | bytes 393224 | tf_op jit(solution)/shard_map/ppermute | solution.py:314
  4.8 2.4 %dynamic-slice_bitcast_fusion = (bf16[416,768]{1,0:T(8,128)(2,1)}, bf16[416,768]{1,0:T(8,128)(2,1)}) fusion(bf16[2,1024,768]{2,1,0:T(8,128)(2,1)} %refs_6_.1, s32[]{:T(128)S(6)} %select_n.43), kind=kLoop, calls=%fused_computation.4 | loop fusion | bytes 2555908 | tf_op jit(solution)/shard_map/squeeze | solution.py:332
  13.5 2.5 %collective-permute-start.3 = (bf16[64,2176]{1,0:T(8,128)(2,1)S(1)}, bf16[64,2176]{1,0:T(8,128)(2,1)S(1)}, u32[]{:S(2)}, u32[]{:S(2)}) collective-permute-start(bf16[64,2176]{1,0:T(8,128)(2,1)S(1)} %shard_map.123.refs_0_.refs_6_), channel_id=1, source_target_pairs={{0,12},{2,14},{4,8},{6,10},{8,4},{10,6},{12,0},{14,2},{1,13},{3,15... | collective-permute-start | bytes 835592 | tf_op jit(solution)/shard_map/ppermute | solution.py:322
  16.1 4.6 %collective-permute-done.1.refs_1_.refs_7_ = bf16[64,2176]{1,0:T(8,128)(2,1)S(1)} collective-permute-done((bf16[64,2176]{1,0:T(8,128)(2,1)S(1)}, bf16[64,2176]{1,0:T(8,128)(2,1)S(1)}, u32[]{:S(2)}, u32[]{:S(2)}) %collective-permute-start.1) | collective-permute-done | bytes 278560 | tf_op jit(solution)/shard_map/ppermute | solution.py:322
  20.8 5.1 %collective-permute-done.4.refs_7_ = bf16[416,768]{1,0:T(8,128)(2,1)} collective-permute-done((bf16[416,768]{1,0:T(8,128)(2,1)}, bf16[416,768]{1,0:T(8,128)(2,1)}, u32[]{:S(2)}, u32[]{:S(2)}) %collective-permute-start.4) | collective-permute-done | bytes 639008 | tf_op jit(solution)/shard_map/ppermute | solution.py:314
  29.7 8.2 %collective-permute-done.7.refs_8_ = bf16[416,768]{1,0:T(8,128)(2,1)} collective-permute-done((bf16[416,768]{1,0:T(8,128)(2,1)}, bf16[416,768]{1,0:T(8,128)(2,1)}, u32[]{:S(2)}, u32[]{:S(2)}) %collective-permute-start.7) | collective-permute-done | bytes 639008 | tf_op jit(solution)/shard_map/ppermute | solution.py:314
  42.3 13.9 %collective-permute-done.10.refs_11_ = bf16[2,192,768]{2,1,0:T(8,128)(2,1)S(1)} collective-permute-done((bf16[2,192,768]{2,1,0:T(8,128)(2,1)S(1)}, bf16[2,192,768]{2,1,0:T(8,128)(2,1)S(1)}, u32[]{:S(2)}, u32[]{:S(2)}) %collective-permute-start.10) | collective-permute-done | bytes 589856 | tf_op jit(solution)/shard_map/ppermute | solution.py:314
  56.3 7.1 %shard_map.124.hidden_ref = bf16[512,768]{1,0:T(8,128)(2,1)S(1)} custom-call(s32[3]{0:T(128)S(1)} %pad_add_fusion.where_ref, bf16[64,2176]{1,0:T(8,128)(2,1)S(1)} %shard_map.123.refs_0_.refs_6_, bf16[64,2176]{1,0:T(8,128)(2,1)S(1)} %collective-permute-done.1.refs_1_.refs_7_, bf16[64,2176]{1,0:T(8,128)(2,1)S(1)} %collective-permute-done.2.refs_2_.refs_8_, ...), custom_call_target="tpu_custom_call" | custom-call | flops 3221225472 | bytes 8388608 | tf_op jit(solution)/shard_map/pallas_call | solution.py:243
  67.2 2.7 %collective-permute-start.14 = (bf16[64,1024]{1,0:T(8,128)(2,1)S(1)}, bf16[64,1024]{1,0:T(8,128)(2,1)S(1)}, u32[]{:S(2)}, u32[]{:S(2)}) collective-permute-start(bf16[64,1024]{1,0:T(8,128)(2,1)S(1)} %get-tuple-element.56), channel_id=1, source_target_pairs={{0,12},{2,14},{4,8},{6,10},{8,4},{10,6},{12,0},{14,2},{1,13},{3,15... | collective-permute-start | bytes 393224 | tf_op jit(solution)/shard_map/ppermute | solution.py:322
  71.7 3.9 %collective-permute-done.14 = bf16[64,1024]{1,0:T(8,128)(2,1)S(1)} collective-permute-done((bf16[64,1024]{1,0:T(8,128)(2,1)S(1)}, bf16[64,1024]{1,0:T(8,128)(2,1)S(1)}, u32[]{:S(2)}, u32[]{:S(2)}) %collective-permute-start.14) | collective-permute-done | bytes 131104 | tf_op jit(solution)/shard_map/ppermute | solution.py:322
  75.6 5.5 %collective-permute-done.13 = bf16[64,1024]{1,0:T(8,128)(2,1)S(1)} collective-permute-done((bf16[64,1024]{1,0:T(8,128)(2,1)S(1)}, bf16[64,1024]{1,0:T(8,128)(2,1)S(1)}, u32[]{:S(2)}, u32[]{:S(2)}) %collective-permute-start.13) | collective-permute-done | bytes 131104 | tf_op jit(solution)/shard_map/ppermute | solution.py:322
  81.1 4.1 %collective-permute-done.15.hidden_ref = bf16[512,768]{1,0:T(8,128)(2,1)S(1)} collective-permute-done((bf16[512,768]{1,0:T(8,128)(2,1)S(1)}, bf16[512,768]{1,0:T(8,128)(2,1)S(1)}, u32[]{:S(2)}, u32[]{:S(2)}) %collective-permute-start.15) | collective-permute-done | bytes 786464 | tf_op jit(solution)/shard_map/ppermute | solution.py:314
  91.9 2.6 %collective-permute-start.19 = (bf16[64,1024]{1,0:T(8,128)(2,1)}, bf16[64,1024]{1,0:T(8,128)(2,1)}, u32[]{:S(2)}, u32[]{:S(2)}) collective-permute-start(bf16[64,1024]{1,0:T(8,128)(2,1)} %get-tuple-element.53), channel_id=1, source_target_pairs={{0,12},{2,14},{4,8},{6,10},{8,4},{10,6},{12,0},{14,2},{1,13},{3,15... | collective-permute-start | bytes 393224 | tf_op jit(solution)/shard_map/ppermute | solution.py:322
  96.8 4.2 %collective-permute-done.26.refs_13_ = bf16[256,768]{1,0:T(8,128)(2,1)} collective-permute-done((bf16[256,768]{1,0:T(8,128)(2,1)}, bf16[256,768]{1,0:T(8,128)(2,1)}, u32[]{:S(2)}, u32[]{:S(2)}) %collective-permute-start.26) | collective-permute-done | bytes 393248 | tf_op jit(solution)/shard_map/ppermute | solution.py:314
  102.5 3.6 %collective-permute-done.18 = bf16[64,1024]{1,0:T(8,128)(2,1)} collective-permute-done((bf16[64,1024]{1,0:T(8,128)(2,1)}, bf16[64,1024]{1,0:T(8,128)(2,1)}, u32[]{:S(2)}, u32[]{:S(2)}) %collective-permute-start.18) | collective-permute-done | bytes 131104 | tf_op jit(solution)/shard_map/ppermute | solution.py:322
  108.9 2.6 %collective-permute-done.27.refs_15_ = bf16[256,768]{1,0:T(8,128)(2,1)S(1)} collective-permute-done((bf16[256,768]{1,0:T(8,128)(2,1)}, bf16[256,768]{1,0:T(8,128)(2,1)S(1)}, u32[]{:S(2)}, u32[]{:S(2)}) %collective-permute-start.27) | collective-permute-done | bytes 393248 | tf_op jit(solution)/shard_map/ppermute | solution.py:318
  115.4 2.8 %collective-permute-start.22 = (bf16[64,1024]{1,0:T(8,128)(2,1)S(1)}, bf16[64,1024]{1,0:T(8,128)(2,1)S(1)}, u32[]{:S(2)}, u32[]{:S(2)}) collective-permute-start(bf16[64,1024]{1,0:T(8,128)(2,1)S(1)} %pad_maximum_fusion.3.refs_0_), channel_id=1, source_target_pairs={{0,8},{2,10},{4,12},{6,14},{8,0},{10,2},{12,4},{14,6},{1,9},{3,11}... | collective-permute-start | bytes 393224 | tf_op jit(solution)/shard_map/ppermute | solution.py:322
  120.4 6.1 %collective-permute-done.22.refs_2_ = bf16[64,1024]{1,0:T(8,128)(2,1)S(1)} collective-permute-done((bf16[64,1024]{1,0:T(8,128)(2,1)S(1)}, bf16[64,1024]{1,0:T(8,128)(2,1)S(1)}, u32[]{:S(2)}, u32[]{:S(2)}) %collective-permute-start.22) | collective-permute-done | bytes 131104 | tf_op jit(solution)/shard_map/ppermute | solution.py:322
  128.5 2.6 %collective-permute-done.30.refs_17_.refs_0_ = bf16[2,384,512]{2,1,0:T(8,128)(2,1)S(1)} collective-permute-done((bf16[2,384,512]{2,1,0:T(8,128)(2,1)S(1)}, bf16[2,384,512]{2,1,0:T(8,128)(2,1)S(1)}, u32[]{:S(2)}, u32[]{:S(2)}) %collective-permute-start.30) | collective-permute-done | bytes 786464 | tf_op jit(solution)/shard_map/ppermute | solution.py:314
  131.1 5.6 %shard_map.128.hidden_ref = bf16[512,768]{1,0:T(8,128)(2,1)S(1)} custom-call(s32[3]{0:T(128)S(1)} %pad_add_fusion.where_ref, bf16[64,1024]{1,0:T(8,128)(2,1)S(1)} %pad_maximum_fusion.3.refs_0_, bf16[64,1024]{1,0:T(8,128)(2,1)S(1)} %collective-permute-done.21.refs_1_, bf16[64,1024]{1,0:T(8,128)(2,1)S(1)} %collective-permute-done.22.refs_2_, ...), custom_call_target="tpu_custom_call" | custom-call | flops 1610612736 | bytes 4194304 | tf_op jit(solution)/shard_map/pallas_call | solution.py:243
  141.5 2.7 %collective-permute-start.34 = (bf16[64,512]{1,0:T(8,128)(2,1)S(1)}, bf16[64,512]{1,0:T(8,128)(2,1)S(1)}, u32[]{:S(2)}, u32[]{:S(2)}) collective-permute-start(bf16[64,512]{1,0:T(8,128)(2,1)S(1)} %get-tuple-element.63), channel_id=1, source_target_pairs={{0,12},{2,14},{4,8},{6,10},{8,4},{10,6},{12,0},{14,2},{1,13},{3,15... | collective-permute-start | bytes 196616 | tf_op jit(solution)/shard_map/ppermute | solution.py:322
  146.0 3.0 %collective-permute-start.39 = (bf16[64,512]{1,0:T(8,128)(2,1)S(1)}, bf16[64,512]{1,0:T(8,128)(2,1)S(1)}, u32[]{:S(2)}, u32[]{:S(2)}) collective-permute-start(bf16[64,512]{1,0:T(8,128)(2,1)S(1)} %get-tuple-element.59), channel_id=1, source_target_pairs={{0,13},{1,12},{2,15},{3,14},{4,9},{5,8},{6,11},{7,10},{8,5},{9,4},... | collective-permute-start | bytes 196616 | tf_op jit(solution)/shard_map/ppermute | solution.py:343
  149.0 2.7 %collective-permute-start.37 = (bf16[64,512]{1,0:T(8,128)(2,1)S(1)}, bf16[64,512]{1,0:T(8,128)(2,1)S(1)}, u32[]{:S(2)}, u32[]{:S(2)}) collective-permute-start(bf16[64,512]{1,0:T(8,128)(2,1)S(1)} %get-tuple-element.61), channel_id=1, source_target_pairs={{0,5},{1,4},{2,7},{3,6},{4,1},{5,0},{6,3},{7,2},{8,13},{9,12},{10,... | collective-permute-start | bytes 196616 | tf_op jit(solution)/shard_map/ppermute | solution.py:343
  153.5 2.9 %collective-permute-done.38 = bf16[64,512]{1,0:T(8,128)(2,1)S(1)} collective-permute-done((bf16[64,512]{1,0:T(8,128)(2,1)S(1)}, bf16[64,512]{1,0:T(8,128)(2,1)S(1)}, u32[]{:S(2)}, u32[]{:S(2)}) %collective-permute-start.38) | collective-permute-done | bytes 65568 | tf_op jit(solution)/shard_map/ppermute | solution.py:343
  (134 shorter events, 52.2 us)
Async XLA Ops:
  8.3 17.6 %collective-permute-start.4 = (bf16[416,768]{1,0:T(8,128)(2,1)}, bf16[416,768]{1,0:T(8,128)(2,1)}, u32[]{:S(2)}, u32[]{:S(2)}) collective-permute-start(bf16[416,768]{1,0:T(8,128)(2,1)} %get-tuple-element.22), channel_id=1, source_target_pairs={{0,1},{1,0},{2,3},{3,2},{4,5},{5,4},{6,7},{7,6},{8,9},{9,8},{10,11... | collective-permute-start | bytes 1916936 | tf_op jit(solution)/shard_map/ppermute | solution.py:314
  10.0 27.8 %collective-permute-start.7 = (bf16[416,768]{1,0:T(8,128)(2,1)}, bf16[416,768]{1,0:T(8,128)(2,1)}, u32[]{:S(2)}, u32[]{:S(2)}) collective-permute-start(bf16[416,768]{1,0:T(8,128)(2,1)} %get-tuple-element.25), channel_id=1, source_target_pairs={{0,1},{1,0},{2,3},{3,2},{4,5},{5,4},{6,7},{7,6},{8,9},{9,8},{10,11... | collective-permute-start | bytes 1916936 | tf_op jit(solution)/shard_map/ppermute | solution.py:314
  11.7 9.1 %collective-permute-start.1 = (bf16[64,2176]{1,0:T(8,128)(2,1)S(1)}, bf16[64,2176]{1,0:T(8,128)(2,1)S(1)}, u32[]{:S(2)}, u32[]{:S(2)}) collective-permute-start(bf16[64,2176]{1,0:T(8,128)(2,1)S(1)} %shard_map.123.refs_0_.refs_6_), channel_id=1, source_target_pairs={{0,4},{2,6},{4,0},{6,2},{8,12},{10,14},{12,8},{14,10},{1,5},{3,7},... | collective-permute-start | bytes 835592 | tf_op jit(solution)/shard_map/ppermute | solution.py:322
  13.5 16.1 %collective-permute-start.3 = (bf16[64,2176]{1,0:T(8,128)(2,1)S(1)}, bf16[64,2176]{1,0:T(8,128)(2,1)S(1)}, u32[]{:S(2)}, u32[]{:S(2)}) collective-permute-start(bf16[64,2176]{1,0:T(8,128)(2,1)S(1)} %shard_map.123.refs_0_.refs_6_), channel_id=1, source_target_pairs={{0,12},{2,14},{4,8},{6,10},{8,4},{10,6},{12,0},{14,2},{1,13},{3,15... | collective-permute-start | bytes 835592 | tf_op jit(solution)/shard_map/ppermute | solution.py:322
  16.0 23.0 %collective-permute-start.2 = (bf16[64,2176]{1,0:T(8,128)(2,1)S(1)}, bf16[64,2176]{1,0:T(8,128)(2,1)S(1)}, u32[]{:S(2)}, u32[]{:S(2)}) collective-permute-start(bf16[64,2176]{1,0:T(8,128)(2,1)S(1)} %shard_map.123.refs_0_.refs_6_), channel_id=1, source_target_pairs={{0,8},{2,10},{4,12},{6,14},{8,0},{10,2},{12,4},{14,6},{1,9},{3,11}... | collective-permute-start | bytes 835592 | tf_op jit(solution)/shard_map/ppermute | solution.py:322
  25.9 16.4 %collective-permute-start.5 = (bf16[416,768]{1,0:T(8,128)(2,1)}, bf16[416,768]{1,0:T(8,128)(2,1)S(1)}, u32[]{:S(2)}, u32[]{:S(2)}) collective-permute-start(bf16[416,768]{1,0:T(8,128)(2,1)} %collective-permute-done.4.refs_7_), channel_id=1, source_target_pairs={{0,16},{16,0},{1,17},{17,1},{2,18},{18,2},{3,19},{19,3},{4,20},{20... | collective-permute-start | bytes 1916936 | tf_op jit(solution)/shard_map/ppermute | solution.py:318
  39.0 17.2 %collective-permute-start.8 = (bf16[192,2176]{1,0:T(8,128)(2,1)S(1)}, bf16[192,2176]{1,0:T(8,128)(2,1)S(1)}, u32[]{:S(2)}, u32[]{:S(2)}) collective-permute-start(bf16[192,2176]{1,0:T(8,128)(2,1)S(1)} %pad_maximum_fusion), channel_id=1, source_target_pairs={{0,2},{2,0},{4,6},{6,4},{8,10},{10,8},{12,14},{14,12},{1,3},{3,1},... | collective-permute-start | bytes 2506760 | tf_op jit(solution)/shard_map/ppermute | solution.py:322
  39.1 17.1 %collective-permute-start.9 = (bf16[416,768]{1,0:T(8,128)(2,1)}, bf16[416,768]{1,0:T(8,128)(2,1)S(1)}, u32[]{:S(2)}, u32[]{:S(2)}) collective-permute-start(bf16[416,768]{1,0:T(8,128)(2,1)} %collective-permute-done.7.refs_8_), channel_id=1, source_target_pairs={{0,16},{16,0},{1,17},{17,1},{2,18},{18,2},{3,19},{19,3},{4,20},{20... | collective-permute-start | bytes 1916936 | tf_op jit(solution)/shard_map/ppermute | solution.py:318
  40.8 15.5 %collective-permute-start.10 = (bf16[2,192,768]{2,1,0:T(8,128)(2,1)S(1)}, bf16[2,192,768]{2,1,0:T(8,128)(2,1)S(1)}, u32[]{:S(2)}, u32[]{:S(2)}) collective-permute-start(bf16[2,192,768]{2,1,0:T(8,128)(2,1)S(1)} %slice.99), channel_id=1, source_target_pairs={{0,1},{1,0},{2,3},{3,2},{4,5},{5,4},{6,7},{7,6},{8,9},{9,8},{10,11... | collective-permute-start | bytes 1769480 | tf_op jit(solution)/shard_map/ppermute | solution.py:314
  42.3 13.9 %collective-permute-start.6 = (bf16[64,2176]{1,0:T(8,128)(2,1)S(1)}, bf16[64,2176]{1,0:T(8,128)(2,1)S(1)}, u32[]{:S(2)}, u32[]{:S(2)}) collective-permute-start(bf16[64,2176]{1,0:T(8,128)(2,1)S(1)} %shard_map.123.refs_0_.refs_6_), channel_id=1, source_target_pairs={{0,2},{2,0},{4,6},{6,4},{8,10},{10,8},{12,14},{14,12},{1,3},{3,1},... | collective-permute-start | bytes 835592 | tf_op jit(solution)/shard_map/ppermute | solution.py:322
  65.2 20.0 %collective-permute-start.15 = (bf16[512,768]{1,0:T(8,128)(2,1)S(1)}, bf16[512,768]{1,0:T(8,128)(2,1)S(1)}, u32[]{:S(2)}, u32[]{:S(2)}) collective-permute-start(bf16[512,768]{1,0:T(8,128)(2,1)S(1)} %shard_map.124.hidden_ref), channel_id=1, source_target_pairs={{0,1},{1,0},{2,3},{3,2},{4,5},{5,4},{6,7},{7,6},{8,9},{9,8},{10,11... | collective-permute-start | bytes 2359304 | tf_op jit(solution)/shard_map/ppermute | solution.py:314
  67.2 8.3 %collective-permute-start.14 = (bf16[64,1024]{1,0:T(8,128)(2,1)S(1)}, bf16[64,1024]{1,0:T(8,128)(2,1)S(1)}, u32[]{:S(2)}, u32[]{:S(2)}) collective-permute-start(bf16[64,1024]{1,0:T(8,128)(2,1)S(1)} %get-tuple-element.56), channel_id=1, source_target_pairs={{0,12},{2,14},{4,8},{6,10},{8,4},{10,6},{12,0},{14,2},{1,13},{3,15... | collective-permute-start | bytes 393224 | tf_op jit(solution)/shard_map/ppermute | solution.py:322
  70.0 11.1 %collective-permute-start.13 = (bf16[64,1024]{1,0:T(8,128)(2,1)S(1)}, bf16[64,1024]{1,0:T(8,128)(2,1)S(1)}, u32[]{:S(2)}, u32[]{:S(2)}) collective-permute-start(bf16[64,1024]{1,0:T(8,128)(2,1)S(1)} %get-tuple-element.57), channel_id=1, source_target_pairs={{0,8},{2,10},{4,12},{6,14},{8,0},{10,2},{12,4},{14,6},{1,9},{3,11}... | collective-permute-start | bytes 393224 | tf_op jit(solution)/shard_map/ppermute | solution.py:322
  70.0 11.1 %collective-permute-start.12 = (bf16[64,1024]{1,0:T(8,128)(2,1)S(1)}, bf16[64,1024]{1,0:T(8,128)(2,1)S(1)}, u32[]{:S(2)}, u32[]{:S(2)}) collective-permute-start(bf16[64,1024]{1,0:T(8,128)(2,1)S(1)} %get-tuple-element.55), channel_id=1, source_target_pairs={{0,4},{2,6},{4,0},{6,2},{8,12},{10,14},{12,8},{14,10},{1,5},{3,7},... | collective-permute-start | bytes 393224 | tf_op jit(solution)/shard_map/ppermute | solution.py:322
  88.7 12.3 %collective-permute-start.26 = (bf16[256,768]{1,0:T(8,128)(2,1)}, bf16[256,768]{1,0:T(8,128)(2,1)}, u32[]{:S(2)}, u32[]{:S(2)}) collective-permute-start(bf16[256,768]{1,0:T(8,128)(2,1)} %get-tuple-element.33), channel_id=1, source_target_pairs={{0,1},{1,0},{2,3},{3,2},{4,5},{5,4},{6,7},{7,6},{8,9},{9,8},{10,11... | collective-permute-start | bytes 1179656 | tf_op jit(solution)/shard_map/ppermute | solution.py:314
  91.9 10.6 %collective-permute-start.19 = (bf16[64,1024]{1,0:T(8,128)(2,1)}, bf16[64,1024]{1,0:T(8,128)(2,1)}, u32[]{:S(2)}, u32[]{:S(2)}) collective-permute-start(bf16[64,1024]{1,0:T(8,128)(2,1)} %get-tuple-element.53), channel_id=1, source_target_pairs={{0,12},{2,14},{4,8},{6,10},{8,4},{10,6},{12,0},{14,2},{1,13},{3,15... | collective-permute-start | bytes 393224 | tf_op jit(solution)/shard_map/ppermute | solution.py:322
  94.5 11.5 %collective-permute-start.18 = (bf16[64,1024]{1,0:T(8,128)(2,1)}, bf16[64,1024]{1,0:T(8,128)(2,1)}, u32[]{:S(2)}, u32[]{:S(2)}) collective-permute-start(bf16[64,1024]{1,0:T(8,128)(2,1)} %get-tuple-element.54), channel_id=1, source_target_pairs={{0,8},{2,10},{4,12},{6,14},{8,0},{10,2},{12,4},{14,6},{1,9},{3,11}... | collective-permute-start | bytes 393224 | tf_op jit(solution)/shard_map/ppermute | solution.py:322
  94.5 11.5 %collective-permute-start.17 = (bf16[64,1024]{1,0:T(8,128)(2,1)}, bf16[64,1024]{1,0:T(8,128)(2,1)}, u32[]{:S(2)}, u32[]{:S(2)}) collective-permute-start(bf16[64,1024]{1,0:T(8,128)(2,1)} %get-tuple-element.52), channel_id=1, source_target_pairs={{0,4},{2,6},{4,0},{6,2},{8,12},{10,14},{12,8},{14,10},{1,5},{3,7},... | collective-permute-start | bytes 393224 | tf_op jit(solution)/shard_map/ppermute | solution.py:322
  96.3 12.7 %collective-permute-start.25 = (bf16[256,768]{1,0:T(8,128)(2,1)}, bf16[256,768]{1,0:T(8,128)(2,1)S(1)}, u32[]{:S(2)}, u32[]{:S(2)}) collective-permute-start(bf16[256,768]{1,0:T(8,128)(2,1)} %get-tuple-element.32), channel_id=1, source_target_pairs={{0,1},{1,0},{2,3},{3,2},{4,5},{5,4},{6,7},{7,6},{8,9},{9,8},{10,11... | collective-permute-start | bytes 1179656 | tf_op jit(solution)/shard_map/ppermute | solution.py:314
  101.0 10.5 %collective-permute-start.27 = (bf16[256,768]{1,0:T(8,128)(2,1)}, bf16[256,768]{1,0:T(8,128)(2,1)S(1)}, u32[]{:S(2)}, u32[]{:S(2)}) collective-permute-start(bf16[256,768]{1,0:T(8,128)(2,1)} %collective-permute-done.26.refs_13_), channel_id=1, source_target_pairs={{0,16},{16,0},{1,17},{17,1},{2,18},{18,2},{3,19},{19,3},{4,20},{20... | collective-permute-start | bytes 1179656 | tf_op jit(solution)/shard_map/ppermute | solution.py:318
  111.5 15.0 %collective-permute-start.28 = (bf16[256,768]{1,0:T(8,128)(2,1)S(1)}, bf16[256,768]{1,0:T(8,128)(2,1)S(1)}, u32[]{:S(2)}, u32[]{:S(2)}) collective-permute-start(bf16[256,768]{1,0:T(8,128)(2,1)S(1)} %collective-permute-done.25.refs_14_), channel_id=1, source_target_pairs={{0,16},{16,0},{1,17},{17,1},{2,18},{18,2},{3,19},{19,3},{4,20},{20... | collective-permute-start | bytes 1179656 | tf_op jit(solution)/shard_map/ppermute | solution.py:318
  113.2 17.9 %collective-permute-start.30 = (bf16[2,384,512]{2,1,0:T(8,128)(2,1)S(1)}, bf16[2,384,512]{2,1,0:T(8,128)(2,1)S(1)}, u32[]{:S(2)}, u32[]{:S(2)}) collective-permute-start(bf16[2,384,512]{2,1,0:T(8,128)(2,1)S(1)} %copy-done.9), channel_id=1, source_target_pairs={{0,1},{1,0},{2,3},{3,2},{4,5},{5,4},{6,7},{7,6},{8,9},{9,8},{10,11... | collective-permute-start | bytes 2359304 | tf_op jit(solution)/shard_map/ppermute | solution.py:314
  115.4 11.1 %collective-permute-start.22 = (bf16[64,1024]{1,0:T(8,128)(2,1)S(1)}, bf16[64,1024]{1,0:T(8,128)(2,1)S(1)}, u32[]{:S(2)}, u32[]{:S(2)}) collective-permute-start(bf16[64,1024]{1,0:T(8,128)(2,1)S(1)} %pad_maximum_fusion.3.refs_0_), channel_id=1, source_target_pairs={{0,8},{2,10},{4,12},{6,14},{8,0},{10,2},{12,4},{14,6},{1,9},{3,11}... | collective-permute-start | bytes 393224 | tf_op jit(solution)/shard_map/ppermute | solution.py:322
  144.2 9.4 %collective-permute-start.32 = (bf16[64,512]{1,0:T(8,128)(2,1)S(1)}, bf16[64,512]{1,0:T(8,128)(2,1)S(1)}, u32[]{:S(2)}, u32[]{:S(2)}) collective-permute-start(bf16[64,512]{1,0:T(8,128)(2,1)S(1)} %get-tuple-element.62), channel_id=1, source_target_pairs={{0,4},{2,6},{4,0},{6,2},{8,12},{10,14},{12,8},{14,10},{1,5},{3,7},... | collective-permute-start | bytes 196616 | tf_op jit(solution)/shard_map/ppermute | solution.py:322
  (40 other events, 551.7 us)

commit v11 on v10

--- a/solution.py
+++ b/solution.py
@@ -200,6 +200,119 @@
     return pairs
 
 
+def gated(summed, lanes, first_lane, experts, where_ref, order):
+    half = summed.shape[1] // 2
+    expert = where_ref[0] * 2 + (where_ref[1] + order) % 2
+    offset = lax.broadcasted_iota(jnp.int32, lanes.shape, 1) - first_lane - expert
+    gain = jnp.sum(
+        jnp.where((offset == 0) | (offset == experts), lanes, 0.0), axis=1, keepdims=True
+    )
+    return (jax.nn.silu(summed[:, :half]) * summed[:, half:] * gain).astype(jnp.bfloat16)
+
+
+def early_kernel(blocks, where_ref, *refs):
+    row_refs, refs = refs[:blocks], refs[blocks:]
+    own_ref, near_refs, far_ref, sums_ref, late_ref, lanes_ref, rows, weights, sems = (
+        refs[0], refs[1:3], *refs[3:]
+    )
+    width, late = own_ref.shape[1], late_ref.shape[1]
+    early = rows.shape[1] - late
+    group = where_ref[1]
+    pairs = chunk_pairs([ref.at[:, pl.ds(0, 2 * width)] for ref in row_refs], rows)
+    pairs += chunk_pairs([ref.at[:, pl.ds(2 * width, LANES)] for ref in row_refs], lanes_ref)
+    pairs += chunk_pairs([own_ref.at[group], *near_refs], weights.at[0])
+    pairs += chunk_pairs([own_ref.at[1 - group], far_ref], weights.at[1])
+    for copy in load(pairs, sems):
+        copy.wait()
+    late_ref[...] = rows[:, early:]
+    near = early + near_refs[1].shape[0]
+    padded = weights.shape[1]
+    if padded > near:
+        weights[0, near:] = jnp.zeros((padded - near, weights.shape[2]), jnp.bfloat16)
+    for order, depth in enumerate((padded, early)):
+        sums_ref[order] = jnp.dot(
+            rows[:, :depth], weights[order, :depth], preferred_element_type=jnp.float32
+        )
+
+
+def run_early(where, row_blocks, own, near, far):
+    blocks, count = len(row_blocks), sum(block.shape[0] for block in row_blocks)
+    _, width, columns = own.shape
+    chunk = far.shape[0]
+    late = width - chunk
+    inputs = [*row_blocks, own, *near, far]
+    return pl.pallas_call(
+        functools.partial(early_kernel, blocks),
+        out_shape=(
+            jax.ShapeDtypeStruct((2, count, columns), jnp.float32),
+            jax.ShapeDtypeStruct((count, late), jnp.bfloat16),
+            jax.ShapeDtypeStruct((count, LANES), jnp.bfloat16),
+        ),
+        in_specs=[pl.BlockSpec(memory_space=pltpu.SMEM)]
+        + [pl.BlockSpec(memory_space=pltpu.HBM)] * len(inputs),
+        out_specs=(pl.BlockSpec(memory_space=pltpu.VMEM),) * 3,
+        scratch_shapes=[
+            pltpu.VMEM((count, 2 * width), jnp.bfloat16),
+            pltpu.VMEM((2, pl.cdiv(width + chunk + near[1].shape[0], LANES) * LANES, columns), jnp.bfloat16),
+            pltpu.SemaphoreType.DMA((2 * blocks + 5,)),
+        ],
+        compiler_params=pltpu.CompilerParams(vmem_limit_bytes=24 * 1024 * 1024),
+        cost_estimate=pl.CostEstimate(
+            flops=2 * count * (2 * width + 3 * chunk) * columns,
+            bytes_accessed=4 * count * width + 2 * (2 * width + 3 * chunk) * columns,
+            transcendentals=0,
+        ),
+    )(where, *inputs)
+
+
+def late_kernel(experts, where_ref, sums_ref, late_ref, lanes_ref, far_ref, direct_ref, out_ref, weights, sems):
+    chunk, rest = far_ref.shape[0], direct_ref.shape[1]
+    half = sums_ref.shape[2] // 2
+    group = where_ref[1]
+    pairs = [
+        (direct_ref.at[group], weights.at[0, pl.ds(chunk, rest)]),
+        (far_ref, weights.at[1, pl.ds(0, chunk)]),
+        (direct_ref.at[1 - group], weights.at[1, pl.ds(chunk, rest)]),
+    ]
+    copies = load(pairs, sems)
+    aligned = chunk // LANES * LANES
+    if chunk > aligned:
+        weights[0, aligned:chunk] = jnp.zeros((chunk - aligned, weights.shape[2]), jnp.bfloat16)
+    lanes = lanes_ref[...].astype(jnp.float32)
+    for order, (first, needed) in enumerate(((aligned, copies[:1]), (0, copies[1:]))):
+        for copy in needed:
+            copy.wait()
+        summed = sums_ref[order] + jnp.dot(
+            late_ref[:, first:], weights[order, first:], preferred_element_type=jnp.float32
+        )
+        out_ref[:, order * half : (order + 1) * half] = gated(
+            summed, lanes, 0, experts, where_ref, order
+        )
+
+
+def run_late(where, early, far, direct, experts):
+    sums, late, lanes = early
+    _, count, columns = sums.shape
+    return pl.pallas_call(
+        functools.partial(late_kernel, experts),
+        out_shape=jax.ShapeDtypeStruct((count, columns), jnp.bfloat16),
+        in_specs=[pl.BlockSpec(memory_space=pltpu.SMEM)]
+        + [pl.BlockSpec(memory_space=pltpu.VMEM)] * 3
+        + [pl.BlockSpec(memory_space=pltpu.HBM)] * 2,
+        out_specs=pl.BlockSpec(memory_space=pltpu.VMEM),
+        scratch_shapes=[
+            pltpu.VMEM((2, late.shape[1], columns), jnp.bfloat16),
+            pltpu.SemaphoreType.DMA((3,)),
+        ],
+        compiler_params=pltpu.CompilerParams(vmem_limit_bytes=16 * 1024 * 1024),
+        cost_estimate=pl.CostEstimate(
+            flops=4 * count * late.shape[1] * columns,
+            bytes_accessed=8 * count * columns,
+            transcendentals=count * columns,
+        ),
+    )(where, sums, late, lanes, far, direct)
+
+
 def hidden_kernel(blocks, gain_blocks, chunks, direct, first_lane, experts, where_ref, *refs):
     refs = list(refs)
     take = lambda count: [refs.pop(0) for _ in range(count)]
@@ -222,17 +335,12 @@
     for copy in row_copies:
         copy.wait()
     lanes = gains[...].astype(jnp.float32)
-    lane = lax.broadcasted_iota(jnp.int32, lanes.shape, 1) - first_lane
     for order in range(2):
         for copy in weight_copies[order]:
             copy.wait()
-        offset = lane - (where_ref[0] * 2 + (where_ref[1] + order) % 2)
-        gain = jnp.sum(
-            jnp.where((offset == 0) | (offset == experts), lanes, 0.0), axis=1, keepdims=True
-        )
         summed = jnp.dot(rows[...], weights[order], preferred_element_type=jnp.float32)
-        hidden = jax.nn.silu(summed[:, :half_hidden]) * summed[:, half_hidden:] * gain
-        out_ref[:, order * half_hidden : (order + 1) * half_hidden] = hidden.astype(jnp.bfloat16)
+        hidden = gated(summed, lanes, first_lane, experts, where_ref, order)
+        out_ref[:, order * half_hidden : (order + 1) * half_hidden] = hidden
 
 
 def run_hidden(where, row_blocks, gain_blocks, own, near, far, direct, before, first_lane, experts):
@@ -390,22 +498,24 @@
     rows = routes.shape[0] // 2
     distances = range(2, owners, 2)
 
-    chunk = w_in.shape[1] * 13 // 32
+    width = w_in.shape[1]
+    ends = [0, width * 3 // 8, width * 13 // 16]
 
     lanes = gain_lanes(
         where, experts, routes, route_gain, speaking, talker_routes, talker_gain
     )
     give = lax.dynamic_slice_in_dim(hidden_in, (1 - replica) * rows, rows, 0)
     other = over_replica(give)
-    near_in = [send(w_in, group, index * chunk, chunk, other) for index in range(2)]
+    near_in = [send(w_in, group, a, b - a, other) for a, b in zip(ends, ends[1:])]
     row = build_row(where, hidden_in, other, lanes)
     same = [row] + [over_expert(row, distance) for distance in distances]
     far_in = [over_groups(after(near_in[0], same[1]))]
     far_in.append(over_groups(near_in[1]))
-    direct_in = over_replica(after(w_in[:, 2 * chunk :], near_in[0]))
-    across = [over_expert(after(row, far_in[0]), 1), over_expert(jnp.concatenate([*same[1:3], after(same[3], near_in[1])]), 1)]
+    direct_in = over_replica(after(w_in[:, ends[2] :], near_in[0]))
+    across = [over_expert(after(row, far_in[0]), 1), over_expert(jnp.concatenate(same[1:]), 1)]
     blocks = same + across
-    hidden = run_hidden(where, blocks, [], w_in, near_in, far_in, [direct_in], [], 0, experts)
+    early = run_early(where, blocks, w_in, near_in, far_in[0])
+    hidden = run_late(where, early, far_in[1], direct_in, experts)
     other_hidden = over_replica(hidden)
     own = spread_sums(*run_down(where, hidden, [], [], [w_out]))
     other_hidden = after(other_hidden, *own[1:])
@@ -440,7 +550,7 @@
         near_talker_in,
         far_talker_in,
         [],
-        [direct_talker_out],
+        [],
         2 * experts,
         experts,
     )

time: 158 us -> 156 us (0.987)
  waiting for transfers between devices: 76.3 us -> 65.6 us
  local copies, waits for them, and re-layouts: 5.37 us -> 9.61 us
  starting transfers between devices: 48.7 us -> 52.2 us
    ppermute x9, waiting for transfers between devices: 39.5 us -> 14.8 us  [over_replica(): return lax.ppermute(array, 'replica', SWAP)]
    ppermute x23, waiting for transfers between devices: 30.6 us -> 49.1 us  [over_expert(): lax.ppermute(array, 'expert', [(at, at ^ distance) for at in range(lax.ax...]
    pallas_call x0 -> x2, Pallas kernels: none -> 7.67 us  [the longest x1 5.11 us: run_early(): pl.pallas_call(functools.partial(early_kernel, blocks), out_shape=(jax.Sh...]
    pallas_call x2 -> x1, Pallas kernels: 12.7 us -> 5.57 us  [run_hidden(): pl.pallas_call(functools.partial(hidden_kernel, blocks, len(gain_blocks),...]
    unnamed x48, local copies, waits for them, and re-layouts: 0.9 us -> 5.56 us
    ppermute x23, starting transfers between devices: 23.6 us -> 27.8 us  [over_expert(): lax.ppermute(array, 'expert', [(at, at ^ distance) for at in range(lax.ax...]
    ppermute x4, waiting for transfers between devices: 3.54 us -> 0.89 us  [over_both(): return lax.ppermute(array, ('expert', 'replica'), pairs)]
    ppermute x4, waiting for transfers between devices: 2.61 us -> 0.83 us  [over_groups(): return lax.ppermute(array, 'groups', SWAP)]
  transfers between devices with their start and end apart: 40 -> 40, of which waited for: 23 -> 19; matrix products, arithmetic and copies ran while one was open for 5% -> 5% of each run, Pallas kernels for 2% -> 9%
where the time goes in v11:
time: 156 us; the launch traced here: 155 us
  waiting for transfers between devices  65.6 us (42%)
  starting transfers between devices  52.2 us (33%)
  Pallas kernels  21.7 us (14%)
  local copies, waits for them, and re-layouts  9.61 us (6%)
  other arithmetic  4.29 us (3%)
    ppermute x23, waiting for transfers between devices, over_expert(): lax.ppermute(array, 'expert', [(at, at ^ distance) for at in range(lax.ax...  49.1 us
    ppermute x23, starting transfers between devices, over_expert(): lax.ppermute(array, 'expert', [(at, at ^ distance) for at in range(lax.ax...  27.8 us
    ppermute x9, waiting for transfers between devices, over_replica(): return lax.ppermute(array, 'replica', SWAP)  14.8 us
    ppermute x9, starting transfers between devices, over_replica(): return lax.ppermute(array, 'replica', SWAP)  11.5 us
    pallas_call x5, Pallas kernels, run_down(): pl.pallas_call(functools.partial(down_kernel, halves, len(near)), out_sha...  7.23 us
    ppermute x4, starting transfers between devices, over_both(): return lax.ppermute(array, ('expert', 'replica'), pairs)  6.81 us
    ppermute x4, starting transfers between devices, over_groups(): return lax.ppermute(array, 'groups', SWAP)  6.14 us
    pallas_call x1, Pallas kernels, run_hidden(): pl.pallas_call(functools.partial(hidden_kernel, blocks, len(gain_blocks),...  5.57 us
  transfers between devices with their start and end apart: 40, of which 19 were waited for; matrix products, arithmetic and copies ran while one was open for 5% of the time, Pallas kernels for 9%

profile of v11, /device:TPU:0, one launch (start us, length us, event | category | flops | bytes accessed | tf_op | source)
XLA Modules:
  0.0 155.4 jit_solution(17259227210279556537)
XLA Ops:
  1.7 3.0 %collective-permute-start = (bf16[64,1024]{1,0:T(8,128)(2,1)S(1)}, bf16[64,1024]{1,0:T(8,128)(2,1)S(1)}, u32[]{:S(2)}, u32[]{:S(2)}) collective-permute-start(bf16[64,1024]{1,0:T(8,128)(2,1)S(1)} %constant_dynamic-slice_fusion), channel_id=1, source_target_pairs={{0,1},{1,0},{2,3},{3,2},{4,5},{5,4},{6,7},{7,6},{8,9},{9,8},{10,11... | collective-permute-start | bytes 393224 | tf_op jit(solution)/shard_map/ppermute | solution.py:422
  4.7 2.0 %dynamic-slice_bitcast_fusion.1 = bf16[384,768]{1,0:T(8,128)(2,1)} fusion(bf16[2,1024,768]{2,1,0:T(8,128)(2,1)} %refs_6_.1, s32[]{:T(128)S(6)} %select_n.43), kind=kLoop, calls=%fused_computation.5 | loop fusion | bytes 1179652 | tf_op jit(solution)/shard_map/squeeze | solution.py:440
  8.2 1.7 %collective-permute-start.4 = (bf16[384,768]{1,0:T(8,128)(2,1)}, bf16[384,768]{1,0:T(8,128)(2,1)}, u32[]{:S(2)}, u32[]{:S(2)}) collective-permute-start(bf16[384,768]{1,0:T(8,128)(2,1)} %dynamic-slice_bitcast_fusion.1), channel_id=1, source_target_pairs={{0,1},{1,0},{2,3},{3,2},{4,5},{5,4},{6,7},{7,6},{8,9},{9,8},{10,11... | collective-permute-start | bytes 1769480 | tf_op jit(solution)/shard_map/ppermute | solution.py:422
  14.7 1.6 %collective-permute-start.1 = (bf16[64,2176]{1,0:T(8,128)(2,1)S(1)}, bf16[64,2176]{1,0:T(8,128)(2,1)S(1)}, u32[]{:S(2)}, u32[]{:S(2)}) collective-permute-start(bf16[64,2176]{1,0:T(8,128)(2,1)S(1)} %shard_map.123.refs_0_.refs_6_), channel_id=1, source_target_pairs={{0,4},{2,6},{4,0},{6,2},{8,12},{10,14},{12,8},{14,10},{1,5},{3,7},... | collective-permute-start | bytes 835592 | tf_op jit(solution)/shard_map/ppermute | solution.py:430
  16.3 2.6 %collective-permute-start.2 = (bf16[64,2176]{1,0:T(8,128)(2,1)S(1)}, bf16[64,2176]{1,0:T(8,128)(2,1)S(1)}, u32[]{:S(2)}, u32[]{:S(2)}) collective-permute-start(bf16[64,2176]{1,0:T(8,128)(2,1)S(1)} %shard_map.123.refs_0_.refs_6_), channel_id=1, source_target_pairs={{0,8},{2,10},{4,12},{6,14},{8,0},{10,2},{12,4},{14,6},{1,9},{3,11}... | collective-permute-start | bytes 835592 | tf_op jit(solution)/shard_map/ppermute | solution.py:430
  19.6 7.0 %collective-permute-done.1.refs_1_.refs_7_ = bf16[64,2176]{1,0:T(8,128)(2,1)S(1)} collective-permute-done((bf16[64,2176]{1,0:T(8,128)(2,1)S(1)}, bf16[64,2176]{1,0:T(8,128)(2,1)S(1)}, u32[]{:S(2)}, u32[]{:S(2)}) %collective-permute-start.1) | collective-permute-done | bytes 278560 | tf_op jit(solution)/shard_map/ppermute | solution.py:430
  28.1 10.6 %collective-permute-done.2.refs_2_.refs_8_ = bf16[64,2176]{1,0:T(8,128)(2,1)S(1)} collective-permute-done((bf16[64,2176]{1,0:T(8,128)(2,1)S(1)}, bf16[64,2176]{1,0:T(8,128)(2,1)S(1)}, u32[]{:S(2)}, u32[]{:S(2)}) %collective-permute-start.2) | collective-permute-done | bytes 278560 | tf_op jit(solution)/shard_map/ppermute | solution.py:430
  42.7 5.1 %shard_map.124 = (f32[2,512,768]{2,1,0:T(8,128)S(1)}, bf16[512,640]{1,0:T(8,128)(2,1)S(1)}, bf16[512,128]{1,0:T(8,128)(2,1)S(1)}) custom-call(s32[3]{0:T(128)S(1)} %pad_add_fusion.where_ref, bf16[64,2176]{1,0:T(8,128)(2,1)S(1)} %shard_map.123.refs_0_.refs_6_, bf16[64,2176]{1,0:T(8,128)(2,1)S(1)} %collective-permute-done.1.refs_1_.refs_7_, ...), custom_call_target="tpu_custom_call" | custom-call | flops 2516582400 | bytes 7012352 | tf_op jit(solution)/shard_map/pallas_call | solution.py:244
  47.9 8.2 %collective-permute-done.10.direct_ref = bf16[2,192,768]{2,1,0:T(8,128)(2,1)S(1)} collective-permute-done((bf16[2,192,768]{2,1,0:T(8,128)(2,1)S(1)}, bf16[2,192,768]{2,1,0:T(8,128)(2,1)S(1)}, u32[]{:S(2)}, u32[]{:S(2)}) %collective-permute-start.10) | collective-permute-done | bytes 589856 | tf_op jit(solution)/shard_map/ppermute | solution.py:422
  56.8 2.6 %shard_map.125.hidden_ref = bf16[512,768]{1,0:T(8,128)(2,1)S(1)} custom-call(s32[3]{0:T(128)S(1)} %pad_add_fusion.where_ref, f32[2,512,768]{2,1,0:T(8,128)S(1)} %get-tuple-element.28.sums_ref, bf16[512,640]{1,0:T(8,128)(2,1)S(1)} %get-tuple-element.29.late_ref, bf16[512,128]{1,0:T(8,128)(2,1)S(1)} %get-tuple-element.30.lanes_ref, ...), custom_call_target="tpu_custom_call" | custom-call | flops 1006632960 | bytes 3145728 | tf_op jit(solution)/shard_map/pallas_call | solution.py:296
  59.3 1.7 %shard_map.126 = (bf16[256,1024]{1,0:T(8,128)(2,1)S(1)}, bf16[256,1024]{1,0:T(8,128)(2,1)S(1)}) custom-call(s32[3]{0:T(128)S(1)} %pad_add_fusion.where_ref, bf16[512,768]{1,0:T(8,128)(2,1)S(1)} %shard_map.125.hidden_ref, bf16[2,384,1024]{2,1,0:T(8,128)(2,1)S(1)} %copy-done.1), custom_call_target="tpu_custom_call" | custom-call | flops 805306368 | bytes 3407872 | tf_op jit(solution)/shard_map/pallas_call | solution.py:402
  63.2 4.0 %collective-permute-start.12 = (bf16[64,1024]{1,0:T(8,128)(2,1)S(1)}, bf16[64,1024]{1,0:T(8,128)(2,1)S(1)}, u32[]{:S(2)}, u32[]{:S(2)}) collective-permute-start(bf16[64,1024]{1,0:T(8,128)(2,1)S(1)} %get-tuple-element.57), channel_id=1, source_target_pairs={{0,4},{2,6},{4,0},{6,2},{8,12},{10,14},{12,8},{14,10},{1,5},{3,7},... | collective-permute-start | bytes 393224 | tf_op jit(solution)/shard_map/ppermute | solution.py:430
  69.6 3.2 %collective-permute-done.12 = bf16[64,1024]{1,0:T(8,128)(2,1)S(1)} collective-permute-done((bf16[64,1024]{1,0:T(8,128)(2,1)S(1)}, bf16[64,1024]{1,0:T(8,128)(2,1)S(1)}, u32[]{:S(2)}, u32[]{:S(2)}) %collective-permute-start.12) | collective-permute-done | bytes 131104 | tf_op jit(solution)/shard_map/ppermute | solution.py:430
  72.9 7.2 %collective-permute-done.13 = bf16[64,1024]{1,0:T(8,128)(2,1)S(1)} collective-permute-done((bf16[64,1024]{1,0:T(8,128)(2,1)S(1)}, bf16[64,1024]{1,0:T(8,128)(2,1)S(1)}, u32[]{:S(2)}, u32[]{:S(2)}) %collective-permute-start.13) | collective-permute-done | bytes 131104 | tf_op jit(solution)/shard_map/ppermute | solution.py:430
  87.2 3.6 %collective-permute-start.17 = (bf16[64,1024]{1,0:T(8,128)(2,1)}, bf16[64,1024]{1,0:T(8,128)(2,1)}, u32[]{:S(2)}, u32[]{:S(2)}) collective-permute-start(bf16[64,1024]{1,0:T(8,128)(2,1)} %get-tuple-element.54), channel_id=1, source_target_pairs={{0,4},{2,6},{4,0},{6,2},{8,12},{10,14},{12,8},{14,10},{1,5},{3,7},... | collective-permute-start | bytes 393224 | tf_op jit(solution)/shard_map/ppermute | solution.py:430
  94.8 2.5 %collective-permute-done.26.refs_13_ = bf16[256,768]{1,0:T(8,128)(2,1)} collective-permute-done((bf16[256,768]{1,0:T(8,128)(2,1)}, bf16[256,768]{1,0:T(8,128)(2,1)}, u32[]{:S(2)}, u32[]{:S(2)}) %collective-permute-start.26) | collective-permute-done | bytes 393248 | tf_op jit(solution)/shard_map/ppermute | solution.py:422
  98.8 5.2 %collective-permute-done.18 = bf16[64,1024]{1,0:T(8,128)(2,1)} collective-permute-done((bf16[64,1024]{1,0:T(8,128)(2,1)}, bf16[64,1024]{1,0:T(8,128)(2,1)}, u32[]{:S(2)}, u32[]{:S(2)}) %collective-permute-start.18) | collective-permute-done | bytes 131104 | tf_op jit(solution)/shard_map/ppermute | solution.py:430
  109.3 1.9 %collective-permute-done.20 = bf16[64,1024]{1,0:T(8,128)(2,1)S(1)} collective-permute-done((bf16[64,1024]{1,0:T(8,128)(2,1)S(1)}, bf16[64,1024]{1,0:T(8,128)(2,1)S(1)}, u32[]{:S(2)}, u32[]{:S(2)}) %collective-permute-start.20) | collective-permute-done | bytes 131104 | tf_op jit(solution)/shard_map/ppermute | solution.py:422
  111.7 2.4 %collective-permute-start.21 = (bf16[64,1024]{1,0:T(8,128)(2,1)S(1)}, bf16[64,1024]{1,0:T(8,128)(2,1)S(1)}, u32[]{:S(2)}, u32[]{:S(2)}) collective-permute-start(bf16[64,1024]{1,0:T(8,128)(2,1)S(1)} %pad_maximum_fusion.3.refs_0_), channel_id=1, source_target_pairs={{0,4},{2,6},{4,0},{6,2},{8,12},{10,14},{12,8},{14,10},{1,5},{3,7},... | collective-permute-start | bytes 393224 | tf_op jit(solution)/shard_map/ppermute | solution.py:430
  118.1 7.1 %collective-permute-done.22.refs_2_ = bf16[64,1024]{1,0:T(8,128)(2,1)S(1)} collective-permute-done((bf16[64,1024]{1,0:T(8,128)(2,1)S(1)}, bf16[64,1024]{1,0:T(8,128)(2,1)S(1)}, u32[]{:S(2)}, u32[]{:S(2)}) %collective-permute-start.22) | collective-permute-done | bytes 131104 | tf_op jit(solution)/shard_map/ppermute | solution.py:430
  127.2 5.6 %shard_map.129.hidden_ref = bf16[512,768]{1,0:T(8,128)(2,1)S(1)} custom-call(s32[3]{0:T(128)S(1)} %pad_add_fusion.where_ref, bf16[64,1024]{1,0:T(8,128)(2,1)S(1)} %pad_maximum_fusion.3.refs_0_, bf16[64,1024]{1,0:T(8,128)(2,1)S(1)} %collective-permute-done.21.refs_1_, bf16[64,1024]{1,0:T(8,128)(2,1)S(1)} %collective-permute-done.22.refs_2_, ...), custom_call_target="tpu_custom_call" | custom-call | flops 1610612736 | bytes 4194304 | tf_op jit(solution)/shard_map/pallas_call | solution.py:351
  140.1 2.6 %collective-permute-start.38 = (bf16[64,512]{1,0:T(8,128)(2,1)S(1)}, bf16[64,512]{1,0:T(8,128)(2,1)S(1)}, u32[]{:S(2)}, u32[]{:S(2)}) collective-permute-start(bf16[64,512]{1,0:T(8,128)(2,1)S(1)} %get-tuple-element.62), channel_id=1, source_target_pairs={{0,9},{1,8},{2,11},{3,10},{4,13},{5,12},{6,15},{7,14},{8,1},{9,0},... | collective-permute-start | bytes 196616 | tf_op jit(solution)/shard_map/ppermute | solution.py:451
  144.6 2.6 %collective-permute-start.33 = (bf16[64,512]{1,0:T(8,128)(2,1)S(1)}, bf16[64,512]{1,0:T(8,128)(2,1)S(1)}, u32[]{:S(2)}, u32[]{:S(2)}) collective-permute-start(bf16[64,512]{1,0:T(8,128)(2,1)S(1)} %get-tuple-element.66), channel_id=1, source_target_pairs={{0,8},{2,10},{4,12},{6,14},{8,0},{10,2},{12,4},{14,6},{1,9},{3,11}... | collective-permute-start | bytes 196616 | tf_op jit(solution)/shard_map/ppermute | solution.py:430
  150.2 4.4 %collective-permute-done.33 = bf16[64,512]{1,0:T(8,128)(2,1)S(1)} collective-permute-done((bf16[64,512]{1,0:T(8,128)(2,1)S(1)}, bf16[64,512]{1,0:T(8,128)(2,1)S(1)}, u32[]{:S(2)}, u32[]{:S(2)}) %collective-permute-start.33) | collective-permute-done | bytes 65568 | tf_op jit(solution)/shard_map/ppermute | solution.py:430
  (136 shorter events, 55.8 us)
Async XLA Ops:
  8.2 18.4 %collective-permute-start.4 = (bf16[384,768]{1,0:T(8,128)(2,1)}, bf16[384,768]{1,0:T(8,128)(2,1)}, u32[]{:S(2)}, u32[]{:S(2)}) collective-permute-start(bf16[384,768]{1,0:T(8,128)(2,1)} %dynamic-slice_bitcast_fusion.1), channel_id=1, source_target_pairs={{0,1},{1,0},{2,3},{3,2},{4,5},{5,4},{6,7},{7,6},{8,9},{9,8},{10,11... | collective-permute-start | bytes 1769480 | tf_op jit(solution)/shard_map/ppermute | solution.py:422
  14.7 11.9 %collective-permute-start.1 = (bf16[64,2176]{1,0:T(8,128)(2,1)S(1)}, bf16[64,2176]{1,0:T(8,128)(2,1)S(1)}, u32[]{:S(2)}, u32[]{:S(2)}) collective-permute-start(bf16[64,2176]{1,0:T(8,128)(2,1)S(1)} %shard_map.123.refs_0_.refs_6_), channel_id=1, source_target_pairs={{0,4},{2,6},{4,0},{6,2},{8,12},{10,14},{12,8},{14,10},{1,5},{3,7},... | collective-permute-start | bytes 835592 | tf_op jit(solution)/shard_map/ppermute | solution.py:430
  16.3 22.4 %collective-permute-start.2 = (bf16[64,2176]{1,0:T(8,128)(2,1)S(1)}, bf16[64,2176]{1,0:T(8,128)(2,1)S(1)}, u32[]{:S(2)}, u32[]{:S(2)}) collective-permute-start(bf16[64,2176]{1,0:T(8,128)(2,1)S(1)} %shard_map.123.refs_0_.refs_6_), channel_id=1, source_target_pairs={{0,8},{2,10},{4,12},{6,14},{8,0},{10,2},{12,4},{14,6},{1,9},{3,11}... | collective-permute-start | bytes 835592 | tf_op jit(solution)/shard_map/ppermute | solution.py:430
  18.9 19.8 %collective-permute-start.3 = (bf16[64,2176]{1,0:T(8,128)(2,1)S(1)}, bf16[64,2176]{1,0:T(8,128)(2,1)S(1)}, u32[]{:S(2)}, u32[]{:S(2)}) collective-permute-start(bf16[64,2176]{1,0:T(8,128)(2,1)S(1)} %shard_map.123.refs_0_.refs_6_), channel_id=1, source_target_pairs={{0,12},{2,14},{4,8},{6,10},{8,4},{10,6},{12,0},{14,2},{1,13},{3,15... | collective-permute-start | bytes 835592 | tf_op jit(solution)/shard_map/ppermute | solution.py:430
  19.2 19.7 %collective-permute-start.8 = (bf16[448,768]{1,0:T(8,128)(2,1)S(1)}, bf16[448,768]{1,0:T(8,128)(2,1)S(1)}, u32[]{:S(2)}, u32[]{:S(2)}) collective-permute-start(bf16[448,768]{1,0:T(8,128)(2,1)S(1)} %dynamic-slice_bitcast_fusion), channel_id=1, source_target_pairs={{0,1},{1,0},{2,3},{3,2},{4,5},{5,4},{6,7},{7,6},{8,9},{9,8},{10,11... | collective-permute-start | bytes 2064392 | tf_op jit(solution)/shard_map/ppermute | solution.py:422
  26.6 14.5 %collective-permute-start.5 = (bf16[384,768]{1,0:T(8,128)(2,1)}, bf16[384,768]{1,0:T(8,128)(2,1)S(1)}, u32[]{:S(2)}, u32[]{:S(2)}) collective-permute-start(bf16[384,768]{1,0:T(8,128)(2,1)} %collective-permute-done.4.refs_7_), channel_id=1, source_target_pairs={{0,16},{16,0},{1,17},{17,1},{2,18},{18,2},{3,19},{19,3},{4,20},{20... | collective-permute-start | bytes 1769480 | tf_op jit(solution)/shard_map/ppermute | solution.py:426
  38.9 17.8 %collective-permute-start.9 = (bf16[448,768]{1,0:T(8,128)(2,1)S(1)}, bf16[448,768]{1,0:T(8,128)(2,1)S(1)}, u32[]{:S(2)}, u32[]{:S(2)}) collective-permute-start(bf16[448,768]{1,0:T(8,128)(2,1)S(1)} %collective-permute-done.8.refs_8_), channel_id=1, source_target_pairs={{0,16},{16,0},{1,17},{17,1},{2,18},{18,2},{3,19},{19,3},{4,20},{20... | collective-permute-start | bytes 2064392 | tf_op jit(solution)/shard_map/ppermute | solution.py:426
  40.5 15.5 %collective-permute-start.10 = (bf16[2,192,768]{2,1,0:T(8,128)(2,1)S(1)}, bf16[2,192,768]{2,1,0:T(8,128)(2,1)S(1)}, u32[]{:S(2)}, u32[]{:S(2)}) collective-permute-start(bf16[2,192,768]{2,1,0:T(8,128)(2,1)S(1)} %slice.99), channel_id=1, source_target_pairs={{0,1},{1,0},{2,3},{3,2},{4,5},{5,4},{6,7},{7,6},{8,9},{9,8},{10,11... | collective-permute-start | bytes 1769480 | tf_op jit(solution)/shard_map/ppermute | solution.py:422
  61.1 20.3 %collective-permute-start.15 = (bf16[512,768]{1,0:T(8,128)(2,1)S(1)}, bf16[512,768]{1,0:T(8,128)(2,1)S(1)}, u32[]{:S(2)}, u32[]{:S(2)}) collective-permute-start(bf16[512,768]{1,0:T(8,128)(2,1)S(1)} %shard_map.125.hidden_ref), channel_id=1, source_target_pairs={{0,1},{1,0},{2,3},{3,2},{4,5},{5,4},{6,7},{7,6},{8,9},{9,8},{10,11... | collective-permute-start | bytes 2359304 | tf_op jit(solution)/shard_map/ppermute | solution.py:422
  63.2 9.7 %collective-permute-start.12 = (bf16[64,1024]{1,0:T(8,128)(2,1)S(1)}, bf16[64,1024]{1,0:T(8,128)(2,1)S(1)}, u32[]{:S(2)}, u32[]{:S(2)}) collective-permute-start(bf16[64,1024]{1,0:T(8,128)(2,1)S(1)} %get-tuple-element.57), channel_id=1, source_target_pairs={{0,4},{2,6},{4,0},{6,2},{8,12},{10,14},{12,8},{14,10},{1,5},{3,7},... | collective-permute-start | bytes 393224 | tf_op jit(solution)/shard_map/ppermute | solution.py:430
  67.2 12.9 %collective-permute-start.13 = (bf16[64,1024]{1,0:T(8,128)(2,1)S(1)}, bf16[64,1024]{1,0:T(8,128)(2,1)S(1)}, u32[]{:S(2)}, u32[]{:S(2)}) collective-permute-start(bf16[64,1024]{1,0:T(8,128)(2,1)S(1)} %get-tuple-element.59), channel_id=1, source_target_pairs={{0,8},{2,10},{4,12},{6,14},{8,0},{10,2},{12,4},{14,6},{1,9},{3,11}... | collective-permute-start | bytes 393224 | tf_op jit(solution)/shard_map/ppermute | solution.py:430
  68.3 11.8 %collective-permute-start.14 = (bf16[64,1024]{1,0:T(8,128)(2,1)S(1)}, bf16[64,1024]{1,0:T(8,128)(2,1)S(1)}, u32[]{:S(2)}, u32[]{:S(2)}) collective-permute-start(bf16[64,1024]{1,0:T(8,128)(2,1)S(1)} %get-tuple-element.58), channel_id=1, source_target_pairs={{0,12},{2,14},{4,8},{6,10},{8,4},{10,6},{12,0},{14,2},{1,13},{3,15... | collective-permute-start | bytes 393224 | tf_op jit(solution)/shard_map/ppermute | solution.py:430
  85.0 12.3 %collective-permute-start.26 = (bf16[256,768]{1,0:T(8,128)(2,1)}, bf16[256,768]{1,0:T(8,128)(2,1)}, u32[]{:S(2)}, u32[]{:S(2)}) collective-permute-start(bf16[256,768]{1,0:T(8,128)(2,1)} %get-tuple-element.37), channel_id=1, source_target_pairs={{0,1},{1,0},{2,3},{3,2},{4,5},{5,4},{6,7},{7,6},{8,9},{9,8},{10,11... | collective-permute-start | bytes 1179656 | tf_op jit(solution)/shard_map/ppermute | solution.py:422
  87.2 11.6 %collective-permute-start.17 = (bf16[64,1024]{1,0:T(8,128)(2,1)}, bf16[64,1024]{1,0:T(8,128)(2,1)}, u32[]{:S(2)}, u32[]{:S(2)}) collective-permute-start(bf16[64,1024]{1,0:T(8,128)(2,1)} %get-tuple-element.54), channel_id=1, source_target_pairs={{0,4},{2,6},{4,0},{6,2},{8,12},{10,14},{12,8},{14,10},{1,5},{3,7},... | collective-permute-start | bytes 393224 | tf_op jit(solution)/shard_map/ppermute | solution.py:430
  90.8 13.2 %collective-permute-start.18 = (bf16[64,1024]{1,0:T(8,128)(2,1)}, bf16[64,1024]{1,0:T(8,128)(2,1)}, u32[]{:S(2)}, u32[]{:S(2)}) collective-permute-start(bf16[64,1024]{1,0:T(8,128)(2,1)} %get-tuple-element.56), channel_id=1, source_target_pairs={{0,8},{2,10},{4,12},{6,14},{8,0},{10,2},{12,4},{14,6},{1,9},{3,11}... | collective-permute-start | bytes 393224 | tf_op jit(solution)/shard_map/ppermute | solution.py:430
  91.8 12.2 %collective-permute-start.19 = (bf16[64,1024]{1,0:T(8,128)(2,1)}, bf16[64,1024]{1,0:T(8,128)(2,1)}, u32[]{:S(2)}, u32[]{:S(2)}) collective-permute-start(bf16[64,1024]{1,0:T(8,128)(2,1)} %get-tuple-element.55), channel_id=1, source_target_pairs={{0,12},{2,14},{4,8},{6,10},{8,4},{10,6},{12,0},{14,2},{1,13},{3,15... | collective-permute-start | bytes 393224 | tf_op jit(solution)/shard_map/ppermute | solution.py:430
  93.3 14.4 %collective-permute-start.25 = (bf16[256,768]{1,0:T(8,128)(2,1)}, bf16[256,768]{1,0:T(8,128)(2,1)S(1)}, u32[]{:S(2)}, u32[]{:S(2)}) collective-permute-start(bf16[256,768]{1,0:T(8,128)(2,1)} %get-tuple-element.36), channel_id=1, source_target_pairs={{0,1},{1,0},{2,3},{3,2},{4,5},{5,4},{6,7},{7,6},{8,9},{9,8},{10,11... | collective-permute-start | bytes 1179656 | tf_op jit(solution)/shard_map/ppermute | solution.py:422
  97.3 10.5 %collective-permute-start.27 = (bf16[256,768]{1,0:T(8,128)(2,1)}, bf16[256,768]{1,0:T(8,128)(2,1)S(1)}, u32[]{:S(2)}, u32[]{:S(2)}) collective-permute-start(bf16[256,768]{1,0:T(8,128)(2,1)} %collective-permute-done.26.refs_13_), channel_id=1, source_target_pairs={{0,16},{16,0},{1,17},{17,1},{2,18},{18,2},{3,19},{19,3},{4,20},{20... | collective-permute-start | bytes 1179656 | tf_op jit(solution)/shard_map/ppermute | solution.py:426
  107.8 17.4 %collective-permute-start.28 = (bf16[256,768]{1,0:T(8,128)(2,1)S(1)}, bf16[256,768]{1,0:T(8,128)(2,1)S(1)}, u32[]{:S(2)}, u32[]{:S(2)}) collective-permute-start(bf16[256,768]{1,0:T(8,128)(2,1)S(1)} %collective-permute-done.25.refs_14_), channel_id=1, source_target_pairs={{0,16},{16,0},{1,17},{17,1},{2,18},{18,2},{3,19},{19,3},{4,20},{20... | collective-permute-start | bytes 1179656 | tf_op jit(solution)/shard_map/ppermute | solution.py:426
  114.1 11.0 %collective-permute-start.22 = (bf16[64,1024]{1,0:T(8,128)(2,1)S(1)}, bf16[64,1024]{1,0:T(8,128)(2,1)S(1)}, u32[]{:S(2)}, u32[]{:S(2)}) collective-permute-start(bf16[64,1024]{1,0:T(8,128)(2,1)S(1)} %pad_maximum_fusion.3.refs_0_), channel_id=1, source_target_pairs={{0,8},{2,10},{4,12},{6,14},{8,0},{10,2},{12,4},{14,6},{1,9},{3,11}... | collective-permute-start | bytes 393224 | tf_op jit(solution)/shard_map/ppermute | solution.py:430
  115.2 10.0 %collective-permute-start.23 = (bf16[64,1024]{1,0:T(8,128)(2,1)S(1)}, bf16[64,1024]{1,0:T(8,128)(2,1)S(1)}, u32[]{:S(2)}, u32[]{:S(2)}) collective-permute-start(bf16[64,1024]{1,0:T(8,128)(2,1)S(1)} %pad_maximum_fusion.3.refs_0_), channel_id=1, source_target_pairs={{0,12},{2,14},{4,8},{6,10},{8,4},{10,6},{12,0},{14,2},{1,13},{3,15... | collective-permute-start | bytes 393224 | tf_op jit(solution)/shard_map/ppermute | solution.py:430
  116.6 16.9 %collective-permute-start.30 = (bf16[2,384,512]{2,1,0:T(8,128)(2,1)S(1)}, bf16[2,384,512]{2,1,0:T(8,128)(2,1)S(1)}, u32[]{:S(2)}, u32[]{:S(2)}) collective-permute-start(bf16[2,384,512]{2,1,0:T(8,128)(2,1)S(1)} %copy-done.9), channel_id=1, source_target_pairs={{0,1},{1,0},{2,3},{3,2},{4,5},{5,4},{6,7},{7,6},{8,9},{9,8},{10,11... | collective-permute-start | bytes 2359304 | tf_op jit(solution)/shard_map/ppermute | solution.py:422
  140.1 9.2 %collective-permute-start.38 = (bf16[64,512]{1,0:T(8,128)(2,1)S(1)}, bf16[64,512]{1,0:T(8,128)(2,1)S(1)}, u32[]{:S(2)}, u32[]{:S(2)}) collective-permute-start(bf16[64,512]{1,0:T(8,128)(2,1)S(1)} %get-tuple-element.62), channel_id=1, source_target_pairs={{0,9},{1,8},{2,11},{3,10},{4,13},{5,12},{6,15},{7,14},{8,1},{9,0},... | collective-permute-start | bytes 196616 | tf_op jit(solution)/shard_map/ppermute | solution.py:451
  144.6 10.0 %collective-permute-start.33 = (bf16[64,512]{1,0:T(8,128)(2,1)S(1)}, bf16[64,512]{1,0:T(8,128)(2,1)S(1)}, u32[]{:S(2)}, u32[]{:S(2)}) collective-permute-start(bf16[64,512]{1,0:T(8,128)(2,1)S(1)} %get-tuple-element.66), channel_id=1, source_target_pairs={{0,8},{2,10},{4,12},{6,14},{8,0},{10,2},{12,4},{14,6},{1,9},{3,11}... | collective-permute-start | bytes 196616 | tf_op jit(solution)/shard_map/ppermute | solution.py:430
  (40 other events, 406.9 us)

commit v12 on v11

--- a/solution.py
+++ b/solution.py
@@ -125,7 +125,10 @@
 
 
 def lanes_kernel(experts, where_ref, *refs):
-    routes_ref, gain_ref, live_ref, talker_routes_ref, talker_gain_ref, out_ref, lanes = refs
+    sources, out_ref, places, (lanes, sems) = refs[:5], refs[5], refs[6:11], refs[11:]
+    for copy in load(list(zip(sources, places)), sems):
+        copy.wait()
+    routes_ref, gain_ref, live_ref, talker_routes_ref, talker_gain_ref = places
     rows = out_ref.shape[0]
     stack = []
     live = live_ref[...].astype(jnp.float32)
@@ -151,9 +154,10 @@
         functools.partial(lanes_kernel, experts),
         out_shape=jax.ShapeDtypeStruct((count // 2, LANES), jnp.bfloat16),
         in_specs=[pl.BlockSpec(memory_space=pltpu.SMEM)]
-        + [pl.BlockSpec(memory_space=pltpu.VMEM)] * len(inputs),
+        + [pl.BlockSpec(memory_space=pltpu.HBM)] * len(inputs),
         out_specs=pl.BlockSpec(memory_space=pltpu.VMEM),
-        scratch_shapes=[pltpu.VMEM((count, LANES), jnp.float32)],
+        scratch_shapes=[pltpu.VMEM(array.shape, array.dtype) for array in inputs]
+        + [pltpu.VMEM((count, LANES), jnp.float32), pltpu.SemaphoreType.DMA((len(inputs),))],
         compiler_params=pltpu.CompilerParams(vmem_limit_bytes=4 * 1024 * 1024),
         cost_estimate=pl.CostEstimate(
             flops=1 << 30, bytes_accessed=64 * count * LANES, transcendentals=0
@@ -256,7 +260,7 @@
             pltpu.VMEM((2, pl.cdiv(width + chunk + near[1].shape[0], LANES) * LANES, columns), jnp.bfloat16),
             pltpu.SemaphoreType.DMA((2 * blocks + 5,)),
         ],
-        compiler_params=pltpu.CompilerParams(vmem_limit_bytes=24 * 1024 * 1024),
+        compiler_params=pltpu.CompilerParams(vmem_limit_bytes=18 * 1024 * 1024),
         cost_estimate=pl.CostEstimate(
             flops=2 * count * (2 * width + 3 * chunk) * columns,
             bytes_accessed=4 * count * width + 2 * (2 * width + 3 * chunk) * columns,
@@ -304,7 +308,7 @@
             pltpu.VMEM((2, late.shape[1], columns), jnp.bfloat16),
             pltpu.SemaphoreType.DMA((3,)),
         ],
-        compiler_params=pltpu.CompilerParams(vmem_limit_bytes=16 * 1024 * 1024),
+        compiler_params=pltpu.CompilerParams(vmem_limit_bytes=10 * 1024 * 1024),
         cost_estimate=pl.CostEstimate(
             flops=4 * count * late.shape[1] * columns,
             bytes_accessed=8 * count * columns,
@@ -362,7 +366,7 @@
             pltpu.VMEM((2, 2 * width, columns), jnp.bfloat16),
             pltpu.SemaphoreType.DMA((3, max(2 * blocks, 2 + len(near)))),
         ],
-        compiler_params=pltpu.CompilerParams(vmem_limit_bytes=20 * 1024 * 1024),
+        compiler_params=pltpu.CompilerParams(vmem_limit_bytes=12 * 1024 * 1024),
         cost_estimate=pl.CostEstimate(
             flops=8 * count * width * columns,
             bytes_accessed=4 * width * (count + 2 * columns),
@@ -409,7 +413,7 @@
             pltpu.VMEM((depth, columns), jnp.bfloat16),
             pltpu.SemaphoreType.DMA((2 * (len(near) + len(whole)),)),
         ],
-        compiler_params=pltpu.CompilerParams(vmem_limit_bytes=16 * 1024 * 1024),
+        compiler_params=pltpu.CompilerParams(vmem_limit_bytes=8 * 1024 * 1024),
         cost_estimate=pl.CostEstimate(
             flops=outs * count * depth * columns,
             bytes_accessed=2 * depth * (count + columns) + outs * count * columns,
@@ -470,6 +474,15 @@
 
 def add_up(terms):
     return sum(term.astype(jnp.float32) for term in terms).astype(jnp.bfloat16)
+
+
+def gather_blocks(row, *hold):
+    blocks, step = {0: row}, lax.axis_size("expert") // 2
+    while step > 1:
+        for at, block in list(blocks.items()):
+            blocks[at + step] = over_expert(after(block, *hold) if at else block, step)
+        step //= 2
+    return [blocks[at] for at in sorted(blocks)]
 
 
 def in_order(replica, own, other, axis):
@@ -506,13 +519,15 @@
     )
     give = lax.dynamic_slice_in_dim(hidden_in, (1 - replica) * rows, rows, 0)
     other = over_replica(give)
-    near_in = [send(w_in, group, a, b - a, other) for a, b in zip(ends, ends[1:])]
+    near_in = [send(w_in, group, 0, ends[1], other)]
     row = build_row(where, hidden_in, other, lanes)
-    same = [row] + [over_expert(row, distance) for distance in distances]
-    far_in = [over_groups(after(near_in[0], same[1]))]
+    near_in.append(send(w_in, group, ends[1], ends[2] - ends[1], row))
+    same = gather_blocks(row, near_in[0])
+    far_in = [over_groups(after(near_in[0], row))]
     far_in.append(over_groups(near_in[1]))
     direct_in = over_replica(after(w_in[:, ends[2] :], near_in[0]))
-    across = [over_expert(after(row, far_in[0]), 1), over_expert(jnp.concatenate(same[1:]), 1)]
+    rest = after(jnp.concatenate(same[1:]), near_in[1])
+    across = [over_expert(after(row, far_in[0]), 1), over_expert(rest, 1)]
     blocks = same + across
     early = run_early(where, blocks, w_in, near_in, far_in[0])
     hidden = run_late(where, early, far_in[1], direct_in, experts)

time: 156 us -> 158 us (1.013)
  waiting for transfers between devices: 65.6 us -> 70.2 us
    ppermute x4, waiting for transfers between devices: 0.83 us -> 13.1 us  [over_groups(): return lax.ppermute(array, 'groups', SWAP)]
    ppermute x23, waiting for transfers between devices: 49.1 us -> 43.3 us  [over_expert(): lax.ppermute(array, 'expert', [(at, at ^ distance) for at in range(lax.ax...]
    ppermute x9, waiting for transfers between devices: 14.8 us -> 12.9 us  [over_replica(): return lax.ppermute(array, 'replica', SWAP)]
    ppermute x23, starting transfers between devices: 27.8 us -> 26 us  [over_expert(): lax.ppermute(array, 'expert', [(at, at ^ distance) for at in range(lax.ax...]
  transfers between devices with their start and end apart: 40 -> 40, of which waited for: 19 -> 20; matrix products, arithmetic and copies ran while one was open for 5% -> 4% of each run, Pallas kernels for 9% -> 9%
where the time goes in v12:
time: 158 us
  waiting for transfers between devices  70.2 us (44%)
  starting transfers between devices  51.5 us (33%)
  Pallas kernels  21.8 us (14%)
  local copies, waits for them, and re-layouts  8.13 us (5%)
  other arithmetic  4.29 us (3%)
    ppermute x23, waiting for transfers between devices, over_expert(): lax.ppermute(array, 'expert', [(at, at ^ distance) for at in range(lax.ax...  43.3 us
    ppermute x23, starting transfers between devices, over_expert(): lax.ppermute(array, 'expert', [(at, at ^ distance) for at in range(lax.ax...  26 us
    ppermute x4, waiting for transfers between devices, over_groups(): return lax.ppermute(array, 'groups', SWAP)  13.1 us
    ppermute x9, waiting for transfers between devices, over_replica(): return lax.ppermute(array, 'replica', SWAP)  12.9 us
    ppermute x9, starting transfers between devices, over_replica(): return lax.ppermute(array, 'replica', SWAP)  12.6 us
    pallas_call x5, Pallas kernels, run_down(): pl.pallas_call(functools.partial(down_kernel, halves, len(near)), out_sha...  7.24 us
    ppermute x4, starting transfers between devices, over_both(): return lax.ppermute(array, ('expert', 'replica'), pairs)  6.81 us
    ppermute x4, starting transfers between devices, over_groups(): return lax.ppermute(array, 'groups', SWAP)  6.01 us
  transfers between devices with their start and end apart: 40, of which 20 were waited for; matrix products, arithmetic and copies ran while one was open for 4% of the time, Pallas kernels for 9%

profile of v12, /device:TPU:0, one launch (start us, length us, event | category | flops | bytes accessed | tf_op | source)
XLA Modules:
  0.0 157.9 jit_solution(5954990513673497443)
XLA Ops:
  1.7 3.0 %collective-permute-start = (bf16[64,1024]{1,0:T(8,128)(2,1)S(1)}, bf16[64,1024]{1,0:T(8,128)(2,1)S(1)}, u32[]{:S(2)}, u32[]{:S(2)}) collective-permute-start(bf16[64,1024]{1,0:T(8,128)(2,1)S(1)} %constant_dynamic-slice_fusion), channel_id=1, source_target_pairs={{0,1},{1,0},{2,3},{3,2},{4,5},{5,4},{6,7},{7,6},{8,9},{9,8},{10,11... | collective-permute-start | bytes 393224 | tf_op jit(solution)/shard_map/ppermute | solution.py:426
  5.8 2.4 %collective-permute-done.other_ref = bf16[64,1024]{1,0:T(8,128)(2,1)S(1)} collective-permute-done((bf16[64,1024]{1,0:T(8,128)(2,1)S(1)}, bf16[64,1024]{1,0:T(8,128)(2,1)S(1)}, u32[]{:S(2)}, u32[]{:S(2)}) %collective-permute-start) | collective-permute-done | bytes 131104 | tf_op jit(solution)/shard_map/ppermute | solution.py:426
  14.8 2.7 %collective-permute-start.2 = (bf16[64,2176]{1,0:T(8,128)(2,1)S(1)}, bf16[64,2176]{1,0:T(8,128)(2,1)S(1)}, u32[]{:S(2)}, u32[]{:S(2)}) collective-permute-start(bf16[64,2176]{1,0:T(8,128)(2,1)S(1)} %shard_map.123.refs_0_.refs_6_), channel_id=1, source_target_pairs={{0,8},{2,10},{4,12},{6,14},{8,0},{10,2},{12,4},{14,6},{1,9},{3,11}... | collective-permute-start | bytes 835592 | tf_op jit(solution)/shard_map/ppermute | solution.py:434
  19.7 9.4 %collective-permute-done.2.refs_2_.refs_8_ = bf16[64,2176]{1,0:T(8,128)(2,1)S(1)} collective-permute-done((bf16[64,2176]{1,0:T(8,128)(2,1)S(1)}, bf16[64,2176]{1,0:T(8,128)(2,1)S(1)}, u32[]{:S(2)}, u32[]{:S(2)}) %collective-permute-start.2) | collective-permute-done | bytes 278560 | tf_op jit(solution)/shard_map/ppermute | solution.py:434
  31.2 5.3 %collective-permute-done.4.refs_3_.refs_9_ = bf16[64,2176]{1,0:T(8,128)(2,1)S(1)} collective-permute-done((bf16[64,2176]{1,0:T(8,128)(2,1)S(1)}, bf16[64,2176]{1,0:T(8,128)(2,1)S(1)}, u32[]{:S(2)}, u32[]{:S(2)}) %collective-permute-start.4) | collective-permute-done | bytes 278560 | tf_op jit(solution)/shard_map/ppermute | solution.py:434
  40.5 5.6 %collective-permute-done.5.refs_9_ = bf16[384,768]{1,0:T(8,128)(2,1)S(1)} collective-permute-done((bf16[384,768]{1,0:T(8,128)(2,1)}, bf16[384,768]{1,0:T(8,128)(2,1)S(1)}, u32[]{:S(2)}, u32[]{:S(2)}) %collective-permute-start.5) | collective-permute-done | bytes 589856 | tf_op jit(solution)/shard_map/ppermute | solution.py:430
  47.7 5.1 %shard_map.124 = (f32[2,512,768]{2,1,0:T(8,128)S(1)}, bf16[512,640]{1,0:T(8,128)(2,1)S(1)}, bf16[512,128]{1,0:T(8,128)(2,1)S(1)}) custom-call(s32[3]{0:T(128)S(1)} %pad_add_fusion.where_ref, bf16[64,2176]{1,0:T(8,128)(2,1)S(1)} %shard_map.123.refs_0_.refs_6_, bf16[64,2176]{1,0:T(8,128)(2,1)S(1)} %collective-permute-done.1.refs_1_.refs_7_, ...), custom_call_target="tpu_custom_call" | custom-call | flops 2516582400 | bytes 7012352 | tf_op jit(solution)/shard_map/pallas_call | solution.py:248
  54.5 5.1 %collective-permute-done.9.far_ref = bf16[448,768]{1,0:T(8,128)(2,1)S(1)} collective-permute-done((bf16[448,768]{1,0:T(8,128)(2,1)S(1)}, bf16[448,768]{1,0:T(8,128)(2,1)S(1)}, u32[]{:S(2)}, u32[]{:S(2)}) %collective-permute-start.9) | collective-permute-done | bytes 688160 | tf_op jit(solution)/shard_map/ppermute | solution.py:430
  59.6 2.6 %shard_map.125.hidden_ref = bf16[512,768]{1,0:T(8,128)(2,1)S(1)} custom-call(s32[3]{0:T(128)S(1)} %pad_add_fusion.where_ref, f32[2,512,768]{2,1,0:T(8,128)S(1)} %get-tuple-element.32.sums_ref, bf16[512,640]{1,0:T(8,128)(2,1)S(1)} %get-tuple-element.33.late_ref, bf16[512,128]{1,0:T(8,128)(2,1)S(1)} %get-tuple-element.34.lanes_ref, ...), custom_call_target="tpu_custom_call" | custom-call | flops 1006632960 | bytes 3145728 | tf_op jit(solution)/shard_map/pallas_call | solution.py:300
  66.4 3.4 %collective-permute-start.13 = (bf16[64,1024]{1,0:T(8,128)(2,1)S(1)}, bf16[64,1024]{1,0:T(8,128)(2,1)S(1)}, u32[]{:S(2)}, u32[]{:S(2)}) collective-permute-start(bf16[64,1024]{1,0:T(8,128)(2,1)S(1)} %get-tuple-element.63), channel_id=1, source_target_pairs={{0,8},{2,10},{4,12},{6,14},{8,0},{10,2},{12,4},{14,6},{1,9},{3,11}... | collective-permute-start | bytes 393224 | tf_op jit(solution)/shard_map/ppermute | solution.py:434
  70.9 3.5 %collective-permute-done.12 = bf16[64,1024]{1,0:T(8,128)(2,1)S(1)} collective-permute-done((bf16[64,1024]{1,0:T(8,128)(2,1)S(1)}, bf16[64,1024]{1,0:T(8,128)(2,1)S(1)}, u32[]{:S(2)}, u32[]{:S(2)}) %collective-permute-start.12) | collective-permute-done | bytes 131104 | tf_op jit(solution)/shard_map/ppermute | solution.py:434
  74.4 5.7 %collective-permute-done.14 = bf16[64,1024]{1,0:T(8,128)(2,1)S(1)} collective-permute-done((bf16[64,1024]{1,0:T(8,128)(2,1)S(1)}, bf16[64,1024]{1,0:T(8,128)(2,1)S(1)}, u32[]{:S(2)}, u32[]{:S(2)}) %collective-permute-start.14) | collective-permute-done | bytes 131104 | tf_op jit(solution)/shard_map/ppermute | solution.py:434
  80.8 3.1 %collective-permute-done.15.hidden_ref = bf16[512,768]{1,0:T(8,128)(2,1)S(1)} collective-permute-done((bf16[512,768]{1,0:T(8,128)(2,1)S(1)}, bf16[512,768]{1,0:T(8,128)(2,1)S(1)}, u32[]{:S(2)}, u32[]{:S(2)}) %collective-permute-start.15) | collective-permute-done | bytes 786464 | tf_op jit(solution)/shard_map/ppermute | solution.py:426
  90.1 3.2 %collective-permute-start.18 = (bf16[64,1024]{1,0:T(8,128)(2,1)}, bf16[64,1024]{1,0:T(8,128)(2,1)}, u32[]{:S(2)}, u32[]{:S(2)}) collective-permute-start(bf16[64,1024]{1,0:T(8,128)(2,1)} %get-tuple-element.60), channel_id=1, source_target_pairs={{0,8},{2,10},{4,12},{6,14},{8,0},{10,2},{12,4},{14,6},{1,9},{3,11}... | collective-permute-start | bytes 393224 | tf_op jit(solution)/shard_map/ppermute | solution.py:434
  96.0 3.8 %collective-permute-done.26.refs_13_ = bf16[256,768]{1,0:T(8,128)(2,1)} collective-permute-done((bf16[256,768]{1,0:T(8,128)(2,1)}, bf16[256,768]{1,0:T(8,128)(2,1)}, u32[]{:S(2)}, u32[]{:S(2)}) %collective-permute-start.26) | collective-permute-done | bytes 393248 | tf_op jit(solution)/shard_map/ppermute | solution.py:426
  101.3 2.9 %collective-permute-done.19 = bf16[64,1024]{1,0:T(8,128)(2,1)} collective-permute-done((bf16[64,1024]{1,0:T(8,128)(2,1)}, bf16[64,1024]{1,0:T(8,128)(2,1)}, u32[]{:S(2)}, u32[]{:S(2)}) %collective-permute-start.19) | collective-permute-done | bytes 131104 | tf_op jit(solution)/shard_map/ppermute | solution.py:434
  107.8 2.5 %collective-permute-done.27.refs_15_ = bf16[256,768]{1,0:T(8,128)(2,1)S(1)} collective-permute-done((bf16[256,768]{1,0:T(8,128)(2,1)}, bf16[256,768]{1,0:T(8,128)(2,1)S(1)}, u32[]{:S(2)}, u32[]{:S(2)}) %collective-permute-start.27) | collective-permute-done | bytes 393248 | tf_op jit(solution)/shard_map/ppermute | solution.py:430
  112.4 2.3 %collective-permute-start.21 = (bf16[64,1024]{1,0:T(8,128)(2,1)S(1)}, bf16[64,1024]{1,0:T(8,128)(2,1)S(1)}, u32[]{:S(2)}, u32[]{:S(2)}) collective-permute-start(bf16[64,1024]{1,0:T(8,128)(2,1)S(1)} %pad_maximum_fusion.3.refs_0_), channel_id=1, source_target_pairs={{0,4},{2,6},{4,0},{6,2},{8,12},{10,14},{12,8},{14,10},{1,5},{3,7},... | collective-permute-start | bytes 393224 | tf_op jit(solution)/shard_map/ppermute | solution.py:434
  114.6 2.0 %collective-permute-start.22 = (bf16[64,1024]{1,0:T(8,128)(2,1)S(1)}, bf16[64,1024]{1,0:T(8,128)(2,1)S(1)}, u32[]{:S(2)}, u32[]{:S(2)}) collective-permute-start(bf16[64,1024]{1,0:T(8,128)(2,1)S(1)} %pad_maximum_fusion.3.refs_0_), channel_id=1, source_target_pairs={{0,8},{2,10},{4,12},{6,14},{8,0},{10,2},{12,4},{14,6},{1,9},{3,11}... | collective-permute-start | bytes 393224 | tf_op jit(solution)/shard_map/ppermute | solution.py:434
  119.5 7.9 %collective-permute-done.22.refs_2_ = bf16[64,1024]{1,0:T(8,128)(2,1)S(1)} collective-permute-done((bf16[64,1024]{1,0:T(8,128)(2,1)S(1)}, bf16[64,1024]{1,0:T(8,128)(2,1)S(1)}, u32[]{:S(2)}, u32[]{:S(2)}) %collective-permute-start.22) | collective-permute-done | bytes 131104 | tf_op jit(solution)/shard_map/ppermute | solution.py:434
  129.5 5.6 %shard_map.129.hidden_ref = bf16[512,768]{1,0:T(8,128)(2,1)S(1)} custom-call(s32[3]{0:T(128)S(1)} %pad_add_fusion.where_ref, bf16[64,1024]{1,0:T(8,128)(2,1)S(1)} %pad_maximum_fusion.3.refs_0_, bf16[64,1024]{1,0:T(8,128)(2,1)S(1)} %collective-permute-done.21.refs_1_, bf16[64,1024]{1,0:T(8,128)(2,1)S(1)} %collective-permute-done.22.refs_2_, ...), custom_call_target="tpu_custom_call" | custom-call | flops 1610612736 | bytes 4194304 | tf_op jit(solution)/shard_map/pallas_call | solution.py:355
  142.5 2.9 %collective-permute-start.38 = (bf16[64,512]{1,0:T(8,128)(2,1)S(1)}, bf16[64,512]{1,0:T(8,128)(2,1)S(1)}, u32[]{:S(2)}, u32[]{:S(2)}) collective-permute-start(bf16[64,512]{1,0:T(8,128)(2,1)S(1)} %get-tuple-element.66), channel_id=1, source_target_pairs={{0,9},{1,8},{2,11},{3,10},{4,13},{5,12},{6,15},{7,14},{8,1},{9,0},... | collective-permute-start | bytes 196616 | tf_op jit(solution)/shard_map/ppermute | solution.py:455
  147.0 2.9 %collective-permute-start.33 = (bf16[64,512]{1,0:T(8,128)(2,1)S(1)}, bf16[64,512]{1,0:T(8,128)(2,1)S(1)}, u32[]{:S(2)}, u32[]{:S(2)}) collective-permute-start(bf16[64,512]{1,0:T(8,128)(2,1)S(1)} %get-tuple-element.70), channel_id=1, source_target_pairs={{0,8},{2,10},{4,12},{6,14},{8,0},{10,2},{12,4},{14,6},{1,9},{3,11}... | collective-permute-start | bytes 196616 | tf_op jit(solution)/shard_map/ppermute | solution.py:434
  152.8 4.3 %collective-permute-done.33 = bf16[64,512]{1,0:T(8,128)(2,1)S(1)} collective-permute-done((bf16[64,512]{1,0:T(8,128)(2,1)S(1)}, bf16[64,512]{1,0:T(8,128)(2,1)S(1)}, u32[]{:S(2)}, u32[]{:S(2)}) %collective-permute-start.33) | collective-permute-done | bytes 65568 | tf_op jit(solution)/shard_map/ppermute | solution.py:434
  (136 shorter events, 59.9 us)
Async XLA Ops:
  8.2 20.8 %collective-permute-start.3 = (bf16[384,768]{1,0:T(8,128)(2,1)S(1)}, bf16[384,768]{1,0:T(8,128)(2,1)}, u32[]{:S(2)}, u32[]{:S(2)}) collective-permute-start(bf16[384,768]{1,0:T(8,128)(2,1)S(1)} %dynamic-slice_bitcast_fusion.1), channel_id=1, source_target_pairs={{0,1},{1,0},{2,3},{3,2},{4,5},{5,4},{6,7},{7,6},{8,9},{9,8},{10,11... | collective-permute-start | bytes 1769480 | tf_op jit(solution)/shard_map/ppermute | solution.py:426
  14.8 14.3 %collective-permute-start.2 = (bf16[64,2176]{1,0:T(8,128)(2,1)S(1)}, bf16[64,2176]{1,0:T(8,128)(2,1)S(1)}, u32[]{:S(2)}, u32[]{:S(2)}) collective-permute-start(bf16[64,2176]{1,0:T(8,128)(2,1)S(1)} %shard_map.123.refs_0_.refs_6_), channel_id=1, source_target_pairs={{0,8},{2,10},{4,12},{6,14},{8,0},{10,2},{12,4},{14,6},{1,9},{3,11}... | collective-permute-start | bytes 835592 | tf_op jit(solution)/shard_map/ppermute | solution.py:434
  17.5 20.0 %collective-permute-start.7 = (bf16[448,768]{1,0:T(8,128)(2,1)S(1)}, bf16[448,768]{1,0:T(8,128)(2,1)S(1)}, u32[]{:S(2)}, u32[]{:S(2)}) collective-permute-start(bf16[448,768]{1,0:T(8,128)(2,1)S(1)} %dynamic-slice_bitcast_fusion), channel_id=1, source_target_pairs={{0,1},{1,0},{2,3},{3,2},{4,5},{5,4},{6,7},{7,6},{8,9},{9,8},{10,11... | collective-permute-start | bytes 2064392 | tf_op jit(solution)/shard_map/ppermute | solution.py:426
  18.1 13.1 %collective-permute-start.1 = (bf16[64,2176]{1,0:T(8,128)(2,1)S(1)}, bf16[64,2176]{1,0:T(8,128)(2,1)S(1)}, u32[]{:S(2)}, u32[]{:S(2)}) collective-permute-start(bf16[64,2176]{1,0:T(8,128)(2,1)S(1)} %shard_map.123.refs_0_.refs_6_), channel_id=1, source_target_pairs={{0,4},{2,6},{4,0},{6,2},{8,12},{10,14},{12,8},{14,10},{1,5},{3,7},... | collective-permute-start | bytes 835592 | tf_op jit(solution)/shard_map/ppermute | solution.py:434
  29.6 16.4 %collective-permute-start.5 = (bf16[384,768]{1,0:T(8,128)(2,1)}, bf16[384,768]{1,0:T(8,128)(2,1)S(1)}, u32[]{:S(2)}, u32[]{:S(2)}) collective-permute-start(bf16[384,768]{1,0:T(8,128)(2,1)} %collective-permute-done.3.refs_7_), channel_id=1, source_target_pairs={{0,16},{16,0},{1,17},{17,1},{2,18},{18,2},{3,19},{19,3},{4,20},{20... | collective-permute-start | bytes 1769480 | tf_op jit(solution)/shard_map/ppermute | solution.py:430
  37.5 10.2 %collective-permute-start.8 = (bf16[192,2176]{1,0:T(8,128)(2,1)S(1)}, bf16[192,2176]{1,0:T(8,128)(2,1)S(1)}, u32[]{:S(2)}, u32[]{:S(2)}) collective-permute-start(bf16[192,2176]{1,0:T(8,128)(2,1)S(1)} %pad_maximum_fusion), channel_id=1, source_target_pairs={{0,2},{2,0},{4,6},{6,4},{8,10},{10,8},{12,14},{14,12},{1,3},{3,1},... | collective-permute-start | bytes 2506760 | tf_op jit(solution)/shard_map/ppermute | solution.py:434
  37.5 22.1 %collective-permute-start.9 = (bf16[448,768]{1,0:T(8,128)(2,1)S(1)}, bf16[448,768]{1,0:T(8,128)(2,1)S(1)}, u32[]{:S(2)}, u32[]{:S(2)}) collective-permute-start(bf16[448,768]{1,0:T(8,128)(2,1)S(1)} %collective-permute-done.7.refs_8_), channel_id=1, source_target_pairs={{0,16},{16,0},{1,17},{17,1},{2,18},{18,2},{3,19},{19,3},{4,20},{20... | collective-permute-start | bytes 2064392 | tf_op jit(solution)/shard_map/ppermute | solution.py:430
  39.0 15.5 %collective-permute-start.10 = (bf16[2,192,768]{2,1,0:T(8,128)(2,1)S(1)}, bf16[2,192,768]{2,1,0:T(8,128)(2,1)S(1)}, u32[]{:S(2)}, u32[]{:S(2)}) collective-permute-start(bf16[2,192,768]{2,1,0:T(8,128)(2,1)S(1)} %slice.99), channel_id=1, source_target_pairs={{0,1},{1,0},{2,3},{3,2},{4,5},{5,4},{6,7},{7,6},{8,9},{9,8},{10,11... | collective-permute-start | bytes 1769480 | tf_op jit(solution)/shard_map/ppermute | solution.py:426
  64.0 20.0 %collective-permute-start.15 = (bf16[512,768]{1,0:T(8,128)(2,1)S(1)}, bf16[512,768]{1,0:T(8,128)(2,1)S(1)}, u32[]{:S(2)}, u32[]{:S(2)}) collective-permute-start(bf16[512,768]{1,0:T(8,128)(2,1)S(1)} %shard_map.125.hidden_ref), channel_id=1, source_target_pairs={{0,1},{1,0},{2,3},{3,2},{4,5},{5,4},{6,7},{7,6},{8,9},{9,8},{10,11... | collective-permute-start | bytes 2359304 | tf_op jit(solution)/shard_map/ppermute | solution.py:426
  66.0 8.4 %collective-permute-start.12 = (bf16[64,1024]{1,0:T(8,128)(2,1)S(1)}, bf16[64,1024]{1,0:T(8,128)(2,1)S(1)}, u32[]{:S(2)}, u32[]{:S(2)}) collective-permute-start(bf16[64,1024]{1,0:T(8,128)(2,1)S(1)} %get-tuple-element.61), channel_id=1, source_target_pairs={{0,4},{2,6},{4,0},{6,2},{8,12},{10,14},{12,8},{14,10},{1,5},{3,7},... | collective-permute-start | bytes 393224 | tf_op jit(solution)/shard_map/ppermute | solution.py:434
  69.7 10.4 %collective-permute-start.14 = (bf16[64,1024]{1,0:T(8,128)(2,1)S(1)}, bf16[64,1024]{1,0:T(8,128)(2,1)S(1)}, u32[]{:S(2)}, u32[]{:S(2)}) collective-permute-start(bf16[64,1024]{1,0:T(8,128)(2,1)S(1)} %get-tuple-element.62), channel_id=1, source_target_pairs={{0,12},{2,14},{4,8},{6,10},{8,4},{10,6},{12,0},{14,2},{1,13},{3,15... | collective-permute-start | bytes 393224 | tf_op jit(solution)/shard_map/ppermute | solution.py:434
  87.5 12.3 %collective-permute-start.26 = (bf16[256,768]{1,0:T(8,128)(2,1)}, bf16[256,768]{1,0:T(8,128)(2,1)}, u32[]{:S(2)}, u32[]{:S(2)}) collective-permute-start(bf16[256,768]{1,0:T(8,128)(2,1)} %get-tuple-element.41), channel_id=1, source_target_pairs={{0,1},{1,0},{2,3},{3,2},{4,5},{5,4},{6,7},{7,6},{8,9},{9,8},{10,11... | collective-permute-start | bytes 1179656 | tf_op jit(solution)/shard_map/ppermute | solution.py:426
  89.7 11.6 %collective-permute-start.17 = (bf16[64,1024]{1,0:T(8,128)(2,1)}, bf16[64,1024]{1,0:T(8,128)(2,1)}, u32[]{:S(2)}, u32[]{:S(2)}) collective-permute-start(bf16[64,1024]{1,0:T(8,128)(2,1)} %get-tuple-element.58), channel_id=1, source_target_pairs={{0,4},{2,6},{4,0},{6,2},{8,12},{10,14},{12,8},{14,10},{1,5},{3,7},... | collective-permute-start | bytes 393224 | tf_op jit(solution)/shard_map/ppermute | solution.py:434
  90.1 11.2 %collective-permute-start.18 = (bf16[64,1024]{1,0:T(8,128)(2,1)}, bf16[64,1024]{1,0:T(8,128)(2,1)}, u32[]{:S(2)}, u32[]{:S(2)}) collective-permute-start(bf16[64,1024]{1,0:T(8,128)(2,1)} %get-tuple-element.60), channel_id=1, source_target_pairs={{0,8},{2,10},{4,12},{6,14},{8,0},{10,2},{12,4},{14,6},{1,9},{3,11}... | collective-permute-start | bytes 393224 | tf_op jit(solution)/shard_map/ppermute | solution.py:434
  93.4 10.8 %collective-permute-start.19 = (bf16[64,1024]{1,0:T(8,128)(2,1)}, bf16[64,1024]{1,0:T(8,128)(2,1)}, u32[]{:S(2)}, u32[]{:S(2)}) collective-permute-start(bf16[64,1024]{1,0:T(8,128)(2,1)} %get-tuple-element.59), channel_id=1, source_target_pairs={{0,12},{2,14},{4,8},{6,10},{8,4},{10,6},{12,0},{14,2},{1,13},{3,15... | collective-permute-start | bytes 393224 | tf_op jit(solution)/shard_map/ppermute | solution.py:434
  94.6 13.3 %collective-permute-start.25 = (bf16[256,768]{1,0:T(8,128)(2,1)}, bf16[256,768]{1,0:T(8,128)(2,1)S(1)}, u32[]{:S(2)}, u32[]{:S(2)}) collective-permute-start(bf16[256,768]{1,0:T(8,128)(2,1)} %get-tuple-element.40), channel_id=1, source_target_pairs={{0,1},{1,0},{2,3},{3,2},{4,5},{5,4},{6,7},{7,6},{8,9},{9,8},{10,11... | collective-permute-start | bytes 1179656 | tf_op jit(solution)/shard_map/ppermute | solution.py:426
  99.8 10.5 %collective-permute-start.27 = (bf16[256,768]{1,0:T(8,128)(2,1)}, bf16[256,768]{1,0:T(8,128)(2,1)S(1)}, u32[]{:S(2)}, u32[]{:S(2)}) collective-permute-start(bf16[256,768]{1,0:T(8,128)(2,1)} %collective-permute-done.26.refs_13_), channel_id=1, source_target_pairs={{0,16},{16,0},{1,17},{17,1},{2,18},{18,2},{3,19},{19,3},{4,20},{20... | collective-permute-start | bytes 1179656 | tf_op jit(solution)/shard_map/ppermute | solution.py:430
  110.3 17.2 %collective-permute-start.28 = (bf16[256,768]{1,0:T(8,128)(2,1)S(1)}, bf16[256,768]{1,0:T(8,128)(2,1)S(1)}, u32[]{:S(2)}, u32[]{:S(2)}) collective-permute-start(bf16[256,768]{1,0:T(8,128)(2,1)S(1)} %collective-permute-done.25.refs_14_), channel_id=1, source_target_pairs={{0,16},{16,0},{1,17},{17,1},{2,18},{18,2},{3,19},{19,3},{4,20},{20... | collective-permute-start | bytes 1179656 | tf_op jit(solution)/shard_map/ppermute | solution.py:430
  114.6 12.8 %collective-permute-start.22 = (bf16[64,1024]{1,0:T(8,128)(2,1)S(1)}, bf16[64,1024]{1,0:T(8,128)(2,1)S(1)}, u32[]{:S(2)}, u32[]{:S(2)}) collective-permute-start(bf16[64,1024]{1,0:T(8,128)(2,1)S(1)} %pad_maximum_fusion.3.refs_0_), channel_id=1, source_target_pairs={{0,8},{2,10},{4,12},{6,14},{8,0},{10,2},{12,4},{14,6},{1,9},{3,11}... | collective-permute-start | bytes 393224 | tf_op jit(solution)/shard_map/ppermute | solution.py:434
  116.6 10.8 %collective-permute-start.23 = (bf16[64,1024]{1,0:T(8,128)(2,1)S(1)}, bf16[64,1024]{1,0:T(8,128)(2,1)S(1)}, u32[]{:S(2)}, u32[]{:S(2)}) collective-permute-start(bf16[64,1024]{1,0:T(8,128)(2,1)S(1)} %pad_maximum_fusion.3.refs_0_), channel_id=1, source_target_pairs={{0,12},{2,14},{4,8},{6,10},{8,4},{10,6},{12,0},{14,2},{1,13},{3,15... | collective-permute-start | bytes 393224 | tf_op jit(solution)/shard_map/ppermute | solution.py:434
  118.0 18.1 %collective-permute-start.30 = (bf16[2,384,512]{2,1,0:T(8,128)(2,1)S(1)}, bf16[2,384,512]{2,1,0:T(8,128)(2,1)S(1)}, u32[]{:S(2)}, u32[]{:S(2)}) collective-permute-start(bf16[2,384,512]{2,1,0:T(8,128)(2,1)S(1)} %copy-done.9), channel_id=1, source_target_pairs={{0,1},{1,0},{2,3},{3,2},{4,5},{5,4},{6,7},{7,6},{8,9},{9,8},{10,11... | collective-permute-start | bytes 2359304 | tf_op jit(solution)/shard_map/ppermute | solution.py:426
  141.4 8.4 %collective-permute-start.37 = (bf16[64,512]{1,0:T(8,128)(2,1)S(1)}, bf16[64,512]{1,0:T(8,128)(2,1)S(1)}, u32[]{:S(2)}, u32[]{:S(2)}) collective-permute-start(bf16[64,512]{1,0:T(8,128)(2,1)S(1)} %get-tuple-element.67), channel_id=1, source_target_pairs={{0,5},{1,4},{2,7},{3,6},{4,1},{5,0},{6,3},{7,2},{8,13},{9,12},{10,... | collective-permute-start | bytes 196616 | tf_op jit(solution)/shard_map/ppermute | solution.py:455
  142.5 9.5 %collective-permute-start.38 = (bf16[64,512]{1,0:T(8,128)(2,1)S(1)}, bf16[64,512]{1,0:T(8,128)(2,1)S(1)}, u32[]{:S(2)}, u32[]{:S(2)}) collective-permute-start(bf16[64,512]{1,0:T(8,128)(2,1)S(1)} %get-tuple-element.66), channel_id=1, source_target_pairs={{0,9},{1,8},{2,11},{3,10},{4,13},{5,12},{6,15},{7,14},{8,1},{9,0},... | collective-permute-start | bytes 196616 | tf_op jit(solution)/shard_map/ppermute | solution.py:455
  147.0 10.1 %collective-permute-start.33 = (bf16[64,512]{1,0:T(8,128)(2,1)S(1)}, bf16[64,512]{1,0:T(8,128)(2,1)S(1)}, u32[]{:S(2)}, u32[]{:S(2)}) collective-permute-start(bf16[64,512]{1,0:T(8,128)(2,1)S(1)} %get-tuple-element.70), channel_id=1, source_target_pairs={{0,8},{2,10},{4,12},{6,14},{8,0},{10,2},{12,4},{14,6},{1,9},{3,11}... | collective-permute-start | bytes 196616 | tf_op jit(solution)/shard_map/ppermute | solution.py:434
  (40 other events, 434.0 us)

commit v13 on v12

--- a/solution.py
+++ b/solution.py
@@ -476,15 +476,6 @@
     return sum(term.astype(jnp.float32) for term in terms).astype(jnp.bfloat16)
 
 
-def gather_blocks(row, *hold):
-    blocks, step = {0: row}, lax.axis_size("expert") // 2
-    while step > 1:
-        for at, block in list(blocks.items()):
-            blocks[at + step] = over_expert(after(block, *hold) if at else block, step)
-        step //= 2
-    return [blocks[at] for at in sorted(blocks)]
-
-
 def in_order(replica, own, other, axis):
     return jnp.concatenate(
         [jnp.where(replica == 0, own, other), jnp.where(replica == 0, other, own)], axis=axis
@@ -519,15 +510,12 @@
     )
     give = lax.dynamic_slice_in_dim(hidden_in, (1 - replica) * rows, rows, 0)
     other = over_replica(give)
-    near_in = [send(w_in, group, 0, ends[1], other)]
+    near_in = [send(w_in, group, a, b - a, other, lanes) for a, b in zip(ends, ends[1:])]
     row = build_row(where, hidden_in, other, lanes)
-    near_in.append(send(w_in, group, ends[1], ends[2] - ends[1], row))
-    same = gather_blocks(row, near_in[0])
-    far_in = [over_groups(after(near_in[0], row))]
-    far_in.append(over_groups(near_in[1]))
+    same = [row] + [over_expert(row, distance) for distance in distances]
+    far_in = [over_groups(after(near_in[0], same[1])), over_groups(near_in[1])]
     direct_in = over_replica(after(w_in[:, ends[2] :], near_in[0]))
-    rest = after(jnp.concatenate(same[1:]), near_in[1])
-    across = [over_expert(after(row, far_in[0]), 1), over_expert(rest, 1)]
+    across = [over_expert(after(row, far_in[0]), 1), over_expert(jnp.concatenate(same[1:]), 1)]
     blocks = same + across
     early = run_early(where, blocks, w_in, near_in, far_in[0])
     hidden = run_late(where, early, far_in[1], direct_in, experts)

time: 158 us -> 153 us (0.968)
  starting transfers between devices: 51.5 us -> 47.2 us
  waiting for transfers between devices: 70.2 us -> 68.3 us
    ppermute x4, waiting for transfers between devices: 13.1 us -> 2.27 us  [over_groups(): return lax.ppermute(array, 'groups', SWAP)]
    ppermute x9, waiting for transfers between devices: 12.9 us -> 21.6 us  [over_replica(): return lax.ppermute(array, 'replica', SWAP)]
    ppermute x9, starting transfers between devices: 12.6 us -> 8.53 us  [over_replica(): return lax.ppermute(array, 'replica', SWAP)]
  transfers between devices with their start and end apart: 40 -> 40, of which waited for: 20 -> 21; matrix products, arithmetic and copies ran while one was open for 4% -> 5% of each run, Pallas kernels for 9% -> 9%
where the time goes in v13:
time: 153 us; the launch traced here: 152 us
  waiting for transfers between devices  68.3 us (45%)
  starting transfers between devices  47.2 us (31%)
  Pallas kernels  21.3 us (14%)
  local copies, waits for them, and re-layouts  9.26 us (6%)
  other arithmetic  4.29 us (3%)
    ppermute x23, waiting for transfers between devices, over_expert(): lax.ppermute(array, 'expert', [(at, at ^ distance) for at in range(lax.ax...  44 us
    ppermute x23, starting transfers between devices, over_expert(): lax.ppermute(array, 'expert', [(at, at ^ distance) for at in range(lax.ax...  25.8 us
    ppermute x9, waiting for transfers between devices, over_replica(): return lax.ppermute(array, 'replica', SWAP)  21.6 us
    ppermute x9, starting transfers between devices, over_replica(): return lax.ppermute(array, 'replica', SWAP)  8.53 us
    pallas_call x5, Pallas kernels, run_down(): pl.pallas_call(functools.partial(down_kernel, halves, len(near)), out_sha...  7.24 us
    ppermute x4, starting transfers between devices, over_both(): return lax.ppermute(array, ('expert', 'replica'), pairs)  6.81 us
    ppermute x4, starting transfers between devices, over_groups(): return lax.ppermute(array, 'groups', SWAP)  6.07 us
    pallas_call x1, Pallas kernels, run_hidden(): pl.pallas_call(functools.partial(hidden_kernel, blocks, len(gain_blocks),...  5.57 us
  transfers between devices with their start and end apart: 40, of which 21 were waited for; matrix products, arithmetic and copies ran while one was open for 5% of the time, Pallas kernels for 9%

profile of v13, /device:TPU:0, one launch (start us, length us, event | category | flops | bytes accessed | tf_op | source)
XLA Modules:
  0.0 152.4 jit_solution(8509678930594390702)
XLA Ops:
  1.7 3.0 %collective-permute-start = (bf16[64,1024]{1,0:T(8,128)(2,1)S(1)}, bf16[64,1024]{1,0:T(8,128)(2,1)S(1)}, u32[]{:S(2)}, u32[]{:S(2)}) collective-permute-start(bf16[64,1024]{1,0:T(8,128)(2,1)S(1)} %constant_dynamic-slice_fusion), channel_id=1, source_target_pairs={{0,1},{1,0},{2,3},{3,2},{4,5},{5,4},{6,7},{7,6},{8,9},{9,8},{10,11... | collective-permute-start | bytes 393224 | tf_op jit(solution)/shard_map/ppermute | solution.py:426
  10.7 2.2 %collective-permute-start.1 = (bf16[64,2176]{1,0:T(8,128)(2,1)S(1)}, bf16[64,2176]{1,0:T(8,128)(2,1)S(1)}, u32[]{:S(2)}, u32[]{:S(2)}) collective-permute-start(bf16[64,2176]{1,0:T(8,128)(2,1)S(1)} %shard_map.123.refs_0_.refs_6_), channel_id=1, source_target_pairs={{0,4},{2,6},{4,0},{6,2},{8,12},{10,14},{12,8},{14,10},{1,5},{3,7},... | collective-permute-start | bytes 835592 | tf_op jit(solution)/shard_map/ppermute | solution.py:434
  12.9 2.6 %collective-permute-start.2 = (bf16[64,2176]{1,0:T(8,128)(2,1)S(1)}, bf16[64,2176]{1,0:T(8,128)(2,1)S(1)}, u32[]{:S(2)}, u32[]{:S(2)}) collective-permute-start(bf16[64,2176]{1,0:T(8,128)(2,1)S(1)} %shard_map.123.refs_0_.refs_6_), channel_id=1, source_target_pairs={{0,8},{2,10},{4,12},{6,14},{8,0},{10,2},{12,4},{14,6},{1,9},{3,11}... | collective-permute-start | bytes 835592 | tf_op jit(solution)/shard_map/ppermute | solution.py:434
  18.4 5.5 %collective-permute-done.1.refs_1_.refs_7_ = bf16[64,2176]{1,0:T(8,128)(2,1)S(1)} collective-permute-done((bf16[64,2176]{1,0:T(8,128)(2,1)S(1)}, bf16[64,2176]{1,0:T(8,128)(2,1)S(1)}, u32[]{:S(2)}, u32[]{:S(2)}) %collective-permute-start.1) | collective-permute-done | bytes 278560 | tf_op jit(solution)/shard_map/ppermute | solution.py:434
  23.9 2.5 %collective-permute-done.4.refs_7_ = bf16[384,768]{1,0:T(8,128)(2,1)S(1)} collective-permute-done((bf16[384,768]{1,0:T(8,128)(2,1)S(1)}, bf16[384,768]{1,0:T(8,128)(2,1)S(1)}, u32[]{:S(2)}, u32[]{:S(2)}) %collective-permute-start.4) | collective-permute-done | bytes 589856 | tf_op jit(solution)/shard_map/ppermute | solution.py:426
  27.9 7.4 %collective-permute-done.2.refs_2_.refs_8_ = bf16[64,2176]{1,0:T(8,128)(2,1)S(1)} collective-permute-done((bf16[64,2176]{1,0:T(8,128)(2,1)S(1)}, bf16[64,2176]{1,0:T(8,128)(2,1)S(1)}, u32[]{:S(2)}, u32[]{:S(2)}) %collective-permute-start.2) | collective-permute-done | bytes 278560 | tf_op jit(solution)/shard_map/ppermute | solution.py:434
  35.5 4.2 %collective-permute-done.8.refs_8_ = bf16[448,768]{1,0:T(8,128)(2,1)S(1)} collective-permute-done((bf16[448,768]{1,0:T(8,128)(2,1)S(1)}, bf16[448,768]{1,0:T(8,128)(2,1)S(1)}, u32[]{:S(2)}, u32[]{:S(2)}) %collective-permute-start.8) | collective-permute-done | bytes 688160 | tf_op jit(solution)/shard_map/ppermute | solution.py:426
  43.4 4.7 %shard_map.124 = (f32[2,512,768]{2,1,0:T(8,128)S(1)}, bf16[512,640]{1,0:T(8,128)(2,1)S(1)}, bf16[512,128]{1,0:T(8,128)(2,1)S(1)}) custom-call(s32[3]{0:T(128)S(1)} %pad_add_fusion.where_ref, bf16[64,2176]{1,0:T(8,128)(2,1)S(1)} %shard_map.123.refs_0_.refs_6_, bf16[64,2176]{1,0:T(8,128)(2,1)S(1)} %collective-permute-done.1.refs_1_.refs_7_, ...), custom_call_target="tpu_custom_call" | custom-call | flops 2516582400 | bytes 7012352 | tf_op jit(solution)/shard_map/pallas_call | solution.py:248
  48.1 6.8 %collective-permute-done.10.direct_ref = bf16[2,192,768]{2,1,0:T(8,128)(2,1)S(1)} collective-permute-done((bf16[2,192,768]{2,1,0:T(8,128)(2,1)S(1)}, bf16[2,192,768]{2,1,0:T(8,128)(2,1)S(1)}, u32[]{:S(2)}, u32[]{:S(2)}) %collective-permute-start.10) | collective-permute-done | bytes 589856 | tf_op jit(solution)/shard_map/ppermute | solution.py:426
  55.7 2.6 %shard_map.125.hidden_ref = bf16[512,768]{1,0:T(8,128)(2,1)S(1)} custom-call(s32[3]{0:T(128)S(1)} %pad_add_fusion.where_ref, f32[2,512,768]{2,1,0:T(8,128)S(1)} %get-tuple-element.28.sums_ref, bf16[512,640]{1,0:T(8,128)(2,1)S(1)} %get-tuple-element.29.late_ref, bf16[512,128]{1,0:T(8,128)(2,1)S(1)} %get-tuple-element.30.lanes_ref, ...), custom_call_target="tpu_custom_call" | custom-call | flops 1006632960 | bytes 3145728 | tf_op jit(solution)/shard_map/pallas_call | solution.py:300
  62.1 2.3 %collective-permute-start.12 = (bf16[64,1024]{1,0:T(8,128)(2,1)S(1)}, bf16[64,1024]{1,0:T(8,128)(2,1)S(1)}, u32[]{:S(2)}, u32[]{:S(2)}) collective-permute-start(bf16[64,1024]{1,0:T(8,128)(2,1)S(1)} %get-tuple-element.57), channel_id=1, source_target_pairs={{0,4},{2,6},{4,0},{6,2},{8,12},{10,14},{12,8},{14,10},{1,5},{3,7},... | collective-permute-start | bytes 393224 | tf_op jit(solution)/shard_map/ppermute | solution.py:434
  66.8 3.2 %collective-permute-done.12 = bf16[64,1024]{1,0:T(8,128)(2,1)S(1)} collective-permute-done((bf16[64,1024]{1,0:T(8,128)(2,1)S(1)}, bf16[64,1024]{1,0:T(8,128)(2,1)S(1)}, u32[]{:S(2)}, u32[]{:S(2)}) %collective-permute-start.12) | collective-permute-done | bytes 131104 | tf_op jit(solution)/shard_map/ppermute | solution.py:434
  70.0 7.2 %collective-permute-done.13 = bf16[64,1024]{1,0:T(8,128)(2,1)S(1)} collective-permute-done((bf16[64,1024]{1,0:T(8,128)(2,1)S(1)}, bf16[64,1024]{1,0:T(8,128)(2,1)S(1)}, u32[]{:S(2)}, u32[]{:S(2)}) %collective-permute-start.13) | collective-permute-done | bytes 131104 | tf_op jit(solution)/shard_map/ppermute | solution.py:434
  77.9 2.1 %collective-permute-done.15.hidden_ref = bf16[512,768]{1,0:T(8,128)(2,1)S(1)} collective-permute-done((bf16[512,768]{1,0:T(8,128)(2,1)S(1)}, bf16[512,768]{1,0:T(8,128)(2,1)S(1)}, u32[]{:S(2)}, u32[]{:S(2)}) %collective-permute-start.15) | collective-permute-done | bytes 786464 | tf_op jit(solution)/shard_map/ppermute | solution.py:426
  85.9 3.1 %collective-permute-start.17 = (bf16[64,1024]{1,0:T(8,128)(2,1)}, bf16[64,1024]{1,0:T(8,128)(2,1)}, u32[]{:S(2)}, u32[]{:S(2)}) collective-permute-start(bf16[64,1024]{1,0:T(8,128)(2,1)} %get-tuple-element.54), channel_id=1, source_target_pairs={{0,4},{2,6},{4,0},{6,2},{8,12},{10,14},{12,8},{14,10},{1,5},{3,7},... | collective-permute-start | bytes 393224 | tf_op jit(solution)/shard_map/ppermute | solution.py:434
  91.9 3.9 %collective-permute-done.26.refs_13_ = bf16[256,768]{1,0:T(8,128)(2,1)} collective-permute-done((bf16[256,768]{1,0:T(8,128)(2,1)}, bf16[256,768]{1,0:T(8,128)(2,1)}, u32[]{:S(2)}, u32[]{:S(2)}) %collective-permute-start.26) | collective-permute-done | bytes 393248 | tf_op jit(solution)/shard_map/ppermute | solution.py:426
  97.4 4.7 %collective-permute-done.18 = bf16[64,1024]{1,0:T(8,128)(2,1)} collective-permute-done((bf16[64,1024]{1,0:T(8,128)(2,1)}, bf16[64,1024]{1,0:T(8,128)(2,1)}, u32[]{:S(2)}, u32[]{:S(2)}) %collective-permute-start.18) | collective-permute-done | bytes 131104 | tf_op jit(solution)/shard_map/ppermute | solution.py:434
  109.8 2.4 %collective-permute-start.21 = (bf16[64,1024]{1,0:T(8,128)(2,1)S(1)}, bf16[64,1024]{1,0:T(8,128)(2,1)S(1)}, u32[]{:S(2)}, u32[]{:S(2)}) collective-permute-start(bf16[64,1024]{1,0:T(8,128)(2,1)S(1)} %pad_maximum_fusion.3.refs_0_), channel_id=1, source_target_pairs={{0,4},{2,6},{4,0},{6,2},{8,12},{10,14},{12,8},{14,10},{1,5},{3,7},... | collective-permute-start | bytes 393224 | tf_op jit(solution)/shard_map/ppermute | solution.py:434
  116.2 7.0 %collective-permute-done.22.refs_2_ = bf16[64,1024]{1,0:T(8,128)(2,1)S(1)} collective-permute-done((bf16[64,1024]{1,0:T(8,128)(2,1)S(1)}, bf16[64,1024]{1,0:T(8,128)(2,1)S(1)}, u32[]{:S(2)}, u32[]{:S(2)}) %collective-permute-start.22) | collective-permute-done | bytes 131104 | tf_op jit(solution)/shard_map/ppermute | solution.py:434
  125.3 5.6 %shard_map.129.hidden_ref = bf16[512,768]{1,0:T(8,128)(2,1)S(1)} custom-call(s32[3]{0:T(128)S(1)} %pad_add_fusion.where_ref, bf16[64,1024]{1,0:T(8,128)(2,1)S(1)} %pad_maximum_fusion.3.refs_0_, bf16[64,1024]{1,0:T(8,128)(2,1)S(1)} %collective-permute-done.21.refs_1_, bf16[64,1024]{1,0:T(8,128)(2,1)S(1)} %collective-permute-done.22.refs_2_, ...), custom_call_target="tpu_custom_call" | custom-call | flops 1610612736 | bytes 4194304 | tf_op jit(solution)/shard_map/pallas_call | solution.py:355
  136.0 2.2 %collective-permute-start.37 = (bf16[64,512]{1,0:T(8,128)(2,1)S(1)}, bf16[64,512]{1,0:T(8,128)(2,1)S(1)}, u32[]{:S(2)}, u32[]{:S(2)}) collective-permute-start(bf16[64,512]{1,0:T(8,128)(2,1)S(1)} %get-tuple-element.63), channel_id=1, source_target_pairs={{0,5},{1,4},{2,7},{3,6},{4,1},{5,0},{6,3},{7,2},{8,13},{9,12},{10,... | collective-permute-start | bytes 196616 | tf_op jit(solution)/shard_map/ppermute | solution.py:455
  139.9 2.3 %collective-permute-start.39 = (bf16[64,512]{1,0:T(8,128)(2,1)S(1)}, bf16[64,512]{1,0:T(8,128)(2,1)S(1)}, u32[]{:S(2)}, u32[]{:S(2)}) collective-permute-start(bf16[64,512]{1,0:T(8,128)(2,1)S(1)} %get-tuple-element.61), channel_id=1, source_target_pairs={{0,13},{1,12},{2,15},{3,14},{4,9},{5,8},{6,11},{7,10},{8,5},{9,4},... | collective-permute-start | bytes 196616 | tf_op jit(solution)/shard_map/ppermute | solution.py:455
  142.7 2.7 %collective-permute-start.33 = (bf16[64,512]{1,0:T(8,128)(2,1)S(1)}, bf16[64,512]{1,0:T(8,128)(2,1)S(1)}, u32[]{:S(2)}, u32[]{:S(2)}) collective-permute-start(bf16[64,512]{1,0:T(8,128)(2,1)S(1)} %get-tuple-element.66), channel_id=1, source_target_pairs={{0,8},{2,10},{4,12},{6,14},{8,0},{10,2},{12,4},{14,6},{1,9},{3,11}... | collective-permute-start | bytes 196616 | tf_op jit(solution)/shard_map/ppermute | solution.py:434
  147.8 3.8 %collective-permute-done.33 = bf16[64,512]{1,0:T(8,128)(2,1)S(1)} collective-permute-done((bf16[64,512]{1,0:T(8,128)(2,1)S(1)}, bf16[64,512]{1,0:T(8,128)(2,1)S(1)}, u32[]{:S(2)}, u32[]{:S(2)}) %collective-permute-start.33) | collective-permute-done | bytes 65568 | tf_op jit(solution)/shard_map/ppermute | solution.py:434
  (136 shorter events, 57.5 us)
Async XLA Ops:
  10.1 16.3 %collective-permute-start.4 = (bf16[384,768]{1,0:T(8,128)(2,1)S(1)}, bf16[384,768]{1,0:T(8,128)(2,1)S(1)}, u32[]{:S(2)}, u32[]{:S(2)}) collective-permute-start(bf16[384,768]{1,0:T(8,128)(2,1)S(1)} %dynamic-slice_bitcast_fusion.1), channel_id=1, source_target_pairs={{0,1},{1,0},{2,3},{3,2},{4,5},{5,4},{6,7},{7,6},{8,9},{9,8},{10,11... | collective-permute-start | bytes 1769480 | tf_op jit(solution)/shard_map/ppermute | solution.py:426
  10.7 13.2 %collective-permute-start.1 = (bf16[64,2176]{1,0:T(8,128)(2,1)S(1)}, bf16[64,2176]{1,0:T(8,128)(2,1)S(1)}, u32[]{:S(2)}, u32[]{:S(2)}) collective-permute-start(bf16[64,2176]{1,0:T(8,128)(2,1)S(1)} %shard_map.123.refs_0_.refs_6_), channel_id=1, source_target_pairs={{0,4},{2,6},{4,0},{6,2},{8,12},{10,14},{12,8},{14,10},{1,5},{3,7},... | collective-permute-start | bytes 835592 | tf_op jit(solution)/shard_map/ppermute | solution.py:434
  12.9 22.4 %collective-permute-start.2 = (bf16[64,2176]{1,0:T(8,128)(2,1)S(1)}, bf16[64,2176]{1,0:T(8,128)(2,1)S(1)}, u32[]{:S(2)}, u32[]{:S(2)}) collective-permute-start(bf16[64,2176]{1,0:T(8,128)(2,1)S(1)} %shard_map.123.refs_0_.refs_6_), channel_id=1, source_target_pairs={{0,8},{2,10},{4,12},{6,14},{8,0},{10,2},{12,4},{14,6},{1,9},{3,11}... | collective-permute-start | bytes 835592 | tf_op jit(solution)/shard_map/ppermute | solution.py:434
  15.5 19.8 %collective-permute-start.3 = (bf16[64,2176]{1,0:T(8,128)(2,1)S(1)}, bf16[64,2176]{1,0:T(8,128)(2,1)S(1)}, u32[]{:S(2)}, u32[]{:S(2)}) collective-permute-start(bf16[64,2176]{1,0:T(8,128)(2,1)S(1)} %shard_map.123.refs_0_.refs_6_), channel_id=1, source_target_pairs={{0,12},{2,14},{4,8},{6,10},{8,4},{10,6},{12,0},{14,2},{1,13},{3,15... | collective-permute-start | bytes 835592 | tf_op jit(solution)/shard_map/ppermute | solution.py:434
  16.6 23.0 %collective-permute-start.8 = (bf16[448,768]{1,0:T(8,128)(2,1)S(1)}, bf16[448,768]{1,0:T(8,128)(2,1)S(1)}, u32[]{:S(2)}, u32[]{:S(2)}) collective-permute-start(bf16[448,768]{1,0:T(8,128)(2,1)S(1)} %dynamic-slice_bitcast_fusion), channel_id=1, source_target_pairs={{0,1},{1,0},{2,3},{3,2},{4,5},{5,4},{6,7},{7,6},{8,9},{9,8},{10,11... | collective-permute-start | bytes 2064392 | tf_op jit(solution)/shard_map/ppermute | solution.py:426
  26.4 15.5 %collective-permute-start.5 = (bf16[384,768]{1,0:T(8,128)(2,1)S(1)}, bf16[384,768]{1,0:T(8,128)(2,1)S(1)}, u32[]{:S(2)}, u32[]{:S(2)}) collective-permute-start(bf16[384,768]{1,0:T(8,128)(2,1)S(1)} %collective-permute-done.4.refs_7_), channel_id=1, source_target_pairs={{0,16},{16,0},{1,17},{17,1},{2,18},{18,2},{3,19},{19,3},{4,20},{20... | collective-permute-start | bytes 1769480 | tf_op jit(solution)/shard_map/ppermute | solution.py:430
  39.7 16.0 %collective-permute-start.9 = (bf16[448,768]{1,0:T(8,128)(2,1)S(1)}, bf16[448,768]{1,0:T(8,128)(2,1)S(1)}, u32[]{:S(2)}, u32[]{:S(2)}) collective-permute-start(bf16[448,768]{1,0:T(8,128)(2,1)S(1)} %collective-permute-done.8.refs_8_), channel_id=1, source_target_pairs={{0,16},{16,0},{1,17},{17,1},{2,18},{18,2},{3,19},{19,3},{4,20},{20... | collective-permute-start | bytes 2064392 | tf_op jit(solution)/shard_map/ppermute | solution.py:430
  41.2 13.7 %collective-permute-start.10 = (bf16[2,192,768]{2,1,0:T(8,128)(2,1)S(1)}, bf16[2,192,768]{2,1,0:T(8,128)(2,1)S(1)}, u32[]{:S(2)}, u32[]{:S(2)}) collective-permute-start(bf16[2,192,768]{2,1,0:T(8,128)(2,1)S(1)} %slice.99), channel_id=1, source_target_pairs={{0,1},{1,0},{2,3},{3,2},{4,5},{5,4},{6,7},{7,6},{8,9},{9,8},{10,11... | collective-permute-start | bytes 1769480 | tf_op jit(solution)/shard_map/ppermute | solution.py:426
  60.0 20.0 %collective-permute-start.15 = (bf16[512,768]{1,0:T(8,128)(2,1)S(1)}, bf16[512,768]{1,0:T(8,128)(2,1)S(1)}, u32[]{:S(2)}, u32[]{:S(2)}) collective-permute-start(bf16[512,768]{1,0:T(8,128)(2,1)S(1)} %shard_map.125.hidden_ref), channel_id=1, source_target_pairs={{0,1},{1,0},{2,3},{3,2},{4,5},{5,4},{6,7},{7,6},{8,9},{9,8},{10,11... | collective-permute-start | bytes 2359304 | tf_op jit(solution)/shard_map/ppermute | solution.py:426
  64.3 12.9 %collective-permute-start.13 = (bf16[64,1024]{1,0:T(8,128)(2,1)S(1)}, bf16[64,1024]{1,0:T(8,128)(2,1)S(1)}, u32[]{:S(2)}, u32[]{:S(2)}) collective-permute-start(bf16[64,1024]{1,0:T(8,128)(2,1)S(1)} %get-tuple-element.59), channel_id=1, source_target_pairs={{0,8},{2,10},{4,12},{6,14},{8,0},{10,2},{12,4},{14,6},{1,9},{3,11}... | collective-permute-start | bytes 393224 | tf_op jit(solution)/shard_map/ppermute | solution.py:434
  66.3 10.9 %collective-permute-start.14 = (bf16[64,1024]{1,0:T(8,128)(2,1)S(1)}, bf16[64,1024]{1,0:T(8,128)(2,1)S(1)}, u32[]{:S(2)}, u32[]{:S(2)}) collective-permute-start(bf16[64,1024]{1,0:T(8,128)(2,1)S(1)} %get-tuple-element.58), channel_id=1, source_target_pairs={{0,12},{2,14},{4,8},{6,10},{8,4},{10,6},{12,0},{14,2},{1,13},{3,15... | collective-permute-start | bytes 393224 | tf_op jit(solution)/shard_map/ppermute | solution.py:434
  83.6 12.3 %collective-permute-start.26 = (bf16[256,768]{1,0:T(8,128)(2,1)}, bf16[256,768]{1,0:T(8,128)(2,1)}, u32[]{:S(2)}, u32[]{:S(2)}) collective-permute-start(bf16[256,768]{1,0:T(8,128)(2,1)} %get-tuple-element.37), channel_id=1, source_target_pairs={{0,1},{1,0},{2,3},{3,2},{4,5},{5,4},{6,7},{7,6},{8,9},{9,8},{10,11... | collective-permute-start | bytes 1179656 | tf_op jit(solution)/shard_map/ppermute | solution.py:426
  85.9 11.5 %collective-permute-start.17 = (bf16[64,1024]{1,0:T(8,128)(2,1)}, bf16[64,1024]{1,0:T(8,128)(2,1)}, u32[]{:S(2)}, u32[]{:S(2)}) collective-permute-start(bf16[64,1024]{1,0:T(8,128)(2,1)} %get-tuple-element.54), channel_id=1, source_target_pairs={{0,4},{2,6},{4,0},{6,2},{8,12},{10,14},{12,8},{14,10},{1,5},{3,7},... | collective-permute-start | bytes 393224 | tf_op jit(solution)/shard_map/ppermute | solution.py:434
  88.9 13.2 %collective-permute-start.18 = (bf16[64,1024]{1,0:T(8,128)(2,1)}, bf16[64,1024]{1,0:T(8,128)(2,1)}, u32[]{:S(2)}, u32[]{:S(2)}) collective-permute-start(bf16[64,1024]{1,0:T(8,128)(2,1)} %get-tuple-element.56), channel_id=1, source_target_pairs={{0,8},{2,10},{4,12},{6,14},{8,0},{10,2},{12,4},{14,6},{1,9},{3,11}... | collective-permute-start | bytes 393224 | tf_op jit(solution)/shard_map/ppermute | solution.py:434
  90.0 12.2 %collective-permute-start.19 = (bf16[64,1024]{1,0:T(8,128)(2,1)}, bf16[64,1024]{1,0:T(8,128)(2,1)}, u32[]{:S(2)}, u32[]{:S(2)}) collective-permute-start(bf16[64,1024]{1,0:T(8,128)(2,1)} %get-tuple-element.55), channel_id=1, source_target_pairs={{0,12},{2,14},{4,8},{6,10},{8,4},{10,6},{12,0},{14,2},{1,13},{3,15... | collective-permute-start | bytes 393224 | tf_op jit(solution)/shard_map/ppermute | solution.py:434
  91.4 13.5 %collective-permute-start.25 = (bf16[256,768]{1,0:T(8,128)(2,1)}, bf16[256,768]{1,0:T(8,128)(2,1)S(1)}, u32[]{:S(2)}, u32[]{:S(2)}) collective-permute-start(bf16[256,768]{1,0:T(8,128)(2,1)} %get-tuple-element.36), channel_id=1, source_target_pairs={{0,1},{1,0},{2,3},{3,2},{4,5},{5,4},{6,7},{7,6},{8,9},{9,8},{10,11... | collective-permute-start | bytes 1179656 | tf_op jit(solution)/shard_map/ppermute | solution.py:426
  95.9 10.5 %collective-permute-start.27 = (bf16[256,768]{1,0:T(8,128)(2,1)}, bf16[256,768]{1,0:T(8,128)(2,1)S(1)}, u32[]{:S(2)}, u32[]{:S(2)}) collective-permute-start(bf16[256,768]{1,0:T(8,128)(2,1)} %collective-permute-done.26.refs_13_), channel_id=1, source_target_pairs={{0,16},{16,0},{1,17},{17,1},{2,18},{18,2},{3,19},{19,3},{4,20},{20... | collective-permute-start | bytes 1179656 | tf_op jit(solution)/shard_map/ppermute | solution.py:430
  106.4 16.9 %collective-permute-start.28 = (bf16[256,768]{1,0:T(8,128)(2,1)S(1)}, bf16[256,768]{1,0:T(8,128)(2,1)S(1)}, u32[]{:S(2)}, u32[]{:S(2)}) collective-permute-start(bf16[256,768]{1,0:T(8,128)(2,1)S(1)} %collective-permute-done.25.refs_14_), channel_id=1, source_target_pairs={{0,16},{16,0},{1,17},{17,1},{2,18},{18,2},{3,19},{19,3},{4,20},{20... | collective-permute-start | bytes 1179656 | tf_op jit(solution)/shard_map/ppermute | solution.py:430
  112.3 11.0 %collective-permute-start.22 = (bf16[64,1024]{1,0:T(8,128)(2,1)S(1)}, bf16[64,1024]{1,0:T(8,128)(2,1)S(1)}, u32[]{:S(2)}, u32[]{:S(2)}) collective-permute-start(bf16[64,1024]{1,0:T(8,128)(2,1)S(1)} %pad_maximum_fusion.3.refs_0_), channel_id=1, source_target_pairs={{0,8},{2,10},{4,12},{6,14},{8,0},{10,2},{12,4},{14,6},{1,9},{3,11}... | collective-permute-start | bytes 393224 | tf_op jit(solution)/shard_map/ppermute | solution.py:434
  113.3 10.0 %collective-permute-start.23 = (bf16[64,1024]{1,0:T(8,128)(2,1)S(1)}, bf16[64,1024]{1,0:T(8,128)(2,1)S(1)}, u32[]{:S(2)}, u32[]{:S(2)}) collective-permute-start(bf16[64,1024]{1,0:T(8,128)(2,1)S(1)} %pad_maximum_fusion.3.refs_0_), channel_id=1, source_target_pairs={{0,12},{2,14},{4,8},{6,10},{8,4},{10,6},{12,0},{14,2},{1,13},{3,15... | collective-permute-start | bytes 393224 | tf_op jit(solution)/shard_map/ppermute | solution.py:434
  114.7 16.9 %collective-permute-start.30 = (bf16[2,384,512]{2,1,0:T(8,128)(2,1)S(1)}, bf16[2,384,512]{2,1,0:T(8,128)(2,1)S(1)}, u32[]{:S(2)}, u32[]{:S(2)}) collective-permute-start(bf16[2,384,512]{2,1,0:T(8,128)(2,1)S(1)} %copy-done.9), channel_id=1, source_target_pairs={{0,1},{1,0},{2,3},{3,2},{4,5},{5,4},{6,7},{7,6},{8,9},{9,8},{10,11... | collective-permute-start | bytes 2359304 | tf_op jit(solution)/shard_map/ppermute | solution.py:426
  136.0 9.3 %collective-permute-start.37 = (bf16[64,512]{1,0:T(8,128)(2,1)S(1)}, bf16[64,512]{1,0:T(8,128)(2,1)S(1)}, u32[]{:S(2)}, u32[]{:S(2)}) collective-permute-start(bf16[64,512]{1,0:T(8,128)(2,1)S(1)} %get-tuple-element.63), channel_id=1, source_target_pairs={{0,5},{1,4},{2,7},{3,6},{4,1},{5,0},{6,3},{7,2},{8,13},{9,12},{10,... | collective-permute-start | bytes 196616 | tf_op jit(solution)/shard_map/ppermute | solution.py:455
  138.2 9.6 %collective-permute-start.38 = (bf16[64,512]{1,0:T(8,128)(2,1)S(1)}, bf16[64,512]{1,0:T(8,128)(2,1)S(1)}, u32[]{:S(2)}, u32[]{:S(2)}) collective-permute-start(bf16[64,512]{1,0:T(8,128)(2,1)S(1)} %get-tuple-element.62), channel_id=1, source_target_pairs={{0,9},{1,8},{2,11},{3,10},{4,13},{5,12},{6,15},{7,14},{8,1},{9,0},... | collective-permute-start | bytes 196616 | tf_op jit(solution)/shard_map/ppermute | solution.py:455
  142.7 8.9 %collective-permute-start.33 = (bf16[64,512]{1,0:T(8,128)(2,1)S(1)}, bf16[64,512]{1,0:T(8,128)(2,1)S(1)}, u32[]{:S(2)}, u32[]{:S(2)}) collective-permute-start(bf16[64,512]{1,0:T(8,128)(2,1)S(1)} %get-tuple-element.66), channel_id=1, source_target_pairs={{0,8},{2,10},{4,12},{6,14},{8,0},{10,2},{12,4},{14,6},{1,9},{3,11}... | collective-permute-start | bytes 196616 | tf_op jit(solution)/shard_map/ppermute | solution.py:434
  (40 other events, 436.7 us)
